TPU v7x, 32 devices: a whole 2x2x4 slice. The times are simulated.
32 devices in a mesh: grp: 2 (over y), ka: 4 (over z), ga: 2 (over x), ba: 2 (over core).
Axes of the slice: x: 2, y: 2, z: 4, core: 2. Of those that a mesh axis runs over, the one named last changes fastest.
Arguments:
- start_vector: float32 [8, 2, 2, 16], P(('grp', 'ka')), parts along dimension 0, may hold values from -250 to 250
- valence_density: bfloat16 [8, 4, 2, 4, 4, 1536], P(('grp', 'ka'), None, None, 'ba', None, 'ga'), parts along dimension 0, may hold values from -1 to 1
- conduction_density: bfloat16 [8, 4, 2, 4, 4, 1536], P(('grp', 'ka'), None, None, None, None, 'ga'), parts along dimension 0, may hold values from -0.0546875 to 0.0546875
- screening: bfloat16 [8, 2, 1536, 1536], P(('grp', 'ka'), None, 'ga'), parts along dimension 0, may hold values from -0.109375 to 0.109375
- qpoint_map: int32 [4, 4], replicated, may hold values from 0 to 3, as said below
- slot_owner: int32 [4], replicated, may hold values from 0 to 3, each once
- band_pairs: int32 [16], replicated, may hold values from 0 to 15, each once
- valence_energy: float32 [8, 4], P(('grp', 'ka')), parts along dimension 0, may hold values from -1.5 to -0.3
- conduction_energy: float32 [8, 4], P(('grp', 'ka')), parts along dimension 0, may hold values from 0.3 to 1.5
Outputs:
- next_vector: float32 [8, 2, 2, 16], P(('grp', 'ka')), parts along dimension 0
- coefficients: float32 [4, 6], P('grp'), parts along dimension 0
There are 2 independent parts, one for each index of `grp`. A program takes and returns all parts, laid end to end along the dimension named above; an argument that names none is the same for every part. Nothing has to cross between parts.
Inputs may be any that keep to these rules, and one draw needn't show every extreme that they name: qpoint_map[k, k2] depends only on (k - k2) mod 4; each row names every q number once. `slot_owner`: every slot number appears exactly once. `band_pairs`: every code of the 4 x 4 band pairs appears exactly once.
All inputs are finite; a program needn't handle non-finite values.
Results may differ from a plain program's by a relative error of at most 0.0029.
Values may be sent and summed in bfloat16 or wider, within the bound.
No kernel may reach another device: no remote copies, remote signals or barrier semaphores. Data moves between devices by JAX's collectives and lax.ppermute only.
A program may use at most 64 MiB of HBM per device.

v0:
```python
import jax
import jax.numpy as jnp
from jax import lax
from jax.sharding import PartitionSpec as P

exact_mode = lax.Precision.HIGHEST
epsilon = 1e-06


def fold_pairs(density, chosen):
    dens_full = density.astype(jnp.float32)
    dens_real = dens_full[:, :, 0]
    dens_imag = dens_full[:, :, 1]
    vec_real = chosen[:, :, :, 0]
    vec_imag = chosen[:, :, :, 1]
    form = "rsvwg,rspwc->rspvcg"
    fold_real = jnp.einsum(form, dens_real, vec_real, precision=exact_mode) - jnp.einsum(
        form, dens_imag, vec_imag, precision=exact_mode
    )
    fold_imag = jnp.einsum(form, dens_real, vec_imag, precision=exact_mode) + jnp.einsum(
        form, dens_imag, vec_real, precision=exact_mode
    )
    return jnp.stack([fold_real, fold_imag], 5).astype(jnp.bfloat16)


def screen_slots(whole, screening):
    plane_count = whole.shape[-1]
    glocal = screening.shape[2]
    slot_rows = whole[:, 0]
    leading = slot_rows.shape[:-2]
    flattened = slot_rows.reshape(-1, plane_count)
    weights = screening[0].reshape(2 * glocal, plane_count)
    images = lax.dot_general(
        flattened, weights, (((1,), (1,)), ((), ())), preferred_element_type=jnp.float32
    )
    images = images.reshape(leading + (2, 2, glocal))
    real_part = images[..., 0, 0, :] - images[..., 1, 1, :]
    imag_part = images[..., 0, 1, :] + images[..., 1, 0, :]
    outputs = [jnp.stack([real_part, imag_part], -2)]
    return jnp.stack(outputs, 1)


def project_pairs(density, screened):
    dens_full = density.astype(jnp.float32)
    cond_real = dens_full[:, :, 0]
    cond_imag = dens_full[:, :, 1]
    scr_real = screened[..., 0, :]
    scr_imag = screened[..., 1, :]
    form = "rsdeg,rspveg->rpvd"
    kern_real = jnp.einsum(form, cond_real, scr_real, precision=exact_mode) + jnp.einsum(
        form, cond_imag, scr_imag, precision=exact_mode
    )
    kern_imag = jnp.einsum(form, cond_real, scr_imag, precision=exact_mode) - jnp.einsum(
        form, cond_imag, scr_real, precision=exact_mode
    )
    return jnp.stack([kern_real, kern_imag], 2)


def kpoint_total(values):
    return lax.psum(values, "ka")


def mean_square(vector, scale_count):
    local_sum = jnp.sum(vector * vector, axis=(0, 2, 3))
    return kpoint_total(local_sum[None, :])[0] / scale_count


def inner_product(left, right, scale_count):
    real_part = jnp.sum(
        left[:, :, 0] * right[:, :, 0] + left[:, :, 1] * right[:, :, 1], axis=(0, 2)
    )
    imag_part = jnp.sum(
        left[:, :, 0] * right[:, :, 1] - left[:, :, 1] * right[:, :, 0], axis=(0, 2)
    )
    totals = kpoint_total(jnp.stack([real_part, imag_part], 0)) / scale_count
    return (totals[0], totals[1])


def scale_complex(coef_real, coef_imag, vector):
    vec_real = vector[:, :, 0]
    vec_imag = vector[:, :, 1]
    real_part = coef_real[None, :, None] * vec_real - coef_imag[None, :, None] * vec_imag
    imag_part = coef_real[None, :, None] * vec_imag + coef_imag[None, :, None] * vec_real
    return jnp.stack([real_part, imag_part], 2)


def local(
    start_vector,
    valence_density,
    conduction_density,
    screening,
    qpoint_map,
    slot_owner,
    band_pairs,
    valence_energy,
    conduction_energy,
):
    kblock = start_vector.shape[0]
    pair_count = start_vector.shape[3]
    kpoint_count = qpoint_map.shape[0]
    slot_count = slot_owner.shape[0]
    val_count = valence_energy.shape[1]
    cond_count = conduction_energy.shape[1]
    scale_count = float(kpoint_count * pair_count)
    first_row = lax.axis_index("ka") * kblock
    code_pick = (band_pairs[:, None] == jnp.arange(pair_count, dtype=jnp.int32)[None, :]).astype(
        jnp.float32
    )
    val_pick = (
        (band_pairs // cond_count)[:, None] == jnp.arange(val_count, dtype=jnp.int32)[None, :]
    ).astype(jnp.float32)
    cond_pick = (
        (band_pairs % cond_count)[:, None] == jnp.arange(cond_count, dtype=jnp.int32)[None, :]
    ).astype(jnp.float32)
    energy = jnp.dot(conduction_energy, cond_pick.T, precision=exact_mode) - jnp.dot(
        valence_energy, val_pick.T, precision=exact_mode
    )
    energy = energy[:, None, None, :]
    slot_numbers = jnp.arange(slot_count, dtype=jnp.int32)
    kpoint_numbers = jnp.arange(kpoint_count, dtype=jnp.int32)
    slots = jnp.sum(
        jnp.where(
            qpoint_map[:, :, None] == slot_numbers[None, None, :], slot_owner[None, None, :], 0
        ),
        axis=2,
    )
    partner = jnp.sum(
        jnp.where(
            slots[:, :, None] == slot_numbers[None, None, :], kpoint_numbers[None, :, None], 0
        ),
        axis=1,
    )
    local_partner = lax.dynamic_slice_in_dim(partner, first_row, kblock, 0)
    block_rows = jnp.arange(kblock, dtype=jnp.int32)[:, None]
    valence_sorted = valence_density[block_rows, local_partner]
    conduction_sorted = conduction_density[block_rows, local_partner]

    def kernel_apply(vector):
        pair_form = jnp.einsum("kpxb,bc->kpxc", vector, code_pick, precision=exact_mode)
        pair_form = pair_form.reshape(vector.shape[0], vector.shape[1], 2, val_count, cond_count)
        every_vector = lax.all_gather(pair_form, "ka", axis=0, tiled=True)
        chosen = jnp.take(every_vector, local_partner, axis=0)
        folded = fold_pairs(valence_sorted, chosen)
        arrived = lax.all_to_all(folded, "ka", split_axis=1, concat_axis=0, tiled=True)
        whole = lax.all_gather(arrived, "ga", axis=6, tiled=True)
        screened = screen_slots(whole, screening)
        returned = lax.all_to_all(screened, "ka", split_axis=0, concat_axis=1, tiled=True)
        partial_value = project_pairs(conduction_sorted, returned)
        summed = lax.psum(partial_value, "ga")
        complete = lax.all_gather(summed, "ba", axis=3, tiled=True)
        flattened = complete.reshape(kblock, complete.shape[1], 2, pair_count)
        return jnp.einsum("kpxc,bc->kpxb", flattened, code_pick, precision=exact_mode)

    def hamiltonian(vector):
        return energy * vector - kernel_apply(vector)

    norm_start = jnp.sqrt(mean_square(start_vector, scale_count) + epsilon)
    first_vector = start_vector / norm_start[None, :, None, None]
    first_image = hamiltonian(first_vector)
    alpha_real, alpha_imag = inner_product(first_vector, first_image, scale_count)
    first_resid = first_image - scale_complex(alpha_real, alpha_imag, first_vector)
    beta_one = jnp.sqrt(mean_square(first_resid, scale_count) + epsilon)
    second_vector = first_resid / beta_one[None, :, None, None]
    second_image = hamiltonian(second_vector)
    gamma_real, gamma_imag = inner_product(second_vector, second_image, scale_count)
    second_resid = (
        second_image
        - scale_complex(gamma_real, gamma_imag, second_vector)
        - beta_one[None, :, None, None] * first_vector
    )
    beta_two = jnp.sqrt(mean_square(second_resid, scale_count) + epsilon)
    next_vector = second_resid / beta_two[None, :, None, None]
    coefficients = jnp.stack(
        [alpha_real, alpha_imag, gamma_real, gamma_imag, beta_one, beta_two], 1
    )
    return (next_vector, coefficients)


def solution(mesh):
    in_specs = (
        P(("grp", "ka"), None, None, None),
        P(("grp", "ka"), None, None, "ba", None, "ga"),
        P(("grp", "ka"), None, None, None, None, "ga"),
        P(("grp", "ka"), None, "ga", None),
        P(),
        P(),
        P(),
        P(("grp", "ka"), None),
        P(("grp", "ka"), None),
    )
    out_specs = (P(("grp", "ka"), None, None, None), P("grp", None))
    return jax.shard_map(local, mesh=mesh, in_specs=in_specs, out_specs=out_specs, check_vma=False)
```

profile of v0, /device:TPU:0, one launch (start us, length us, event | category | flops | bytes accessed | tf_op | source)
XLA Modules:
  0.0 180.8 jit_solution(16948619336271918317)
XLA Ops:
  0.7 1.0 select_reduce_fusion.1
  1.8 0.8 multiply_reduce_fusion.2
  2.5 13.4 %psum.49 = f32[1,2]{1,0:T(1,128)S(1)} all-reduce(f32[1,2]{1,0:T(1,128)S(1)} %bitcast.363), channel_id=1, replica_groups=mesh['grp'=2,'ka'=4,'ga'=2,'ba'=2] {'ka'}, use_global_device_ids=true, to_apply=%region_1.2 | all-reduce | flops 2 | bytes 16 | tf_op jit(solution)/shard_map/psum | solution.py:60
  16.0 0.8 broadcast_divide_fusion.2
  16.7 0.7 compare_bitcast_fusion
  17.5 0.2 fusion.45
  17.7 13.1 %all-gather = f32[8,2,4,4]{3,2,1,0:T(4,128)S(1)} all-gather(f32[2,2,4,4]{3,2,1,0:T(4,128)S(1)} %copy.99), channel_id=2, replica_groups=mesh['grp'=2,'ka'=4,'ga'=2,'ba'=2] {'ka'}, dimensions={0}, use_global_device_ids=true | all-gather | bytes 1280 | tf_op jit(solution)/shard_map/all_gather | solution.py:141
  30.8 1.5 gather_fusion
  32.4 0.6 gather_fusion.2
  33.1 0.4 fusion.31
  33.5 0.4 fusion.32
  33.8 0.4 fusion.11
  34.2 0.4 fusion.10
  34.6 0.1 pad_maximum_fusion
  34.8 9.2 %all_to_all.48 = bf16[1,4,2,2,4,2,768]{6,4,3,2,5,0,1:T(4,128)(2,1)S(1)} all-to-all(bf16[1,4,2,2,4,2,768]{6,4,3,2,5,0,1:T(4,128)(2,1)S(1)} %copy.105), channel_id=1, replica_groups=mesh['grp'=2,'ka'=4,'ga'=2,'ba'=2] {'ka'}, dimensions={1} | all-to-all | bytes 393216 | tf_op jit(solution)/shard_map/all_to_all | solution.py:144
  44.1 6.3 %all-gather.1 = bf16[1,4,2,2,4,2,1536]{6,4,5,3,2,1,0:T(4,128)(2,1)S(1)} all-gather(bf16[1,4,2,2,4,2,768]{6,4,5,3,2,1,0:T(4,128)(2,1)S(1)} %copy.106), channel_id=3, replica_groups=mesh['grp'=2,'ka'=4,'ga'=2,'ba'=2] {'ga'}, dimensions={6}, use_global_device_ids=true | all-gather | bytes 589824 | tf_op jit(solution)/shard_map/all_gather | solution.py:145
  50.4 4.2 %fusion.2 = f32[4,2,2,4,2,2,768]{6,3,5,4,2,1,0:T(4,128)S(1)} fusion(bf16[1,2,768,1536]{3,2,1,0:T(8,128)(2,1)} %param.14, bf16[1,4,2,2,4,2,1536]{6,4,5,3,2,1,0:T(4,128)(2,1)S(1)} %all-gather.1), kind=kOutput, calls=%fused_computation.6 | convolution fusion | flops 603979776 | bytes 5898240 | tf_op jit(solution)/shard_map/dot_general | solution.py:33
  54.8 0.1 maximum_bitcast_fusion
  54.9 0.8 copy.109
  55.7 3.5 %all-to-all-start.1 = ((f32[4,1,2,2,4,2,768]{6,4,3,2,5,1,0:T(4,128)}), f32[4,1,2,2,4,2,768]{6,4,3,2,5,1,0:T(4,128)S(1)}, u32[]{:S(2)}, u32[]{:S(2)}) async-start(f32[4,1,2,2,4,2,768]{6,4,3,2,5,1,0:T(4,128)} %copy.109), calls=%async_computation.1 | async-start | bytes 786432 | tf_op jit(solution)/shard_map/all_to_all | solution.py:147
  59.1 0.7 gather_fusion.1
  60.0 0.2 convolution_bitcast_fusion.11
  60.2 0.2 fusion.14
  60.4 7.6 %all-to-all-done.1 = f32[4,1,2,2,4,2,768]{6,4,3,2,5,1,0:T(4,128)S(1)} async-done(((f32[4,1,2,2,4,2,768]{6,4,3,2,5,1,0:T(4,128)}), f32[4,1,2,2,4,2,768]{6,4,3,2,5,1,0:T(4,128)S(1)}, u32[]{:S(2)}, u32[]{:S(2)}) %all-to-all-start.1) | async-done | bytes 393248 | tf_op jit(solution)/shard_map/all_to_all | solution.py:147
  68.0 0.2 copy.183
  68.2 1.2 convolution_bitcast_fusion.8
  69.3 1.2 convolution_bitcast_fusion.6
  70.5 1.2 fusion.16
  71.7 1.2 fusion.18
  72.9 4.9 %psum.50 = f32[1,2,2,2,4]{4,3,1,2,0:T(2,128)S(1)} all-reduce(f32[1,2,2,2,4]{4,3,1,2,0:T(2,128)S(1)} %pad_maximum_fusion.2), channel_id=1, replica_groups=mesh['grp'=2,'ka'=4,'ga'=2,'ba'=2] {'ga'}, use_global_device_ids=true, to_apply=%region_4.6 | all-reduce | flops 32 | bytes 256 | tf_op jit(solution)/shard_map/psum | solution.py:149
  77.8 1.8 all_gather.20
  79.7 0.2 fusion.12
  79.9 0.1 add_reduce_fusion.1
  80.0 9.8 %psum.51 = f32[2,2]{1,0:T(2,128)S(1)} all-reduce(f32[2,2]{1,0:T(2,128)S(1)} %pad_maximum_fusion.4), channel_id=1, replica_groups=mesh['grp'=2,'ka'=4,'ga'=2,'ba'=2] {'ka'}, use_global_device_ids=true, to_apply=%region_7.9 | all-reduce | flops 4 | bytes 32 | tf_op jit(solution)/shard_map/psum | solution.py:60
  90.0 0.1 multiply_reduce_fusion.1
  90.1 8.9 %psum.52 = f32[1,2]{1,0:T(1,128)S(1)} all-reduce(f32[1,2]{1,0:T(1,128)S(1)} %bitcast.364), channel_id=1, replica_groups=mesh['grp'=2,'ka'=4,'ga'=2,'ba'=2] {'ka'}, use_global_device_ids=true, to_apply=%region_9.11 | all-reduce | flops 2 | bytes 16 | tf_op jit(solution)/shard_map/psum | solution.py:60
  99.1 0.2 fusion.43
  99.3 13.1 %all-gather.2 = f32[8,2,4,4]{3,2,1,0:T(4,128)S(1)} all-gather(f32[2,2,4,4]{3,2,1,0:T(4,128)S(1)} %copy.114), channel_id=4, replica_groups=mesh['grp'=2,'ka'=4,'ga'=2,'ba'=2] {'ka'}, dimensions={0}, use_global_device_ids=true | all-gather | bytes 1280 | tf_op jit(solution)/shard_map/all_gather | solution.py:141
  112.4 0.6 gather_fusion.3
  113.1 0.4 fusion.33
  113.5 0.4 fusion.34
  113.8 0.4 fusion.9
  114.2 0.4 fusion.8
  114.6 0.1 pad_maximum_fusion.1
  114.8 9.3 %all_to_all.49 = bf16[1,4,2,2,4,2,768]{6,4,3,2,5,0,1:T(4,128)(2,1)S(1)} all-to-all(bf16[1,4,2,2,4,2,768]{6,4,3,2,5,0,1:T(4,128)(2,1)S(1)} %copy.119), channel_id=1, replica_groups=mesh['grp'=2,'ka'=4,'ga'=2,'ba'=2] {'ka'}, dimensions={1} | all-to-all | bytes 393216 | tf_op jit(solution)/shard_map/all_to_all | solution.py:144
  124.2 6.3 %all-gather.3 = bf16[1,4,2,2,4,2,1536]{6,4,5,3,2,1,0:T(4,128)(2,1)S(1)} all-gather(bf16[1,4,2,2,4,2,768]{6,4,5,3,2,1,0:T(4,128)(2,1)S(1)} %copy.120), channel_id=5, replica_groups=mesh['grp'=2,'ka'=4,'ga'=2,'ba'=2] {'ga'}, dimensions={6}, use_global_device_ids=true | all-gather | bytes 589824 | tf_op jit(solution)/shard_map/all_gather | solution.py:145
  130.6 4.2 %fusion = f32[4,2,2,4,2,2,768]{6,3,5,4,2,1,0:T(4,128)S(1)} fusion(bf16[1,2,768,1536]{3,2,1,0:T(8,128)(2,1)} %param.14, bf16[1,4,2,2,4,2,1536]{6,4,5,3,2,1,0:T(4,128)(2,1)S(1)} %all-gather.3), kind=kOutput, calls=%fused_computation.4 | convolution fusion | flops 603979776 | bytes 5898240 | tf_op jit(solution)/shard_map/dot_general | solution.py:33
  135.0 0.8 copy.123
  135.8 3.6 %all-to-all-start.3 = ((f32[4,1,2,2,4,2,768]{6,4,3,2,5,1,0:T(4,128)}), f32[4,1,2,2,4,2,768]{6,4,3,2,5,1,0:T(4,128)S(1)}, u32[]{:S(2)}, u32[]{:S(2)}) async-start(f32[4,1,2,2,4,2,768]{6,4,3,2,5,1,0:T(4,128)} %copy.123), calls=%async_computation.3 | async-start | bytes 786432 | tf_op jit(solution)/shard_map/all_to_all | solution.py:147
  139.6 8.5 %all-to-all-done.3 = f32[4,1,2,2,4,2,768]{6,4,3,2,5,1,0:T(4,128)S(1)} async-done(((f32[4,1,2,2,4,2,768]{6,4,3,2,5,1,0:T(4,128)}), f32[4,1,2,2,4,2,768]{6,4,3,2,5,1,0:T(4,128)S(1)}, u32[]{:S(2)}, u32[]{:S(2)}) %all-to-all-start.3) | async-done | bytes 393248 | tf_op jit(solution)/shard_map/all_to_all | solution.py:147
  148.1 0.2 copy.182
  148.3 1.2 convolution_bitcast_fusion.3
  149.5 1.2 convolution_bitcast_fusion.1
  150.6 1.2 fusion.20
  151.8 1.2 fusion.22
  153.0 4.9 %psum.53 = f32[1,2,2,2,4]{4,3,1,2,0:T(2,128)S(1)} all-reduce(f32[1,2,2,2,4]{4,3,1,2,0:T(2,128)S(1)} %pad_maximum_fusion.3), channel_id=1, replica_groups=mesh['grp'=2,'ka'=4,'ga'=2,'ba'=2] {'ga'}, use_global_device_ids=true, to_apply=%region_10.12 | all-reduce | flops 32 | bytes 256 | tf_op jit(solution)/shard_map/psum | solution.py:149
  158.0 1.8 all_gather.23
  159.8 0.2 fusion.13
  160.0 0.1 add_reduce_fusion
  160.3 9.8 %psum.54 = f32[2,2]{1,0:T(2,128)S(1)} all-reduce(f32[2,2]{1,0:T(2,128)S(1)} %pad_maximum_fusion.5), channel_id=1, replica_groups=mesh['grp'=2,'ka'=4,'ga'=2,'ba'=2] {'ka'}, use_global_device_ids=true, to_apply=%region_13.15 | all-reduce | flops 4 | bytes 32 | tf_op jit(solution)/shard_map/psum | solution.py:60
  170.1 0.2 multiply_reduce_fusion
  170.3 8.9 %psum.55 = f32[1,2]{1,0:T(1,128)S(1)} all-reduce(f32[1,2]{1,0:T(1,128)S(1)} %bitcast.362), channel_id=1, replica_groups=mesh['grp'=2,'ka'=4,'ga'=2,'ba'=2] {'ka'}, use_global_device_ids=true, to_apply=%region_15.17 | all-reduce | flops 2 | bytes 16 | tf_op jit(solution)/shard_map/psum | solution.py:60
  179.5 0.7 broadcast_divide_fusion
  180.2 0.7 stack.109
  (58 shorter events, 2.1 us)
Async XLA Ops:
  0.6 58.5 %copy-start = (bf16[1,4,2,4,4,768]{5,4,3,2,1,0:T(4,128)(2,1)S(1)}, bf16[1,4,2,4,4,768]{5,4,3,2,1,0:T(4,128)(2,1)}, u32[]{:S(2)}) copy-start(bf16[1,4,2,4,4,768]{5,4,3,2,1,0:T(4,128)(2,1)} %param.13) | copy-start | bytes 589828
  50.4 9.5 %copy-start.2 = (s32[16]{0:T(128)S(1)}, s32[16]{0:T(128)}, u32[]{:S(2)}) copy-start(s32[16]{0:T(128)} %param.17) | copy-start | bytes 196
  50.4 9.5 %copy-start.3 = (f32[1,4]{1,0:T(1,128)S(1)}, f32[1,4]{1,0:T(1,128)}, u32[]{:S(2)}) copy-start(f32[1,4]{1,0:T(1,128)} %param.19) | copy-start | bytes 52
  50.4 9.7 %copy-start.4 = (f32[1,4]{1,0:T(1,128)S(1)}, f32[1,4]{1,0:T(1,128)}, u32[]{:S(2)}) copy-start(f32[1,4]{1,0:T(1,128)} %param.18) | copy-start | bytes 52
  55.7 12.3 %all-to-all-start.1 = ((f32[4,1,2,2,4,2,768]{6,4,3,2,5,1,0:T(4,128)}), f32[4,1,2,2,4,2,768]{6,4,3,2,5,1,0:T(4,128)S(1)}, u32[]{:S(2)}, u32[]{:S(2)}) async-start(f32[4,1,2,2,4,2,768]{6,4,3,2,5,1,0:T(4,128)} %copy.109), calls=%async_computation.1 | async-start | bytes 786432 | tf_op jit(solution)/shard_map/all_to_all | solution.py:147
  134.8 35.4 %copy-start.1 = (f32[1,2,2,16]{3,2,1,0:T(2,128)S(1)}, f32[1,2,2,16]{3,2,1,0:T(2,128)}, u32[]{:S(2)}) copy-start(f32[1,2,2,16]{3,2,1,0:T(2,128)} %param.11) | copy-start | bytes 772
  135.8 12.3 %all-to-all-start.3 = ((f32[4,1,2,2,4,2,768]{6,4,3,2,5,1,0:T(4,128)}), f32[4,1,2,2,4,2,768]{6,4,3,2,5,1,0:T(4,128)S(1)}, u32[]{:S(2)}, u32[]{:S(2)}) async-start(f32[4,1,2,2,4,2,768]{6,4,3,2,5,1,0:T(4,128)} %copy.123), calls=%async_computation.3 | async-start | bytes 786432 | tf_op jit(solution)/shard_map/all_to_all | solution.py:147
where the time goes:
time: 181 us
  blocking collectives  122 us (67%)
  matrix products  22 us (12%)
  waiting for transfers between devices  16.1 us (9%)
  local copies, waits for them, and re-layouts  7.21 us (4%)
  starting transfers between devices  7.1 us (4%)
  other arithmetic  5.69 us (3%)
    psum x5, blocking collectives, kpoint_total(): return lax.psum(values, 'ka')  50.8 us
    all_gather x2, blocking collectives, kernel_apply(): every_vector = lax.all_gather(pair_form, 'ka', axis=0, tiled=True)  26.3 us
    all_to_all x2, blocking collectives, kernel_apply(): lax.all_to_all(folded, 'ka', split_axis=1, concat_axis=0, tiled=True)  18.5 us
    all_to_all x2, waiting for transfers between devices, kernel_apply(): lax.all_to_all(screened, 'ka', split_axis=0, concat_axis=1, tiled=True)  16.1 us
    all_gather x2, blocking collectives, kernel_apply(): whole = lax.all_gather(arrived, 'ga', axis=6, tiled=True)  12.7 us
    psum x2, blocking collectives, kernel_apply(): summed = lax.psum(partial_value, 'ga')  9.89 us
    dot_general x2, matrix products, screen_slots(): lax.dot_general(flattened, weights, (((1,), (1,)), ((), ())), preferred_e...  8.39 us
    all_to_all x2, starting transfers between devices, kernel_apply(): lax.all_to_all(screened, 'ka', split_axis=0, concat_axis=1, tiled=True)  7.1 us
  transfers between devices with their start and end apart: 2, of which 2 were waited for; matrix products, arithmetic and copies ran while one was open for 1% of the time, Pallas kernels for 0%

commit v1 on v0

v1 whole, which is shorter than its diff:
```python
import functools

import jax
import jax.numpy as jnp
from jax import lax
from jax.experimental import pallas as pl
from jax.experimental.pallas import tpu as pltpu
from jax.sharding import PartitionSpec as P

EPSILON = 1e-06
EXACT = lax.Precision.HIGHEST
VMEM_LIMIT = 56 * 1024 * 1024

vmem = pl.BlockSpec(memory_space=pltpu.VMEM)
smem = pl.BlockSpec(memory_space=pltpu.SMEM)
anywhere = pl.BlockSpec(memory_space=pl.ANY)


def iota(shape, axis):
    return lax.broadcasted_iota(jnp.int32, shape, axis)


def split(values):
    high = values.astype(jnp.bfloat16)
    low = (values - high.astype(jnp.float32)).astype(jnp.bfloat16)
    return high, low


def route_kernel(ka, qmap, owner, valence, conduction, *rest):
    val_out, cond_out = rest[:ka], rest[ka : 2 * ka]
    partner, sems = rest[2 * ka :]
    me = lax.axis_index("ka")
    count = valence.shape[0]

    def note(k2, carry):
        partner[owner[qmap[me, k2]]] = k2
        return carry

    lax.fori_loop(0, count, note, 0)
    copies = []
    for j in range(ka):
        k2 = partner[lax.rem(me + j, ka)]
        copies.append(pltpu.make_async_copy(valence.at[k2], val_out[j], sems.at[0, j]))
        copies.append(pltpu.make_async_copy(conduction.at[k2], cond_out[j], sems.at[1, j]))
    for copy in copies:
        copy.start()
    for copy in copies:
        copy.wait()


def route(ka, qmap, owner, valence, conduction):
    val_shape = jax.ShapeDtypeStruct(valence.shape[1:], valence.dtype)
    cond_shape = jax.ShapeDtypeStruct(conduction.shape[1:], conduction.dtype)
    outs = pl.pallas_call(
        functools.partial(route_kernel, ka),
        out_shape=[val_shape] * ka + [cond_shape] * ka,
        in_specs=[smem, smem, anywhere, anywhere],
        out_specs=[anywhere] * (2 * ka),
        scratch_shapes=[pltpu.SMEM((owner.shape[0],), jnp.int32), pltpu.SemaphoreType.DMA((2, ka))],
        name="route",
    )(qmap, owner, valence, conduction)
    return outs[:ka], outs[ka:]


def screen_kernel(ka, ga, dims, *refs):
    vloc, val_count, cond_count = dims
    band_pairs, val_energy, cond_energy, start, screening = refs[:5]
    val_in = refs[5 : 5 + ka * ga]
    cond_in = refs[5 + ka * ga : 5 + ka * ga + ka]
    out = refs[5 + ka * ga + ka]
    near, far, cond = refs[5 + ka * ga + ka + 1 :]
    me = lax.axis_index("ka")
    mine = lax.axis_index("ga")
    half = lax.axis_index("ba")
    pairs = vloc * val_count
    block = 2 * pairs
    rows = ka * block
    codes = val_count * cond_count
    lanes = 2 * ka * codes
    cond_rows = cond_count * cond_count

    for r in range(ga):
        place = lax.rem(mine + ga - r, ga)
        for j in range(ka):
            piece = val_in[j * ga + r][...]
            wide = piece.astype(jnp.float32)
            turned = jnp.concatenate([-wide[pairs:], wide[:pairs]], 0).astype(jnp.bfloat16)
            near[place, j * block : (j + 1) * block, :] = piece
            near[place, rows + j * block : rows + (j + 1) * block, :] = turned
            far[place, j * block : (j + 1) * block, :] = turned
            far[place, rows + j * block : rows + (j + 1) * block, :] = -piece
    for j in range(ka):
        cond[j * 2 * cond_rows : (j + 1) * 2 * cond_rows, :] = cond_in[j][...]

    width = near.shape[2]
    fields = None
    for g in range(ga):
        for part, other in ((0, near), (1, far)):
            term = lax.dot_general(
                screening[part, :, g * width : (g + 1) * width],
                other[g],
                (((1,), (1,)), ((), ())),
                preferred_element_type=jnp.float32,
            )
            fields = term if fields is None else fields + term
    high, low = split(fields)
    cond_all = cond[...]
    crossed = jnp.dot(cond_all, high, preferred_element_type=jnp.float32) + jnp.dot(
        cond_all, low, preferred_element_type=jnp.float32
    )
    lane = iota((cond_rows, 2 * rows), 1)
    lane_j = lane % rows // block
    turned_lane = lane // rows
    kernel = jnp.zeros((cond_rows, 2 * rows), jnp.float32)
    for j in range(ka):
        base = j * 2 * cond_rows
        same = lane_j == j
        kernel = kernel + jnp.where(same & (turned_lane == 0), crossed[base : base + cond_rows], 0.0)
        kernel = kernel - jnp.where(
            same & (turned_lane == 1), crossed[base + cond_rows : base + 2 * cond_rows], 0.0
        )

    row = iota((2 * rows, lanes), 0)
    col = iota((2 * rows, lanes), 1)
    k_of_row = lax.rem(me + ka - row % rows // block, ka)
    want = (
        (row % block // pairs) * (ka * codes)
        + k_of_row * codes
        + (half * vloc + row % pairs // val_count) * cond_count
    )
    joined = (col - want >= 0) & (col - want < cond_count)
    kernel_high, kernel_low = split(kernel)
    stacked = jnp.concatenate([kernel_high, kernel_low], 0)
    same_c = iota((cond_rows, lanes), 0) // cond_count == iota((cond_rows, lanes), 1) % cond_count
    spread = []
    for v2 in range(val_count):
        pick = jnp.where(joined & (row % val_count == v2), 1.0, 0.0).astype(jnp.bfloat16)
        both = jnp.dot(stacked, pick, preferred_element_type=jnp.float32)
        spread.append(jnp.where(same_c, both[:cond_rows] + both[cond_rows:], 0.0))
    spread = jnp.concatenate(spread, 0)
    out_row = iota((codes, val_count * cond_rows), 0)
    out_col = iota((codes, val_count * cond_rows), 1)
    fold = (out_row // cond_count == out_col // cond_rows) & (
        out_row % cond_count == out_col % cond_count
    )
    fold = jnp.where(fold, 1.0, 0.0).astype(jnp.bfloat16)
    spread_high, spread_low = split(spread)
    out[0:codes, :] = jnp.dot(fold, spread_high, preferred_element_type=jnp.float32) + jnp.dot(
        fold, spread_low, preferred_element_type=jnp.float32
    )

    first = jnp.where((mine == 0) & (half == 0), 1.0, 0.0)
    band_row = iota((codes, lanes), 0)
    band_lane = iota((codes, lanes), 1)
    code = jnp.zeros((codes, lanes), jnp.int32)
    for b in range(codes):
        code = jnp.where(band_row == b, band_pairs[b], code)
    vectors = jnp.zeros((start.shape[1], lanes), jnp.float32)
    for part in range(2):
        spot = part * ka * codes + me * codes
        pick = jnp.where(band_lane == spot + code, first, 0.0)
        vectors = vectors + jnp.dot(start[0, :, part, :], pick, precision=EXACT)
    lane = iota((1, lanes), 1)
    energy = jnp.zeros((1, lanes), jnp.float32)
    for c in range(cond_count):
        energy = jnp.where(lane % cond_count == c, cond_energy[0, c], energy)
    for v in range(val_count):
        energy = energy - jnp.where(lane % codes // cond_count == v, val_energy[0, v], 0.0)
    energy = jnp.where(lane % (ka * codes) // codes == me, energy * first, 0.0)
    npol = start.shape[1]
    out[codes : codes + npol, :] = vectors
    out[codes + npol : codes + npol + 1, :] = energy


def screen(ka, ga, dims, band_pairs, val_energy, cond_energy, start, screening, val_blocks, cond_blocks):
    vloc, val_count, cond_count = dims
    codes = val_count * cond_count
    rows = ka * 2 * vloc * val_count
    width = screening.shape[2] // ga
    glocal = screening.shape[1]
    return pl.pallas_call(
        functools.partial(screen_kernel, ka, ga, dims),
        out_shape=jax.ShapeDtypeStruct((codes + 8, 2 * ka * codes), jnp.float32),
        in_specs=[smem, smem, smem] + [vmem] * (2 + len(val_blocks) + len(cond_blocks)),
        out_specs=vmem,
        scratch_shapes=[
            pltpu.VMEM((ga, 2 * rows, width), jnp.bfloat16),
            pltpu.VMEM((ga, 2 * rows, width), jnp.bfloat16),
            pltpu.VMEM((ka * 2 * cond_count * cond_count, glocal), jnp.bfloat16),
        ],
        compiler_params=pltpu.CompilerParams(vmem_limit_bytes=VMEM_LIMIT),
        name="screen",
    )(band_pairs, val_energy, cond_energy, start, screening, *val_blocks, *cond_blocks)


def haydock_kernel(ka, scale_count, npol, qmap, owner, band_pairs, pieces, next_out, coef_out, whole, matrix):
    me = lax.axis_index("ka")
    copies = pieces.shape[1]
    lanes = pieces.shape[3]
    codes = pieces.shape[2] - 8
    mid = lanes // 2
    for s in range(ka):
        total = pieces[s, 0]
        for other in range(1, copies):
            total = total + pieces[s, other]
        whole[s] = total
    extras = whole[0, codes:, :]
    for s in range(1, ka):
        extras = extras + whole[s, codes:, :]
    lane_k = iota((codes, lanes), 1) % mid // codes
    sign = jnp.where(iota((1, lanes), 1) < mid, -1.0, 1.0)
    for k2 in range(ka):
        block = jnp.zeros((codes, lanes), jnp.float32)
        for back in range(ka):
            slot = owner[qmap[0, back]]
            k = (k2 - back) % ka
            block = jnp.where(lane_k == k, whole[slot, :codes, :], block)
        matrix[k2 * codes : (k2 + 1) * codes, :] = block
        matrix[mid + k2 * codes : mid + (k2 + 1) * codes, :] = sign * pltpu.roll(block, mid, 1)
    full = matrix[...]
    energy = extras[npol : npol + 1]
    start = extras[:npol]

    def mean(values):
        return jnp.sum(values, axis=1, keepdims=True) / scale_count

    def norm(vector):
        return jnp.sqrt(mean(vector * vector) + EPSILON)

    def swap(vector):
        return pltpu.roll(vector, mid, 1)

    def hamiltonian(vector):
        return energy * vector - jnp.dot(vector, full, precision=EXACT)

    def inner(left, right):
        return mean(left * right), mean(-sign * left * swap(right))

    def times(real, imag, vector):
        return real * vector + imag * (sign * swap(vector))

    first = start / norm(start)
    first_image = hamiltonian(first)
    alpha_real, alpha_imag = inner(first, first_image)
    first_resid = first_image - times(alpha_real, alpha_imag, first)
    beta_one = norm(first_resid)
    second = first_resid / beta_one
    second_image = hamiltonian(second)
    gamma_real, gamma_imag = inner(second, second_image)
    second_resid = second_image - times(gamma_real, gamma_imag, second) - beta_one * first
    beta_two = norm(second_resid)
    following = second_resid / beta_two

    coef_lane = iota(coef_out.shape, 1)
    coefs = jnp.zeros(coef_out.shape, jnp.float32)
    for at, value in enumerate((alpha_real, alpha_imag, gamma_real, gamma_imag, beta_one, beta_two)):
        coefs = jnp.where(coef_lane == at, value, coefs)
    coef_out[...] = coefs
    band = iota((lanes, codes), 1)
    code = jnp.zeros((lanes, codes), jnp.int32)
    for b in range(codes):
        code = jnp.where(band == b, band_pairs[b], code)
    row = iota((lanes, codes), 0)
    for part in range(2):
        pick = jnp.where(row == part * mid + me * codes + code, 1.0, 0.0)
        next_out[0, :, part, :] = jnp.dot(following, pick, precision=EXACT)


def haydock(ka, scale_count, npol, qmap, owner, band_pairs, pieces):
    lanes = pieces.shape[3]
    codes = pieces.shape[2] - 8
    return pl.pallas_call(
        functools.partial(haydock_kernel, ka, scale_count, npol),
        out_shape=[
            jax.ShapeDtypeStruct((1, npol, 2, codes), jnp.float32),
            jax.ShapeDtypeStruct((npol, 6), jnp.float32),
        ],
        in_specs=[smem, smem, smem, vmem],
        out_specs=[vmem, vmem],
        scratch_shapes=[
            pltpu.VMEM((ka, codes + 8, lanes), jnp.float32),
            pltpu.VMEM((lanes, lanes), jnp.float32),
        ],
        compiler_params=pltpu.CompilerParams(vmem_limit_bytes=VMEM_LIMIT),
        name="haydock",
    )(qmap, owner, band_pairs, pieces)


def local(
    ka,
    ga,
    start_vector,
    valence_density,
    conduction_density,
    screening,
    qpoint_map,
    slot_owner,
    band_pairs,
    valence_energy,
    conduction_energy,
):
    npol = start_vector.shape[1]
    pair_count = start_vector.shape[3]
    kcount, vloc, val_count = qpoint_map.shape[0], valence_density.shape[3], valence_density.shape[4]
    cond_count = conduction_density.shape[3]
    glocal = valence_density.shape[5]
    valence = valence_density.reshape(kcount, 2 * vloc * val_count, glocal)
    conduction = conduction_density.reshape(kcount, 2 * cond_count * cond_count, glocal)
    val_out, cond_out = route(ka, qpoint_map, slot_owner, valence, conduction)

    def shifted(value, axis, size, by):
        if by == 0:
            return value
        return lax.ppermute(value, axis, [(i, (i + by) % size) for i in range(size)])

    arrived = [shifted(val_out[j], "ka", ka, j) for j in range(ka)]
    val_blocks = [shifted(arrived[j], "ga", ga, r) for j in range(ka) for r in range(ga)]
    cond_blocks = [shifted(cond_out[j], "ka", ka, j) for j in range(ka)]
    piece = screen(
        ka,
        ga,
        (vloc, val_count, cond_count),
        band_pairs,
        valence_energy,
        conduction_energy,
        start_vector,
        screening[0],
        val_blocks,
        cond_blocks,
    )
    pieces = lax.all_gather(piece, ("ka", "ga", "ba"), axis=0, tiled=False)
    pieces = pieces.reshape((ka, -1) + piece.shape)
    scale_count = float(kcount * pair_count)
    return tuple(haydock(ka, scale_count, npol, qpoint_map, slot_owner, band_pairs, pieces))


def solution(mesh):
    in_specs = (
        P(("grp", "ka"), None, None, None),
        P(("grp", "ka"), None, None, "ba", None, "ga"),
        P(("grp", "ka"), None, None, None, None, "ga"),
        P(("grp", "ka"), None, "ga", None),
        P(),
        P(),
        P(),
        P(("grp", "ka"), None),
        P(("grp", "ka"), None),
    )
    out_specs = (P(("grp", "ka"), None, None, None), P("grp", None))
    body = functools.partial(local, mesh.shape["ka"], mesh.shape["ga"])
    return jax.shard_map(body, mesh=mesh, in_specs=in_specs, out_specs=out_specs, check_vma=False)
```

time: 181 us -> 62.7 us (0.35)
  blocking collectives: 122 us -> 20.9 us
  matrix products: 22 us -> 0 us
  Pallas kernels: 0 us -> 18.8 us
  waiting for transfers between devices: 16.1 us -> 3.15 us
  starting transfers between devices: 7.1 us -> 15.1 us
  other arithmetic: 5.69 us -> 0 us
  local copies, waits for them, and re-layouts: 7.21 us -> 3.79 us
    psum x7 -> x0, blocking collectives: 60.7 us -> none  [the longest x5 50.8 us: kpoint_total(): return lax.psum(values, 'ka')]
    dot_general x24 -> x0, matrix products: 22 us -> none  [the longest x2 8.39 us: screen_slots(): lax.dot_general(flattened, weights, (((1,), (1,)), ((), ())), preferred_e...]
    all_gather x6 -> x1, blocking collectives: 42.5 us -> 20.9 us  [local(): pieces = lax.all_gather(piece, ('ka', 'ga', 'ba'), axis=0, tiled=False)]
    pallas_call x0 -> x3, Pallas kernels: none -> 18.8 us  [the longest x1 10.9 us: route(): pl.pallas_call(functools.partial(route_kernel, ka), out_shape=[val_shape]...]
    all_to_all x2 -> x0, blocking collectives: 18.5 us -> none  [kernel_apply(): lax.all_to_all(folded, 'ka', split_axis=1, concat_axis=0, tiled=True)]
    all_to_all x2 -> x0, waiting for transfers between devices: 16.1 us -> none  [kernel_apply(): lax.all_to_all(screened, 'ka', split_axis=0, concat_axis=1, tiled=True)]
    ppermute x0 -> x10, starting transfers between devices: none -> 15.1 us  [shifted(): lax.ppermute(value, axis, [(i, (i + by) % size) for i in range(size)])]
    all_to_all x2 -> x0, starting transfers between devices: 7.1 us -> none  [kernel_apply(): lax.all_to_all(screened, 'ka', split_axis=0, concat_axis=1, tiled=True)]
  transfers between devices with their start and end apart: 2 -> 10, of which waited for: 2 -> 2; matrix products, arithmetic and copies ran while one was open for 1% -> 0% of each run, Pallas kernels for 0% -> 0%
where the time goes in v1:
time: 62.7 us; the launch traced here: 62.5 us
  blocking collectives  20.9 us (33%)
  Pallas kernels  18.8 us (30%)
  starting transfers between devices  15.1 us (24%)
  local copies, waits for them, and re-layouts  3.79 us (6%)
  waiting for transfers between devices  3.15 us (5%)
  between operations  0.73 us (1%)
    all_gather x1, blocking collectives, local(): pieces = lax.all_gather(piece, ('ka', 'ga', 'ba'), axis=0, tiled=False)  20.9 us
    ppermute x10, starting transfers between devices, shifted(): lax.ppermute(value, axis, [(i, (i + by) % size) for i in range(size)])  15.1 us
    pallas_call x1, Pallas kernels, route(): pl.pallas_call(functools.partial(route_kernel, ka), out_shape=[val_shape]...  10.9 us
    pallas_call x1, Pallas kernels, screen(): pl.pallas_call(functools.partial(screen_kernel, ka, ga, dims), out_shape=...  5.18 us
    ppermute x10, waiting for transfers between devices, shifted(): lax.ppermute(value, axis, [(i, (i + by) % size) for i in range(size)])  3.15 us
    pallas_call x1, Pallas kernels, haydock(): pl.pallas_call(functools.partial(haydock_kernel, ka, scale_count, npol),...  2.72 us
    reshape x1, local copies, waits for them, and re-layouts, local(): conduction_density.reshape(kcount, 2 * cond_count * cond_count, glocal)  1.64 us
    reshape x1, local copies, waits for them, and re-layouts, local(): valence = valence_density.reshape(kcount, 2 * vloc * val_count, glocal)  1.56 us
  transfers between devices with their start and end apart: 10, of which 2 were waited for; matrix products, arithmetic and copies ran while one was open for 0% of the time, Pallas kernels for 0%

profile of v1, /device:TPU:0, one launch (start us, length us, event | category | flops | bytes accessed | tf_op | source)
XLA Modules:
  0.0 62.5 jit_solution(8441536656463718894)
XLA Ops:
  0.6 1.6 %reshape.13.valence = bf16[4,16,768]{2,1,0:T(8,128)(2,1)} reshape(bf16[1,4,2,2,4,768]{5,4,3,2,1,0:T(4,128)(2,1)} %param.10) | data formatting | bytes 196608 | tf_op jit(solution)/shard_map/reshape | solution.py:307
  2.2 1.6 %reshape.14.conduction = bf16[4,32,768]{2,1,0:T(8,128)(2,1)} reshape(bf16[1,4,2,4,4,768]{5,4,3,2,1,0:T(4,128)(2,1)} %param.11) | data formatting | bytes 393216 | tf_op jit(solution)/shard_map/reshape | solution.py:308
  3.8 10.9 %route.1 = (bf16[16,768]{1,0:T(8,128)(2,1)}, bf16[16,768]{1,0:T(8,128)(2,1)}, bf16[16,768]{1,0:T(8,128)(2,1)}, bf16[16,768]{1,0:T(8,128)(2,1)}, bf16[32,768]{1,0...) custom-call(s32[4,4]{1,0:T(4,128)} %qmap.3, s32[4]{0:T(128)} %owner.3, ...), custom_call_target="tpu_custom_call" | custom-call | tf_op jit(solution)/shard_map/route/pallas_call | solution.py:54
  14.7 3.1 %collective-permute-start.1 = (bf16[16,768]{1,0:T(8,128)(2,1)}, bf16[16,768]{1,0:T(8,128)(2,1)S(1)}, u32[]{:S(2)}, u32[]{:S(2)}) collective-permute-start(bf16[16,768]{1,0:T(8,128)(2,1)} %get-tuple-element.11), channel_id=1, source_target_pairs={{0,4},{4,8},{8,12},{12,0},{1,5},{5,9},{9,13},{13,1},{2,6},{6,10},{... | collective-permute-start | bytes 73736 | tf_op jit(solution)/shard_map/ppermute | solution.py:314
  17.8 2.6 %collective-permute-start.3 = (bf16[16,768]{1,0:T(8,128)(2,1)}, bf16[16,768]{1,0:T(8,128)(2,1)S(1)}, u32[]{:S(2)}, u32[]{:S(2)}) collective-permute-start(bf16[16,768]{1,0:T(8,128)(2,1)} %get-tuple-element.12), channel_id=1, source_target_pairs={{0,8},{4,12},{8,0},{12,4},{1,9},{5,13},{9,1},{13,5},{2,10},{6,14},... | collective-permute-start | bytes 73736 | tf_op jit(solution)/shard_map/ppermute | solution.py:314
  20.4 1.3 %collective-permute-start.5 = (bf16[16,768]{1,0:T(8,128)(2,1)}, bf16[16,768]{1,0:T(8,128)(2,1)S(1)}, u32[]{:S(2)}, u32[]{:S(2)}) collective-permute-start(bf16[16,768]{1,0:T(8,128)(2,1)} %get-tuple-element.13), channel_id=1, source_target_pairs={{0,12},{4,0},{8,4},{12,8},{1,13},{5,1},{9,5},{13,9},{2,14},{6,2},{... | collective-permute-start | bytes 73736 | tf_op jit(solution)/shard_map/ppermute | solution.py:314
  21.7 1.5 %collective-permute-start = (bf16[16,768]{1,0:T(8,128)(2,1)}, bf16[16,768]{1,0:T(8,128)(2,1)S(1)}, u32[]{:S(2)}, u32[]{:S(2)}) collective-permute-start(bf16[16,768]{1,0:T(8,128)(2,1)} %get-tuple-element.10.refs_5_), channel_id=1, source_target_pairs={{0,2},{2,0},{1,3},{3,1},{4,6},{6,4},{5,7},{7,5},{8,10},{10,8},{9,1... | collective-permute-start | bytes 73736 | tf_op jit(solution)/shard_map/ppermute | solution.py:314
  23.2 0.7 %collective-permute-start.7 = (bf16[32,768]{1,0:T(8,128)(2,1)}, bf16[32,768]{1,0:T(8,128)(2,1)S(1)}, u32[]{:S(2)}, u32[]{:S(2)}) collective-permute-start(bf16[32,768]{1,0:T(8,128)(2,1)} %get-tuple-element.15), channel_id=1, source_target_pairs={{0,4},{4,8},{8,12},{12,0},{1,5},{5,9},{9,13},{13,1},{2,6},{6,10},{... | collective-permute-start | bytes 147464 | tf_op jit(solution)/shard_map/ppermute | solution.py:314
  23.9 0.0 collective-permute-done.1.refs_7_
  23.9 0.0 copy-start.3
  23.9 0.5 collective-permute-start.2
  24.4 0.0 collective-permute-done.3.refs_9_
  24.4 0.0 copy-start.4
  24.4 0.9 %collective-permute-start.8 = (bf16[32,768]{1,0:T(8,128)(2,1)}, bf16[32,768]{1,0:T(8,128)(2,1)S(1)}, u32[]{:S(2)}, u32[]{:S(2)}) collective-permute-start(bf16[32,768]{1,0:T(8,128)(2,1)} %get-tuple-element.16), channel_id=1, source_target_pairs={{0,8},{4,12},{8,0},{12,4},{1,9},{5,13},{9,1},{13,5},{2,10},{6,14},... | collective-permute-start | bytes 147464 | tf_op jit(solution)/shard_map/ppermute | solution.py:314
  25.3 0.0 collective-permute-done.5.refs_11_
  25.3 0.0 copy-start.5
  25.3 2.5 %collective-permute-start.9 = (bf16[32,768]{1,0:T(8,128)(2,1)}, bf16[32,768]{1,0:T(8,128)(2,1)S(1)}, u32[]{:S(2)}, u32[]{:S(2)}) collective-permute-start(bf16[32,768]{1,0:T(8,128)(2,1)} %get-tuple-element.17), channel_id=1, source_target_pairs={{0,12},{4,0},{8,4},{12,8},{1,13},{5,1},{9,5},{13,9},{2,14},{6,2},{... | collective-permute-start | bytes 147464 | tf_op jit(solution)/shard_map/ppermute | solution.py:314
  27.8 0.0 collective-permute-done.refs_6_
  27.8 0.0 copy-start.6
  27.8 1.3 %collective-permute-start.4 = (bf16[16,768]{1,0:T(8,128)(2,1)S(1)}, bf16[16,768]{1,0:T(8,128)(2,1)S(1)}, u32[]{:S(2)}, u32[]{:S(2)}) collective-permute-start(bf16[16,768]{1,0:T(8,128)(2,1)S(1)} %collective-permute-done.3.refs_9_), channel_id=1, source_target_pairs={{0,2},{2,0},{1,3},{3,1},{4,6},{6,4},{5,7},{7,5},{8,10},{10,8},{9,1... | collective-permute-start | bytes 73736 | tf_op jit(solution)/shard_map/ppermute | solution.py:314
  29.2 0.0 collective-permute-done.2.refs_8_
  29.2 0.0 copy-start.7
  29.2 0.7 %collective-permute-start.6 = (bf16[16,768]{1,0:T(8,128)(2,1)S(1)}, bf16[16,768]{1,0:T(8,128)(2,1)S(1)}, u32[]{:S(2)}, u32[]{:S(2)}) collective-permute-start(bf16[16,768]{1,0:T(8,128)(2,1)S(1)} %collective-permute-done.5.refs_11_), channel_id=1, source_target_pairs={{0,2},{2,0},{1,3},{3,1},{4,6},{6,4},{5,7},{7,5},{8,10},{10,8},{9,1... | collective-permute-start | bytes 73736 | tf_op jit(solution)/shard_map/ppermute | solution.py:314
  29.9 1.8 %collective-permute-done.4.refs_10_ = bf16[16,768]{1,0:T(8,128)(2,1)S(1)} collective-permute-done((bf16[16,768]{1,0:T(8,128)(2,1)S(1)}, bf16[16,768]{1,0:T(8,128)(2,1)S(1)}, u32[]{:S(2)}, u32[]{:S(2)}) %collective-permute-start.4) | collective-permute-done | bytes 24608 | tf_op jit(solution)/shard_map/ppermute | solution.py:314
  31.7 0.0 copy-start.8
  31.7 1.3 %collective-permute-done.6.refs_12_ = bf16[16,768]{1,0:T(8,128)(2,1)S(1)} collective-permute-done((bf16[16,768]{1,0:T(8,128)(2,1)S(1)}, bf16[16,768]{1,0:T(8,128)(2,1)S(1)}, u32[]{:S(2)}, u32[]{:S(2)}) %collective-permute-start.6) | collective-permute-done | bytes 24608 | tf_op jit(solution)/shard_map/ppermute | solution.py:314
  33.0 0.0 copy-start.9
  33.0 0.0 collective-permute-done.7.refs_14_
  33.0 0.0 copy-start
  33.0 0.0 collective-permute-done.8.refs_15_
  33.0 0.0 copy-start.1
  33.0 0.0 collective-permute-done.9.refs_16_
  33.0 0.0 copy-start.2
  33.1 0.0 copy-done.3
  33.1 0.0 copy-done.4
  33.1 0.0 copy-done.5
  33.1 0.0 copy-done.6
  33.1 0.0 copy-done.7
  33.1 0.0 copy-done.8
  33.1 0.5 copy-done.9
  33.6 0.0 copy-done
  33.6 0.0 copy-done.1
  33.7 0.0 copy-done.2
  33.7 5.2 %screen.1 = f32[24,128]{1,0:T(8,128)} custom-call(s32[16]{0:T(128)} %band_pairs.1, f32[1,4]{1,0:T(1,128)} %refs_1_.1, f32[1,4]{1,0:T(1,128)} %refs_2_.1, f32[1,2,2,16]{3,2,1,0:T(2,128)} %refs_3_.1, bf16[2,768,1536]{2,1,0:T(8,128)(2,1)} %bitcast.2, bf16[16,768]{1,0:T(8,128)(2,1)} %get-tuple-element.10.refs_5_, bf16[16,768]{1,0:T(8,128)(2,1)} %copy-done.6, ...), custom_call_target="tpu_custom_call" | custom-call | tf_op jit(solution)/shard_map/screen/pallas_call | solution.py:181
  38.9 20.9 %all-gather = f32[384,128]{1,0:T(8,128)} all-gather(f32[24,128]{1,0:T(8,128)} %screen.1), channel_id=2, replica_groups=mesh['grp'=2,'ka'=4,'ga'=2,'ba'=2] {'ka','ga','ba'}, dimensions={0}, use_global_device_ids=true | all-gather | bytes 208896 | tf_op jit(solution)/shard_map/all_gather | solution.py:331
  59.8 2.7 %haydock.1 = (f32[1,2,2,16]{3,2,1,0:T(2,128)}, f32[2,6]{1,0:T(2,128)}) custom-call(s32[4,4]{1,0:T(4,128)} %qmap.3, s32[4]{0:T(128)} %owner.3, s32[16]{0:T(128)} %band_pairs.1, f32[4,4,24,128]{3,2,1,0:T(8,128)} %bitcast.3), custom_call_target="tpu_custom_call" | custom-call | tf_op jit(solution)/shard_map/haydock/pallas_call | solution.py:272
Async XLA Ops:
  14.7 9.2 %collective-permute-start.1 = (bf16[16,768]{1,0:T(8,128)(2,1)}, bf16[16,768]{1,0:T(8,128)(2,1)S(1)}, u32[]{:S(2)}, u32[]{:S(2)}) collective-permute-start(bf16[16,768]{1,0:T(8,128)(2,1)} %get-tuple-element.11), channel_id=1, source_target_pairs={{0,4},{4,8},{8,12},{12,0},{1,5},{5,9},{9,13},{13,1},{2,6},{6,10},{... | collective-permute-start | bytes 73736 | tf_op jit(solution)/shard_map/ppermute | solution.py:314
  17.8 6.7 %collective-permute-start.3 = (bf16[16,768]{1,0:T(8,128)(2,1)}, bf16[16,768]{1,0:T(8,128)(2,1)S(1)}, u32[]{:S(2)}, u32[]{:S(2)}) collective-permute-start(bf16[16,768]{1,0:T(8,128)(2,1)} %get-tuple-element.12), channel_id=1, source_target_pairs={{0,8},{4,12},{8,0},{12,4},{1,9},{5,13},{9,1},{13,5},{2,10},{6,14},... | collective-permute-start | bytes 73736 | tf_op jit(solution)/shard_map/ppermute | solution.py:314
  20.4 4.9 %collective-permute-start.5 = (bf16[16,768]{1,0:T(8,128)(2,1)}, bf16[16,768]{1,0:T(8,128)(2,1)S(1)}, u32[]{:S(2)}, u32[]{:S(2)}) collective-permute-start(bf16[16,768]{1,0:T(8,128)(2,1)} %get-tuple-element.13), channel_id=1, source_target_pairs={{0,12},{4,0},{8,4},{12,8},{1,13},{5,1},{9,5},{13,9},{2,14},{6,2},{... | collective-permute-start | bytes 73736 | tf_op jit(solution)/shard_map/ppermute | solution.py:314
  21.7 6.1 %collective-permute-start = (bf16[16,768]{1,0:T(8,128)(2,1)}, bf16[16,768]{1,0:T(8,128)(2,1)S(1)}, u32[]{:S(2)}, u32[]{:S(2)}) collective-permute-start(bf16[16,768]{1,0:T(8,128)(2,1)} %get-tuple-element.10.refs_5_), channel_id=1, source_target_pairs={{0,2},{2,0},{1,3},{3,1},{4,6},{6,4},{5,7},{7,5},{8,10},{10,8},{9,1... | collective-permute-start | bytes 73736 | tf_op jit(solution)/shard_map/ppermute | solution.py:314
  23.2 9.8 %collective-permute-start.7 = (bf16[32,768]{1,0:T(8,128)(2,1)}, bf16[32,768]{1,0:T(8,128)(2,1)S(1)}, u32[]{:S(2)}, u32[]{:S(2)}) collective-permute-start(bf16[32,768]{1,0:T(8,128)(2,1)} %get-tuple-element.15), channel_id=1, source_target_pairs={{0,4},{4,8},{8,12},{12,0},{1,5},{5,9},{9,13},{13,1},{2,6},{6,10},{... | collective-permute-start | bytes 147464 | tf_op jit(solution)/shard_map/ppermute | solution.py:314
  23.9 9.2 %copy-start.3 = (bf16[16,768]{1,0:T(8,128)(2,1)}, bf16[16,768]{1,0:T(8,128)(2,1)S(1)}, u32[]{:S(2)}) copy-start(bf16[16,768]{1,0:T(8,128)(2,1)S(1)} %collective-permute-done.1.refs_7_) | copy-start | bytes 73732
  23.9 5.3 %collective-permute-start.2 = (bf16[16,768]{1,0:T(8,128)(2,1)S(1)}, bf16[16,768]{1,0:T(8,128)(2,1)S(1)}, u32[]{:S(2)}, u32[]{:S(2)}) collective-permute-start(bf16[16,768]{1,0:T(8,128)(2,1)S(1)} %collective-permute-done.1.refs_7_), channel_id=1, source_target_pairs={{0,2},{2,0},{1,3},{3,1},{4,6},{6,4},{5,7},{7,5},{8,10},{10,8},{9,1... | collective-permute-start | bytes 73736 | tf_op jit(solution)/shard_map/ppermute | solution.py:314
  24.4 8.6 %copy-start.4 = (bf16[16,768]{1,0:T(8,128)(2,1)}, bf16[16,768]{1,0:T(8,128)(2,1)S(1)}, u32[]{:S(2)}) copy-start(bf16[16,768]{1,0:T(8,128)(2,1)S(1)} %collective-permute-done.3.refs_9_) | copy-start | bytes 73732
  24.4 8.6 %collective-permute-start.8 = (bf16[32,768]{1,0:T(8,128)(2,1)}, bf16[32,768]{1,0:T(8,128)(2,1)S(1)}, u32[]{:S(2)}, u32[]{:S(2)}) collective-permute-start(bf16[32,768]{1,0:T(8,128)(2,1)} %get-tuple-element.16), channel_id=1, source_target_pairs={{0,8},{4,12},{8,0},{12,4},{1,9},{5,13},{9,1},{13,5},{2,10},{6,14},... | collective-permute-start | bytes 147464 | tf_op jit(solution)/shard_map/ppermute | solution.py:314
  25.3 7.7 %copy-start.5 = (bf16[16,768]{1,0:T(8,128)(2,1)}, bf16[16,768]{1,0:T(8,128)(2,1)S(1)}, u32[]{:S(2)}) copy-start(bf16[16,768]{1,0:T(8,128)(2,1)S(1)} %collective-permute-done.5.refs_11_) | copy-start | bytes 73732
  25.3 7.7 %collective-permute-start.9 = (bf16[32,768]{1,0:T(8,128)(2,1)}, bf16[32,768]{1,0:T(8,128)(2,1)S(1)}, u32[]{:S(2)}, u32[]{:S(2)}) collective-permute-start(bf16[32,768]{1,0:T(8,128)(2,1)} %get-tuple-element.17), channel_id=1, source_target_pairs={{0,12},{4,0},{8,4},{12,8},{1,13},{5,1},{9,5},{13,9},{2,14},{6,2},{... | collective-permute-start | bytes 147464 | tf_op jit(solution)/shard_map/ppermute | solution.py:314
  27.8 5.2 %copy-start.6 = (bf16[16,768]{1,0:T(8,128)(2,1)}, bf16[16,768]{1,0:T(8,128)(2,1)S(1)}, u32[]{:S(2)}) copy-start(bf16[16,768]{1,0:T(8,128)(2,1)S(1)} %collective-permute-done.refs_6_) | copy-start | bytes 73732
  27.8 3.8 %collective-permute-start.4 = (bf16[16,768]{1,0:T(8,128)(2,1)S(1)}, bf16[16,768]{1,0:T(8,128)(2,1)S(1)}, u32[]{:S(2)}, u32[]{:S(2)}) collective-permute-start(bf16[16,768]{1,0:T(8,128)(2,1)S(1)} %collective-permute-done.3.refs_9_), channel_id=1, source_target_pairs={{0,2},{2,0},{1,3},{3,1},{4,6},{6,4},{5,7},{7,5},{8,10},{10,8},{9,1... | collective-permute-start | bytes 73736 | tf_op jit(solution)/shard_map/ppermute | solution.py:314
  29.2 3.9 %copy-start.7 = (bf16[16,768]{1,0:T(8,128)(2,1)}, bf16[16,768]{1,0:T(8,128)(2,1)S(1)}, u32[]{:S(2)}) copy-start(bf16[16,768]{1,0:T(8,128)(2,1)S(1)} %collective-permute-done.2.refs_8_) | copy-start | bytes 73732
  29.2 3.8 %collective-permute-start.6 = (bf16[16,768]{1,0:T(8,128)(2,1)S(1)}, bf16[16,768]{1,0:T(8,128)(2,1)S(1)}, u32[]{:S(2)}, u32[]{:S(2)}) collective-permute-start(bf16[16,768]{1,0:T(8,128)(2,1)S(1)} %collective-permute-done.5.refs_11_), channel_id=1, source_target_pairs={{0,2},{2,0},{1,3},{3,1},{4,6},{6,4},{5,7},{7,5},{8,10},{10,8},{9,1... | collective-permute-start | bytes 73736 | tf_op jit(solution)/shard_map/ppermute | solution.py:314
  31.7 1.4 %copy-start.8 = (bf16[16,768]{1,0:T(8,128)(2,1)}, bf16[16,768]{1,0:T(8,128)(2,1)S(1)}, u32[]{:S(2)}) copy-start(bf16[16,768]{1,0:T(8,128)(2,1)S(1)} %collective-permute-done.4.refs_10_) | copy-start | bytes 73732
  33.0 0.6 copy-start.9
  33.0 0.6 copy-start
  33.0 0.6 %copy-start.1 = (bf16[32,768]{1,0:T(8,128)(2,1)}, bf16[32,768]{1,0:T(8,128)(2,1)S(1)}, u32[]{:S(2)}) copy-start(bf16[32,768]{1,0:T(8,128)(2,1)S(1)} %collective-permute-done.8.refs_15_) | copy-start | bytes 147460
  33.0 0.6 %copy-start.2 = (bf16[32,768]{1,0:T(8,128)(2,1)}, bf16[32,768]{1,0:T(8,128)(2,1)S(1)}, u32[]{:S(2)}) copy-start(bf16[32,768]{1,0:T(8,128)(2,1)S(1)} %collective-permute-done.9.refs_16_) | copy-start | bytes 147460

commit v2 on v1

v2 whole, which is shorter than its diff:
```python
import functools
import math

import jax
import jax.numpy as jnp
from jax import lax
from jax.experimental import pallas as pl
from jax.experimental.pallas import tpu as pltpu
from jax.sharding import PartitionSpec as P

EPSILON = 1e-06
EXACT = lax.Precision.HIGHEST
VMEM_LEAST = 8 * 1024 * 1024
VMEM_MOST = 56 * 1024 * 1024

vmem = pl.BlockSpec(memory_space=pltpu.VMEM)
smem = pl.BlockSpec(memory_space=pltpu.SMEM)


def iota(shape, axis):
    return lax.broadcasted_iota(jnp.int32, shape, axis)


def split(values):
    high = values.astype(jnp.bfloat16)
    low = (values - high.astype(jnp.float32)).astype(jnp.bfloat16)
    return high, low


def in_vmem(shape, dtype):
    return pltpu.VMEM(shape, dtype)


def limits(*arrays):
    held = sum(math.prod(a.shape) * a.dtype.itemsize for a in arrays)
    return pltpu.CompilerParams(vmem_limit_bytes=min(VMEM_MOST, VMEM_LEAST + 4 * held))


def pack_kernel(ka, qmap, owner, valence, conduction, *rest):
    outs, partner = rest[:ka], rest[ka]
    me = lax.axis_index("ka")
    half = lax.axis_index("ba")
    count, width = valence.shape[1], valence.shape[5]
    cond_count = conduction.shape[3]
    share = cond_count // lax.axis_size("ba")
    val_rows = 2 * valence.shape[3] * valence.shape[4]
    cond_rows = 2 * share * cond_count

    def note(k2, carry):
        partner[owner[qmap[me, k2]]] = k2
        return carry

    lax.fori_loop(0, count, note, 0)
    for j in range(ka):
        k2 = partner[lax.rem(me + j, ka)]
        block = valence[0, k2].astype(jnp.float32).reshape(val_rows, width)
        outs[j][:val_rows, :] = block.astype(jnp.bfloat16)
        block = conduction[0, k2, :, pl.ds(half * share, share)].astype(jnp.float32)
        outs[j][val_rows:, :] = block.reshape(cond_rows, width).astype(jnp.bfloat16)


def pack(ka, ba, qmap, owner, valence, conduction):
    cond_count = conduction.shape[3]
    rows = 2 * valence.shape[3] * valence.shape[4] + 2 * cond_count // ba * cond_count
    shape = in_vmem((rows, valence.shape[5]), valence.dtype)
    return pl.pallas_call(
        functools.partial(pack_kernel, ka),
        out_shape=[shape] * ka,
        in_specs=[smem, smem, vmem, vmem],
        out_specs=[vmem] * ka,
        scratch_shapes=[pltpu.SMEM((owner.shape[0],), jnp.int32)],
        compiler_params=limits(valence, conduction),
        name="pack",
    )(qmap, owner, valence, conduction)


def regroup_kernel(ka, val_rows, *refs):
    blocks, val_all, cond_half = refs[:ka], refs[ka], refs[ka + 1]
    cond_rows = blocks[0].shape[0] - val_rows
    for j in range(ka):
        val_all[j * val_rows : (j + 1) * val_rows, :] = blocks[j][:val_rows, :]
        cond_half[j * cond_rows : (j + 1) * cond_rows, :] = blocks[j][val_rows:, :]


def regroup(ka, val_rows, blocks):
    rows, width = blocks[0].shape
    kind = blocks[0].dtype
    return pl.pallas_call(
        functools.partial(regroup_kernel, ka, val_rows),
        out_shape=[in_vmem((ka * val_rows, width), kind), in_vmem((ka * (rows - val_rows), width), kind)],
        in_specs=[vmem] * ka,
        out_specs=[vmem] * 2,
        compiler_params=limits(*blocks),
        name="regroup",
    )(*blocks)


def screened_block(screening, valence, pairs, place):
    wide = valence[...].astype(jnp.float32)
    parts = []
    for at in range(0, wide.shape[0], 2 * pairs):
        parts += [-wide[at + pairs : at + 2 * pairs], wide[at : at + pairs]]
    turned = jnp.concatenate(parts, 0)
    real = jnp.concatenate([wide, turned], 0).astype(jnp.bfloat16)
    imag = jnp.concatenate([turned, -wide], 0).astype(jnp.bfloat16)
    width = valence.shape[1]
    columns = pl.ds(pl.multiple_of(place * width, 128), width)
    form = (((1,), (1,)), ((), ()))
    return lax.dot_general(
        screening[0, 0, :, columns], real, form, preferred_element_type=jnp.float32
    ) + lax.dot_general(screening[0, 1, :, columns], imag, form, preferred_element_type=jnp.float32)


def near_kernel(pairs, screening, valence, out):
    out[...] = screened_block(screening, valence, pairs, lax.axis_index("ga"))


def near_field(pairs, screening, valence):
    rows, width = valence.shape
    glocal = screening.shape[2]
    return pl.pallas_call(
        functools.partial(near_kernel, pairs),
        out_shape=in_vmem((glocal, 2 * rows), jnp.float32),
        in_specs=[vmem, vmem],
        out_specs=vmem,
        cost_estimate=pl.CostEstimate(
            flops=8 * glocal * width * rows, bytes_accessed=screening.size, transcendentals=0
        ),
        compiler_params=limits(screening, valence),
        name="near_field",
    )(screening, valence)


def project_kernel(ka, ga, ba, dims, *refs):
    vloc, val_count, cond_count = dims
    band_pairs, val_energy, cond_energy, start, screening, near = refs[:6]
    val_in = refs[6 : 6 + ga - 1]
    cond_in = refs[6 + ga - 1 : 6 + ga - 1 + ba]
    out = refs[6 + ga - 1 + ba]
    me = lax.axis_index("ka")
    mine = lax.axis_index("ga")
    half = lax.axis_index("ba")
    pairs = vloc * val_count
    block = 2 * pairs
    rows = ka * block
    codes = val_count * cond_count
    lanes = 2 * ka * codes
    share = cond_count // ba
    cond_rows = cond_count * cond_count
    share_rows = share * cond_count

    fields = near[...]
    for r in range(1, ga):
        place = lax.rem(mine + ga - r, ga)
        fields = fields + screened_block(screening, val_in[r - 1], pairs, place)
    high, low = split(fields)
    lane = iota((share_rows, 2 * rows), 1)
    lane_j = lane % rows // block
    turned_lane = lane // rows
    kernel = []
    for h in range(ba):
        cond_all = cond_in[h][...]
        crossed = jnp.dot(cond_all, high, preferred_element_type=jnp.float32) + jnp.dot(
            cond_all, low, preferred_element_type=jnp.float32
        )
        total = jnp.zeros((share_rows, 2 * rows), jnp.float32)
        for j in range(ka):
            base = j * 2 * share_rows
            same = lane_j == j
            total = total + jnp.where(
                same & (turned_lane == 0), crossed[base : base + share_rows], 0.0
            )
            total = total - jnp.where(
                same & (turned_lane == 1), crossed[base + share_rows : base + 2 * share_rows], 0.0
            )
        kernel.append(total)
    kernel = jnp.concatenate(kernel, 0)

    row = iota((2 * rows, lanes), 0)
    col = iota((2 * rows, lanes), 1)
    k_of_row = lax.rem(me + ka - row % rows // block, ka)
    want = (
        (row % block // pairs) * (ka * codes)
        + k_of_row * codes
        + (half * vloc + row % pairs // val_count) * cond_count
    )
    joined = (col - want >= 0) & (col - want < cond_count)
    kernel_high, kernel_low = split(kernel)
    stacked = jnp.concatenate([kernel_high, kernel_low], 0)
    crow = iota((cond_rows, lanes), 0)
    c_of_row = lax.rem(half + ba - crow // share_rows, ba) * share + crow % share_rows // cond_count
    same_c = c_of_row == iota((cond_rows, lanes), 1) % cond_count
    spread = []
    for v2 in range(val_count):
        pick = jnp.where(joined & (row % val_count == v2), 1.0, 0.0).astype(jnp.bfloat16)
        both = jnp.dot(stacked, pick, preferred_element_type=jnp.float32)
        spread.append(jnp.where(same_c, both[:cond_rows] + both[cond_rows:], 0.0))
    spread = jnp.concatenate(spread, 0)
    out_row = iota((codes, val_count * cond_rows), 0)
    out_col = iota((codes, val_count * cond_rows), 1)
    fold = (out_row // cond_count == out_col // cond_rows) & (
        out_row % cond_count == out_col % cond_count
    )
    fold = jnp.where(fold, 1.0, 0.0).astype(jnp.bfloat16)
    spread_high, spread_low = split(spread)
    out[0:codes, :] = jnp.dot(fold, spread_high, preferred_element_type=jnp.float32) + jnp.dot(
        fold, spread_low, preferred_element_type=jnp.float32
    )

    first = jnp.where((mine == 0) & (half == 0), 1.0, 0.0)
    band_row = iota((codes, lanes), 0)
    band_lane = iota((codes, lanes), 1)
    code = jnp.zeros((codes, lanes), jnp.int32)
    for b in range(codes):
        code = jnp.where(band_row == b, band_pairs[b], code)
    npol = start.shape[1]
    vectors = jnp.zeros((npol, lanes), jnp.float32)
    for part in range(2):
        spot = part * ka * codes + me * codes
        pick = jnp.where(band_lane == spot + code, first, 0.0)
        vectors = vectors + jnp.dot(start[0, :, part, :], pick, precision=EXACT)
    lane = iota((1, lanes), 1)
    energy = jnp.zeros((1, lanes), jnp.float32)
    for c in range(cond_count):
        energy = jnp.where(lane % cond_count == c, cond_energy[0, c], energy)
    for v in range(val_count):
        energy = energy - jnp.where(lane % codes // cond_count == v, val_energy[0, v], 0.0)
    energy = jnp.where(lane % (ka * codes) // codes == me, energy * first, 0.0)
    rest = jnp.zeros((7 - npol, lanes), jnp.float32)
    out[codes:, :] = jnp.concatenate([vectors, energy, rest], 0)


def project(ka, ga, ba, dims, band_pairs, val_energy, cond_energy, start, screening, near, val_far, cond_all):
    vloc, val_count, cond_count = dims
    codes = val_count * cond_count
    return pl.pallas_call(
        functools.partial(project_kernel, ka, ga, ba, dims),
        out_shape=in_vmem((codes + 8, 2 * ka * codes), jnp.float32),
        in_specs=[smem, smem, smem] + [vmem] * (3 + len(val_far) + len(cond_all)),
        out_specs=vmem,
        compiler_params=limits(screening, near, *val_far, *cond_all),
        name="project",
    )(band_pairs, val_energy, cond_energy, start, screening, near, *val_far, *cond_all)


def haydock_kernel(ka, scale_count, npol, qmap, owner, band_pairs, *refs):
    pieces = refs[:ka]
    next_out, coef_out, whole, matrix = refs[ka:]
    me = lax.axis_index("ka")
    lanes = pieces[0].shape[1]
    codes = pieces[0].shape[0] - 8
    mid = lanes // 2
    for r in range(ka):
        whole[lax.rem(me + ka - r, ka)] = pieces[r][...]
    extras = whole[0, codes:, :]
    for s in range(1, ka):
        extras = extras + whole[s, codes:, :]
    lane_k = iota((codes, lanes), 1) % mid // codes
    sign = jnp.where(iota((1, lanes), 1) < mid, -1.0, 1.0)
    for k2 in range(ka):
        block = jnp.zeros((codes, lanes), jnp.float32)
        for back in range(ka):
            slot = owner[qmap[0, back]]
            k = (k2 - back) % ka
            block = jnp.where(lane_k == k, whole[slot, :codes, :], block)
        matrix[k2 * codes : (k2 + 1) * codes, :] = block
        matrix[mid + k2 * codes : mid + (k2 + 1) * codes, :] = sign * pltpu.roll(block, mid, 1)
    full = matrix[...]
    energy = extras[npol : npol + 1]
    start = extras[:npol]

    def mean(values):
        return jnp.sum(values, axis=1, keepdims=True) / scale_count

    def norm(vector):
        return jnp.sqrt(mean(vector * vector) + EPSILON)

    def swap(vector):
        return pltpu.roll(vector, mid, 1)

    def hamiltonian(vector):
        return energy * vector - jnp.dot(vector, full, precision=EXACT)

    def inner(left, right):
        return mean(left * right), mean(-sign * left * swap(right))

    def times(real, imag, vector):
        return real * vector + imag * (sign * swap(vector))

    first = start / norm(start)
    first_image = hamiltonian(first)
    alpha_real, alpha_imag = inner(first, first_image)
    first_resid = first_image - times(alpha_real, alpha_imag, first)
    beta_one = norm(first_resid)
    second = first_resid / beta_one
    second_image = hamiltonian(second)
    gamma_real, gamma_imag = inner(second, second_image)
    second_resid = second_image - times(gamma_real, gamma_imag, second) - beta_one * first
    beta_two = norm(second_resid)
    following = second_resid / beta_two

    coef_lane = iota(coef_out.shape, 1)
    coefs = jnp.zeros(coef_out.shape, jnp.float32)
    for at, value in enumerate((alpha_real, alpha_imag, gamma_real, gamma_imag, beta_one, beta_two)):
        coefs = jnp.where(coef_lane == at, value, coefs)
    coef_out[...] = coefs
    band = iota((lanes, codes), 1)
    code = jnp.zeros((lanes, codes), jnp.int32)
    for b in range(codes):
        code = jnp.where(band == b, band_pairs[b], code)
    row = iota((lanes, codes), 0)
    for part in range(2):
        pick = jnp.where(row == part * mid + me * codes + code, 1.0, 0.0)
        next_out[0, :, part, :] = jnp.dot(following, pick, precision=EXACT)


def haydock(ka, scale_count, npol, qmap, owner, band_pairs, pieces):
    lanes = pieces[0].shape[1]
    codes = pieces[0].shape[0] - 8
    return pl.pallas_call(
        functools.partial(haydock_kernel, ka, scale_count, npol),
        out_shape=[
            jax.ShapeDtypeStruct((1, npol, 2, codes), jnp.float32),
            jax.ShapeDtypeStruct((npol, 6), jnp.float32),
        ],
        in_specs=[smem, smem, smem] + [vmem] * ka,
        out_specs=[vmem, vmem],
        scratch_shapes=[
            pltpu.VMEM((ka, codes + 8, lanes), jnp.float32),
            pltpu.VMEM((lanes, lanes), jnp.float32),
        ],
        compiler_params=limits(*pieces, jax.ShapeDtypeStruct((lanes, lanes), jnp.float32)),
        name="haydock",
    )(qmap, owner, band_pairs, *pieces)


def shifted(value, axis, by):
    size = lax.axis_size(axis)
    return lax.ppermute(value, axis, [(i, (i + by) % size) for i in range(size)])


def summed(value, axis):
    size = lax.axis_size(axis)
    if size & (size - 1):
        return lax.psum(value, axis)
    step = 1
    while step < size:
        value = value + lax.ppermute(value, axis, [(i, i ^ step) for i in range(size)])
        step *= 2
    return value


def local(
    ka,
    ga,
    ba,
    start_vector,
    valence_density,
    conduction_density,
    screening,
    qpoint_map,
    slot_owner,
    band_pairs,
    valence_energy,
    conduction_energy,
):
    npol = start_vector.shape[1]
    pair_count = start_vector.shape[3]
    kcount, vloc, val_count = qpoint_map.shape[0], valence_density.shape[3], valence_density.shape[4]
    cond_count = conduction_density.shape[3]
    pairs = vloc * val_count
    screening = pltpu.with_memory_space_constraint(screening, pltpu.VMEM)
    packed = pack(ka, ba, qpoint_map, slot_owner, valence_density, conduction_density)
    blocks = [packed[0]] + [shifted(packed[j], "ka", j) for j in range(1, ka)]
    val_all, cond_half = regroup(ka, 2 * pairs, blocks)
    val_far = [shifted(val_all, "ga", r) for r in range(1, ga)]
    cond_all = [cond_half] + [shifted(cond_half, "ba", r) for r in range(1, ba)]
    near = near_field(pairs, screening, val_all)
    piece = project(
        ka,
        ga,
        ba,
        (vloc, val_count, cond_count),
        band_pairs,
        valence_energy,
        conduction_energy,
        start_vector,
        screening,
        near,
        val_far,
        cond_all,
    )
    piece = summed(summed(piece, "ba"), "ga")
    pieces = [piece] + [shifted(piece, "ka", j) for j in range(1, ka)]
    scale_count = float(kcount * pair_count)
    return tuple(haydock(ka, scale_count, npol, qpoint_map, slot_owner, band_pairs, pieces))


def solution(mesh):
    in_specs = (
        P(("grp", "ka"), None, None, None),
        P(("grp", "ka"), None, None, "ba", None, "ga"),
        P(("grp", "ka"), None, None, None, None, "ga"),
        P(("grp", "ka"), None, "ga", None),
        P(),
        P(),
        P(),
        P(("grp", "ka"), None),
        P(("grp", "ka"), None),
    )
    out_specs = (P(("grp", "ka"), None, None, None), P("grp", None))
    body = functools.partial(local, mesh.shape["ka"], mesh.shape["ga"], mesh.shape["ba"])
    return jax.shard_map(body, mesh=mesh, in_specs=in_specs, out_specs=out_specs, check_vma=False)
```

time: 62.7 us -> 37.4 us (0.60)
  blocking collectives: 20.9 us -> 0 us
  Pallas kernels: 18.8 us -> 5.67 us
  waiting for transfers between devices: 3.15 us -> 10.3 us
  local copies, waits for them, and re-layouts: 3.79 us -> 7 us
  starting transfers between devices: 15.1 us -> 13.5 us
    all_gather x1 -> x0, blocking collectives: 20.9 us -> none  [local(): pieces = lax.all_gather(piece, ('ka', 'ga', 'ba'), axis=0, tiled=False)]
    pallas_call x2 -> x4, Pallas kernels: 16.1 us -> 3.3 us  [the longest x1 1.83 us: project(): pl.pallas_call(functools.partial(project_kernel, ka, ga, ba, dims), out_s...]
    unnamed x20 -> x24, local copies, waits for them, and re-layouts: 0.59 us -> 7 us
    ppermute x0 -> x2, waiting for transfers between devices: none -> 4.1 us  [summed(): lax.ppermute(value, axis, [(i, i ^ step) for i in range(size)])]
    reshape x2 -> x0, local copies, waits for them, and re-layouts: 3.2 us -> none  [the longest x1 1.64 us: local(): conduction_density.reshape(kcount, 2 * cond_count * cond_count, glocal)]
    ppermute x10 -> x8, waiting for transfers between devices: 3.15 us -> 6.16 us  [shifted(): lax.ppermute(value, axis, [(i, (i + by) % size) for i in range(size)])]
    ppermute x10 -> x8, starting transfers between devices: 15.1 us -> 12.6 us  [shifted(): lax.ppermute(value, axis, [(i, (i + by) % size) for i in range(size)])]
    ppermute x0 -> x2, starting transfers between devices: none -> 0.96 us  [summed(): lax.ppermute(value, axis, [(i, i ^ step) for i in range(size)])]
  transfers between devices with their start and end apart: 10 -> 10, of which waited for: 2 -> 7; matrix products, arithmetic and copies ran while one was open for 0% -> 0% of each run, Pallas kernels for 0% -> 2%
where the time goes in v2:
time: 37.4 us; the launch traced here: 37.2 us
  starting transfers between devices  13.5 us (36%)
  waiting for transfers between devices  10.3 us (28%)
  local copies, waits for them, and re-layouts  7 us (19%)
  Pallas kernels  5.67 us (15%)
  between operations  0.73 us (2%)
    ppermute x8, starting transfers between devices, shifted(): lax.ppermute(value, axis, [(i, (i + by) % size) for i in range(size)])  12.6 us
    unnamed x24, local copies, waits for them, and re-layouts  7 us
    ppermute x8, waiting for transfers between devices, shifted(): lax.ppermute(value, axis, [(i, (i + by) % size) for i in range(size)])  6.16 us
    ppermute x2, waiting for transfers between devices, summed(): lax.ppermute(value, axis, [(i, i ^ step) for i in range(size)])  4.1 us
    pallas_call x1, Pallas kernels, haydock(): pl.pallas_call(functools.partial(haydock_kernel, ka, scale_count, npol),...  2.38 us
    pallas_call x1, Pallas kernels, project(): pl.pallas_call(functools.partial(project_kernel, ka, ga, ba, dims), out_s...  1.83 us
    ppermute x2, starting transfers between devices, summed(): lax.ppermute(value, axis, [(i, i ^ step) for i in range(size)])  0.96 us
    pallas_call x1, Pallas kernels, near_field(): pl.pallas_call(functools.partial(near_kernel, pairs), out_shape=in_vmem((...  0.77 us
  transfers between devices with their start and end apart: 10, of which 7 were waited for; matrix products, arithmetic and copies ran while one was open for 0% of the time, Pallas kernels for 2%

profile of v2, /device:TPU:0, one launch (start us, length us, event | category | flops | bytes accessed | tf_op | source)
XLA Modules:
  0.0 37.2 jit_solution(602184054093875788)
XLA Ops:
  0.6 0.0 copy-start.2
  0.6 0.9 %copy-done.2 = bf16[1,4,2,4,4,768]{5,4,3,2,1,0:T(4,128)(2,1)S(1)} copy-done((bf16[1,4,2,4,4,768]{5,4,3,2,1,0:T(4,128)(2,1)S(1)}, bf16[1,4,2,4,4,768]{5,4,3,2,1,0:T(4,128)(2,1)}, u32[]{:S(2)}) %copy-start.2) | copy-done | bytes 196632
  1.6 0.0 copy-start.3
  1.6 0.9 %copy-done.3 = bf16[1,4,2,2,4,768]{5,4,3,2,1,0:T(4,128)(2,1)S(1)} copy-done((bf16[1,4,2,2,4,768]{5,4,3,2,1,0:T(4,128)(2,1)S(1)}, bf16[1,4,2,2,4,768]{5,4,3,2,1,0:T(4,128)(2,1)}, u32[]{:S(2)}) %copy-start.3) | copy-done | bytes 98328
  2.5 0.0 copy-start.4
  2.5 0.7 %copy-done.4 = s32[4,4]{1,0:T(4,128)S(1)} copy-done((s32[4,4]{1,0:T(4,128)S(1)}, s32[4,4]{1,0:T(4,128)}, u32[]{:S(2)}) %copy-start.4) | copy-done | bytes 88
  3.1 0.0 copy-start.7
  3.1 0.7 %copy-done.7 = s32[4]{0:T(128)S(1)} copy-done((s32[4]{0:T(128)S(1)}, s32[4]{0:T(128)}, u32[]{:S(2)}) %copy-start.7) | copy-done | bytes 40
  3.8 0.0 copy-start.6
  3.8 0.0 copy-start.9
  3.8 0.0 copy-start.10
  3.8 0.0 copy-start.11
  3.8 0.7 %pack.1 = (bf16[32,768]{1,0:T(8,128)(2,1)S(1)}, bf16[32,768]{1,0:T(8,128)(2,1)S(1)}, bf16[32,768]{1,0:T(8,128)(2,1)S(1)}, bf16[32,768]{1,0:T(8,128)(2,1)S(1)}) custom-call(s32[4,4]{1,0:T(4,128)S(1)} %copy-done.4, s32[4]{0:T(128)S(1)} %copy-done.7, bf16[1,4,2,2,4,768]{5,4,3,2,1,0:T(4,128)(2,1)S(1)} %copy-done.3, bf16[1,4,2,4,4,768]{5,4,3,2,1,0:T(4,128)(2,1)S(1)} %copy-done.2), custom_call_target="tpu_custom_call" | custom-call | tf_op jit(solution)/shard_map/pack/pallas_call | solution.py:66
  4.5 3.1 %collective-permute-start = (bf16[32,768]{1,0:T(8,128)(2,1)S(1)}, bf16[32,768]{1,0:T(8,128)(2,1)S(1)}, u32[]{:S(2)}, u32[]{:S(2)}) collective-permute-start(bf16[32,768]{1,0:T(8,128)(2,1)S(1)} %get-tuple-element.9), channel_id=1, source_target_pairs={{0,4},{4,8},{8,12},{12,0},{1,5},{5,9},{9,13},{13,1},{2,6},{6,10},{... | collective-permute-start | bytes 147464 | tf_op jit(solution)/shard_map/ppermute | solution.py:339
  7.6 2.6 %collective-permute-start.1 = (bf16[32,768]{1,0:T(8,128)(2,1)S(1)}, bf16[32,768]{1,0:T(8,128)(2,1)S(1)}, u32[]{:S(2)}, u32[]{:S(2)}) collective-permute-start(bf16[32,768]{1,0:T(8,128)(2,1)S(1)} %get-tuple-element.10), channel_id=1, source_target_pairs={{0,8},{4,12},{8,0},{12,4},{1,9},{5,13},{9,1},{13,5},{2,10},{6,14},... | collective-permute-start | bytes 147464 | tf_op jit(solution)/shard_map/ppermute | solution.py:339
  10.2 1.3 %collective-permute-start.2 = (bf16[32,768]{1,0:T(8,128)(2,1)S(1)}, bf16[32,768]{1,0:T(8,128)(2,1)S(1)}, u32[]{:S(2)}, u32[]{:S(2)}) collective-permute-start(bf16[32,768]{1,0:T(8,128)(2,1)S(1)} %get-tuple-element.11), channel_id=1, source_target_pairs={{0,12},{4,0},{8,4},{12,8},{1,13},{5,1},{9,5},{13,9},{2,14},{6,2},{... | collective-permute-start | bytes 147464 | tf_op jit(solution)/shard_map/ppermute | solution.py:339
  11.5 0.3 collective-permute-done.refs_1_
  11.8 2.0 %collective-permute-done.1.refs_2_ = bf16[32,768]{1,0:T(8,128)(2,1)S(1)} collective-permute-done((bf16[32,768]{1,0:T(8,128)(2,1)S(1)}, bf16[32,768]{1,0:T(8,128)(2,1)S(1)}, u32[]{:S(2)}, u32[]{:S(2)}) %collective-permute-start.1) | collective-permute-done | bytes 49184 | tf_op jit(solution)/shard_map/ppermute | solution.py:339
  13.8 0.5 %collective-permute-done.2.refs_3_ = bf16[32,768]{1,0:T(8,128)(2,1)S(1)} collective-permute-done((bf16[32,768]{1,0:T(8,128)(2,1)S(1)}, bf16[32,768]{1,0:T(8,128)(2,1)S(1)}, u32[]{:S(2)}, u32[]{:S(2)}) %collective-permute-start.2) | collective-permute-done | bytes 49184 | tf_op jit(solution)/shard_map/ppermute | solution.py:339
  14.3 1.7 %collective-permute-start.3 = (bf16[64,768]{1,0:T(8,128)(2,1)S(1)}, bf16[64,768]{1,0:T(8,128)(2,1)S(1)}, u32[]{:S(2)}, u32[]{:S(2)}) collective-permute-start(bf16[64,768]{1,0:T(8,128)(2,1)S(1)} %get-tuple-element.12.valence), channel_id=1, source_target_pairs={{0,2},{2,0},{1,3},{3,1},{4,6},{6,4},{5,7},{7,5},{8,10},{10,8},{9,1... | collective-permute-start | bytes 294920 | tf_op jit(solution)/shard_map/ppermute | solution.py:339
  16.0 0.0 collective-permute-start.4
  16.0 0.0 copy-start
  16.0 2.3 %copy-done = bf16[1,2,768,1536]{3,2,1,0:T(8,128)(2,1)S(1)} copy-done((bf16[1,2,768,1536]{3,2,1,0:T(8,128)(2,1)S(1)}, bf16[1,2,768,1536]{3,2,1,0:T(8,128)(2,1)}, u32[]{:S(2)}) %copy-start) | copy-done | bytes 4718616
  18.3 0.0 copy-start.1
  18.3 0.0 copy-start.5
  18.3 0.0 copy-start.8
  18.3 0.8 %near_field.1.refs_5_ = f32[768,128]{1,0:T(8,128)S(1)} custom-call(bf16[1,2,768,1536]{3,2,1,0:T(8,128)(2,1)S(1)} %copy-done, bf16[64,768]{1,0:T(8,128)(2,1)S(1)} %get-tuple-element.12.valence), custom_call_target="tpu_custom_call" | custom-call | flops 301989888 | bytes 2359296 | tf_op jit(solution)/shard_map/near_field/pallas_call | solution.py:121
  19.1 0.0 collective-permute-done.3.refs_6_
  19.1 0.0 collective-permute-done.4.refs_8_
  19.1 0.0 copy-done.6
  19.1 0.0 copy-done.9
  19.1 0.0 copy-done.10
  19.1 0.0 copy-done.11
  19.1 1.5 %copy-done.1 = bf16[1,2,768,1536]{3,2,1,0:T(8,128)(2,1)S(1)} copy-done((bf16[1,2,768,1536]{3,2,1,0:T(8,128)(2,1)S(1)}, bf16[1,2,768,1536]{3,2,1,0:T(8,128)(2,1)}, u32[]{:S(2)}) %copy-start.1) | copy-done | bytes 4718616
  20.6 1.8 %project.1 = f32[24,128]{1,0:T(8,128)S(1)} custom-call(s32[16]{0:T(128)S(1)} %copy-done.9, f32[1,4]{1,0:T(1,128)S(1)} %copy-done.10, f32[1,4]{1,0:T(1,128)S(1)} %copy-done.11, f32[1,2,2,16]{3,2,1,0:T(2,128)S(1)} %copy-done.6, bf16[1,2,768,1536]{3,2,1,0:T(8,128)(2,1)S(1)} %copy-done.1, f32[768,128]{1,0:T(8,128)S(1)} %near_field.1.refs_5_, ...), custom_call_target="tpu_custom_call" | custom-call | tf_op jit(solution)/shard_map/project/pallas_call | solution.py:236
  22.5 0.5 %collective-permute-start.5 = (f32[24,128]{1,0:T(8,128)S(1)}, f32[24,128]{1,0:T(8,128)S(1)}, u32[]{:S(2)}, u32[]{:S(2)}) collective-permute-start(f32[24,128]{1,0:T(8,128)S(1)} %project.1), channel_id=1, source_target_pairs={{0,1},{1,0},{2,3},{3,2},{4,5},{5,4},{6,7},{7,6},{8,9},{9,8},{10,11... | collective-permute-start | bytes 36872 | tf_op jit(solution)/shard_map/ppermute | solution.py:348
  23.0 0.8 %collective-permute-done.5 = f32[24,128]{1,0:T(8,128)S(1)} collective-permute-done((f32[24,128]{1,0:T(8,128)S(1)}, f32[24,128]{1,0:T(8,128)S(1)}, u32[]{:S(2)}, u32[]{:S(2)}) %collective-permute-start.5) | collective-permute-done | bytes 12320 | tf_op jit(solution)/shard_map/ppermute | solution.py:348
  23.8 0.4 %collective-permute-start.6 = (f32[24,128]{1,0:T(8,128)S(1)}, f32[24,128]{1,0:T(8,128)S(1)}, u32[]{:S(2)}, u32[]{:S(2)}) collective-permute-start(f32[24,128]{1,0:T(8,128)S(1)} %add.6), channel_id=1, source_target_pairs={{0,2},{2,0},{1,3},{3,1},{4,6},{6,4},{5,7},{7,5},{8,10},{10,8},{9,1... | collective-permute-start | bytes 36872 | tf_op jit(solution)/shard_map/ppermute | solution.py:348
  24.3 3.3 %collective-permute-done.6 = f32[24,128]{1,0:T(8,128)S(1)} collective-permute-done((f32[24,128]{1,0:T(8,128)S(1)}, f32[24,128]{1,0:T(8,128)S(1)}, u32[]{:S(2)}, u32[]{:S(2)}) %collective-permute-start.6) | collective-permute-done | bytes 12320 | tf_op jit(solution)/shard_map/ppermute | solution.py:348
  27.5 0.7 %collective-permute-start.7 = (f32[24,128]{1,0:T(8,128)S(1)}, f32[24,128]{1,0:T(8,128)S(1)}, u32[]{:S(2)}, u32[]{:S(2)}) collective-permute-start(f32[24,128]{1,0:T(8,128)S(1)} %add.7.refs_0_), channel_id=1, source_target_pairs={{0,4},{4,8},{8,12},{12,0},{1,5},{5,9},{9,13},{13,1},{2,6},{6,10},{... | collective-permute-start | bytes 36872 | tf_op jit(solution)/shard_map/ppermute | solution.py:339
  28.2 2.9 %collective-permute-start.8 = (f32[24,128]{1,0:T(8,128)S(1)}, f32[24,128]{1,0:T(8,128)S(1)}, u32[]{:S(2)}, u32[]{:S(2)}) collective-permute-start(f32[24,128]{1,0:T(8,128)S(1)} %add.7.refs_0_), channel_id=1, source_target_pairs={{0,8},{4,12},{8,0},{12,4},{1,9},{5,13},{9,1},{13,5},{2,10},{6,14},... | collective-permute-start | bytes 36872 | tf_op jit(solution)/shard_map/ppermute | solution.py:339
  31.1 0.3 collective-permute-start.9
  31.4 1.6 %collective-permute-done.7.refs_1_ = f32[24,128]{1,0:T(8,128)S(1)} collective-permute-done((f32[24,128]{1,0:T(8,128)S(1)}, f32[24,128]{1,0:T(8,128)S(1)}, u32[]{:S(2)}, u32[]{:S(2)}) %collective-permute-start.7) | collective-permute-done | bytes 12320 | tf_op jit(solution)/shard_map/ppermute | solution.py:339
  33.0 0.0 collective-permute-done.8.refs_2_
  33.0 1.8 %collective-permute-done.9.refs_3_ = f32[24,128]{1,0:T(8,128)S(1)} collective-permute-done((f32[24,128]{1,0:T(8,128)S(1)}, f32[24,128]{1,0:T(8,128)S(1)}, u32[]{:S(2)}, u32[]{:S(2)}) %collective-permute-start.9) | collective-permute-done | bytes 12320 | tf_op jit(solution)/shard_map/ppermute | solution.py:339
  34.8 0.0 copy-done.5
  34.8 0.0 copy-done.8
  34.8 2.4 %haydock.1 = (f32[1,2,2,16]{3,2,1,0:T(2,128)}, f32[2,6]{1,0:T(2,128)}) custom-call(s32[4,4]{1,0:T(4,128)S(1)} %copy-done.5, s32[4]{0:T(128)S(1)} %copy-done.8, s32[16]{0:T(128)S(1)} %copy-done.9, f32[24,128]{1,0:T(8,128)S(1)} %add.7.refs_0_, f32[24,128]{1,0:T(8,128)S(1)} %collective-permute-done.7.refs_1_, f32[24,128]{1,0:T(8,128)S(1)} %collective-permute-done.8.refs_2_, ...), custom_call_target="tpu_custom_call" | custom-call | tf_op jit(solution)/shard_map/haydock/pallas_call | solution.py:320
  (3 shorter events, 0.0 us)
Async XLA Ops:
  0.6 0.9 %copy-start.2 = (bf16[1,4,2,4,4,768]{5,4,3,2,1,0:T(4,128)(2,1)S(1)}, bf16[1,4,2,4,4,768]{5,4,3,2,1,0:T(4,128)(2,1)}, u32[]{:S(2)}) copy-start(bf16[1,4,2,4,4,768]{5,4,3,2,1,0:T(4,128)(2,1)} %conduction.1) | copy-start | bytes 589828
  1.6 0.9 %copy-start.3 = (bf16[1,4,2,2,4,768]{5,4,3,2,1,0:T(4,128)(2,1)S(1)}, bf16[1,4,2,2,4,768]{5,4,3,2,1,0:T(4,128)(2,1)}, u32[]{:S(2)}) copy-start(bf16[1,4,2,2,4,768]{5,4,3,2,1,0:T(4,128)(2,1)} %valence.1) | copy-start | bytes 294916
  2.5 0.7 %copy-start.4 = (s32[4,4]{1,0:T(4,128)S(1)}, s32[4,4]{1,0:T(4,128)}, u32[]{:S(2)}) copy-start(s32[4,4]{1,0:T(4,128)} %qmap.3) | copy-start | bytes 196
  3.1 0.7 %copy-start.7 = (s32[4]{0:T(128)S(1)}, s32[4]{0:T(128)}, u32[]{:S(2)}) copy-start(s32[4]{0:T(128)} %owner.3) | copy-start | bytes 52
  3.8 15.3 %copy-start.6 = (f32[1,2,2,16]{3,2,1,0:T(2,128)S(1)}, f32[1,2,2,16]{3,2,1,0:T(2,128)}, u32[]{:S(2)}) copy-start(f32[1,2,2,16]{3,2,1,0:T(2,128)} %refs_3_.1) | copy-start | bytes 772
  3.8 15.3 %copy-start.9 = (s32[16]{0:T(128)S(1)}, s32[16]{0:T(128)}, u32[]{:S(2)}) copy-start(s32[16]{0:T(128)} %band_pairs.1) | copy-start | bytes 196
  3.8 15.3 %copy-start.10 = (f32[1,4]{1,0:T(1,128)S(1)}, f32[1,4]{1,0:T(1,128)}, u32[]{:S(2)}) copy-start(f32[1,4]{1,0:T(1,128)} %refs_1_.1) | copy-start | bytes 52
  3.8 15.3 %copy-start.11 = (f32[1,4]{1,0:T(1,128)S(1)}, f32[1,4]{1,0:T(1,128)}, u32[]{:S(2)}) copy-start(f32[1,4]{1,0:T(1,128)} %refs_2_.1) | copy-start | bytes 52
  4.5 7.3 %collective-permute-start = (bf16[32,768]{1,0:T(8,128)(2,1)S(1)}, bf16[32,768]{1,0:T(8,128)(2,1)S(1)}, u32[]{:S(2)}, u32[]{:S(2)}) collective-permute-start(bf16[32,768]{1,0:T(8,128)(2,1)S(1)} %get-tuple-element.9), channel_id=1, source_target_pairs={{0,4},{4,8},{8,12},{12,0},{1,5},{5,9},{9,13},{13,1},{2,6},{6,10},{... | collective-permute-start | bytes 147464 | tf_op jit(solution)/shard_map/ppermute | solution.py:339
  7.6 6.2 %collective-permute-start.1 = (bf16[32,768]{1,0:T(8,128)(2,1)S(1)}, bf16[32,768]{1,0:T(8,128)(2,1)S(1)}, u32[]{:S(2)}, u32[]{:S(2)}) collective-permute-start(bf16[32,768]{1,0:T(8,128)(2,1)S(1)} %get-tuple-element.10), channel_id=1, source_target_pairs={{0,8},{4,12},{8,0},{12,4},{1,9},{5,13},{9,1},{13,5},{2,10},{6,14},... | collective-permute-start | bytes 147464 | tf_op jit(solution)/shard_map/ppermute | solution.py:339
  10.2 4.1 %collective-permute-start.2 = (bf16[32,768]{1,0:T(8,128)(2,1)S(1)}, bf16[32,768]{1,0:T(8,128)(2,1)S(1)}, u32[]{:S(2)}, u32[]{:S(2)}) collective-permute-start(bf16[32,768]{1,0:T(8,128)(2,1)S(1)} %get-tuple-element.11), channel_id=1, source_target_pairs={{0,12},{4,0},{8,4},{12,8},{1,13},{5,1},{9,5},{13,9},{2,14},{6,2},{... | collective-permute-start | bytes 147464 | tf_op jit(solution)/shard_map/ppermute | solution.py:339
  14.3 4.8 %collective-permute-start.3 = (bf16[64,768]{1,0:T(8,128)(2,1)S(1)}, bf16[64,768]{1,0:T(8,128)(2,1)S(1)}, u32[]{:S(2)}, u32[]{:S(2)}) collective-permute-start(bf16[64,768]{1,0:T(8,128)(2,1)S(1)} %get-tuple-element.12.valence), channel_id=1, source_target_pairs={{0,2},{2,0},{1,3},{3,1},{4,6},{6,4},{5,7},{7,5},{8,10},{10,8},{9,1... | collective-permute-start | bytes 294920 | tf_op jit(solution)/shard_map/ppermute | solution.py:339
  16.0 3.1 %collective-permute-start.4 = (bf16[64,768]{1,0:T(8,128)(2,1)S(1)}, bf16[64,768]{1,0:T(8,128)(2,1)S(1)}, u32[]{:S(2)}, u32[]{:S(2)}) collective-permute-start(bf16[64,768]{1,0:T(8,128)(2,1)S(1)} %get-tuple-element.13.refs_7_), channel_id=1, source_target_pairs={{0,1},{1,0},{2,3},{3,2},{4,5},{5,4},{6,7},{7,6},{8,9},{9,8},{10,11... | collective-permute-start | bytes 294920 | tf_op jit(solution)/shard_map/ppermute | solution.py:339
  16.0 2.3 %copy-start = (bf16[1,2,768,1536]{3,2,1,0:T(8,128)(2,1)S(1)}, bf16[1,2,768,1536]{3,2,1,0:T(8,128)(2,1)}, u32[]{:S(2)}) copy-start(bf16[1,2,768,1536]{3,2,1,0:T(8,128)(2,1)} %refs_4_.1) | copy-start | bytes 14155780
  18.3 2.3 %copy-start.1 = (bf16[1,2,768,1536]{3,2,1,0:T(8,128)(2,1)S(1)}, bf16[1,2,768,1536]{3,2,1,0:T(8,128)(2,1)}, u32[]{:S(2)}) copy-start(bf16[1,2,768,1536]{3,2,1,0:T(8,128)(2,1)} %refs_4_.1) | copy-start | bytes 14155780
  18.3 16.5 %copy-start.5 = (s32[4,4]{1,0:T(4,128)S(1)}, s32[4,4]{1,0:T(4,128)}, u32[]{:S(2)}) copy-start(s32[4,4]{1,0:T(4,128)} %qmap.3) | copy-start | bytes 196
  18.3 16.5 %copy-start.8 = (s32[4]{0:T(128)S(1)}, s32[4]{0:T(128)}, u32[]{:S(2)}) copy-start(s32[4]{0:T(128)} %owner.3) | copy-start | bytes 52
  22.5 1.4 %collective-permute-start.5 = (f32[24,128]{1,0:T(8,128)S(1)}, f32[24,128]{1,0:T(8,128)S(1)}, u32[]{:S(2)}, u32[]{:S(2)}) collective-permute-start(f32[24,128]{1,0:T(8,128)S(1)} %project.1), channel_id=1, source_target_pairs={{0,1},{1,0},{2,3},{3,2},{4,5},{5,4},{6,7},{7,6},{8,9},{9,8},{10,11... | collective-permute-start | bytes 36872 | tf_op jit(solution)/shard_map/ppermute | solution.py:348
  23.8 3.7 %collective-permute-start.6 = (f32[24,128]{1,0:T(8,128)S(1)}, f32[24,128]{1,0:T(8,128)S(1)}, u32[]{:S(2)}, u32[]{:S(2)}) collective-permute-start(f32[24,128]{1,0:T(8,128)S(1)} %add.6), channel_id=1, source_target_pairs={{0,2},{2,0},{1,3},{3,1},{4,6},{6,4},{5,7},{7,5},{8,10},{10,8},{9,1... | collective-permute-start | bytes 36872 | tf_op jit(solution)/shard_map/ppermute | solution.py:348
  27.5 5.5 %collective-permute-start.7 = (f32[24,128]{1,0:T(8,128)S(1)}, f32[24,128]{1,0:T(8,128)S(1)}, u32[]{:S(2)}, u32[]{:S(2)}) collective-permute-start(f32[24,128]{1,0:T(8,128)S(1)} %add.7.refs_0_), channel_id=1, source_target_pairs={{0,4},{4,8},{8,12},{12,0},{1,5},{5,9},{9,13},{13,1},{2,6},{6,10},{... | collective-permute-start | bytes 36872 | tf_op jit(solution)/shard_map/ppermute | solution.py:339
  28.2 4.8 %collective-permute-start.8 = (f32[24,128]{1,0:T(8,128)S(1)}, f32[24,128]{1,0:T(8,128)S(1)}, u32[]{:S(2)}, u32[]{:S(2)}) collective-permute-start(f32[24,128]{1,0:T(8,128)S(1)} %add.7.refs_0_), channel_id=1, source_target_pairs={{0,8},{4,12},{8,0},{12,4},{1,9},{5,13},{9,1},{13,5},{2,10},{6,14},... | collective-permute-start | bytes 36872 | tf_op jit(solution)/shard_map/ppermute | solution.py:339
  31.1 3.7 %collective-permute-start.9 = (f32[24,128]{1,0:T(8,128)S(1)}, f32[24,128]{1,0:T(8,128)S(1)}, u32[]{:S(2)}, u32[]{:S(2)}) collective-permute-start(f32[24,128]{1,0:T(8,128)S(1)} %add.7.refs_0_), channel_id=1, source_target_pairs={{0,12},{4,0},{8,4},{12,8},{1,13},{5,1},{9,5},{13,9},{2,14},{6,2},{... | collective-permute-start | bytes 36872 | tf_op jit(solution)/shard_map/ppermute | solution.py:339

commit v3 on v2

v3 whole, which is shorter than its diff:
```python
import functools
import math

import jax
import jax.numpy as jnp
from jax import lax
from jax.experimental import pallas as pl
from jax.experimental.pallas import tpu as pltpu
from jax.sharding import PartitionSpec as P

EPSILON = 1e-06
EXACT = lax.Precision.HIGHEST
VMEM_LEAST = 8 * 1024 * 1024
VMEM_MOST = 56 * 1024 * 1024

vmem = pl.BlockSpec(memory_space=pltpu.VMEM)
anywhere = pl.BlockSpec(memory_space=pl.ANY)
EXTRA_ROWS = 8


def in_vmem(shape, dtype):
    return pltpu.VMEM(shape, dtype)


def placed(value, space):
    return pltpu.with_memory_space_constraint(value, space)


def iota(shape, axis):
    return lax.broadcasted_iota(jnp.int32, shape, axis)


def split(values):
    high = values.astype(jnp.bfloat16)
    low = (values - high.astype(jnp.float32)).astype(jnp.bfloat16)
    return high, low


def limits(*arrays):
    held = sum(math.prod(a.shape) * a.dtype.itemsize for a in arrays)
    return pltpu.CompilerParams(vmem_limit_bytes=min(VMEM_MOST, VMEM_LEAST + 4 * held))


def paired(me, step, size):
    if size & (size - 1):
        return lax.rem(me + step, size)
    return lax.bitwise_xor(me, step)


def origin(me, step, size):
    if size & (size - 1):
        return lax.rem(me + size - step, size)
    return lax.bitwise_xor(me, step)


def exchanged(value, axis, step):
    size = lax.axis_size(axis)
    if size & (size - 1):
        return lax.ppermute(value, axis, [(i, (i + step) % size) for i in range(size)])
    return lax.ppermute(value, axis, [(i, i ^ step) for i in range(size)])


def pack_kernel(ka, qmap_in, owner_in, valence_in, conduction_in, *rest):
    outs = rest[:ka]
    qmap, owner, partner, valence, conduction, sems = rest[ka:]
    copies = [
        pltpu.make_async_copy(src, dst, sems.at[at])
        for at, (src, dst) in enumerate(
            ((qmap_in, qmap), (owner_in, owner), (valence_in, valence), (conduction_in, conduction))
        )
    ]
    for copy in copies:
        copy.start()
    me = lax.axis_index("ka")
    half = lax.axis_index("ba")
    count, width = valence.shape[1], valence.shape[5]
    cond_count = conduction.shape[3]
    share = cond_count // lax.axis_size("ba")
    val_rows = 2 * valence.shape[3] * valence.shape[4]
    cond_rows = 2 * share * cond_count

    def note(k2, carry):
        partner[owner[qmap[me, k2]]] = k2
        return carry

    copies[0].wait()
    copies[1].wait()
    lax.fori_loop(0, count, note, 0)
    copies[2].wait()
    copies[3].wait()
    for j in range(ka):
        k2 = partner[paired(me, j, ka)]
        block = valence[0, k2].astype(jnp.float32).reshape(val_rows, width)
        outs[j][:val_rows, :] = block.astype(jnp.bfloat16)
        block = conduction[0, k2, :, pl.ds(half * share, share)].astype(jnp.float32)
        outs[j][val_rows:, :] = block.reshape(cond_rows, width).astype(jnp.bfloat16)


def pack(ka, ba, qmap, owner, valence, conduction):
    cond_count = conduction.shape[3]
    rows = 2 * valence.shape[3] * valence.shape[4] + 2 * cond_count // ba * cond_count
    shape = in_vmem((rows, valence.shape[5]), valence.dtype)
    operands = [placed(x, pltpu.HBM) for x in (qmap, owner, valence, conduction)]
    return pl.pallas_call(
        functools.partial(pack_kernel, ka),
        out_shape=[shape] * ka,
        in_specs=[anywhere] * 4,
        out_specs=[vmem] * ka,
        scratch_shapes=[
            pltpu.SMEM(qmap.shape, jnp.int32),
            pltpu.SMEM(owner.shape, jnp.int32),
            pltpu.SMEM(owner.shape, jnp.int32),
            pltpu.VMEM(valence.shape, valence.dtype),
            pltpu.VMEM(conduction.shape, conduction.dtype),
            pltpu.SemaphoreType.DMA((4,)),
        ],
        compiler_params=limits(valence, conduction),
        name="pack",
    )(*operands)


def prepare_kernel(ka, dims, *refs):
    vloc, val_count, cond_count, npol = dims
    ins, (screen_out, table, extras), scratch = refs[:7], refs[7:10], refs[10:]
    screen_in = ins[6]
    qmap, owner, band_pairs, val_energy, cond_energy, start, sems = scratch
    copies = [
        pltpu.make_async_copy(src, dst, sems.at[at])
        for at, (src, dst) in enumerate(
            zip(ins, (qmap, owner, band_pairs, val_energy, cond_energy, start, screen_out))
        )
    ]
    for copy in copies:
        copy.start()
    me = lax.axis_index("ka")
    half = lax.axis_index("ba")
    mine = lax.axis_index("ga")
    pairs = vloc * val_count
    block = 2 * pairs
    rows = ka * block
    codes = val_count * cond_count
    mid = ka * codes
    lanes = 2 * mid
    row = iota((2 * rows, lanes), 0)
    col = iota((2 * rows, lanes), 1)
    k_of_row = origin(me, row % rows // block, ka)
    want = (
        (row % block // pairs) * mid
        + k_of_row * codes
        + (half * vloc + row % pairs // val_count) * cond_count
    )
    joined = (col - want >= 0) & (col - want < cond_count)
    for v2 in range(val_count):
        pick = jnp.where(joined & (row % val_count == v2), 1.0, 0.0)
        table[:, v2 * lanes : (v2 + 1) * lanes] = pick.astype(jnp.bfloat16)

    for copy in copies[:6]:
        copy.wait()
    first = jnp.where((mine == 0) & (half == 0), 1.0, 0.0)
    lane = iota((1, lanes), 1)
    lane_k = lane % mid // codes
    band_row = iota((codes, lanes), 0)
    band_lane = iota((codes, lanes), 1)
    code = jnp.zeros((codes, lanes), jnp.int32)
    bands = jnp.full((1, lanes), -1.0, jnp.float32)
    for b in range(codes):
        code = jnp.where(band_row == b, band_pairs[b], code)
        bands = jnp.where(lane % codes == band_pairs[b], float(b), bands)
    vectors = jnp.zeros((npol, lanes), jnp.float32)
    for part in range(2):
        spot = part * mid + me * codes
        pick = jnp.where(band_lane == spot + code, first, 0.0)
        vectors = vectors + jnp.dot(start[0, :, part, :], pick, precision=EXACT)
    energy = jnp.zeros((1, lanes), jnp.float32)
    for c in range(cond_count):
        energy = jnp.where(lane % cond_count == c, cond_energy[0, c], energy)
    for v in range(val_count):
        energy = energy - jnp.where(lane % codes // cond_count == v, val_energy[0, v], 0.0)
    energy = jnp.where(lane_k == me, energy * first, 0.0)
    kcount = qmap.shape[0]

    def find(k2, found):
        return jnp.where(owner[qmap[0, k2]] == me, k2, found)

    back = lax.fori_loop(0, kcount, find, 0)
    second = lane_k + back
    second = jnp.where(second >= kcount, second - kcount, second).astype(jnp.float32) * first
    rest = jnp.zeros((EXTRA_ROWS - 3 - npol, lanes), jnp.float32)
    extras[...] = jnp.concatenate([vectors, energy, bands * first, second, rest], 0)
    copies[6].wait()


def prepare(ka, dims, qmap, owner, band_pairs, val_energy, cond_energy, start, screening):
    vloc, val_count, cond_count, npol = dims
    rows = 4 * ka * vloc * val_count
    lanes = 2 * ka * val_count * cond_count
    operands = (qmap, owner, band_pairs, val_energy, cond_energy, start, screening)
    table = jax.ShapeDtypeStruct((rows, val_count * lanes), jnp.bfloat16)
    return pl.pallas_call(
        functools.partial(prepare_kernel, ka, dims),
        out_shape=[
            in_vmem(screening.shape, screening.dtype),
            in_vmem(table.shape, table.dtype),
            in_vmem((EXTRA_ROWS, lanes), jnp.float32),
        ],
        in_specs=[anywhere] * 7,
        out_specs=[vmem] * 3,
        scratch_shapes=[pltpu.SMEM(x.shape, x.dtype) for x in operands[:5]]
        + [pltpu.VMEM(start.shape, start.dtype), pltpu.SemaphoreType.DMA((7,))],
        cost_estimate=pl.CostEstimate(
            flops=0, bytes_accessed=2 * screening.size * screening.dtype.itemsize, transcendentals=0
        ),
        compiler_params=limits(table),
        name="prepare",
    )(*[placed(x, pltpu.HBM) for x in operands])


def regroup_kernel(ka, val_rows, *refs):
    blocks, val_all, cond_half = refs[:ka], refs[ka], refs[ka + 1]
    cond_rows = blocks[0].shape[0] - val_rows
    for j in range(ka):
        val_all[j * val_rows : (j + 1) * val_rows, :] = blocks[j][:val_rows, :]
        cond_half[j * cond_rows : (j + 1) * cond_rows, :] = blocks[j][val_rows:, :]


def regroup(ka, val_rows, blocks):
    rows, width = blocks[0].shape
    kind = blocks[0].dtype
    return pl.pallas_call(
        functools.partial(regroup_kernel, ka, val_rows),
        out_shape=[in_vmem((ka * val_rows, width), kind), in_vmem((ka * (rows - val_rows), width), kind)],
        in_specs=[vmem] * ka,
        out_specs=[vmem] * 2,
        compiler_params=limits(*blocks),
        name="regroup",
    )(*blocks)


def screened_block(screening, valence, pairs, place):
    wide = valence[...].astype(jnp.float32)
    parts = []
    for at in range(0, wide.shape[0], 2 * pairs):
        parts += [-wide[at + pairs : at + 2 * pairs], wide[at : at + pairs]]
    turned = jnp.concatenate(parts, 0)
    real = jnp.concatenate([wide, turned], 0).astype(jnp.bfloat16)
    imag = jnp.concatenate([turned, -wide], 0).astype(jnp.bfloat16)
    width = valence.shape[1]
    columns = pl.ds(pl.multiple_of(place * width, 128), width)
    form = (((1,), (1,)), ((), ()))
    return lax.dot_general(
        screening[0, 0, :, columns], real, form, preferred_element_type=jnp.float32
    ) + lax.dot_general(screening[0, 1, :, columns], imag, form, preferred_element_type=jnp.float32)


def near_kernel(pairs, screening, valence, out):
    out[...] = screened_block(screening, valence, pairs, lax.axis_index("ga"))


def near_field(pairs, screening, valence):
    rows, width = valence.shape
    glocal = screening.shape[2]
    return pl.pallas_call(
        functools.partial(near_kernel, pairs),
        out_shape=in_vmem((glocal, 2 * rows), jnp.float32),
        in_specs=[vmem, vmem],
        out_specs=vmem,
        cost_estimate=pl.CostEstimate(
            flops=8 * glocal * width * rows, bytes_accessed=screening.size, transcendentals=0
        ),
        compiler_params=limits(screening, valence),
        name="near_field",
    )(screening, valence)


def project_kernel(ka, ga, ba, dims, *refs):
    vloc, val_count, cond_count, npol = dims
    screening, table, extras, near = refs[:4]
    val_in = refs[4 : 4 + ga - 1]
    cond_in = refs[4 + ga - 1 : 4 + ga - 1 + ba]
    out = refs[4 + ga - 1 + ba]
    mine = lax.axis_index("ga")
    half = lax.axis_index("ba")
    pairs = vloc * val_count
    block = 2 * pairs
    rows = ka * block
    codes = val_count * cond_count
    lanes = 2 * ka * codes
    share = cond_count // ba
    cond_rows = cond_count * cond_count
    share_rows = share * cond_count

    fields = near[...]
    for r in range(1, ga):
        fields = fields + screened_block(screening, val_in[r - 1], pairs, origin(mine, r, ga))
    high, low = split(fields)
    lane = iota((share_rows, 2 * rows), 1)
    lane_j = lane % rows // block
    turned_lane = lane // rows
    kernel = []
    for h in range(ba):
        cond_all = cond_in[h][...]
        crossed = jnp.dot(cond_all, high, preferred_element_type=jnp.float32) + jnp.dot(
            cond_all, low, preferred_element_type=jnp.float32
        )
        total = jnp.zeros((share_rows, 2 * rows), jnp.float32)
        for j in range(ka):
            base = j * 2 * share_rows
            same = lane_j == j
            total = total + jnp.where(
                same & (turned_lane == 0), crossed[base : base + share_rows], 0.0
            )
            total = total - jnp.where(
                same & (turned_lane == 1), crossed[base + share_rows : base + 2 * share_rows], 0.0
            )
        kernel.append(total)
    kernel = jnp.concatenate(kernel, 0)

    kernel_high, kernel_low = split(kernel)
    stacked = jnp.concatenate([kernel_high, kernel_low], 0)
    crow = iota((cond_rows, lanes), 0)
    c_of_row = origin(half, crow // share_rows, ba) * share + crow % share_rows // cond_count
    same_c = c_of_row == iota((cond_rows, lanes), 1) % cond_count
    spread = []
    for v2 in range(val_count):
        both = jnp.dot(
            stacked, table[:, v2 * lanes : (v2 + 1) * lanes], preferred_element_type=jnp.float32
        )
        spread.append(jnp.where(same_c, both[:cond_rows] + both[cond_rows:], 0.0))
    spread = jnp.concatenate(spread, 0)
    out_row = iota((codes, val_count * cond_rows), 0)
    out_col = iota((codes, val_count * cond_rows), 1)
    fold = (out_row // cond_count == out_col // cond_rows) & (
        out_row % cond_count == out_col % cond_count
    )
    fold = jnp.where(fold, 1.0, 0.0).astype(jnp.bfloat16)
    spread_high, spread_low = split(spread)
    out[:codes, :] = jnp.dot(fold, spread_high, preferred_element_type=jnp.float32) + jnp.dot(
        fold, spread_low, preferred_element_type=jnp.float32
    )
    out[codes:, :] = extras[...]


def project(ka, ga, ba, dims, screening, table, extras, near, val_far, cond_all):
    vloc, val_count, cond_count, npol = dims
    codes = val_count * cond_count
    operands = [screening, table, extras, near, *val_far, *cond_all]
    return pl.pallas_call(
        functools.partial(project_kernel, ka, ga, ba, dims),
        out_shape=in_vmem((codes + EXTRA_ROWS, 2 * ka * codes), jnp.float32),
        in_specs=[vmem] * len(operands),
        out_specs=vmem,
        compiler_params=limits(*operands[1:]),
        name="project",
    )(*operands)


def haydock_kernel(ka, codes, scale_count, npol, *refs):
    pieces = refs[:-3]
    next_out, coef_out, matrix = refs[-3:]
    lanes = pieces[0].shape[1]
    mid = lanes // 2
    height = codes + EXTRA_ROWS
    found = [(ref, at) for ref in pieces for at in range(0, ref.shape[0], height)]
    extras = None
    slots = []
    for ref, at in found:
        rows = ref[at + codes : at + height, :]
        extras = rows if extras is None else extras + rows
        slots.append((ref[at : at + codes, :], rows[npol + 2 : npol + 3]))
    own = pieces[0][codes:height, :]
    sign = jnp.where(iota((1, lanes), 1) < mid, -1.0, 1.0)
    for k2 in range(ka):
        block = jnp.zeros((codes, lanes), jnp.float32)
        for piece, second in slots:
            block = jnp.where(second == float(k2), piece, block)
        matrix[k2 * codes : (k2 + 1) * codes, :] = block
        matrix[mid + k2 * codes : mid + (k2 + 1) * codes, :] = sign * pltpu.roll(block, mid, 1)
    full = matrix[...]
    start = extras[:npol]
    energy = extras[npol : npol + 1]

    def mean(values):
        return jnp.sum(values, axis=1, keepdims=True) / scale_count

    def norm(vector):
        return jnp.sqrt(mean(vector * vector) + EPSILON)

    def swap(vector):
        return pltpu.roll(vector, mid, 1)

    def hamiltonian(vector):
        return energy * vector - jnp.dot(vector, full, precision=EXACT)

    def inner(left, right):
        return mean(left * right), mean(-sign * left * swap(right))

    def times(real, imag, vector):
        return real * vector + imag * (sign * swap(vector))

    first = start / norm(start)
    first_image = hamiltonian(first)
    alpha_real, alpha_imag = inner(first, first_image)
    first_resid = first_image - times(alpha_real, alpha_imag, first)
    beta_one = norm(first_resid)
    second = first_resid / beta_one
    second_image = hamiltonian(second)
    gamma_real, gamma_imag = inner(second, second_image)
    second_resid = second_image - times(gamma_real, gamma_imag, second) - beta_one * first
    beta_two = norm(second_resid)
    following = second_resid / beta_two

    coef_lane = iota(coef_out.shape, 1)
    coefs = jnp.zeros(coef_out.shape, jnp.float32)
    for at, value in enumerate((alpha_real, alpha_imag, gamma_real, gamma_imag, beta_one, beta_two)):
        coefs = jnp.where(coef_lane == at, value, coefs)
    coef_out[...] = coefs
    band = iota((codes, lanes), 0).astype(jnp.float32)
    here = iota((codes, lanes), 1) % mid // codes == lax.axis_index("ka")
    for part in range(2):
        half = iota((codes, lanes), 1) // mid == part
        pick = jnp.where(here & half & (own[npol + 1 : npol + 2] == band), 1.0, 0.0)
        next_out[0, :, part, :] = lax.dot_general(
            following, pick, (((1,), (1,)), ((), ())), precision=EXACT
        )


def haydock(ka, codes, scale_count, npol, pieces):
    lanes = pieces[0].shape[1]
    square = jax.ShapeDtypeStruct((lanes, lanes), jnp.float32)
    return pl.pallas_call(
        functools.partial(haydock_kernel, ka, codes, scale_count, npol),
        out_shape=[
            jax.ShapeDtypeStruct((1, npol, 2, codes), jnp.float32),
            jax.ShapeDtypeStruct((npol, 6), jnp.float32),
        ],
        in_specs=[vmem] * len(pieces),
        out_specs=[vmem, vmem],
        scratch_shapes=[pltpu.VMEM(square.shape, square.dtype)],
        compiler_params=limits(*pieces, square),
        name="haydock",
    )(*pieces)


def summed(value, axis):
    size = lax.axis_size(axis)
    if size & (size - 1):
        return lax.psum(value, axis)
    step = 1
    while step < size:
        value = value + exchanged(value, axis, step)
        step *= 2
    return value


def gathered(value, axis):
    size = lax.axis_size(axis)
    if size & (size - 1):
        return [value] + [exchanged(value, axis, j) for j in range(1, size)]
    step = 1
    while True:
        other = exchanged(value, axis, step)
        step *= 2
        if step >= size:
            return [value, other]
        value = jnp.concatenate([value, other], 0)


def local(
    ka,
    ga,
    ba,
    start_vector,
    valence_density,
    conduction_density,
    screening,
    qpoint_map,
    slot_owner,
    band_pairs,
    valence_energy,
    conduction_energy,
):
    npol = start_vector.shape[1]
    pair_count = start_vector.shape[3]
    kcount, vloc, val_count = qpoint_map.shape[0], valence_density.shape[3], valence_density.shape[4]
    cond_count = conduction_density.shape[3]
    pairs = vloc * val_count
    dims = (vloc, val_count, cond_count, npol)
    packed = pack(ka, ba, qpoint_map, slot_owner, valence_density, conduction_density)
    blocks = [packed[0]] + [exchanged(packed[j], "ka", j) for j in range(1, ka)]
    screening, table, extras = prepare(
        ka,
        dims,
        qpoint_map,
        slot_owner,
        band_pairs,
        valence_energy,
        conduction_energy,
        start_vector,
        screening,
    )
    val_all, cond_half = regroup(ka, 2 * pairs, blocks)
    cond_all = [cond_half] + [exchanged(cond_half, "ba", r) for r in range(1, ba)]
    val_far = [exchanged(val_all, "ga", r) for r in range(1, ga)]
    near = near_field(pairs, screening, val_all)
    piece = project(ka, ga, ba, dims, screening, table, extras, near, val_far, cond_all)
    piece = summed(summed(piece, "ba"), "ga")
    pieces = gathered(piece, "ka") if ka > 1 else [piece]
    scale_count = float(kcount * pair_count)
    return tuple(haydock(ka, pair_count, scale_count, npol, pieces))


def solution(mesh):
    in_specs = (
        P(("grp", "ka"), None, None, None),
        P(("grp", "ka"), None, None, "ba", None, "ga"),
        P(("grp", "ka"), None, None, None, None, "ga"),
        P(("grp", "ka"), None, "ga", None),
        P(),
        P(),
        P(),
        P(("grp", "ka"), None),
        P(("grp", "ka"), None),
    )
    out_specs = (P(("grp", "ka"), None, None, None), P("grp", None))
    body = functools.partial(local, mesh.shape["ka"], mesh.shape["ga"], mesh.shape["ba"])
    return jax.shard_map(body, mesh=mesh, in_specs=in_specs, out_specs=out_specs, check_vma=False)
```

time: 37.4 us -> 34.7 us (0.928)
  local copies, waits for them, and re-layouts: 7 us -> 0 us
  waiting for transfers between devices: 10.3 us -> 17.3 us
  starting transfers between devices: 13.5 us -> 9.33 us
  Pallas kernels: 5.67 us -> 7.25 us
    ppermute x10 -> x9, waiting for transfers between devices: 10.3 us -> 17.3 us  [exchanged(): return lax.ppermute(value, axis, [(i, i ^ step) for i in range(size)])]
    unnamed x24 -> x0, local copies, waits for them, and re-layouts: 7 us -> none
    ppermute x10 -> x9, starting transfers between devices: 13.5 us -> 9.33 us  [exchanged(): return lax.ppermute(value, axis, [(i, i ^ step) for i in range(size)])]
    pallas_call x1 -> x2, Pallas kernels: 2.38 us -> 4.14 us  [the longest x1 2.42 us: prepare(): pl.pallas_call(functools.partial(prepare_kernel, ka, dims), out_shape=[in...]
    pallas_call x1, Pallas kernels: 1.83 us -> 1.28 us  [project(): pl.pallas_call(functools.partial(project_kernel, ka, ga, ba, dims), out_s...]
  transfers between devices with their start and end apart: 10 -> 9, of which waited for: 7 -> 6; matrix products, arithmetic and copies ran while one was open for 0% -> 0% of each run, Pallas kernels for 2% -> 9%
where the time goes in v3:
time: 34.7 us; the launch traced here: 34.5 us
  waiting for transfers between devices  17.3 us (50%)
  starting transfers between devices  9.33 us (27%)
  Pallas kernels  7.25 us (21%)
  between operations  0.68 us (2%)
    ppermute x9, waiting for transfers between devices, exchanged(): return lax.ppermute(value, axis, [(i, i ^ step) for i in range(size)])  17.3 us
    ppermute x9, starting transfers between devices, exchanged(): return lax.ppermute(value, axis, [(i, i ^ step) for i in range(size)])  9.33 us
    pallas_call x1, Pallas kernels, prepare(): pl.pallas_call(functools.partial(prepare_kernel, ka, dims), out_shape=[in...  2.42 us
    pallas_call x1, Pallas kernels, haydock(): pl.pallas_call(functools.partial(haydock_kernel, ka, codes, scale_count,...  1.72 us
    pallas_call x1, Pallas kernels, project(): pl.pallas_call(functools.partial(project_kernel, ka, ga, ba, dims), out_s...  1.28 us
    pallas_call x1, Pallas kernels, pack(): pl.pallas_call(functools.partial(pack_kernel, ka), out_shape=[shape] * ka...  1.05 us
    pallas_call x1, Pallas kernels, near_field(): pl.pallas_call(functools.partial(near_kernel, pairs), out_shape=in_vmem((...  0.77 us
  transfers between devices with their start and end apart: 9, of which 6 were waited for; matrix products, arithmetic and copies ran while one was open for 0% of the time, Pallas kernels for 9%

profile of v3, /device:TPU:0, one launch (start us, length us, event | category | flops | bytes accessed | tf_op | source)
XLA Modules:
  0.0 34.5 jit_solution(12735198506533184523)
XLA Ops:
  0.6 1.0 %pack.1 = (bf16[32,768]{1,0:T(8,128)(2,1)S(1)}, bf16[32,768]{1,0:T(8,128)(2,1)S(1)}, bf16[32,768]{1,0:T(8,128)(2,1)S(1)}, bf16[32,768]{1,0:T(8,128)(2,1)S(1)}) custom-call(s32[4,4]{1,0:T(4,128)} %qmap_in.1, s32[4]{0:T(128)} %owner_in.1, bf16[1,4,2,2,4,768]{5,4,3,2,1,0:T(4,128)(2,1)} %valence_in.1, bf16[1,4,2,4,4,768]{5,4,3,2,1,0:T(4,128)(2,1)} %conduction_in.1), custom_call_target="tpu_custom_call" | custom-call | tf_op jit(solution)/shard_map/pack/pallas_call | solution.py:104
  1.7 3.1 %collective-permute-start = (bf16[32,768]{1,0:T(8,128)(2,1)S(1)}, bf16[32,768]{1,0:T(8,128)(2,1)S(1)}, u32[]{:S(2)}, u32[]{:S(2)}) collective-permute-start(bf16[32,768]{1,0:T(8,128)(2,1)S(1)} %get-tuple-element.15), channel_id=1, source_target_pairs={{0,4},{4,0},{8,12},{12,8},{1,5},{5,1},{9,13},{13,9},{2,6},{6,2},{1... | collective-permute-start | bytes 147464 | tf_op jit(solution)/shard_map/ppermute | solution.py:60
  4.8 2.6 %collective-permute-start.1 = (bf16[32,768]{1,0:T(8,128)(2,1)S(1)}, bf16[32,768]{1,0:T(8,128)(2,1)S(1)}, u32[]{:S(2)}, u32[]{:S(2)}) collective-permute-start(bf16[32,768]{1,0:T(8,128)(2,1)S(1)} %get-tuple-element.16), channel_id=1, source_target_pairs={{0,8},{4,12},{8,0},{12,4},{1,9},{5,13},{9,1},{13,5},{2,10},{6,14},... | collective-permute-start | bytes 147464 | tf_op jit(solution)/shard_map/ppermute | solution.py:60
  7.4 0.0 collective-permute-start.2
  7.4 0.0 collective-permute-done.refs_1_
  7.4 3.3 %collective-permute-done.1.refs_2_ = bf16[32,768]{1,0:T(8,128)(2,1)S(1)} collective-permute-done((bf16[32,768]{1,0:T(8,128)(2,1)S(1)}, bf16[32,768]{1,0:T(8,128)(2,1)S(1)}, u32[]{:S(2)}, u32[]{:S(2)}) %collective-permute-start.1) | collective-permute-done | bytes 49184 | tf_op jit(solution)/shard_map/ppermute | solution.py:60
  10.7 2.6 %collective-permute-done.2.refs_3_ = bf16[32,768]{1,0:T(8,128)(2,1)S(1)} collective-permute-done((bf16[32,768]{1,0:T(8,128)(2,1)S(1)}, bf16[32,768]{1,0:T(8,128)(2,1)S(1)}, u32[]{:S(2)}, u32[]{:S(2)}) %collective-permute-start.2) | collective-permute-done | bytes 49184 | tf_op jit(solution)/shard_map/ppermute | solution.py:60
  13.3 1.6 %collective-permute-start.3 = (bf16[64,768]{1,0:T(8,128)(2,1)S(1)}, bf16[64,768]{1,0:T(8,128)(2,1)S(1)}, u32[]{:S(2)}, u32[]{:S(2)}) collective-permute-start(bf16[64,768]{1,0:T(8,128)(2,1)S(1)} %get-tuple-element.18.valence), channel_id=1, source_target_pairs={{0,2},{2,0},{1,3},{3,1},{4,6},{6,4},{5,7},{7,5},{8,10},{10,8},{9,1... | collective-permute-start | bytes 294920 | tf_op jit(solution)/shard_map/ppermute | solution.py:60
  14.8 0.0 collective-permute-start.4
  14.8 2.4 %prepare.1 = (bf16[1,2,768,1536]{3,2,1,0:T(8,128)(2,1)S(1)}, bf16[128,512]{1,0:T(8,128)(2,1)S(1)}, f32[8,128]{1,0:T(8,128)S(1)}) custom-call(s32[4,4]{1,0:T(4,128)} %qmap_in.1, s32[4]{0:T(128)} %owner_in.1, s32[16]{0:T(128)} %refs_2_.1, f32[1,4]{1,0:T(1,128)} %refs_3_.1, f32[1,4]{1,0:T(1,128)} %refs_4_.1, f32[1,2,2,16]{3,2,1,0:T(2,128)} %refs_5_.1, ...), custom_call_target="tpu_custom_call" | custom-call | bytes 9437184 | tf_op jit(solution)/shard_map/prepare/pallas_call | solution.py:199
  17.3 0.8 %near_field.1.refs_3_ = f32[768,128]{1,0:T(8,128)S(1)} custom-call(bf16[1,2,768,1536]{3,2,1,0:T(8,128)(2,1)S(1)} %get-tuple-element.11.screening.refs_0_, bf16[64,768]{1,0:T(8,128)(2,1)S(1)} %get-tuple-element.18.valence), custom_call_target="tpu_custom_call" | custom-call | flops 301989888 | bytes 2359296 | tf_op jit(solution)/shard_map/near_field/pallas_call | solution.py:262
  18.0 0.0 collective-permute-done.3.refs_4_
  18.0 0.0 collective-permute-done.4.refs_6_
  18.1 1.3 %project.1 = f32[24,128]{1,0:T(8,128)S(1)} custom-call(bf16[1,2,768,1536]{3,2,1,0:T(8,128)(2,1)S(1)} %get-tuple-element.11.screening.refs_0_, bf16[128,512]{1,0:T(8,128)(2,1)S(1)} %get-tuple-element.12.refs_1_, f32[8,128]{1,0:T(8,128)S(1)} %get-tuple-element.13.refs_2_, f32[768,128]{1,0:T(8,128)S(1)} %near_field.1.refs_3_, ...), custom_call_target="tpu_custom_call" | custom-call | tf_op jit(solution)/shard_map/project/pallas_call | solution.py:347
  19.3 0.5 %collective-permute-start.5 = (f32[24,128]{1,0:T(8,128)S(1)}, f32[24,128]{1,0:T(8,128)S(1)}, u32[]{:S(2)}, u32[]{:S(2)}) collective-permute-start(f32[24,128]{1,0:T(8,128)S(1)} %project.1), channel_id=1, source_target_pairs={{0,1},{1,0},{2,3},{3,2},{4,5},{5,4},{6,7},{7,6},{8,9},{9,8},{10,11... | collective-permute-start | bytes 36872 | tf_op jit(solution)/shard_map/ppermute | solution.py:60
  19.9 0.8 %collective-permute-done.5 = f32[24,128]{1,0:T(8,128)S(1)} collective-permute-done((f32[24,128]{1,0:T(8,128)S(1)}, f32[24,128]{1,0:T(8,128)S(1)}, u32[]{:S(2)}, u32[]{:S(2)}) %collective-permute-start.5) | collective-permute-done | bytes 12320 | tf_op jit(solution)/shard_map/ppermute | solution.py:60
  20.7 1.2 %collective-permute-start.6 = (f32[24,128]{1,0:T(8,128)S(1)}, f32[24,128]{1,0:T(8,128)S(1)}, u32[]{:S(2)}, u32[]{:S(2)}) collective-permute-start(f32[24,128]{1,0:T(8,128)S(1)} %add.6), channel_id=1, source_target_pairs={{0,2},{2,0},{1,3},{3,1},{4,6},{6,4},{5,7},{7,5},{8,10},{10,8},{9,1... | collective-permute-start | bytes 36872 | tf_op jit(solution)/shard_map/ppermute | solution.py:60
  21.9 2.5 %collective-permute-done.6 = f32[24,128]{1,0:T(8,128)S(1)} collective-permute-done((f32[24,128]{1,0:T(8,128)S(1)}, f32[24,128]{1,0:T(8,128)S(1)}, u32[]{:S(2)}, u32[]{:S(2)}) %collective-permute-start.6) | collective-permute-done | bytes 12320 | tf_op jit(solution)/shard_map/ppermute | solution.py:60
  24.4 0.0 collective-permute-start.7
  24.4 3.7 %collective-permute-done.7 = f32[24,128]{1,0:T(8,128)S(1)} collective-permute-done((f32[24,128]{1,0:T(8,128)S(1)}, f32[24,128]{1,0:T(8,128)S(1)}, u32[]{:S(2)}, u32[]{:S(2)}) %collective-permute-start.7) | collective-permute-done | bytes 12320 | tf_op jit(solution)/shard_map/ppermute | solution.py:60
  28.1 0.4 %collective-permute-start.8 = (f32[48,128]{1,0:T(8,128)S(1)}, f32[48,128]{1,0:T(8,128)S(1)}, u32[]{:S(2)}, u32[]{:S(2)}) collective-permute-start(f32[48,128]{1,0:T(8,128)S(1)} %pad_maximum_fusion.refs_0_), channel_id=1, source_target_pairs={{0,8},{4,12},{8,0},{12,4},{1,9},{5,13},{9,1},{13,5},{2,10},{6,14},... | collective-permute-start | bytes 73736 | tf_op jit(solution)/shard_map/ppermute | solution.py:60
  28.5 4.4 %collective-permute-done.8.refs_1_ = f32[48,128]{1,0:T(8,128)S(1)} collective-permute-done((f32[48,128]{1,0:T(8,128)S(1)}, f32[48,128]{1,0:T(8,128)S(1)}, u32[]{:S(2)}, u32[]{:S(2)}) %collective-permute-start.8) | collective-permute-done | bytes 24608 | tf_op jit(solution)/shard_map/ppermute | solution.py:60
  32.8 1.7 %haydock.1 = (f32[1,2,2,16]{3,2,1,0:T(2,128)}, f32[2,6]{1,0:T(2,128)}) custom-call(f32[48,128]{1,0:T(8,128)S(1)} %pad_maximum_fusion.refs_0_, f32[48,128]{1,0:T(8,128)S(1)} %collective-permute-done.8.refs_1_), custom_call_target="tpu_custom_call" | custom-call | tf_op jit(solution)/shard_map/haydock/pallas_call | solution.py:430
  (4 shorter events, 0.0 us)
Async XLA Ops:
  1.7 5.7 %collective-permute-start = (bf16[32,768]{1,0:T(8,128)(2,1)S(1)}, bf16[32,768]{1,0:T(8,128)(2,1)S(1)}, u32[]{:S(2)}, u32[]{:S(2)}) collective-permute-start(bf16[32,768]{1,0:T(8,128)(2,1)S(1)} %get-tuple-element.15), channel_id=1, source_target_pairs={{0,4},{4,0},{8,12},{12,8},{1,5},{5,1},{9,13},{13,9},{2,6},{6,2},{1... | collective-permute-start | bytes 147464 | tf_op jit(solution)/shard_map/ppermute | solution.py:60
  4.8 5.9 %collective-permute-start.1 = (bf16[32,768]{1,0:T(8,128)(2,1)S(1)}, bf16[32,768]{1,0:T(8,128)(2,1)S(1)}, u32[]{:S(2)}, u32[]{:S(2)}) collective-permute-start(bf16[32,768]{1,0:T(8,128)(2,1)S(1)} %get-tuple-element.16), channel_id=1, source_target_pairs={{0,8},{4,12},{8,0},{12,4},{1,9},{5,13},{9,1},{13,5},{2,10},{6,14},... | collective-permute-start | bytes 147464 | tf_op jit(solution)/shard_map/ppermute | solution.py:60
  7.4 5.9 %collective-permute-start.2 = (bf16[32,768]{1,0:T(8,128)(2,1)S(1)}, bf16[32,768]{1,0:T(8,128)(2,1)S(1)}, u32[]{:S(2)}, u32[]{:S(2)}) collective-permute-start(bf16[32,768]{1,0:T(8,128)(2,1)S(1)} %get-tuple-element.17), channel_id=1, source_target_pairs={{0,12},{4,8},{8,4},{12,0},{1,13},{5,9},{9,5},{13,1},{2,14},{6,10},... | collective-permute-start | bytes 147464 | tf_op jit(solution)/shard_map/ppermute | solution.py:60
  13.3 4.8 %collective-permute-start.3 = (bf16[64,768]{1,0:T(8,128)(2,1)S(1)}, bf16[64,768]{1,0:T(8,128)(2,1)S(1)}, u32[]{:S(2)}, u32[]{:S(2)}) collective-permute-start(bf16[64,768]{1,0:T(8,128)(2,1)S(1)} %get-tuple-element.18.valence), channel_id=1, source_target_pairs={{0,2},{2,0},{1,3},{3,1},{4,6},{6,4},{5,7},{7,5},{8,10},{10,8},{9,1... | collective-permute-start | bytes 294920 | tf_op jit(solution)/shard_map/ppermute | solution.py:60
  14.8 3.2 %collective-permute-start.4 = (bf16[64,768]{1,0:T(8,128)(2,1)S(1)}, bf16[64,768]{1,0:T(8,128)(2,1)S(1)}, u32[]{:S(2)}, u32[]{:S(2)}) collective-permute-start(bf16[64,768]{1,0:T(8,128)(2,1)S(1)} %get-tuple-element.19.refs_5_), channel_id=1, source_target_pairs={{0,1},{1,0},{2,3},{3,2},{4,5},{5,4},{6,7},{7,6},{8,9},{9,8},{10,11... | collective-permute-start | bytes 294920 | tf_op jit(solution)/shard_map/ppermute | solution.py:60
  19.3 1.4 %collective-permute-start.5 = (f32[24,128]{1,0:T(8,128)S(1)}, f32[24,128]{1,0:T(8,128)S(1)}, u32[]{:S(2)}, u32[]{:S(2)}) collective-permute-start(f32[24,128]{1,0:T(8,128)S(1)} %project.1), channel_id=1, source_target_pairs={{0,1},{1,0},{2,3},{3,2},{4,5},{5,4},{6,7},{7,6},{8,9},{9,8},{10,11... | collective-permute-start | bytes 36872 | tf_op jit(solution)/shard_map/ppermute | solution.py:60
  20.7 3.7 %collective-permute-start.6 = (f32[24,128]{1,0:T(8,128)S(1)}, f32[24,128]{1,0:T(8,128)S(1)}, u32[]{:S(2)}, u32[]{:S(2)}) collective-permute-start(f32[24,128]{1,0:T(8,128)S(1)} %add.6), channel_id=1, source_target_pairs={{0,2},{2,0},{1,3},{3,1},{4,6},{6,4},{5,7},{7,5},{8,10},{10,8},{9,1... | collective-permute-start | bytes 36872 | tf_op jit(solution)/shard_map/ppermute | solution.py:60
  24.4 3.7 %collective-permute-start.7 = (f32[24,128]{1,0:T(8,128)S(1)}, f32[24,128]{1,0:T(8,128)S(1)}, u32[]{:S(2)}, u32[]{:S(2)}) collective-permute-start(f32[24,128]{1,0:T(8,128)S(1)} %add.7), channel_id=1, source_target_pairs={{0,4},{4,0},{8,12},{12,8},{1,5},{5,1},{9,13},{13,9},{2,6},{6,2},{1... | collective-permute-start | bytes 36872 | tf_op jit(solution)/shard_map/ppermute | solution.py:60
  28.1 4.7 %collective-permute-start.8 = (f32[48,128]{1,0:T(8,128)S(1)}, f32[48,128]{1,0:T(8,128)S(1)}, u32[]{:S(2)}, u32[]{:S(2)}) collective-permute-start(f32[48,128]{1,0:T(8,128)S(1)} %pad_maximum_fusion.refs_0_), channel_id=1, source_target_pairs={{0,8},{4,12},{8,0},{12,4},{1,9},{5,13},{9,1},{13,5},{2,10},{6,14},... | collective-permute-start | bytes 73736 | tf_op jit(solution)/shard_map/ppermute | solution.py:60

commit v4 on v3

--- a/solution.py
+++ b/solution.py
@@ -61,7 +61,7 @@
 
 
 def pack_kernel(ka, qmap_in, owner_in, valence_in, conduction_in, *rest):
-    outs = rest[:ka]
+    outs = rest[:1] + rest[1:ka][::-1]
     qmap, owner, partner, valence, conduction, sems = rest[ka:]
     copies = [
         pltpu.make_async_copy(src, dst, sems.at[at])
@@ -101,7 +101,7 @@
     rows = 2 * valence.shape[3] * valence.shape[4] + 2 * cond_count // ba * cond_count
     shape = in_vmem((rows, valence.shape[5]), valence.dtype)
     operands = [placed(x, pltpu.HBM) for x in (qmap, owner, valence, conduction)]
-    return pl.pallas_call(
+    outs = pl.pallas_call(
         functools.partial(pack_kernel, ka),
         out_shape=[shape] * ka,
         in_specs=[anywhere] * 4,
@@ -117,6 +117,7 @@
         compiler_params=limits(valence, conduction),
         name="pack",
     )(*operands)
+    return outs[:1] + outs[1:][::-1]
 
 
 def prepare_kernel(ka, dims, *refs):
@@ -216,24 +217,24 @@
 
 
 def regroup_kernel(ka, val_rows, *refs):
-    blocks, val_all, cond_half = refs[:ka], refs[ka], refs[ka + 1]
+    blocks, (val_all, cond_half) = refs[:ka], refs[-2:]
     cond_rows = blocks[0].shape[0] - val_rows
     for j in range(ka):
         val_all[j * val_rows : (j + 1) * val_rows, :] = blocks[j][:val_rows, :]
         cond_half[j * cond_rows : (j + 1) * cond_rows, :] = blocks[j][val_rows:, :]
 
 
-def regroup(ka, val_rows, blocks):
+def regroup(ka, val_rows, blocks, after):
     rows, width = blocks[0].shape
     kind = blocks[0].dtype
     return pl.pallas_call(
         functools.partial(regroup_kernel, ka, val_rows),
         out_shape=[in_vmem((ka * val_rows, width), kind), in_vmem((ka * (rows - val_rows), width), kind)],
-        in_specs=[vmem] * ka,
+        in_specs=[vmem] * (ka + 1),
         out_specs=[vmem] * 2,
         compiler_params=limits(*blocks),
         name="regroup",
-    )(*blocks)
+    )(*blocks, after)
 
 
 def screened_block(screening, valence, pairs, place):
@@ -452,17 +453,17 @@
     return value
 
 
-def gathered(value, axis):
-    size = lax.axis_size(axis)
-    if size & (size - 1):
-        return [value] + [exchanged(value, axis, j) for j in range(1, size)]
-    step = 1
-    while True:
-        other = exchanged(value, axis, step)
-        step *= 2
-        if step >= size:
-            return [value, other]
-        value = jnp.concatenate([value, other], 0)
+def spread(values, axis):
+    steps = range(lax.axis_size(axis) - 1, 0, -1)
+    return [exchanged(values[step], axis, step) for step in steps][::-1]
+
+
+def combined(value, first, second):
+    if lax.axis_size(first) != 2 or lax.axis_size(second) != 2:
+        return summed(summed(value, first), second)
+    other = exchanged(value, second, 1)
+    cross = lax.ppermute(value, (second, first), [(i, 3 - i) for i in range(4)])
+    return (value + exchanged(value, first, 1)) + (other + cross)
 
 
 def local(
@@ -486,7 +487,7 @@
     pairs = vloc * val_count
     dims = (vloc, val_count, cond_count, npol)
     packed = pack(ka, ba, qpoint_map, slot_owner, valence_density, conduction_density)
-    blocks = [packed[0]] + [exchanged(packed[j], "ka", j) for j in range(1, ka)]
+    blocks = [packed[0]] + spread(packed, "ka")
     screening, table, extras = prepare(
         ka,
         dims,
@@ -498,13 +499,13 @@
         start_vector,
         screening,
     )
-    val_all, cond_half = regroup(ka, 2 * pairs, blocks)
+    val_all, cond_half = regroup(ka, 2 * pairs, blocks, extras)
     cond_all = [cond_half] + [exchanged(cond_half, "ba", r) for r in range(1, ba)]
     val_far = [exchanged(val_all, "ga", r) for r in range(1, ga)]
     near = near_field(pairs, screening, val_all)
     piece = project(ka, ga, ba, dims, screening, table, extras, near, val_far, cond_all)
-    piece = summed(summed(piece, "ba"), "ga")
-    pieces = gathered(piece, "ka") if ka > 1 else [piece]
+    piece = combined(piece, "ba", "ga")
+    pieces = [piece] + spread([piece] * ka, "ka")
     scale_count = float(kcount * pair_count)
     return tuple(haydock(ka, pair_count, scale_count, npol, pieces))
 

time: 34.7 us -> 31.9 us (0.919)
  waiting for transfers between devices: 17.3 us -> 10.2 us
  starting transfers between devices: 9.33 us -> 13.5 us
    ppermute x9 -> x10, waiting for transfers between devices: 17.3 us -> 9.34 us  [exchanged(): return lax.ppermute(value, axis, [(i, i ^ step) for i in range(size)])]
    ppermute x9 -> x10, starting transfers between devices: 9.33 us -> 13.2 us  [exchanged(): return lax.ppermute(value, axis, [(i, i ^ step) for i in range(size)])]
    ppermute x0 -> x1, waiting for transfers between devices: none -> 0.9 us  [combined(): cross = lax.ppermute(value, (second, first), [(i, 3 - i) for i in range(4)])]
    ppermute x0 -> x1, starting transfers between devices: none -> 0.35 us  [combined(): cross = lax.ppermute(value, (second, first), [(i, 3 - i) for i in range(4)])]
  transfers between devices with their start and end apart: 9 -> 11, of which waited for: 6 -> 7; matrix products, arithmetic and copies ran while one was open for 0% -> 0% of each run, Pallas kernels for 9% -> 10%
where the time goes in v4:
time: 31.9 us; the launch traced here: 31.7 us
  starting transfers between devices  13.5 us (42%)
  waiting for transfers between devices  10.2 us (32%)
  Pallas kernels  7.25 us (23%)
  between operations  0.68 us (2%)
    ppermute x10, starting transfers between devices, exchanged(): return lax.ppermute(value, axis, [(i, i ^ step) for i in range(size)])  13.2 us
    ppermute x10, waiting for transfers between devices, exchanged(): return lax.ppermute(value, axis, [(i, i ^ step) for i in range(size)])  9.34 us
    pallas_call x1, Pallas kernels, prepare(): pl.pallas_call(functools.partial(prepare_kernel, ka, dims), out_shape=[in...  2.42 us
    pallas_call x1, Pallas kernels, haydock(): pl.pallas_call(functools.partial(haydock_kernel, ka, codes, scale_count,...  1.72 us
    pallas_call x1, Pallas kernels, project(): pl.pallas_call(functools.partial(project_kernel, ka, ga, ba, dims), out_s...  1.27 us
    pallas_call x1, Pallas kernels, pack(): pl.pallas_call(functools.partial(pack_kernel, ka), out_shape=[shape] * ka...  1.05 us
    ppermute x1, waiting for transfers between devices, combined(): cross = lax.ppermute(value, (second, first), [(i, 3 - i) for i in range(4)])  0.9 us
    pallas_call x1, Pallas kernels, near_field(): pl.pallas_call(functools.partial(near_kernel, pairs), out_shape=in_vmem((...  0.77 us
  transfers between devices with their start and end apart: 11, of which 7 were waited for; matrix products, arithmetic and copies ran while one was open for 0% of the time, Pallas kernels for 10%

profile of v4, /device:TPU:0, one launch (start us, length us, event | category | flops | bytes accessed | tf_op | source)
XLA Modules:
  0.0 31.7 jit_solution(6923243711675691940)
XLA Ops:
  0.6 1.0 %pack.1 = (bf16[32,768]{1,0:T(8,128)(2,1)S(1)}, bf16[32,768]{1,0:T(8,128)(2,1)S(1)}, bf16[32,768]{1,0:T(8,128)(2,1)S(1)}, bf16[32,768]{1,0:T(8,128)(2,1)S(1)}) custom-call(s32[4,4]{1,0:T(4,128)} %qmap_in.1, s32[4]{0:T(128)} %owner_in.1, bf16[1,4,2,2,4,768]{5,4,3,2,1,0:T(4,128)(2,1)} %valence_in.1, bf16[1,4,2,4,4,768]{5,4,3,2,1,0:T(4,128)(2,1)} %conduction_in.1), custom_call_target="tpu_custom_call" | custom-call | tf_op jit(solution)/shard_map/pack/pallas_call | solution.py:104
  1.7 3.1 %collective-permute-start = (bf16[32,768]{1,0:T(8,128)(2,1)S(1)}, bf16[32,768]{1,0:T(8,128)(2,1)S(1)}, u32[]{:S(2)}, u32[]{:S(2)}) collective-permute-start(bf16[32,768]{1,0:T(8,128)(2,1)S(1)} %get-tuple-element.15), channel_id=1, source_target_pairs={{0,4},{4,0},{8,12},{12,8},{1,5},{5,1},{9,13},{13,9},{2,6},{6,2},{1... | collective-permute-start | bytes 147464 | tf_op jit(solution)/shard_map/ppermute | solution.py:60
  4.8 2.6 %collective-permute-start.1 = (bf16[32,768]{1,0:T(8,128)(2,1)S(1)}, bf16[32,768]{1,0:T(8,128)(2,1)S(1)}, u32[]{:S(2)}, u32[]{:S(2)}) collective-permute-start(bf16[32,768]{1,0:T(8,128)(2,1)S(1)} %get-tuple-element.16), channel_id=1, source_target_pairs={{0,8},{4,12},{8,0},{12,4},{1,9},{5,13},{9,1},{13,5},{2,10},{6,14},... | collective-permute-start | bytes 147464 | tf_op jit(solution)/shard_map/ppermute | solution.py:60
  7.4 0.0 collective-permute-start.2
  7.4 2.4 %prepare.1 = (bf16[1,2,768,1536]{3,2,1,0:T(8,128)(2,1)S(1)}, bf16[128,512]{1,0:T(8,128)(2,1)S(1)}, f32[8,128]{1,0:T(8,128)S(1)}) custom-call(s32[4,4]{1,0:T(4,128)} %qmap_in.1, s32[4]{0:T(128)} %owner_in.1, s32[16]{0:T(128)} %refs_2_.1, f32[1,4]{1,0:T(1,128)} %refs_3_.1, f32[1,4]{1,0:T(1,128)} %refs_4_.1, f32[1,2,2,16]{3,2,1,0:T(2,128)} %refs_5_.1, ...), custom_call_target="tpu_custom_call" | custom-call | bytes 9437184 | tf_op jit(solution)/shard_map/prepare/pallas_call | solution.py:200
  9.8 0.0 collective-permute-done.refs_1_
  9.8 0.9 %collective-permute-done.1.refs_2_ = bf16[32,768]{1,0:T(8,128)(2,1)S(1)} collective-permute-done((bf16[32,768]{1,0:T(8,128)(2,1)S(1)}, bf16[32,768]{1,0:T(8,128)(2,1)S(1)}, u32[]{:S(2)}, u32[]{:S(2)}) %collective-permute-start.1) | collective-permute-done | bytes 49184 | tf_op jit(solution)/shard_map/ppermute | solution.py:60
  10.7 2.6 %collective-permute-done.2.refs_3_ = bf16[32,768]{1,0:T(8,128)(2,1)S(1)} collective-permute-done((bf16[32,768]{1,0:T(8,128)(2,1)S(1)}, bf16[32,768]{1,0:T(8,128)(2,1)S(1)}, u32[]{:S(2)}, u32[]{:S(2)}) %collective-permute-start.2) | collective-permute-done | bytes 49184 | tf_op jit(solution)/shard_map/ppermute | solution.py:60
  13.3 1.6 %collective-permute-start.3 = (bf16[64,768]{1,0:T(8,128)(2,1)S(1)}, bf16[64,768]{1,0:T(8,128)(2,1)S(1)}, u32[]{:S(2)}, u32[]{:S(2)}) collective-permute-start(bf16[64,768]{1,0:T(8,128)(2,1)S(1)} %get-tuple-element.18.valence), channel_id=1, source_target_pairs={{0,2},{2,0},{1,3},{3,1},{4,6},{6,4},{5,7},{7,5},{8,10},{10,8},{9,1... | collective-permute-start | bytes 294920 | tf_op jit(solution)/shard_map/ppermute | solution.py:60
  14.8 0.0 collective-permute-start.4
  14.8 0.8 %near_field.1.refs_3_ = f32[768,128]{1,0:T(8,128)S(1)} custom-call(bf16[1,2,768,1536]{3,2,1,0:T(8,128)(2,1)S(1)} %get-tuple-element.11.screening.refs_0_, bf16[64,768]{1,0:T(8,128)(2,1)S(1)} %get-tuple-element.18.valence), custom_call_target="tpu_custom_call" | custom-call | flops 301989888 | bytes 2359296 | tf_op jit(solution)/shard_map/near_field/pallas_call | solution.py:263
  15.6 2.3 %collective-permute-done.3.refs_4_ = bf16[64,768]{1,0:T(8,128)(2,1)S(1)} collective-permute-done((bf16[64,768]{1,0:T(8,128)(2,1)S(1)}, bf16[64,768]{1,0:T(8,128)(2,1)S(1)}, u32[]{:S(2)}, u32[]{:S(2)}) %collective-permute-start.3) | collective-permute-done | bytes 98336 | tf_op jit(solution)/shard_map/ppermute | solution.py:60
  18.0 0.0 collective-permute-done.4.refs_6_
  18.0 1.3 %project.1 = f32[24,128]{1,0:T(8,128)S(1)} custom-call(bf16[1,2,768,1536]{3,2,1,0:T(8,128)(2,1)S(1)} %get-tuple-element.11.screening.refs_0_, bf16[128,512]{1,0:T(8,128)(2,1)S(1)} %get-tuple-element.12.refs_1_, f32[8,128]{1,0:T(8,128)S(1)} %get-tuple-element.13.refs_4_.refs_2_, f32[768,128]{1,0:T(8,128)S(1)} %near_field.1.refs_3_, ...), custom_call_target="tpu_custom_call" | custom-call | tf_op jit(solution)/shard_map/project/pallas_call | solution.py:348
  19.2 0.0 collective-permute-start.5
  19.2 1.5 %collective-permute-start.6 = (f32[24,128]{1,0:T(8,128)S(1)}, f32[24,128]{1,0:T(8,128)S(1)}, u32[]{:S(2)}, u32[]{:S(2)}) collective-permute-start(f32[24,128]{1,0:T(8,128)S(1)} %project.1), channel_id=1, source_target_pairs={{0,2},{2,0},{1,3},{3,1},{4,6},{6,4},{5,7},{7,5},{8,10},{10,8},{9,1... | collective-permute-start | bytes 36872 | tf_op jit(solution)/shard_map/ppermute | solution.py:60
  20.8 0.3 %collective-permute-start.7 = (f32[24,128]{1,0:T(8,128)S(1)}, f32[24,128]{1,0:T(8,128)S(1)}, u32[]{:S(2)}, u32[]{:S(2)}) collective-permute-start(f32[24,128]{1,0:T(8,128)S(1)} %project.1), channel_id=1, source_target_pairs={{0,3},{1,2},{2,1},{3,0},{4,7},{5,6},{6,5},{7,4},{8,11},{9,10},{10,... | collective-permute-start | bytes 36872 | tf_op jit(solution)/shard_map/ppermute | solution.py:465
  21.1 0.0 collective-permute-done.5
  21.1 1.9 %collective-permute-done.6 = f32[24,128]{1,0:T(8,128)S(1)} collective-permute-done((f32[24,128]{1,0:T(8,128)S(1)}, f32[24,128]{1,0:T(8,128)S(1)}, u32[]{:S(2)}, u32[]{:S(2)}) %collective-permute-start.6) | collective-permute-done | bytes 12320 | tf_op jit(solution)/shard_map/ppermute | solution.py:60
  23.0 0.9 %collective-permute-done.7 = f32[24,128]{1,0:T(8,128)S(1)} collective-permute-done((f32[24,128]{1,0:T(8,128)S(1)}, f32[24,128]{1,0:T(8,128)S(1)}, u32[]{:S(2)}, u32[]{:S(2)}) %collective-permute-start.7) | collective-permute-done | bytes 12320 | tf_op jit(solution)/shard_map/ppermute | solution.py:465
  23.9 0.7 %collective-permute-start.10 = (f32[24,128]{1,0:T(8,128)S(1)}, f32[24,128]{1,0:T(8,128)S(1)}, u32[]{:S(2)}, u32[]{:S(2)}) collective-permute-start(f32[24,128]{1,0:T(8,128)S(1)} %add_add_fusion.refs_0_), channel_id=1, source_target_pairs={{0,12},{4,8},{8,4},{12,0},{1,13},{5,9},{9,5},{13,1},{2,14},{6,10},... | collective-permute-start | bytes 36872 | tf_op jit(solution)/shard_map/ppermute | solution.py:60
  24.6 0.2 collective-permute-start.8
  24.8 3.5 %collective-permute-start.9 = (f32[24,128]{1,0:T(8,128)S(1)}, f32[24,128]{1,0:T(8,128)S(1)}, u32[]{:S(2)}, u32[]{:S(2)}) collective-permute-start(f32[24,128]{1,0:T(8,128)S(1)} %add_add_fusion.refs_0_), channel_id=1, source_target_pairs={{0,8},{4,12},{8,0},{12,4},{1,9},{5,13},{9,1},{13,5},{2,10},{6,14},... | collective-permute-start | bytes 36872 | tf_op jit(solution)/shard_map/ppermute | solution.py:60
  28.3 1.2 %collective-permute-done.10.refs_3_ = f32[24,128]{1,0:T(8,128)S(1)} collective-permute-done((f32[24,128]{1,0:T(8,128)S(1)}, f32[24,128]{1,0:T(8,128)S(1)}, u32[]{:S(2)}, u32[]{:S(2)}) %collective-permute-start.10) | collective-permute-done | bytes 12320 | tf_op jit(solution)/shard_map/ppermute | solution.py:60
  29.5 0.0 collective-permute-done.8.refs_1_
  29.5 0.5 %collective-permute-done.9.refs_2_ = f32[24,128]{1,0:T(8,128)S(1)} collective-permute-done((f32[24,128]{1,0:T(8,128)S(1)}, f32[24,128]{1,0:T(8,128)S(1)}, u32[]{:S(2)}, u32[]{:S(2)}) %collective-permute-start.9) | collective-permute-done | bytes 12320 | tf_op jit(solution)/shard_map/ppermute | solution.py:60
  30.0 1.7 %haydock.1 = (f32[1,2,2,16]{3,2,1,0:T(2,128)}, f32[2,6]{1,0:T(2,128)}) custom-call(f32[24,128]{1,0:T(8,128)S(1)} %add_add_fusion.refs_0_, f32[24,128]{1,0:T(8,128)S(1)} %collective-permute-done.8.refs_1_, f32[24,128]{1,0:T(8,128)S(1)} %collective-permute-done.9.refs_2_, f32[24,128]{1,0:T(8,128)S(1)} %collective-permute-done.10.refs_3_), custom_call_target="tpu_custom_call" | custom-call | tf_op jit(solution)/shard_map/haydock/pallas_call | solution.py:431
  (2 shorter events, 0.0 us)
Async XLA Ops:
  1.7 8.1 %collective-permute-start = (bf16[32,768]{1,0:T(8,128)(2,1)S(1)}, bf16[32,768]{1,0:T(8,128)(2,1)S(1)}, u32[]{:S(2)}, u32[]{:S(2)}) collective-permute-start(bf16[32,768]{1,0:T(8,128)(2,1)S(1)} %get-tuple-element.15), channel_id=1, source_target_pairs={{0,4},{4,0},{8,12},{12,8},{1,5},{5,1},{9,13},{13,9},{2,6},{6,2},{1... | collective-permute-start | bytes 147464 | tf_op jit(solution)/shard_map/ppermute | solution.py:60
  4.8 5.9 %collective-permute-start.1 = (bf16[32,768]{1,0:T(8,128)(2,1)S(1)}, bf16[32,768]{1,0:T(8,128)(2,1)S(1)}, u32[]{:S(2)}, u32[]{:S(2)}) collective-permute-start(bf16[32,768]{1,0:T(8,128)(2,1)S(1)} %get-tuple-element.16), channel_id=1, source_target_pairs={{0,8},{4,12},{8,0},{12,4},{1,9},{5,13},{9,1},{13,5},{2,10},{6,14},... | collective-permute-start | bytes 147464 | tf_op jit(solution)/shard_map/ppermute | solution.py:60
  7.4 5.9 %collective-permute-start.2 = (bf16[32,768]{1,0:T(8,128)(2,1)S(1)}, bf16[32,768]{1,0:T(8,128)(2,1)S(1)}, u32[]{:S(2)}, u32[]{:S(2)}) collective-permute-start(bf16[32,768]{1,0:T(8,128)(2,1)S(1)} %get-tuple-element.17), channel_id=1, source_target_pairs={{0,12},{4,8},{8,4},{12,0},{1,13},{5,9},{9,5},{13,1},{2,14},{6,10},... | collective-permute-start | bytes 147464 | tf_op jit(solution)/shard_map/ppermute | solution.py:60
  13.3 4.7 %collective-permute-start.3 = (bf16[64,768]{1,0:T(8,128)(2,1)S(1)}, bf16[64,768]{1,0:T(8,128)(2,1)S(1)}, u32[]{:S(2)}, u32[]{:S(2)}) collective-permute-start(bf16[64,768]{1,0:T(8,128)(2,1)S(1)} %get-tuple-element.18.valence), channel_id=1, source_target_pairs={{0,2},{2,0},{1,3},{3,1},{4,6},{6,4},{5,7},{7,5},{8,10},{10,8},{9,1... | collective-permute-start | bytes 294920 | tf_op jit(solution)/shard_map/ppermute | solution.py:60
  14.8 3.1 %collective-permute-start.4 = (bf16[64,768]{1,0:T(8,128)(2,1)S(1)}, bf16[64,768]{1,0:T(8,128)(2,1)S(1)}, u32[]{:S(2)}, u32[]{:S(2)}) collective-permute-start(bf16[64,768]{1,0:T(8,128)(2,1)S(1)} %get-tuple-element.19.refs_5_), channel_id=1, source_target_pairs={{0,1},{1,0},{2,3},{3,2},{4,5},{5,4},{6,7},{7,6},{8,9},{9,8},{10,11... | collective-permute-start | bytes 294920 | tf_op jit(solution)/shard_map/ppermute | solution.py:60
  19.2 1.9 %collective-permute-start.5 = (f32[24,128]{1,0:T(8,128)S(1)}, f32[24,128]{1,0:T(8,128)S(1)}, u32[]{:S(2)}, u32[]{:S(2)}) collective-permute-start(f32[24,128]{1,0:T(8,128)S(1)} %project.1), channel_id=1, source_target_pairs={{0,1},{1,0},{2,3},{3,2},{4,5},{5,4},{6,7},{7,6},{8,9},{9,8},{10,11... | collective-permute-start | bytes 36872 | tf_op jit(solution)/shard_map/ppermute | solution.py:60
  19.2 3.8 %collective-permute-start.6 = (f32[24,128]{1,0:T(8,128)S(1)}, f32[24,128]{1,0:T(8,128)S(1)}, u32[]{:S(2)}, u32[]{:S(2)}) collective-permute-start(f32[24,128]{1,0:T(8,128)S(1)} %project.1), channel_id=1, source_target_pairs={{0,2},{2,0},{1,3},{3,1},{4,6},{6,4},{5,7},{7,5},{8,10},{10,8},{9,1... | collective-permute-start | bytes 36872 | tf_op jit(solution)/shard_map/ppermute | solution.py:60
  20.8 3.1 %collective-permute-start.7 = (f32[24,128]{1,0:T(8,128)S(1)}, f32[24,128]{1,0:T(8,128)S(1)}, u32[]{:S(2)}, u32[]{:S(2)}) collective-permute-start(f32[24,128]{1,0:T(8,128)S(1)} %project.1), channel_id=1, source_target_pairs={{0,3},{1,2},{2,1},{3,0},{4,7},{5,6},{6,5},{7,4},{8,11},{9,10},{10,... | collective-permute-start | bytes 36872 | tf_op jit(solution)/shard_map/ppermute | solution.py:465
  23.9 5.6 %collective-permute-start.10 = (f32[24,128]{1,0:T(8,128)S(1)}, f32[24,128]{1,0:T(8,128)S(1)}, u32[]{:S(2)}, u32[]{:S(2)}) collective-permute-start(f32[24,128]{1,0:T(8,128)S(1)} %add_add_fusion.refs_0_), channel_id=1, source_target_pairs={{0,12},{4,8},{8,4},{12,0},{1,13},{5,9},{9,5},{13,1},{2,14},{6,10},... | collective-permute-start | bytes 36872 | tf_op jit(solution)/shard_map/ppermute | solution.py:60
  24.6 4.9 %collective-permute-start.8 = (f32[24,128]{1,0:T(8,128)S(1)}, f32[24,128]{1,0:T(8,128)S(1)}, u32[]{:S(2)}, u32[]{:S(2)}) collective-permute-start(f32[24,128]{1,0:T(8,128)S(1)} %add_add_fusion.refs_0_), channel_id=1, source_target_pairs={{0,4},{4,0},{8,12},{12,8},{1,5},{5,1},{9,13},{13,9},{2,6},{6,2},{1... | collective-permute-start | bytes 36872 | tf_op jit(solution)/shard_map/ppermute | solution.py:60
  24.8 5.1 %collective-permute-start.9 = (f32[24,128]{1,0:T(8,128)S(1)}, f32[24,128]{1,0:T(8,128)S(1)}, u32[]{:S(2)}, u32[]{:S(2)}) collective-permute-start(f32[24,128]{1,0:T(8,128)S(1)} %add_add_fusion.refs_0_), channel_id=1, source_target_pairs={{0,8},{4,12},{8,0},{12,4},{1,9},{5,13},{9,1},{13,5},{2,10},{6,14},... | collective-permute-start | bytes 36872 | tf_op jit(solution)/shard_map/ppermute | solution.py:60

commit v5 on v3

--- a/solution.py
+++ b/solution.py
@@ -16,6 +16,7 @@
 vmem = pl.BlockSpec(memory_space=pltpu.VMEM)
 anywhere = pl.BlockSpec(memory_space=pl.ANY)
 EXTRA_ROWS = 8
+CHUNKS = 4
 
 
 def in_vmem(shape, dtype):
@@ -39,6 +40,10 @@
 def limits(*arrays):
     held = sum(math.prod(a.shape) * a.dtype.itemsize for a in arrays)
     return pltpu.CompilerParams(vmem_limit_bytes=min(VMEM_MOST, VMEM_LEAST + 4 * held))
+
+
+def order(size):
+    return [0] + list(range(size - 1, 0, -1))
 
 
 def paired(me, step, size):
@@ -88,12 +93,12 @@
     lax.fori_loop(0, count, note, 0)
     copies[2].wait()
     copies[3].wait()
-    for j in range(ka):
-        k2 = partner[paired(me, j, ka)]
+    for at, step in enumerate(order(ka)):
+        k2 = partner[paired(me, step, ka)]
         block = valence[0, k2].astype(jnp.float32).reshape(val_rows, width)
-        outs[j][:val_rows, :] = block.astype(jnp.bfloat16)
+        outs[at][:val_rows, :] = block.astype(jnp.bfloat16)
         block = conduction[0, k2, :, pl.ds(half * share, share)].astype(jnp.float32)
-        outs[j][val_rows:, :] = block.reshape(cond_rows, width).astype(jnp.bfloat16)
+        outs[at][val_rows:, :] = block.reshape(cond_rows, width).astype(jnp.bfloat16)
 
 
 def pack(ka, ba, qmap, owner, valence, conduction):
@@ -119,22 +124,40 @@
     )(*operands)
 
 
+def step_of(position, size):
+    return lax.rem(size - position, size)
+
+
+def column_copies(screening, out, place, sems):
+    width, height = out.shape[2], out.shape[1] // CHUNKS
+    columns = pl.ds(pl.multiple_of(place * width, 128), width)
+    return [
+        pltpu.make_async_copy(
+            screening.at[0, part, pl.ds(c * height, height), columns],
+            out.at[part, pl.ds(c * height, height)],
+            sems.at[part, c],
+        )
+        for part in range(2)
+        for c in range(CHUNKS)
+    ]
+
+
 def prepare_kernel(ka, dims, *refs):
     vloc, val_count, cond_count, npol = dims
-    ins, (screen_out, table, extras), scratch = refs[:7], refs[7:10], refs[10:]
-    screen_in = ins[6]
-    qmap, owner, band_pairs, val_energy, cond_energy, start, sems = scratch
+    ins, screening, (screen_out, table, extras), scratch = refs[:6], refs[6], refs[8:11], refs[11:]
+    qmap, owner, band_pairs, val_energy, cond_energy, start, sems, screen_sems = scratch
+    me = lax.axis_index("ka")
+    half = lax.axis_index("ba")
+    mine = lax.axis_index("ga")
     copies = [
         pltpu.make_async_copy(src, dst, sems.at[at])
         for at, (src, dst) in enumerate(
-            zip(ins, (qmap, owner, band_pairs, val_energy, cond_energy, start, screen_out))
+            zip(ins, (qmap, owner, band_pairs, val_energy, cond_energy, start))
         )
     ]
-    for copy in copies:
+    columns = column_copies(screening, screen_out, mine, screen_sems)
+    for copy in copies + columns:
         copy.start()
-    me = lax.axis_index("ka")
-    half = lax.axis_index("ba")
-    mine = lax.axis_index("ga")
     pairs = vloc * val_count
     block = 2 * pairs
     rows = ka * block
@@ -143,7 +166,7 @@
     lanes = 2 * mid
     row = iota((2 * rows, lanes), 0)
     col = iota((2 * rows, lanes), 1)
-    k_of_row = origin(me, row % rows // block, ka)
+    k_of_row = origin(me, step_of(row % rows // block, ka), ka)
     want = (
         (row % block // pairs) * mid
         + k_of_row * codes
@@ -154,7 +177,7 @@
         pick = jnp.where(joined & (row % val_count == v2), 1.0, 0.0)
         table[:, v2 * lanes : (v2 + 1) * lanes] = pick.astype(jnp.bfloat16)
 
-    for copy in copies[:6]:
+    for copy in copies:
         copy.wait()
     first = jnp.where((mine == 0) & (half == 0), 1.0, 0.0)
     lane = iota((1, lanes), 1)
@@ -187,98 +210,130 @@
     second = jnp.where(second >= kcount, second - kcount, second).astype(jnp.float32) * first
     rest = jnp.zeros((EXTRA_ROWS - 3 - npol, lanes), jnp.float32)
     extras[...] = jnp.concatenate([vectors, energy, bands * first, second, rest], 0)
-    copies[6].wait()
-
-
-def prepare(ka, dims, qmap, owner, band_pairs, val_energy, cond_energy, start, screening):
+    for copy in columns:
+        copy.wait()
+
+
+def prepare(ka, dims, qmap, owner, band_pairs, val_energy, cond_energy, start, screening, after):
     vloc, val_count, cond_count, npol = dims
     rows = 4 * ka * vloc * val_count
     lanes = 2 * ka * val_count * cond_count
     operands = (qmap, owner, band_pairs, val_energy, cond_energy, start, screening)
+    block = (2, screening.shape[2], after.shape[1])
     table = jax.ShapeDtypeStruct((rows, val_count * lanes), jnp.bfloat16)
     return pl.pallas_call(
         functools.partial(prepare_kernel, ka, dims),
         out_shape=[
-            in_vmem(screening.shape, screening.dtype),
+            in_vmem(block, screening.dtype),
             in_vmem(table.shape, table.dtype),
             in_vmem((EXTRA_ROWS, lanes), jnp.float32),
         ],
-        in_specs=[anywhere] * 7,
+        in_specs=[anywhere] * 8,
         out_specs=[vmem] * 3,
         scratch_shapes=[pltpu.SMEM(x.shape, x.dtype) for x in operands[:5]]
-        + [pltpu.VMEM(start.shape, start.dtype), pltpu.SemaphoreType.DMA((7,))],
+        + [
+            pltpu.VMEM(start.shape, start.dtype),
+            pltpu.SemaphoreType.DMA((6,)),
+            pltpu.SemaphoreType.DMA((2, CHUNKS)),
+        ],
         cost_estimate=pl.CostEstimate(
-            flops=0, bytes_accessed=2 * screening.size * screening.dtype.itemsize, transcendentals=0
+            flops=0, bytes_accessed=4 * math.prod(block), transcendentals=0
         ),
         compiler_params=limits(table),
         name="prepare",
-    )(*[placed(x, pltpu.HBM) for x in operands])
-
-
-def regroup_kernel(ka, val_rows, *refs):
-    blocks, val_all, cond_half = refs[:ka], refs[ka], refs[ka + 1]
-    cond_rows = blocks[0].shape[0] - val_rows
-    for j in range(ka):
-        val_all[j * val_rows : (j + 1) * val_rows, :] = blocks[j][:val_rows, :]
-        cond_half[j * cond_rows : (j + 1) * cond_rows, :] = blocks[j][val_rows:, :]
-
-
-def regroup(ka, val_rows, blocks):
-    rows, width = blocks[0].shape
-    kind = blocks[0].dtype
+    )(*[placed(x, pltpu.HBM) for x in operands], after)
+
+
+def hold_kernel(value, token, out):
+    out[...] = value[...]
+
+
+def hold(value, token):
     return pl.pallas_call(
-        functools.partial(regroup_kernel, ka, val_rows),
-        out_shape=[in_vmem((ka * val_rows, width), kind), in_vmem((ka * (rows - val_rows), width), kind)],
-        in_specs=[vmem] * ka,
-        out_specs=[vmem] * 2,
+        hold_kernel,
+        out_shape=in_vmem(value.shape, value.dtype),
+        in_specs=[vmem, anywhere],
+        out_specs=vmem,
+        compiler_params=limits(value),
+        name="hold",
+    )(value, token)
+
+
+def regroup_kernel(count, first, last, *refs):
+    blocks, out = refs[:count], refs[-1]
+    rows = last - first
+    for at in range(count):
+        out[at * rows : (at + 1) * rows, :] = blocks[at][first:last, :]
+
+
+def regroup(blocks, first, last, after=()):
+    shape = (len(blocks) * (last - first), blocks[0].shape[1])
+    return pl.pallas_call(
+        functools.partial(regroup_kernel, len(blocks), first, last),
+        out_shape=in_vmem(shape, blocks[0].dtype),
+        in_specs=[vmem] * len(blocks) + [anywhere] * len(after),
+        out_specs=vmem,
         compiler_params=limits(*blocks),
         name="regroup",
-    )(*blocks)
-
-
-def screened_block(screening, valence, pairs, place):
-    wide = valence[...].astype(jnp.float32)
+    )(*blocks, *after)
+
+
+def screened_block(screening, blocks, pairs):
+    wide = jnp.concatenate([block[...].astype(jnp.float32) for block in blocks], 0)
     parts = []
     for at in range(0, wide.shape[0], 2 * pairs):
         parts += [-wide[at + pairs : at + 2 * pairs], wide[at : at + pairs]]
     turned = jnp.concatenate(parts, 0)
     real = jnp.concatenate([wide, turned], 0).astype(jnp.bfloat16)
     imag = jnp.concatenate([turned, -wide], 0).astype(jnp.bfloat16)
-    width = valence.shape[1]
-    columns = pl.ds(pl.multiple_of(place * width, 128), width)
     form = (((1,), (1,)), ((), ()))
     return lax.dot_general(
-        screening[0, 0, :, columns], real, form, preferred_element_type=jnp.float32
-    ) + lax.dot_general(screening[0, 1, :, columns], imag, form, preferred_element_type=jnp.float32)
-
-
-def near_kernel(pairs, screening, valence, out):
-    out[...] = screened_block(screening, valence, pairs, lax.axis_index("ga"))
-
-
-def near_field(pairs, screening, valence):
-    rows, width = valence.shape
-    glocal = screening.shape[2]
-    return pl.pallas_call(
-        functools.partial(near_kernel, pairs),
-        out_shape=in_vmem((glocal, 2 * rows), jnp.float32),
-        in_specs=[vmem, vmem],
-        out_specs=vmem,
+        screening[0], real, form, preferred_element_type=jnp.float32
+    ) + lax.dot_general(screening[1], imag, form, preferred_element_type=jnp.float32)
+
+
+def near_kernel(ka, ga, pairs, *refs):
+    screening, near = refs[:2]
+    blocks = refs[2 : 2 + ka]
+    out, sems = refs[2 + ka], refs[-1]
+    far = refs[3 + ka : -1]
+    mine = lax.axis_index("ga")
+    copies = []
+    for r in range(1, ga):
+        copies += column_copies(screening, far[r - 1], origin(mine, r, ga), sems.at[r - 1])
+    for copy in copies:
+        copy.start()
+    out[...] = screened_block(near, [block.at[: 2 * pairs, :] for block in blocks], pairs)
+    for copy in copies:
+        copy.wait()
+
+
+def near_field(ga, pairs, screening, near, blocks):
+    ka, width = len(blocks), blocks[0].shape[1]
+    rows = 2 * pairs * ka
+    glocal = near.shape[1]
+    outs = pl.pallas_call(
+        functools.partial(near_kernel, ka, ga, pairs),
+        out_shape=[in_vmem((glocal, 2 * rows), jnp.float32)] + [in_vmem(near.shape, near.dtype)] * (ga - 1),
+        in_specs=[anywhere] + [vmem] * (ka + 1),
+        out_specs=[vmem] * ga,
+        scratch_shapes=[pltpu.SemaphoreType.DMA((max(ga - 1, 1), 2, CHUNKS))],
         cost_estimate=pl.CostEstimate(
-            flops=8 * glocal * width * rows, bytes_accessed=screening.size, transcendentals=0
+            flops=8 * glocal * width * rows, bytes_accessed=near.size * 4, transcendentals=0
         ),
-        compiler_params=limits(screening, valence),
+        compiler_params=limits(near, *blocks),
         name="near_field",
-    )(screening, valence)
+    )(placed(screening, pltpu.HBM), near, *blocks)
+    return outs[0], outs[1:]
 
 
 def project_kernel(ka, ga, ba, dims, *refs):
     vloc, val_count, cond_count, npol = dims
-    screening, table, extras, near = refs[:4]
-    val_in = refs[4 : 4 + ga - 1]
-    cond_in = refs[4 + ga - 1 : 4 + ga - 1 + ba]
-    out = refs[4 + ga - 1 + ba]
-    mine = lax.axis_index("ga")
+    table, extras, near = refs[:3]
+    screens = refs[3 : 2 + ga]
+    val_in = refs[2 + ga : 2 + ga + 2 * (ga - 1)]
+    cond_in = refs[-1 - ba : -1]
+    out = refs[-1]
     half = lax.axis_index("ba")
     pairs = vloc * val_count
     block = 2 * pairs
@@ -290,8 +345,8 @@
     share_rows = share * cond_count
 
     fields = near[...]
-    for r in range(1, ga):
-        fields = fields + screened_block(screening, val_in[r - 1], pairs, origin(mine, r, ga))
+    for r in range(ga - 1):
+        fields = fields + screened_block(screens[r], val_in[2 * r : 2 * r + 2], pairs)
     high, low = split(fields)
     lane = iota((share_rows, 2 * rows), 1)
     lane_j = lane % rows // block
@@ -340,16 +395,16 @@
     out[codes:, :] = extras[...]
 
 
-def project(ka, ga, ba, dims, screening, table, extras, near, val_far, cond_all):
+def project(ka, ga, ba, dims, table, extras, near, screens, val_far, cond_all):
     vloc, val_count, cond_count, npol = dims
     codes = val_count * cond_count
-    operands = [screening, table, extras, near, *val_far, *cond_all]
+    operands = [table, extras, near, *screens, *val_far, *cond_all]
     return pl.pallas_call(
         functools.partial(project_kernel, ka, ga, ba, dims),
         out_shape=in_vmem((codes + EXTRA_ROWS, 2 * ka * codes), jnp.float32),
         in_specs=[vmem] * len(operands),
         out_specs=vmem,
-        compiler_params=limits(*operands[1:]),
+        compiler_params=limits(*operands),
         name="project",
     )(*operands)
 
@@ -375,10 +430,15 @@
             block = jnp.where(second == float(k2), piece, block)
         matrix[k2 * codes : (k2 + 1) * codes, :] = block
         matrix[mid + k2 * codes : mid + (k2 + 1) * codes, :] = sign * pltpu.roll(block, mid, 1)
-    full = matrix[...]
+    high, low = split(matrix[...])
+    full = jnp.concatenate([high, low], 1)
     start = extras[:npol]
     energy = extras[npol : npol + 1]
 
+    def halves(vector):
+        top = vector.astype(jnp.bfloat16).astype(jnp.float32)
+        return jnp.concatenate([top, vector - top], 0).astype(jnp.bfloat16)
+
     def mean(values):
         return jnp.sum(values, axis=1, keepdims=True) / scale_count
 
@@ -389,7 +449,9 @@
         return pltpu.roll(vector, mid, 1)
 
     def hamiltonian(vector):
-        return energy * vector - jnp.dot(vector, full, precision=EXACT)
+        product = jnp.dot(halves(vector), full, preferred_element_type=jnp.float32)
+        main = product[:npol, :lanes] + product[npol:, :lanes]
+        return energy * vector - (main + product[:npol, lanes:])
 
     def inner(left, right):
         return mean(left * right), mean(-sign * left * swap(right))
@@ -414,14 +476,17 @@
     for at, value in enumerate((alpha_real, alpha_imag, gamma_real, gamma_imag, beta_one, beta_two)):
         coefs = jnp.where(coef_lane == at, value, coefs)
     coef_out[...] = coefs
-    band = iota((codes, lanes), 0).astype(jnp.float32)
-    here = iota((codes, lanes), 1) % mid // codes == lax.axis_index("ka")
-    for part in range(2):
-        half = iota((codes, lanes), 1) // mid == part
-        pick = jnp.where(here & half & (own[npol + 1 : npol + 2] == band), 1.0, 0.0)
-        next_out[0, :, part, :] = lax.dot_general(
-            following, pick, (((1,), (1,)), ((), ())), precision=EXACT
-        )
+    row = iota((2 * codes, lanes), 0)
+    lane = iota((2 * codes, lanes), 1)
+    here = (lane % mid // codes == lax.axis_index("ka")) & (lane // mid == row // codes)
+    band = (row % codes).astype(jnp.float32)
+    pick = jnp.where(here & (own[npol + 1 : npol + 2] == band), 1.0, 0.0).astype(jnp.bfloat16)
+    picked = lax.dot_general(
+        halves(following), pick, (((1,), (1,)), ((), ())), preferred_element_type=jnp.float32
+    )
+    picked = picked[:npol] + picked[npol:]
+    next_out[0, :, 0, :] = picked[:, :codes]
+    next_out[0, :, 1, :] = picked[:, codes:]
 
 
 def haydock(ka, codes, scale_count, npol, pieces):
@@ -452,17 +517,12 @@
     return value
 
 
-def gathered(value, axis):
-    size = lax.axis_size(axis)
-    if size & (size - 1):
-        return [value] + [exchanged(value, axis, j) for j in range(1, size)]
-    step = 1
-    while True:
-        other = exchanged(value, axis, step)
-        step *= 2
-        if step >= size:
-            return [value, other]
-        value = jnp.concatenate([value, other], 0)
+def sent(values, axis):
+    found, token = [values[0]], None
+    for step, value in zip(order(lax.axis_size(axis))[1:], values[1:]):
+        token = value if token is None else hold(value, token)
+        found.append(exchanged(token, axis, step))
+    return found
 
 
 def local(
@@ -486,8 +546,11 @@
     pairs = vloc * val_count
     dims = (vloc, val_count, cond_count, npol)
     packed = pack(ka, ba, qpoint_map, slot_owner, valence_density, conduction_density)
-    blocks = [packed[0]] + [exchanged(packed[j], "ka", j) for j in range(1, ka)]
-    screening, table, extras = prepare(
+    blocks = sent(packed, "ka")
+    early = ka // 2
+    val_early = regroup(blocks[:early], 0, 2 * pairs)
+    far_early = [exchanged(val_early, "ga", r) for r in range(1, ga)]
+    screen_near, table, extras = prepare(
         ka,
         dims,
         qpoint_map,
@@ -497,14 +560,17 @@
         conduction_energy,
         start_vector,
         screening,
+        val_early,
     )
-    val_all, cond_half = regroup(ka, 2 * pairs, blocks)
+    val_late = regroup(blocks[early:], 0, 2 * pairs, (extras, *far_early))
+    far_late = [exchanged(val_late, "ga", r) for r in range(1, ga)]
+    cond_half = regroup(blocks, 2 * pairs, blocks[0].shape[0], (val_late,))
     cond_all = [cond_half] + [exchanged(cond_half, "ba", r) for r in range(1, ba)]
-    val_far = [exchanged(val_all, "ga", r) for r in range(1, ga)]
-    near = near_field(pairs, screening, val_all)
-    piece = project(ka, ga, ba, dims, screening, table, extras, near, val_far, cond_all)
+    near, screens = near_field(ga, pairs, screening, screen_near, blocks)
+    val_far = [x for both in zip(far_early, far_late) for x in both]
+    piece = project(ka, ga, ba, dims, table, extras, near, screens, val_far, cond_all)
     piece = summed(summed(piece, "ba"), "ga")
-    pieces = gathered(piece, "ka") if ka > 1 else [piece]
+    pieces = sent([piece] * ka, "ka")
     scale_count = float(kcount * pair_count)
     return tuple(haydock(ka, pair_count, scale_count, npol, pieces))
 

time: 34.7 us -> 34.1 us (0.983)
  waiting for transfers between devices: 17.3 us -> 9.05 us
  starting transfers between devices: 9.33 us -> 16.2 us
  Pallas kernels: 7.25 us -> 7.96 us
    ppermute x9 -> x11, waiting for transfers between devices: 17.3 us -> 9.05 us  [exchanged(): return lax.ppermute(value, axis, [(i, i ^ step) for i in range(size)])]
    ppermute x9 -> x11, starting transfers between devices: 9.33 us -> 16.2 us  [exchanged(): return lax.ppermute(value, axis, [(i, i ^ step) for i in range(size)])]
    pallas_call x2 -> x8, Pallas kernels: 0.79 us -> 2.32 us  [the longest x1 2.29 us: near_field(): pl.pallas_call(functools.partial(near_kernel, ka, ga, pairs), out_shape=[...]
    pallas_call x1, Pallas kernels: 2.42 us -> 1.74 us  [prepare(): pl.pallas_call(functools.partial(prepare_kernel, ka, dims), out_shape=[in...]
  transfers between devices with their start and end apart: 9 -> 11, of which waited for: 6 -> 6; matrix products, arithmetic and copies ran while one was open for 0% -> 0% of each run, Pallas kernels for 9% -> 12%
where the time goes in v5:
time: 34.1 us; the launch traced here: 33.9 us
  starting transfers between devices  16.2 us (48%)
  waiting for transfers between devices  9.05 us (27%)
  Pallas kernels  7.96 us (23%)
  between operations  0.7 us (2%)
    ppermute x11, starting transfers between devices, exchanged(): return lax.ppermute(value, axis, [(i, i ^ step) for i in range(size)])  16.2 us
    ppermute x11, waiting for transfers between devices, exchanged(): return lax.ppermute(value, axis, [(i, i ^ step) for i in range(size)])  9.05 us
    pallas_call x1, Pallas kernels, near_field(): pl.pallas_call(functools.partial(near_kernel, ka, ga, pairs), out_shape=[...  2.29 us
    pallas_call x1, Pallas kernels, prepare(): pl.pallas_call(functools.partial(prepare_kernel, ka, dims), out_shape=[in...  1.74 us
    pallas_call x1, Pallas kernels, haydock(): pl.pallas_call(functools.partial(haydock_kernel, ka, codes, scale_count,...  1.61 us
    pallas_call x1, Pallas kernels, project(): pl.pallas_call(functools.partial(project_kernel, ka, ga, ba, dims), out_s...  1.25 us
    pallas_call x1, Pallas kernels, pack(): pl.pallas_call(functools.partial(pack_kernel, ka), out_shape=[shape] * ka...  1.05 us
  transfers between devices with their start and end apart: 11, of which 6 were waited for; matrix products, arithmetic and copies ran while one was open for 0% of the time, Pallas kernels for 12%

profile of v5, /device:TPU:0, one launch (start us, length us, event | category | flops | bytes accessed | tf_op | source)
XLA Modules:
  0.0 33.9 jit_solution(13524599872310866418)
XLA Ops:
  0.6 1.0 %pack.1 = (bf16[32,768]{1,0:T(8,128)(2,1)S(1)}, bf16[32,768]{1,0:T(8,128)(2,1)S(1)}, bf16[32,768]{1,0:T(8,128)(2,1)S(1)}, bf16[32,768]{1,0:T(8,128)(2,1)S(1)}) custom-call(s32[4,4]{1,0:T(4,128)} %refs_0_.2, s32[4]{0:T(128)} %refs_1_.1, bf16[1,4,2,2,4,768]{5,4,3,2,1,0:T(4,128)(2,1)} %valence_in.1, bf16[1,4,2,4,4,768]{5,4,3,2,1,0:T(4,128)(2,1)} %conduction_in.1), custom_call_target="tpu_custom_call" | custom-call | tf_op jit(solution)/shard_map/pack/pallas_call | solution.py:109
  1.7 5.1 %collective-permute-start = (bf16[32,768]{1,0:T(8,128)(2,1)S(1)}, bf16[32,768]{1,0:T(8,128)(2,1)S(1)}, u32[]{:S(2)}, u32[]{:S(2)}) collective-permute-start(bf16[32,768]{1,0:T(8,128)(2,1)S(1)} %get-tuple-element.12.token), channel_id=1, source_target_pairs={{0,12},{4,8},{8,4},{12,0},{1,13},{5,9},{9,5},{13,1},{2,14},{6,10},... | collective-permute-start | bytes 147464 | tf_op jit(solution)/shard_map/ppermute | solution.py:65
  6.8 0.0 collective-permute-start.1
  6.8 0.6 %collective-permute-start.2 = (bf16[32,768]{1,0:T(8,128)(2,1)S(1)}, bf16[32,768]{1,0:T(8,128)(2,1)S(1)}, u32[]{:S(2)}, u32[]{:S(2)}) collective-permute-start(bf16[32,768]{1,0:T(8,128)(2,1)S(1)} %hold.5), channel_id=1, source_target_pairs={{0,4},{4,0},{8,12},{12,8},{1,5},{5,1},{9,13},{13,9},{2,6},{6,2},{1... | collective-permute-start | bytes 147464 | tf_op jit(solution)/shard_map/ppermute | solution.py:65
  7.5 1.6 %collective-permute-done.refs_1_.refs_3_ = bf16[32,768]{1,0:T(8,128)(2,1)S(1)} collective-permute-done((bf16[32,768]{1,0:T(8,128)(2,1)S(1)}, bf16[32,768]{1,0:T(8,128)(2,1)S(1)}, u32[]{:S(2)}, u32[]{:S(2)}) %collective-permute-start) | collective-permute-done | bytes 49184 | tf_op jit(solution)/shard_map/ppermute | solution.py:65
  9.0 1.8 %collective-permute-start.3 = (bf16[32,768]{1,0:T(8,128)(2,1)S(1)}, bf16[32,768]{1,0:T(8,128)(2,1)S(1)}, u32[]{:S(2)}, u32[]{:S(2)}) collective-permute-start(bf16[32,768]{1,0:T(8,128)(2,1)S(1)} %regroup.3.refs_7_), channel_id=1, source_target_pairs={{0,2},{2,0},{1,3},{3,1},{4,6},{6,4},{5,7},{7,5},{8,10},{10,8},{9,1... | collective-permute-start | bytes 147464 | tf_op jit(solution)/shard_map/ppermute | solution.py:65
  10.8 1.7 %prepare.1 = (bf16[2,768,768]{2,1,0:T(8,128)(2,1)S(1)}, bf16[128,512]{1,0:T(8,128)(2,1)S(1)}, f32[8,128]{1,0:T(8,128)S(1)}) custom-call(s32[4,4]{1,0:T(4,128)} %refs_0_.2, s32[4]{0:T(128)} %refs_1_.1, s32[16]{0:T(128)} %refs_2_.1, f32[1,4]{1,0:T(1,128)} %refs_3_.1, f32[1,4]{1,0:T(1,128)} %refs_4_.1, f32[1,2,2,16]{3,2,1,0:T(2,128)} %refs_5_.1, ...), custom_call_target="tpu_custom_call" | custom-call | bytes 4718592 | tf_op jit(solution)/shard_map/prepare/pallas_call | solution.py:224
  12.6 0.0 collective-permute-done.1.refs_4_.refs_0_.refs_2_
  12.6 0.0 collective-permute-done.2.refs_5_.refs_1_.refs_3_
  12.6 0.5 %collective-permute-done.3.refs_3_.refs_4_ = bf16[32,768]{1,0:T(8,128)(2,1)S(1)} collective-permute-done((bf16[32,768]{1,0:T(8,128)(2,1)S(1)}, bf16[32,768]{1,0:T(8,128)(2,1)S(1)}, u32[]{:S(2)}, u32[]{:S(2)}) %collective-permute-start.3) | collective-permute-done | bytes 49184 | tf_op jit(solution)/shard_map/ppermute | solution.py:65
  13.1 0.1 collective-permute-start.5
  13.2 1.9 %collective-permute-start.4 = (bf16[32,768]{1,0:T(8,128)(2,1)S(1)}, bf16[32,768]{1,0:T(8,128)(2,1)S(1)}, u32[]{:S(2)}, u32[]{:S(2)}) collective-permute-start(bf16[32,768]{1,0:T(8,128)(2,1)S(1)} %regroup.4.refs_4_), channel_id=1, source_target_pairs={{0,2},{2,0},{1,3},{3,1},{4,6},{6,4},{5,7},{7,5},{8,10},{10,8},{9,1... | collective-permute-start | bytes 147464 | tf_op jit(solution)/shard_map/ppermute | solution.py:65
  15.1 2.3 %near_field.1 = (f32[768,128]{1,0:T(8,128)S(1)}, bf16[2,768,768]{2,1,0:T(8,128)(2,1)S(1)}) custom-call(bf16[1,2,768,1536]{3,2,1,0:T(8,128)(2,1)} %refs_0_.3, bf16[2,768,768]{2,1,0:T(8,128)(2,1)S(1)} %get-tuple-element.15.refs_1_, bf16[32,768]{1,0:T(8,128)(2,1)S(1)} %get-tuple-element.11.refs_0_.refs_2_, ...), custom_call_target="tpu_custom_call" | custom-call | flops 301989888 | bytes 4718592 | tf_op jit(solution)/shard_map/near_field/pallas_call | solution.py:315
  17.4 0.0 collective-permute-done.4.refs_5_
  17.4 0.0 collective-permute-done.5.refs_7_
  17.4 1.3 %project.1 = f32[24,128]{1,0:T(8,128)S(1)} custom-call(bf16[128,512]{1,0:T(8,128)(2,1)S(1)} %get-tuple-element.13.refs_0_, f32[8,128]{1,0:T(8,128)S(1)} %get-tuple-element.14.refs_2_.refs_1_, f32[768,128]{1,0:T(8,128)S(1)} %get-tuple-element.18.refs_2_, bf16[2,768,768]{2,1,0:T(8,128)(2,1)S(1)} %get-tuple-element.19.refs_3_, ...), custom_call_target="tpu_custom_call" | custom-call | tf_op jit(solution)/shard_map/project/pallas_call | solution.py:402
  18.7 0.2 collective-permute-start.6
  18.8 1.0 %collective-permute-done.6 = f32[24,128]{1,0:T(8,128)S(1)} collective-permute-done((f32[24,128]{1,0:T(8,128)S(1)}, f32[24,128]{1,0:T(8,128)S(1)}, u32[]{:S(2)}, u32[]{:S(2)}) %collective-permute-start.6) | collective-permute-done | bytes 12320 | tf_op jit(solution)/shard_map/ppermute | solution.py:65
  19.9 1.8 %collective-permute-start.7 = (f32[24,128]{1,0:T(8,128)S(1)}, f32[24,128]{1,0:T(8,128)S(1)}, u32[]{:S(2)}, u32[]{:S(2)}) collective-permute-start(f32[24,128]{1,0:T(8,128)S(1)} %add.6), channel_id=1, source_target_pairs={{0,2},{2,0},{1,3},{3,1},{4,6},{6,4},{5,7},{7,5},{8,10},{10,8},{9,1... | collective-permute-start | bytes 36872 | tf_op jit(solution)/shard_map/ppermute | solution.py:65
  21.6 1.9 %collective-permute-done.7 = f32[24,128]{1,0:T(8,128)S(1)} collective-permute-done((f32[24,128]{1,0:T(8,128)S(1)}, f32[24,128]{1,0:T(8,128)S(1)}, u32[]{:S(2)}, u32[]{:S(2)}) %collective-permute-start.7) | collective-permute-done | bytes 12320 | tf_op jit(solution)/shard_map/ppermute | solution.py:65
  23.6 4.2 %collective-permute-start.8 = (f32[24,128]{1,0:T(8,128)S(1)}, f32[24,128]{1,0:T(8,128)S(1)}, u32[]{:S(2)}, u32[]{:S(2)}) collective-permute-start(f32[24,128]{1,0:T(8,128)S(1)} %add.7.value.token.refs_0_), channel_id=1, source_target_pairs={{0,12},{4,8},{8,4},{12,0},{1,13},{5,9},{9,5},{13,1},{2,14},{6,10},... | collective-permute-start | bytes 36872 | tf_op jit(solution)/shard_map/ppermute | solution.py:65
  27.7 0.0 collective-permute-start.9
  27.7 0.6 %collective-permute-start.10 = (f32[24,128]{1,0:T(8,128)S(1)}, f32[24,128]{1,0:T(8,128)S(1)}, u32[]{:S(2)}, u32[]{:S(2)}) collective-permute-start(f32[24,128]{1,0:T(8,128)S(1)} %hold.7), channel_id=1, source_target_pairs={{0,4},{4,0},{8,12},{12,8},{1,5},{5,1},{9,13},{13,9},{2,6},{6,2},{1... | collective-permute-start | bytes 36872 | tf_op jit(solution)/shard_map/ppermute | solution.py:65
  28.4 1.0 %collective-permute-done.8.refs_1_ = f32[24,128]{1,0:T(8,128)S(1)} collective-permute-done((f32[24,128]{1,0:T(8,128)S(1)}, f32[24,128]{1,0:T(8,128)S(1)}, u32[]{:S(2)}, u32[]{:S(2)}) %collective-permute-start.8) | collective-permute-done | bytes 12320 | tf_op jit(solution)/shard_map/ppermute | solution.py:65
  29.4 2.9 %collective-permute-done.9.refs_2_ = f32[24,128]{1,0:T(8,128)S(1)} collective-permute-done((f32[24,128]{1,0:T(8,128)S(1)}, f32[24,128]{1,0:T(8,128)S(1)}, u32[]{:S(2)}, u32[]{:S(2)}) %collective-permute-start.9) | collective-permute-done | bytes 12320 | tf_op jit(solution)/shard_map/ppermute | solution.py:65
  32.3 0.0 collective-permute-done.10.refs_3_
  32.3 1.6 %haydock.1 = (f32[1,2,2,16]{3,2,1,0:T(2,128)}, f32[2,6]{1,0:T(2,128)}) custom-call(f32[24,128]{1,0:T(8,128)S(1)} %add.7.value.token.refs_0_, f32[24,128]{1,0:T(8,128)S(1)} %collective-permute-done.8.refs_1_, f32[24,128]{1,0:T(8,128)S(1)} %collective-permute-done.9.refs_2_, f32[24,128]{1,0:T(8,128)S(1)} %collective-permute-done.10.refs_3_), custom_call_target="tpu_custom_call" | custom-call | tf_op jit(solution)/shard_map/haydock/pallas_call | solution.py:495
  (9 shorter events, 0.0 us)
Async XLA Ops:
  1.7 7.3 %collective-permute-start = (bf16[32,768]{1,0:T(8,128)(2,1)S(1)}, bf16[32,768]{1,0:T(8,128)(2,1)S(1)}, u32[]{:S(2)}, u32[]{:S(2)}) collective-permute-start(bf16[32,768]{1,0:T(8,128)(2,1)S(1)} %get-tuple-element.12.token), channel_id=1, source_target_pairs={{0,12},{4,8},{8,4},{12,0},{1,13},{5,9},{9,5},{13,1},{2,14},{6,10},... | collective-permute-start | bytes 147464 | tf_op jit(solution)/shard_map/ppermute | solution.py:65
  6.8 5.8 %collective-permute-start.1 = (bf16[32,768]{1,0:T(8,128)(2,1)S(1)}, bf16[32,768]{1,0:T(8,128)(2,1)S(1)}, u32[]{:S(2)}, u32[]{:S(2)}) collective-permute-start(bf16[32,768]{1,0:T(8,128)(2,1)S(1)} %hold.4.token), channel_id=1, source_target_pairs={{0,8},{4,12},{8,0},{12,4},{1,9},{5,13},{9,1},{13,5},{2,10},{6,14},... | collective-permute-start | bytes 147464 | tf_op jit(solution)/shard_map/ppermute | solution.py:65
  6.8 5.8 %collective-permute-start.2 = (bf16[32,768]{1,0:T(8,128)(2,1)S(1)}, bf16[32,768]{1,0:T(8,128)(2,1)S(1)}, u32[]{:S(2)}, u32[]{:S(2)}) collective-permute-start(bf16[32,768]{1,0:T(8,128)(2,1)S(1)} %hold.5), channel_id=1, source_target_pairs={{0,4},{4,0},{8,12},{12,8},{1,5},{5,1},{9,13},{13,9},{2,6},{6,2},{1... | collective-permute-start | bytes 147464 | tf_op jit(solution)/shard_map/ppermute | solution.py:65
  9.0 4.1 %collective-permute-start.3 = (bf16[32,768]{1,0:T(8,128)(2,1)S(1)}, bf16[32,768]{1,0:T(8,128)(2,1)S(1)}, u32[]{:S(2)}, u32[]{:S(2)}) collective-permute-start(bf16[32,768]{1,0:T(8,128)(2,1)S(1)} %regroup.3.refs_7_), channel_id=1, source_target_pairs={{0,2},{2,0},{1,3},{3,1},{4,6},{6,4},{5,7},{7,5},{8,10},{10,8},{9,1... | collective-permute-start | bytes 147464 | tf_op jit(solution)/shard_map/ppermute | solution.py:65
  13.1 4.3 %collective-permute-start.5 = (bf16[64,768]{1,0:T(8,128)(2,1)S(1)}, bf16[64,768]{1,0:T(8,128)(2,1)S(1)}, u32[]{:S(2)}, u32[]{:S(2)}) collective-permute-start(bf16[64,768]{1,0:T(8,128)(2,1)S(1)} %regroup.5.refs_6_), channel_id=1, source_target_pairs={{0,1},{1,0},{2,3},{3,2},{4,5},{5,4},{6,7},{7,6},{8,9},{9,8},{10,11... | collective-permute-start | bytes 294920 | tf_op jit(solution)/shard_map/ppermute | solution.py:65
  13.2 4.2 %collective-permute-start.4 = (bf16[32,768]{1,0:T(8,128)(2,1)S(1)}, bf16[32,768]{1,0:T(8,128)(2,1)S(1)}, u32[]{:S(2)}, u32[]{:S(2)}) collective-permute-start(bf16[32,768]{1,0:T(8,128)(2,1)S(1)} %regroup.4.refs_4_), channel_id=1, source_target_pairs={{0,2},{2,0},{1,3},{3,1},{4,6},{6,4},{5,7},{7,5},{8,10},{10,8},{9,1... | collective-permute-start | bytes 147464 | tf_op jit(solution)/shard_map/ppermute | solution.py:65
  18.7 1.2 %collective-permute-start.6 = (f32[24,128]{1,0:T(8,128)S(1)}, f32[24,128]{1,0:T(8,128)S(1)}, u32[]{:S(2)}, u32[]{:S(2)}) collective-permute-start(f32[24,128]{1,0:T(8,128)S(1)} %project.1), channel_id=1, source_target_pairs={{0,1},{1,0},{2,3},{3,2},{4,5},{5,4},{6,7},{7,6},{8,9},{9,8},{10,11... | collective-permute-start | bytes 36872 | tf_op jit(solution)/shard_map/ppermute | solution.py:65
  19.9 3.7 %collective-permute-start.7 = (f32[24,128]{1,0:T(8,128)S(1)}, f32[24,128]{1,0:T(8,128)S(1)}, u32[]{:S(2)}, u32[]{:S(2)}) collective-permute-start(f32[24,128]{1,0:T(8,128)S(1)} %add.6), channel_id=1, source_target_pairs={{0,2},{2,0},{1,3},{3,1},{4,6},{6,4},{5,7},{7,5},{8,10},{10,8},{9,1... | collective-permute-start | bytes 36872 | tf_op jit(solution)/shard_map/ppermute | solution.py:65
  23.6 5.8 %collective-permute-start.8 = (f32[24,128]{1,0:T(8,128)S(1)}, f32[24,128]{1,0:T(8,128)S(1)}, u32[]{:S(2)}, u32[]{:S(2)}) collective-permute-start(f32[24,128]{1,0:T(8,128)S(1)} %add.7.value.token.refs_0_), channel_id=1, source_target_pairs={{0,12},{4,8},{8,4},{12,0},{1,13},{5,9},{9,5},{13,1},{2,14},{6,10},... | collective-permute-start | bytes 36872 | tf_op jit(solution)/shard_map/ppermute | solution.py:65
  27.7 4.6 %collective-permute-start.9 = (f32[24,128]{1,0:T(8,128)S(1)}, f32[24,128]{1,0:T(8,128)S(1)}, u32[]{:S(2)}, u32[]{:S(2)}) collective-permute-start(f32[24,128]{1,0:T(8,128)S(1)} %hold.6.token), channel_id=1, source_target_pairs={{0,8},{4,12},{8,0},{12,4},{1,9},{5,13},{9,1},{13,5},{2,10},{6,14},... | collective-permute-start | bytes 36872 | tf_op jit(solution)/shard_map/ppermute | solution.py:65
  27.7 4.6 %collective-permute-start.10 = (f32[24,128]{1,0:T(8,128)S(1)}, f32[24,128]{1,0:T(8,128)S(1)}, u32[]{:S(2)}, u32[]{:S(2)}) collective-permute-start(f32[24,128]{1,0:T(8,128)S(1)} %hold.7), channel_id=1, source_target_pairs={{0,4},{4,0},{8,12},{12,8},{1,5},{5,1},{9,13},{13,9},{2,6},{6,2},{1... | collective-permute-start | bytes 36872 | tf_op jit(solution)/shard_map/ppermute | solution.py:65

commit v6 on v5

--- a/solution.py
+++ b/solution.py
@@ -42,27 +42,17 @@
     return pltpu.CompilerParams(vmem_limit_bytes=min(VMEM_MOST, VMEM_LEAST + 4 * held))
 
 
-def order(size):
-    return [0] + list(range(size - 1, 0, -1))
-
-
-def paired(me, step, size):
-    if size & (size - 1):
-        return lax.rem(me + step, size)
-    return lax.bitwise_xor(me, step)
+def target(me, step, size):
+    return lax.rem(me + step, size)
 
 
 def origin(me, step, size):
-    if size & (size - 1):
-        return lax.rem(me + size - step, size)
-    return lax.bitwise_xor(me, step)
+    return lax.rem(me + size - step, size)
 
 
 def exchanged(value, axis, step):
     size = lax.axis_size(axis)
-    if size & (size - 1):
-        return lax.ppermute(value, axis, [(i, (i + step) % size) for i in range(size)])
-    return lax.ppermute(value, axis, [(i, i ^ step) for i in range(size)])
+    return lax.ppermute(value, axis, [(i, (i + step) % size) for i in range(size)])
 
 
 def pack_kernel(ka, qmap_in, owner_in, valence_in, conduction_in, *rest):
@@ -93,8 +83,8 @@
     lax.fori_loop(0, count, note, 0)
     copies[2].wait()
     copies[3].wait()
-    for at, step in enumerate(order(ka)):
-        k2 = partner[paired(me, step, ka)]
+    for at in range(ka):
+        k2 = partner[target(me, at, ka)]
         block = valence[0, k2].astype(jnp.float32).reshape(val_rows, width)
         outs[at][:val_rows, :] = block.astype(jnp.bfloat16)
         block = conduction[0, k2, :, pl.ds(half * share, share)].astype(jnp.float32)
@@ -124,24 +114,6 @@
     )(*operands)
 
 
-def step_of(position, size):
-    return lax.rem(size - position, size)
-
-
-def column_copies(screening, out, place, sems):
-    width, height = out.shape[2], out.shape[1] // CHUNKS
-    columns = pl.ds(pl.multiple_of(place * width, 128), width)
-    return [
-        pltpu.make_async_copy(
-            screening.at[0, part, pl.ds(c * height, height), columns],
-            out.at[part, pl.ds(c * height, height)],
-            sems.at[part, c],
-        )
-        for part in range(2)
-        for c in range(CHUNKS)
-    ]
-
-
 def prepare_kernel(ka, dims, *refs):
     vloc, val_count, cond_count, npol = dims
     ins, screening, (screen_out, table, extras), scratch = refs[:6], refs[6], refs[8:11], refs[11:]
@@ -155,8 +127,17 @@
             zip(ins, (qmap, owner, band_pairs, val_energy, cond_energy, start))
         )
     ]
-    columns = column_copies(screening, screen_out, mine, screen_sems)
-    for copy in copies + columns:
+    height = screening.shape[2] // CHUNKS
+    chunks = [
+        pltpu.make_async_copy(
+            screening.at[0, part, pl.ds(c * height, height)],
+            screen_out.at[part, pl.ds(c * height, height)],
+            screen_sems.at[part, c],
+        )
+        for part in range(2)
+        for c in range(CHUNKS)
+    ]
+    for copy in copies + chunks:
         copy.start()
     pairs = vloc * val_count
     block = 2 * pairs
@@ -166,7 +147,7 @@
     lanes = 2 * mid
     row = iota((2 * rows, lanes), 0)
     col = iota((2 * rows, lanes), 1)
-    k_of_row = origin(me, step_of(row % rows // block, ka), ka)
+    k_of_row = origin(me, row % rows // block, ka)
     want = (
         (row % block // pairs) * mid
         + k_of_row * codes
@@ -210,7 +191,7 @@
     second = jnp.where(second >= kcount, second - kcount, second).astype(jnp.float32) * first
     rest = jnp.zeros((EXTRA_ROWS - 3 - npol, lanes), jnp.float32)
     extras[...] = jnp.concatenate([vectors, energy, bands * first, second, rest], 0)
-    for copy in columns:
+    for copy in chunks:
         copy.wait()
 
 
@@ -219,12 +200,11 @@
     rows = 4 * ka * vloc * val_count
     lanes = 2 * ka * val_count * cond_count
     operands = (qmap, owner, band_pairs, val_energy, cond_energy, start, screening)
-    block = (2, screening.shape[2], after.shape[1])
     table = jax.ShapeDtypeStruct((rows, val_count * lanes), jnp.bfloat16)
     return pl.pallas_call(
         functools.partial(prepare_kernel, ka, dims),
         out_shape=[
-            in_vmem(block, screening.dtype),
+            in_vmem(screening.shape[1:], screening.dtype),
             in_vmem(table.shape, table.dtype),
             in_vmem((EXTRA_ROWS, lanes), jnp.float32),
         ],
@@ -237,26 +217,11 @@
             pltpu.SemaphoreType.DMA((2, CHUNKS)),
         ],
         cost_estimate=pl.CostEstimate(
-            flops=0, bytes_accessed=4 * math.prod(block), transcendentals=0
+            flops=0, bytes_accessed=4 * screening.size, transcendentals=0
         ),
         compiler_params=limits(table),
         name="prepare",
     )(*[placed(x, pltpu.HBM) for x in operands], after)
-
-
-def hold_kernel(value, token, out):
-    out[...] = value[...]
-
-
-def hold(value, token):
-    return pl.pallas_call(
-        hold_kernel,
-        out_shape=in_vmem(value.shape, value.dtype),
-        in_specs=[vmem, anywhere],
-        out_specs=vmem,
-        compiler_params=limits(value),
-        name="hold",
-    )(value, token)
 
 
 def regroup_kernel(count, first, last, *refs):
@@ -278,7 +243,7 @@
     )(*blocks, *after)
 
 
-def screened_block(screening, blocks, pairs):
+def screened_block(screening, blocks, pairs, place):
     wide = jnp.concatenate([block[...].astype(jnp.float32) for block in blocks], 0)
     parts = []
     for at in range(0, wide.shape[0], 2 * pairs):
@@ -286,54 +251,41 @@
     turned = jnp.concatenate(parts, 0)
     real = jnp.concatenate([wide, turned], 0).astype(jnp.bfloat16)
     imag = jnp.concatenate([turned, -wide], 0).astype(jnp.bfloat16)
+    width = wide.shape[1]
+    columns = pl.ds(pl.multiple_of(place * width, 128), width)
     form = (((1,), (1,)), ((), ()))
     return lax.dot_general(
-        screening[0], real, form, preferred_element_type=jnp.float32
-    ) + lax.dot_general(screening[1], imag, form, preferred_element_type=jnp.float32)
-
-
-def near_kernel(ka, ga, pairs, *refs):
-    screening, near = refs[:2]
-    blocks = refs[2 : 2 + ka]
-    out, sems = refs[2 + ka], refs[-1]
-    far = refs[3 + ka : -1]
-    mine = lax.axis_index("ga")
-    copies = []
-    for r in range(1, ga):
-        copies += column_copies(screening, far[r - 1], origin(mine, r, ga), sems.at[r - 1])
-    for copy in copies:
-        copy.start()
-    out[...] = screened_block(near, [block.at[: 2 * pairs, :] for block in blocks], pairs)
-    for copy in copies:
-        copy.wait()
-
-
-def near_field(ga, pairs, screening, near, blocks):
-    ka, width = len(blocks), blocks[0].shape[1]
-    rows = 2 * pairs * ka
-    glocal = near.shape[1]
-    outs = pl.pallas_call(
-        functools.partial(near_kernel, ka, ga, pairs),
-        out_shape=[in_vmem((glocal, 2 * rows), jnp.float32)] + [in_vmem(near.shape, near.dtype)] * (ga - 1),
-        in_specs=[anywhere] + [vmem] * (ka + 1),
-        out_specs=[vmem] * ga,
-        scratch_shapes=[pltpu.SemaphoreType.DMA((max(ga - 1, 1), 2, CHUNKS))],
+        screening[0, :, columns], real, form, preferred_element_type=jnp.float32
+    ) + lax.dot_general(screening[1, :, columns], imag, form, preferred_element_type=jnp.float32)
+
+
+def near_kernel(pairs, screening, *refs):
+    refs[-1][...] = screened_block(screening, refs[:-1], pairs, lax.axis_index("ga"))
+
+
+def near_field(pairs, screening, blocks):
+    rows = sum(block.shape[0] for block in blocks)
+    glocal, width = screening.shape[1], blocks[0].shape[1]
+    return pl.pallas_call(
+        functools.partial(near_kernel, pairs),
+        out_shape=in_vmem((glocal, 2 * rows), jnp.float32),
+        in_specs=[vmem] * (1 + len(blocks)),
+        out_specs=vmem,
         cost_estimate=pl.CostEstimate(
-            flops=8 * glocal * width * rows, bytes_accessed=near.size * 4, transcendentals=0
+            flops=8 * glocal * width * rows, bytes_accessed=screening.size, transcendentals=0
         ),
-        compiler_params=limits(near, *blocks),
+        compiler_params=limits(screening, *blocks),
         name="near_field",
-    )(placed(screening, pltpu.HBM), near, *blocks)
-    return outs[0], outs[1:]
+    )(screening, *blocks)
 
 
 def project_kernel(ka, ga, ba, dims, *refs):
     vloc, val_count, cond_count, npol = dims
-    table, extras, near = refs[:3]
-    screens = refs[3 : 2 + ga]
-    val_in = refs[2 + ga : 2 + ga + 2 * (ga - 1)]
+    screening, table, extras, near = refs[:4]
+    val_in = refs[4 : 4 + 2 * (ga - 1)]
     cond_in = refs[-1 - ba : -1]
     out = refs[-1]
+    mine = lax.axis_index("ga")
     half = lax.axis_index("ba")
     pairs = vloc * val_count
     block = 2 * pairs
@@ -345,8 +297,9 @@
     share_rows = share * cond_count
 
     fields = near[...]
-    for r in range(ga - 1):
-        fields = fields + screened_block(screens[r], val_in[2 * r : 2 * r + 2], pairs)
+    for r in range(1, ga):
+        halves = val_in[2 * r - 2 : 2 * r]
+        fields = fields + screened_block(screening, halves, pairs, origin(mine, r, ga))
     high, low = split(fields)
     lane = iota((share_rows, 2 * rows), 1)
     lane_j = lane % rows // block
@@ -395,10 +348,10 @@
     out[codes:, :] = extras[...]
 
 
-def project(ka, ga, ba, dims, table, extras, near, screens, val_far, cond_all):
+def project(ka, ga, ba, dims, screening, table, extras, near, val_far, cond_all):
     vloc, val_count, cond_count, npol = dims
     codes = val_count * cond_count
-    operands = [table, extras, near, *screens, *val_far, *cond_all]
+    operands = [screening, table, extras, near, *val_far, *cond_all]
     return pl.pallas_call(
         functools.partial(project_kernel, ka, ga, ba, dims),
         out_shape=in_vmem((codes + EXTRA_ROWS, 2 * ka * codes), jnp.float32),
@@ -512,17 +465,13 @@
         return lax.psum(value, axis)
     step = 1
     while step < size:
-        value = value + exchanged(value, axis, step)
+        value = value + lax.ppermute(value, axis, [(i, i ^ step) for i in range(size)])
         step *= 2
     return value
 
 
 def sent(values, axis):
-    found, token = [values[0]], None
-    for step, value in zip(order(lax.axis_size(axis))[1:], values[1:]):
-        token = value if token is None else hold(value, token)
-        found.append(exchanged(token, axis, step))
-    return found
+    return [values[0]] + [exchanged(values[j], axis, j) for j in range(1, lax.axis_size(axis))]
 
 
 def local(
@@ -550,7 +499,7 @@
     early = ka // 2
     val_early = regroup(blocks[:early], 0, 2 * pairs)
     far_early = [exchanged(val_early, "ga", r) for r in range(1, ga)]
-    screen_near, table, extras = prepare(
+    whole, table, extras = prepare(
         ka,
         dims,
         qpoint_map,
@@ -562,13 +511,13 @@
         screening,
         val_early,
     )
-    val_late = regroup(blocks[early:], 0, 2 * pairs, (extras, *far_early))
+    val_late = regroup(blocks[early:], 0, 2 * pairs, (extras,))
     far_late = [exchanged(val_late, "ga", r) for r in range(1, ga)]
-    cond_half = regroup(blocks, 2 * pairs, blocks[0].shape[0], (val_late,))
+    cond_half = regroup(blocks, 2 * pairs, blocks[0].shape[0], (val_late, *far_early))
     cond_all = [cond_half] + [exchanged(cond_half, "ba", r) for r in range(1, ba)]
-    near, screens = near_field(ga, pairs, screening, screen_near, blocks)
+    near = near_field(pairs, whole, [val_early, val_late])
     val_far = [x for both in zip(far_early, far_late) for x in both]
-    piece = project(ka, ga, ba, dims, table, extras, near, screens, val_far, cond_all)
+    piece = project(ka, ga, ba, dims, whole, table, extras, near, val_far, cond_all)
     piece = summed(summed(piece, "ba"), "ga")
     pieces = sent([piece] * ka, "ka")
     scale_count = float(kcount * pair_count)

time: 34.1 us -> 33.1 us (0.971)
  starting transfers between devices: 16.2 us -> 15.3 us
  Pallas kernels: 7.96 us -> 7.17 us
  waiting for transfers between devices: 9.05 us -> 9.76 us
    pallas_call x5 -> x1, Pallas kernels: 2.3 us -> 0.77 us  [near_field(): pl.pallas_call(functools.partial(near_kernel, pairs), out_shape=in_vmem((...]
    ppermute x11, starting transfers between devices: 16.2 us -> 15.3 us  [the longest x9 13.7 us: exchanged(): lax.ppermute(value, axis, [(i, (i + step) % size) for i in range(size)])]
    pallas_call x1, Pallas kernels: 1.74 us -> 2.45 us  [prepare(): pl.pallas_call(functools.partial(prepare_kernel, ka, dims), out_shape=[in...]
    ppermute x11, waiting for transfers between devices: 9.05 us -> 9.76 us  [the longest x9 6.43 us: exchanged(): lax.ppermute(value, axis, [(i, (i + step) % size) for i in range(size)])]
  transfers between devices with their start and end apart: 11 -> 11, of which waited for: 6 -> 6; matrix products, arithmetic and copies ran while one was open for 0% -> 0% of each run, Pallas kernels for 12% -> 10%
where the time goes in v6:
time: 33.1 us; the launch traced here: 32.9 us
  starting transfers between devices  15.3 us (46%)
  waiting for transfers between devices  9.76 us (29%)
  Pallas kernels  7.17 us (22%)
  between operations  0.71 us (2%)
    ppermute x9, starting transfers between devices, exchanged(): lax.ppermute(value, axis, [(i, (i + step) % size) for i in range(size)])  13.7 us
    ppermute x9, waiting for transfers between devices, exchanged(): lax.ppermute(value, axis, [(i, (i + step) % size) for i in range(size)])  6.43 us
    ppermute x2, waiting for transfers between devices, summed(): lax.ppermute(value, axis, [(i, i ^ step) for i in range(size)])  3.32 us
    pallas_call x1, Pallas kernels, prepare(): pl.pallas_call(functools.partial(prepare_kernel, ka, dims), out_shape=[in...  2.45 us
    pallas_call x1, Pallas kernels, haydock(): pl.pallas_call(functools.partial(haydock_kernel, ka, codes, scale_count,...  1.61 us
    ppermute x2, starting transfers between devices, summed(): lax.ppermute(value, axis, [(i, i ^ step) for i in range(size)])  1.57 us
    pallas_call x1, Pallas kernels, project(): pl.pallas_call(functools.partial(project_kernel, ka, ga, ba, dims), out_s...  1.27 us
    pallas_call x1, Pallas kernels, pack(): pl.pallas_call(functools.partial(pack_kernel, ka), out_shape=[shape] * ka...  1.05 us
  transfers between devices with their start and end apart: 11, of which 6 were waited for; matrix products, arithmetic and copies ran while one was open for 0% of the time, Pallas kernels for 10%

profile of v6, /device:TPU:0, one launch (start us, length us, event | category | flops | bytes accessed | tf_op | source)
XLA Modules:
  0.0 32.9 jit_solution(1127720570920884736)
XLA Ops:
  0.6 1.0 %pack.1 = (bf16[32,768]{1,0:T(8,128)(2,1)S(1)}, bf16[32,768]{1,0:T(8,128)(2,1)S(1)}, bf16[32,768]{1,0:T(8,128)(2,1)S(1)}, bf16[32,768]{1,0:T(8,128)(2,1)S(1)}) custom-call(s32[4,4]{1,0:T(4,128)} %refs_0_.1, s32[4]{0:T(128)} %refs_1_.1, bf16[1,4,2,2,4,768]{5,4,3,2,1,0:T(4,128)(2,1)} %valence_in.1, bf16[1,4,2,4,4,768]{5,4,3,2,1,0:T(4,128)(2,1)} %conduction_in.1), custom_call_target="tpu_custom_call" | custom-call | tf_op jit(solution)/shard_map/pack/pallas_call | solution.py:99
  1.7 3.1 %collective-permute-start = (bf16[32,768]{1,0:T(8,128)(2,1)S(1)}, bf16[32,768]{1,0:T(8,128)(2,1)S(1)}, u32[]{:S(2)}, u32[]{:S(2)}) collective-permute-start(bf16[32,768]{1,0:T(8,128)(2,1)S(1)} %get-tuple-element.10), channel_id=1, source_target_pairs={{0,4},{4,8},{8,12},{12,0},{1,5},{5,9},{9,13},{13,1},{2,6},{6,10},{... | collective-permute-start | bytes 147464 | tf_op jit(solution)/shard_map/ppermute | solution.py:55
  4.8 2.6 %collective-permute-start.1 = (bf16[32,768]{1,0:T(8,128)(2,1)S(1)}, bf16[32,768]{1,0:T(8,128)(2,1)S(1)}, u32[]{:S(2)}, u32[]{:S(2)}) collective-permute-start(bf16[32,768]{1,0:T(8,128)(2,1)S(1)} %get-tuple-element.14), channel_id=1, source_target_pairs={{0,8},{4,12},{8,0},{12,4},{1,9},{5,13},{9,1},{13,5},{2,10},{6,14},... | collective-permute-start | bytes 147464 | tf_op jit(solution)/shard_map/ppermute | solution.py:55
  7.4 1.3 %collective-permute-start.2 = (bf16[32,768]{1,0:T(8,128)(2,1)S(1)}, bf16[32,768]{1,0:T(8,128)(2,1)S(1)}, u32[]{:S(2)}, u32[]{:S(2)}) collective-permute-start(bf16[32,768]{1,0:T(8,128)(2,1)S(1)} %get-tuple-element.15), channel_id=1, source_target_pairs={{0,12},{4,0},{8,4},{12,8},{1,13},{5,1},{9,5},{13,9},{2,14},{6,2},{... | collective-permute-start | bytes 147464 | tf_op jit(solution)/shard_map/ppermute | solution.py:55
  8.7 0.3 collective-permute-done.refs_1_
  9.0 1.9 %collective-permute-start.3 = (bf16[32,768]{1,0:T(8,128)(2,1)S(1)}, bf16[32,768]{1,0:T(8,128)(2,1)S(1)}, u32[]{:S(2)}, u32[]{:S(2)}) collective-permute-start(bf16[32,768]{1,0:T(8,128)(2,1)S(1)} %regroup.3.refs_7_.refs_0_), channel_id=1, source_target_pairs={{0,2},{2,0},{1,3},{3,1},{4,6},{6,4},{5,7},{7,5},{8,10},{10,8},{9,1... | collective-permute-start | bytes 147464 | tf_op jit(solution)/shard_map/ppermute | solution.py:55
  10.9 2.5 %prepare.1 = (bf16[2,768,1536]{2,1,0:T(8,128)(2,1)S(1)}, bf16[128,512]{1,0:T(8,128)(2,1)S(1)}, f32[8,128]{1,0:T(8,128)S(1)}) custom-call(s32[4,4]{1,0:T(4,128)} %refs_0_.1, s32[4]{0:T(128)} %refs_1_.1, s32[16]{0:T(128)} %refs_2_.1, f32[1,4]{1,0:T(1,128)} %refs_3_.1, f32[1,4]{1,0:T(1,128)} %refs_4_.1, f32[1,2,2,16]{3,2,1,0:T(2,128)} %refs_5_.1, ...), custom_call_target="tpu_custom_call" | custom-call | bytes 9437184 | tf_op jit(solution)/shard_map/prepare/pallas_call | solution.py:204
  13.4 0.0 collective-permute-done.1.refs_0_.refs_2_
  13.4 0.0 collective-permute-done.2.refs_1_.refs_3_
  13.4 0.0 collective-permute-done.3.refs_5_.refs_4_
  13.4 0.1 collective-permute-start.5
  13.5 1.6 %collective-permute-start.4 = (bf16[32,768]{1,0:T(8,128)(2,1)S(1)}, bf16[32,768]{1,0:T(8,128)(2,1)S(1)}, u32[]{:S(2)}, u32[]{:S(2)}) collective-permute-start(bf16[32,768]{1,0:T(8,128)(2,1)S(1)} %regroup.4.refs_1_.refs_4_), channel_id=1, source_target_pairs={{0,2},{2,0},{1,3},{3,1},{4,6},{6,4},{5,7},{7,5},{8,10},{10,8},{9,1... | collective-permute-start | bytes 147464 | tf_op jit(solution)/shard_map/ppermute | solution.py:55
  15.1 0.8 %near_field.1.refs_3_ = f32[768,128]{1,0:T(8,128)S(1)} custom-call(bf16[2,768,1536]{2,1,0:T(8,128)(2,1)S(1)} %get-tuple-element.11.screening.refs_0_, bf16[32,768]{1,0:T(8,128)(2,1)S(1)} %regroup.3.refs_7_.refs_0_, bf16[32,768]{1,0:T(8,128)(2,1)S(1)} %regroup.4.refs_1_.refs_4_), custom_call_target="tpu_custom_call" | custom-call | flops 301989888 | bytes 2359296 | tf_op jit(solution)/shard_map/near_field/pallas_call | solution.py:269
  15.9 1.7 %collective-permute-done.4.refs_5_ = bf16[32,768]{1,0:T(8,128)(2,1)S(1)} collective-permute-done((bf16[32,768]{1,0:T(8,128)(2,1)S(1)}, bf16[32,768]{1,0:T(8,128)(2,1)S(1)}, u32[]{:S(2)}, u32[]{:S(2)}) %collective-permute-start.4) | collective-permute-done | bytes 49184 | tf_op jit(solution)/shard_map/ppermute | solution.py:55
  17.7 0.0 collective-permute-done.5.refs_7_
  17.7 1.3 %project.1 = f32[24,128]{1,0:T(8,128)S(1)} custom-call(bf16[2,768,1536]{2,1,0:T(8,128)(2,1)S(1)} %get-tuple-element.11.screening.refs_0_, bf16[128,512]{1,0:T(8,128)(2,1)S(1)} %get-tuple-element.12.refs_1_, f32[8,128]{1,0:T(8,128)S(1)} %get-tuple-element.13.refs_2_, f32[768,128]{1,0:T(8,128)S(1)} %near_field.1.refs_3_, ...), custom_call_target="tpu_custom_call" | custom-call | tf_op jit(solution)/shard_map/project/pallas_call | solution.py:355
  18.9 0.0 collective-permute-start.6
  18.9 1.2 %collective-permute-done.6 = f32[24,128]{1,0:T(8,128)S(1)} collective-permute-done((f32[24,128]{1,0:T(8,128)S(1)}, f32[24,128]{1,0:T(8,128)S(1)}, u32[]{:S(2)}, u32[]{:S(2)}) %collective-permute-start.6) | collective-permute-done | bytes 12320 | tf_op jit(solution)/shard_map/ppermute | solution.py:468
  20.1 1.6 %collective-permute-start.7 = (f32[24,128]{1,0:T(8,128)S(1)}, f32[24,128]{1,0:T(8,128)S(1)}, u32[]{:S(2)}, u32[]{:S(2)}) collective-permute-start(f32[24,128]{1,0:T(8,128)S(1)} %add.6), channel_id=1, source_target_pairs={{0,2},{2,0},{1,3},{3,1},{4,6},{6,4},{5,7},{7,5},{8,10},{10,8},{9,1... | collective-permute-start | bytes 36872 | tf_op jit(solution)/shard_map/ppermute | solution.py:468
  21.7 2.1 %collective-permute-done.7 = f32[24,128]{1,0:T(8,128)S(1)} collective-permute-done((f32[24,128]{1,0:T(8,128)S(1)}, f32[24,128]{1,0:T(8,128)S(1)}, u32[]{:S(2)}, u32[]{:S(2)}) %collective-permute-start.7) | collective-permute-done | bytes 12320 | tf_op jit(solution)/shard_map/ppermute | solution.py:468
  23.8 2.0 %collective-permute-start.10 = (f32[24,128]{1,0:T(8,128)S(1)}, f32[24,128]{1,0:T(8,128)S(1)}, u32[]{:S(2)}, u32[]{:S(2)}) collective-permute-start(f32[24,128]{1,0:T(8,128)S(1)} %add.7.refs_0_), channel_id=1, source_target_pairs={{0,12},{4,0},{8,4},{12,8},{1,13},{5,1},{9,5},{13,9},{2,14},{6,2},{... | collective-permute-start | bytes 36872 | tf_op jit(solution)/shard_map/ppermute | solution.py:55
  25.8 0.0 collective-permute-start.8
  25.9 1.0 %collective-permute-start.9 = (f32[24,128]{1,0:T(8,128)S(1)}, f32[24,128]{1,0:T(8,128)S(1)}, u32[]{:S(2)}, u32[]{:S(2)}) collective-permute-start(f32[24,128]{1,0:T(8,128)S(1)} %add.7.refs_0_), channel_id=1, source_target_pairs={{0,8},{4,12},{8,0},{12,4},{1,9},{5,13},{9,1},{13,5},{2,10},{6,14},... | collective-permute-start | bytes 36872 | tf_op jit(solution)/shard_map/ppermute | solution.py:55
  26.9 0.6 %collective-permute-done.10.refs_3_ = f32[24,128]{1,0:T(8,128)S(1)} collective-permute-done((f32[24,128]{1,0:T(8,128)S(1)}, f32[24,128]{1,0:T(8,128)S(1)}, u32[]{:S(2)}, u32[]{:S(2)}) %collective-permute-start.10) | collective-permute-done | bytes 12320 | tf_op jit(solution)/shard_map/ppermute | solution.py:55
  27.5 3.8 %collective-permute-done.8.refs_1_ = f32[24,128]{1,0:T(8,128)S(1)} collective-permute-done((f32[24,128]{1,0:T(8,128)S(1)}, f32[24,128]{1,0:T(8,128)S(1)}, u32[]{:S(2)}, u32[]{:S(2)}) %collective-permute-start.8) | collective-permute-done | bytes 12320 | tf_op jit(solution)/shard_map/ppermute | solution.py:55
  31.3 0.0 collective-permute-done.9.refs_2_
  31.3 1.6 %haydock.1 = (f32[1,2,2,16]{3,2,1,0:T(2,128)}, f32[2,6]{1,0:T(2,128)}) custom-call(f32[24,128]{1,0:T(8,128)S(1)} %add.7.refs_0_, f32[24,128]{1,0:T(8,128)S(1)} %collective-permute-done.8.refs_1_, f32[24,128]{1,0:T(8,128)S(1)} %collective-permute-done.9.refs_2_, f32[24,128]{1,0:T(8,128)S(1)} %collective-permute-done.10.refs_3_), custom_call_target="tpu_custom_call" | custom-call | tf_op jit(solution)/shard_map/haydock/pallas_call | solution.py:448
  (5 shorter events, 0.0 us)
Async XLA Ops:
  1.7 7.3 %collective-permute-start = (bf16[32,768]{1,0:T(8,128)(2,1)S(1)}, bf16[32,768]{1,0:T(8,128)(2,1)S(1)}, u32[]{:S(2)}, u32[]{:S(2)}) collective-permute-start(bf16[32,768]{1,0:T(8,128)(2,1)S(1)} %get-tuple-element.10), channel_id=1, source_target_pairs={{0,4},{4,8},{8,12},{12,0},{1,5},{5,9},{9,13},{13,1},{2,6},{6,10},{... | collective-permute-start | bytes 147464 | tf_op jit(solution)/shard_map/ppermute | solution.py:55
  4.8 8.6 %collective-permute-start.1 = (bf16[32,768]{1,0:T(8,128)(2,1)S(1)}, bf16[32,768]{1,0:T(8,128)(2,1)S(1)}, u32[]{:S(2)}, u32[]{:S(2)}) collective-permute-start(bf16[32,768]{1,0:T(8,128)(2,1)S(1)} %get-tuple-element.14), channel_id=1, source_target_pairs={{0,8},{4,12},{8,0},{12,4},{1,9},{5,13},{9,1},{13,5},{2,10},{6,14},... | collective-permute-start | bytes 147464 | tf_op jit(solution)/shard_map/ppermute | solution.py:55
  7.4 6.0 %collective-permute-start.2 = (bf16[32,768]{1,0:T(8,128)(2,1)S(1)}, bf16[32,768]{1,0:T(8,128)(2,1)S(1)}, u32[]{:S(2)}, u32[]{:S(2)}) collective-permute-start(bf16[32,768]{1,0:T(8,128)(2,1)S(1)} %get-tuple-element.15), channel_id=1, source_target_pairs={{0,12},{4,0},{8,4},{12,8},{1,13},{5,1},{9,5},{13,9},{2,14},{6,2},{... | collective-permute-start | bytes 147464 | tf_op jit(solution)/shard_map/ppermute | solution.py:55
  9.0 4.4 %collective-permute-start.3 = (bf16[32,768]{1,0:T(8,128)(2,1)S(1)}, bf16[32,768]{1,0:T(8,128)(2,1)S(1)}, u32[]{:S(2)}, u32[]{:S(2)}) collective-permute-start(bf16[32,768]{1,0:T(8,128)(2,1)S(1)} %regroup.3.refs_7_.refs_0_), channel_id=1, source_target_pairs={{0,2},{2,0},{1,3},{3,1},{4,6},{6,4},{5,7},{7,5},{8,10},{10,8},{9,1... | collective-permute-start | bytes 147464 | tf_op jit(solution)/shard_map/ppermute | solution.py:55
  13.4 4.2 %collective-permute-start.5 = (bf16[64,768]{1,0:T(8,128)(2,1)S(1)}, bf16[64,768]{1,0:T(8,128)(2,1)S(1)}, u32[]{:S(2)}, u32[]{:S(2)}) collective-permute-start(bf16[64,768]{1,0:T(8,128)(2,1)S(1)} %regroup.5.refs_6_), channel_id=1, source_target_pairs={{0,1},{1,0},{2,3},{3,2},{4,5},{5,4},{6,7},{7,6},{8,9},{9,8},{10,11... | collective-permute-start | bytes 294920 | tf_op jit(solution)/shard_map/ppermute | solution.py:55
  13.5 4.2 %collective-permute-start.4 = (bf16[32,768]{1,0:T(8,128)(2,1)S(1)}, bf16[32,768]{1,0:T(8,128)(2,1)S(1)}, u32[]{:S(2)}, u32[]{:S(2)}) collective-permute-start(bf16[32,768]{1,0:T(8,128)(2,1)S(1)} %regroup.4.refs_1_.refs_4_), channel_id=1, source_target_pairs={{0,2},{2,0},{1,3},{3,1},{4,6},{6,4},{5,7},{7,5},{8,10},{10,8},{9,1... | collective-permute-start | bytes 147464 | tf_op jit(solution)/shard_map/ppermute | solution.py:55
  18.9 1.2 %collective-permute-start.6 = (f32[24,128]{1,0:T(8,128)S(1)}, f32[24,128]{1,0:T(8,128)S(1)}, u32[]{:S(2)}, u32[]{:S(2)}) collective-permute-start(f32[24,128]{1,0:T(8,128)S(1)} %project.1), channel_id=1, source_target_pairs={{0,1},{1,0},{2,3},{3,2},{4,5},{5,4},{6,7},{7,6},{8,9},{9,8},{10,11... | collective-permute-start | bytes 36872 | tf_op jit(solution)/shard_map/ppermute | solution.py:468
  20.1 3.7 %collective-permute-start.7 = (f32[24,128]{1,0:T(8,128)S(1)}, f32[24,128]{1,0:T(8,128)S(1)}, u32[]{:S(2)}, u32[]{:S(2)}) collective-permute-start(f32[24,128]{1,0:T(8,128)S(1)} %add.6), channel_id=1, source_target_pairs={{0,2},{2,0},{1,3},{3,1},{4,6},{6,4},{5,7},{7,5},{8,10},{10,8},{9,1... | collective-permute-start | bytes 36872 | tf_op jit(solution)/shard_map/ppermute | solution.py:468
  23.8 3.7 %collective-permute-start.10 = (f32[24,128]{1,0:T(8,128)S(1)}, f32[24,128]{1,0:T(8,128)S(1)}, u32[]{:S(2)}, u32[]{:S(2)}) collective-permute-start(f32[24,128]{1,0:T(8,128)S(1)} %add.7.refs_0_), channel_id=1, source_target_pairs={{0,12},{4,0},{8,4},{12,8},{1,13},{5,1},{9,5},{13,9},{2,14},{6,2},{... | collective-permute-start | bytes 36872 | tf_op jit(solution)/shard_map/ppermute | solution.py:55
  25.8 5.5 %collective-permute-start.8 = (f32[24,128]{1,0:T(8,128)S(1)}, f32[24,128]{1,0:T(8,128)S(1)}, u32[]{:S(2)}, u32[]{:S(2)}) collective-permute-start(f32[24,128]{1,0:T(8,128)S(1)} %add.7.refs_0_), channel_id=1, source_target_pairs={{0,4},{4,8},{8,12},{12,0},{1,5},{5,9},{9,13},{13,1},{2,6},{6,10},{... | collective-permute-start | bytes 36872 | tf_op jit(solution)/shard_map/ppermute | solution.py:55
  25.9 5.5 %collective-permute-start.9 = (f32[24,128]{1,0:T(8,128)S(1)}, f32[24,128]{1,0:T(8,128)S(1)}, u32[]{:S(2)}, u32[]{:S(2)}) collective-permute-start(f32[24,128]{1,0:T(8,128)S(1)} %add.7.refs_0_), channel_id=1, source_target_pairs={{0,8},{4,12},{8,0},{12,4},{1,9},{5,13},{9,1},{13,5},{2,10},{6,14},... | collective-permute-start | bytes 36872 | tf_op jit(solution)/shard_map/ppermute | solution.py:55

commit v7 on v6

--- a/solution.py
+++ b/solution.py
@@ -224,27 +224,29 @@
     )(*[placed(x, pltpu.HBM) for x in operands], after)
 
 
-def regroup_kernel(count, first, last, *refs):
-    blocks, out = refs[:count], refs[-1]
-    rows = last - first
-    for at in range(count):
-        out[at * rows : (at + 1) * rows, :] = blocks[at][first:last, :]
-
-
-def regroup(blocks, first, last, after=()):
-    shape = (len(blocks) * (last - first), blocks[0].shape[1])
+def regroup_kernel(ka, val_rows, *refs):
+    blocks, (val_all, cond_half) = refs[:ka], refs[-2:]
+    cond_rows = blocks[0].shape[0] - val_rows
+    for j in range(ka):
+        val_all[j * val_rows : (j + 1) * val_rows, :] = blocks[j][:val_rows, :]
+        cond_half[j * cond_rows : (j + 1) * cond_rows, :] = blocks[j][val_rows:, :]
+
+
+def regroup(ka, val_rows, blocks, after):
+    rows, width = blocks[0].shape
+    kind = blocks[0].dtype
     return pl.pallas_call(
-        functools.partial(regroup_kernel, len(blocks), first, last),
-        out_shape=in_vmem(shape, blocks[0].dtype),
-        in_specs=[vmem] * len(blocks) + [anywhere] * len(after),
-        out_specs=vmem,
+        functools.partial(regroup_kernel, ka, val_rows),
+        out_shape=[in_vmem((ka * val_rows, width), kind), in_vmem((ka * (rows - val_rows), width), kind)],
+        in_specs=[vmem] * ka + [anywhere],
+        out_specs=[vmem] * 2,
         compiler_params=limits(*blocks),
         name="regroup",
-    )(*blocks, *after)
-
-
-def screened_block(screening, blocks, pairs, place):
-    wide = jnp.concatenate([block[...].astype(jnp.float32) for block in blocks], 0)
+    )(*blocks, after)
+
+
+def screened_block(screening, valence, pairs, place):
+    wide = valence[...].astype(jnp.float32)
     parts = []
     for at in range(0, wide.shape[0], 2 * pairs):
         parts += [-wide[at + pairs : at + 2 * pairs], wide[at : at + pairs]]
@@ -259,30 +261,30 @@
     ) + lax.dot_general(screening[1, :, columns], imag, form, preferred_element_type=jnp.float32)
 
 
-def near_kernel(pairs, screening, *refs):
-    refs[-1][...] = screened_block(screening, refs[:-1], pairs, lax.axis_index("ga"))
-
-
-def near_field(pairs, screening, blocks):
-    rows = sum(block.shape[0] for block in blocks)
-    glocal, width = screening.shape[1], blocks[0].shape[1]
+def near_kernel(pairs, screening, valence, out):
+    out[...] = screened_block(screening, valence, pairs, lax.axis_index("ga"))
+
+
+def near_field(pairs, screening, valence):
+    rows, width = valence.shape
+    glocal = screening.shape[1]
     return pl.pallas_call(
         functools.partial(near_kernel, pairs),
         out_shape=in_vmem((glocal, 2 * rows), jnp.float32),
-        in_specs=[vmem] * (1 + len(blocks)),
+        in_specs=[vmem, vmem],
         out_specs=vmem,
         cost_estimate=pl.CostEstimate(
             flops=8 * glocal * width * rows, bytes_accessed=screening.size, transcendentals=0
         ),
-        compiler_params=limits(screening, *blocks),
+        compiler_params=limits(screening, valence),
         name="near_field",
-    )(screening, *blocks)
+    )(screening, valence)
 
 
 def project_kernel(ka, ga, ba, dims, *refs):
     vloc, val_count, cond_count, npol = dims
     screening, table, extras, near = refs[:4]
-    val_in = refs[4 : 4 + 2 * (ga - 1)]
+    val_in = refs[4 : 4 + ga - 1]
     cond_in = refs[-1 - ba : -1]
     out = refs[-1]
     mine = lax.axis_index("ga")
@@ -298,53 +300,48 @@
 
     fields = near[...]
     for r in range(1, ga):
-        halves = val_in[2 * r - 2 : 2 * r]
-        fields = fields + screened_block(screening, halves, pairs, origin(mine, r, ga))
-    high, low = split(fields)
+        fields = fields + screened_block(screening, val_in[r - 1], pairs, origin(mine, r, ga))
+    both = jnp.concatenate(split(fields), 1)
+    cond_all = jnp.concatenate([ref[...] for ref in cond_in], 0)
+    crossed = jnp.dot(cond_all, both, preferred_element_type=jnp.float32)
+    crossed = crossed[:, : 2 * rows] + crossed[:, 2 * rows :]
     lane = iota((share_rows, 2 * rows), 1)
     lane_j = lane % rows // block
     turned_lane = lane // rows
     kernel = []
     for h in range(ba):
-        cond_all = cond_in[h][...]
-        crossed = jnp.dot(cond_all, high, preferred_element_type=jnp.float32) + jnp.dot(
-            cond_all, low, preferred_element_type=jnp.float32
-        )
         total = jnp.zeros((share_rows, 2 * rows), jnp.float32)
         for j in range(ka):
-            base = j * 2 * share_rows
-            same = lane_j == j
-            total = total + jnp.where(
-                same & (turned_lane == 0), crossed[base : base + share_rows], 0.0
-            )
-            total = total - jnp.where(
-                same & (turned_lane == 1), crossed[base + share_rows : base + 2 * share_rows], 0.0
-            )
+            base = (h * ka + j) * 2 * share_rows
+            real = crossed[base : base + share_rows]
+            imag = crossed[base + share_rows : base + 2 * share_rows]
+            value = jnp.where(turned_lane == 0, real, -imag)
+            total = jnp.where(lane_j == j, value, total)
         kernel.append(total)
     kernel = jnp.concatenate(kernel, 0)
 
-    kernel_high, kernel_low = split(kernel)
-    stacked = jnp.concatenate([kernel_high, kernel_low], 0)
+    spread = jnp.dot(
+        jnp.concatenate(split(kernel), 0), table[...], preferred_element_type=jnp.float32
+    )
+    spread = spread[:cond_rows] + spread[cond_rows:]
     crow = iota((cond_rows, lanes), 0)
     c_of_row = origin(half, crow // share_rows, ba) * share + crow % share_rows // cond_count
     same_c = c_of_row == iota((cond_rows, lanes), 1) % cond_count
-    spread = []
-    for v2 in range(val_count):
-        both = jnp.dot(
-            stacked, table[:, v2 * lanes : (v2 + 1) * lanes], preferred_element_type=jnp.float32
-        )
-        spread.append(jnp.where(same_c, both[:cond_rows] + both[cond_rows:], 0.0))
-    spread = jnp.concatenate(spread, 0)
+    spread = jnp.concatenate(
+        [
+            jnp.where(same_c, spread[:, v2 * lanes : (v2 + 1) * lanes], 0.0)
+            for v2 in range(val_count)
+        ],
+        0,
+    )
     out_row = iota((codes, val_count * cond_rows), 0)
     out_col = iota((codes, val_count * cond_rows), 1)
     fold = (out_row // cond_count == out_col // cond_rows) & (
         out_row % cond_count == out_col % cond_count
     )
     fold = jnp.where(fold, 1.0, 0.0).astype(jnp.bfloat16)
-    spread_high, spread_low = split(spread)
-    out[:codes, :] = jnp.dot(fold, spread_high, preferred_element_type=jnp.float32) + jnp.dot(
-        fold, spread_low, preferred_element_type=jnp.float32
-    )
+    piece = jnp.dot(fold, jnp.concatenate(split(spread), 1), preferred_element_type=jnp.float32)
+    out[:codes, :] = piece[:, :lanes] + piece[:, lanes:]
     out[codes:, :] = extras[...]
 
 
@@ -412,17 +409,20 @@
     def times(real, imag, vector):
         return real * vector + imag * (sign * swap(vector))
 
-    first = start / norm(start)
-    first_image = hamiltonian(first)
+    start_image = hamiltonian(start)
+    scale = 1.0 / norm(start)
+    first = start * scale
+    first_image = start_image * scale
     alpha_real, alpha_imag = inner(first, first_image)
     first_resid = first_image - times(alpha_real, alpha_imag, first)
+    resid_image = hamiltonian(first_resid)
     beta_one = norm(first_resid)
-    second = first_resid / beta_one
-    second_image = hamiltonian(second)
+    scale = 1.0 / beta_one
+    second = first_resid * scale
+    second_image = resid_image * scale
     gamma_real, gamma_imag = inner(second, second_image)
     second_resid = second_image - times(gamma_real, gamma_imag, second) - beta_one * first
     beta_two = norm(second_resid)
-    following = second_resid / beta_two
 
     coef_lane = iota(coef_out.shape, 1)
     coefs = jnp.zeros(coef_out.shape, jnp.float32)
@@ -435,9 +435,9 @@
     band = (row % codes).astype(jnp.float32)
     pick = jnp.where(here & (own[npol + 1 : npol + 2] == band), 1.0, 0.0).astype(jnp.bfloat16)
     picked = lax.dot_general(
-        halves(following), pick, (((1,), (1,)), ((), ())), preferred_element_type=jnp.float32
-    )
-    picked = picked[:npol] + picked[npol:]
+        halves(second_resid), pick, (((1,), (1,)), ((), ())), preferred_element_type=jnp.float32
+    )
+    picked = (picked[:npol] + picked[npol:]) / beta_two
     next_out[0, :, 0, :] = picked[:, :codes]
     next_out[0, :, 1, :] = picked[:, codes:]
 
@@ -496,9 +496,6 @@
     dims = (vloc, val_count, cond_count, npol)
     packed = pack(ka, ba, qpoint_map, slot_owner, valence_density, conduction_density)
     blocks = sent(packed, "ka")
-    early = ka // 2
-    val_early = regroup(blocks[:early], 0, 2 * pairs)
-    far_early = [exchanged(val_early, "ga", r) for r in range(1, ga)]
     whole, table, extras = prepare(
         ka,
         dims,
@@ -509,14 +506,12 @@
         conduction_energy,
         start_vector,
         screening,
-        val_early,
-    )
-    val_late = regroup(blocks[early:], 0, 2 * pairs, (extras,))
-    far_late = [exchanged(val_late, "ga", r) for r in range(1, ga)]
-    cond_half = regroup(blocks, 2 * pairs, blocks[0].shape[0], (val_late, *far_early))
+        packed[0],
+    )
+    val_all, cond_half = regroup(ka, 2 * pairs, blocks, extras)
+    val_far = [exchanged(val_all, "ga", r) for r in range(1, ga)]
     cond_all = [cond_half] + [exchanged(cond_half, "ba", r) for r in range(1, ba)]
-    near = near_field(pairs, whole, [val_early, val_late])
-    val_far = [x for both in zip(far_early, far_late) for x in both]
+    near = near_field(pairs, whole, val_all)
     piece = project(ka, ga, ba, dims, whole, table, extras, near, val_far, cond_all)
     piece = summed(summed(piece, "ba"), "ga")
     pieces = sent([piece] * ka, "ka")

time: 33.1 us -> 31.3 us (0.946)
  starting transfers between devices: 15.3 us -> 14.3 us
  waiting for transfers between devices: 9.76 us -> 9.2 us
    ppermute x9 -> x8, starting transfers between devices: 13.7 us -> 12.7 us  [exchanged(): lax.ppermute(value, axis, [(i, (i + step) % size) for i in range(size)])]
    ppermute x9 -> x8, waiting for transfers between devices: 6.43 us -> 5.92 us  [exchanged(): lax.ppermute(value, axis, [(i, (i + step) % size) for i in range(size)])]
  transfers between devices with their start and end apart: 11 -> 10, of which waited for: 6 -> 6; matrix products, arithmetic and copies ran while one was open for 0% -> 0% of each run, Pallas kernels for 10% -> 10%
where the time goes in v7:
time: 31.3 us; the launch traced here: 31.1 us
  starting transfers between devices  14.3 us (46%)
  waiting for transfers between devices  9.2 us (29%)
  Pallas kernels  6.92 us (22%)
  between operations  0.68 us (2%)
    ppermute x8, starting transfers between devices, exchanged(): lax.ppermute(value, axis, [(i, (i + step) % size) for i in range(size)])  12.7 us
    ppermute x8, waiting for transfers between devices, exchanged(): lax.ppermute(value, axis, [(i, (i + step) % size) for i in range(size)])  5.92 us
    ppermute x2, waiting for transfers between devices, summed(): lax.ppermute(value, axis, [(i, i ^ step) for i in range(size)])  3.28 us
    pallas_call x1, Pallas kernels, prepare(): pl.pallas_call(functools.partial(prepare_kernel, ka, dims), out_shape=[in...  2.45 us
    ppermute x2, starting transfers between devices, summed(): lax.ppermute(value, axis, [(i, i ^ step) for i in range(size)])  1.61 us
    pallas_call x1, Pallas kernels, haydock(): pl.pallas_call(functools.partial(haydock_kernel, ka, codes, scale_count,...  1.41 us
    pallas_call x1, Pallas kernels, project(): pl.pallas_call(functools.partial(project_kernel, ka, ga, ba, dims), out_s...  1.23 us
    pallas_call x1, Pallas kernels, pack(): pl.pallas_call(functools.partial(pack_kernel, ka), out_shape=[shape] * ka...  1.05 us
  transfers between devices with their start and end apart: 10, of which 6 were waited for; matrix products, arithmetic and copies ran while one was open for 0% of the time, Pallas kernels for 10%

profile of v7, /device:TPU:0, one launch (start us, length us, event | category | flops | bytes accessed | tf_op | source)
XLA Modules:
  0.0 31.1 jit_solution(13832443342196617687)
XLA Ops:
  0.6 1.0 %pack.1 = (bf16[32,768]{1,0:T(8,128)(2,1)S(1)}, bf16[32,768]{1,0:T(8,128)(2,1)S(1)}, bf16[32,768]{1,0:T(8,128)(2,1)S(1)}, bf16[32,768]{1,0:T(8,128)(2,1)S(1)}) custom-call(s32[4,4]{1,0:T(4,128)} %refs_0_.1, s32[4]{0:T(128)} %refs_1_.1, bf16[1,4,2,2,4,768]{5,4,3,2,1,0:T(4,128)(2,1)} %valence_in.1, bf16[1,4,2,4,4,768]{5,4,3,2,1,0:T(4,128)(2,1)} %conduction_in.1), custom_call_target="tpu_custom_call" | custom-call | tf_op jit(solution)/shard_map/pack/pallas_call | solution.py:99
  1.7 3.1 %collective-permute-start = (bf16[32,768]{1,0:T(8,128)(2,1)S(1)}, bf16[32,768]{1,0:T(8,128)(2,1)S(1)}, u32[]{:S(2)}, u32[]{:S(2)}) collective-permute-start(bf16[32,768]{1,0:T(8,128)(2,1)S(1)} %get-tuple-element.15), channel_id=1, source_target_pairs={{0,4},{4,8},{8,12},{12,0},{1,5},{5,9},{9,13},{13,1},{2,6},{6,10},{... | collective-permute-start | bytes 147464 | tf_op jit(solution)/shard_map/ppermute | solution.py:55
  4.8 2.6 %collective-permute-start.1 = (bf16[32,768]{1,0:T(8,128)(2,1)S(1)}, bf16[32,768]{1,0:T(8,128)(2,1)S(1)}, u32[]{:S(2)}, u32[]{:S(2)}) collective-permute-start(bf16[32,768]{1,0:T(8,128)(2,1)S(1)} %get-tuple-element.16), channel_id=1, source_target_pairs={{0,8},{4,12},{8,0},{12,4},{1,9},{5,13},{9,1},{13,5},{2,10},{6,14},... | collective-permute-start | bytes 147464 | tf_op jit(solution)/shard_map/ppermute | solution.py:55
  7.4 1.3 %collective-permute-start.2 = (bf16[32,768]{1,0:T(8,128)(2,1)S(1)}, bf16[32,768]{1,0:T(8,128)(2,1)S(1)}, u32[]{:S(2)}, u32[]{:S(2)}) collective-permute-start(bf16[32,768]{1,0:T(8,128)(2,1)S(1)} %get-tuple-element.17), channel_id=1, source_target_pairs={{0,12},{4,0},{8,4},{12,8},{1,13},{5,1},{9,5},{13,9},{2,14},{6,2},{... | collective-permute-start | bytes 147464 | tf_op jit(solution)/shard_map/ppermute | solution.py:55
  8.7 2.5 %prepare.1 = (bf16[2,768,1536]{2,1,0:T(8,128)(2,1)S(1)}, bf16[128,512]{1,0:T(8,128)(2,1)S(1)}, f32[8,128]{1,0:T(8,128)S(1)}) custom-call(s32[4,4]{1,0:T(4,128)} %refs_0_.1, s32[4]{0:T(128)} %refs_1_.1, s32[16]{0:T(128)} %refs_2_.1, f32[1,4]{1,0:T(1,128)} %refs_3_.1, f32[1,4]{1,0:T(1,128)} %refs_4_.1, f32[1,2,2,16]{3,2,1,0:T(2,128)} %refs_5_.1, ...), custom_call_target="tpu_custom_call" | custom-call | bytes 9437184 | tf_op jit(solution)/shard_map/prepare/pallas_call | solution.py:204
  11.2 0.0 collective-permute-done.refs_1_
  11.2 0.0 collective-permute-done.1.refs_2_
  11.2 0.3 collective-permute-done.2.refs_3_
  11.5 1.7 %collective-permute-start.3 = (bf16[64,768]{1,0:T(8,128)(2,1)S(1)}, bf16[64,768]{1,0:T(8,128)(2,1)S(1)}, u32[]{:S(2)}, u32[]{:S(2)}) collective-permute-start(bf16[64,768]{1,0:T(8,128)(2,1)S(1)} %get-tuple-element.18.valence), channel_id=1, source_target_pairs={{0,2},{2,0},{1,3},{3,1},{4,6},{6,4},{5,7},{7,5},{8,10},{10,8},{9,1... | collective-permute-start | bytes 294920 | tf_op jit(solution)/shard_map/ppermute | solution.py:55
  13.2 0.0 collective-permute-start.4
  13.2 0.8 %near_field.1.refs_3_ = f32[768,128]{1,0:T(8,128)S(1)} custom-call(bf16[2,768,1536]{2,1,0:T(8,128)(2,1)S(1)} %get-tuple-element.12.screening.refs_0_, bf16[64,768]{1,0:T(8,128)(2,1)S(1)} %get-tuple-element.18.valence), custom_call_target="tpu_custom_call" | custom-call | flops 301989888 | bytes 2359296 | tf_op jit(solution)/shard_map/near_field/pallas_call | solution.py:271
  13.9 2.2 %collective-permute-done.3.refs_4_ = bf16[64,768]{1,0:T(8,128)(2,1)S(1)} collective-permute-done((bf16[64,768]{1,0:T(8,128)(2,1)S(1)}, bf16[64,768]{1,0:T(8,128)(2,1)S(1)}, u32[]{:S(2)}, u32[]{:S(2)}) %collective-permute-start.3) | collective-permute-done | bytes 98336 | tf_op jit(solution)/shard_map/ppermute | solution.py:55
  16.2 0.0 collective-permute-done.4.refs_6_
  16.2 1.2 %project.1 = f32[24,128]{1,0:T(8,128)S(1)} custom-call(bf16[2,768,1536]{2,1,0:T(8,128)(2,1)S(1)} %get-tuple-element.12.screening.refs_0_, bf16[128,512]{1,0:T(8,128)(2,1)S(1)} %get-tuple-element.13.refs_1_, f32[8,128]{1,0:T(8,128)S(1)} %get-tuple-element.14.refs_4_.refs_2_, f32[768,128]{1,0:T(8,128)S(1)} %near_field.1.refs_3_, ...), custom_call_target="tpu_custom_call" | custom-call | tf_op jit(solution)/shard_map/project/pallas_call | solution.py:352
  17.4 0.0 collective-permute-start.5
  17.4 1.2 %collective-permute-done.5 = f32[24,128]{1,0:T(8,128)S(1)} collective-permute-done((f32[24,128]{1,0:T(8,128)S(1)}, f32[24,128]{1,0:T(8,128)S(1)}, u32[]{:S(2)}, u32[]{:S(2)}) %collective-permute-start.5) | collective-permute-done | bytes 12320 | tf_op jit(solution)/shard_map/ppermute | solution.py:468
  18.6 1.6 %collective-permute-start.6 = (f32[24,128]{1,0:T(8,128)S(1)}, f32[24,128]{1,0:T(8,128)S(1)}, u32[]{:S(2)}, u32[]{:S(2)}) collective-permute-start(f32[24,128]{1,0:T(8,128)S(1)} %add.6), channel_id=1, source_target_pairs={{0,2},{2,0},{1,3},{3,1},{4,6},{6,4},{5,7},{7,5},{8,10},{10,8},{9,1... | collective-permute-start | bytes 36872 | tf_op jit(solution)/shard_map/ppermute | solution.py:468
  20.2 2.1 %collective-permute-done.6 = f32[24,128]{1,0:T(8,128)S(1)} collective-permute-done((f32[24,128]{1,0:T(8,128)S(1)}, f32[24,128]{1,0:T(8,128)S(1)}, u32[]{:S(2)}, u32[]{:S(2)}) %collective-permute-start.6) | collective-permute-done | bytes 12320 | tf_op jit(solution)/shard_map/ppermute | solution.py:468
  22.3 0.8 %collective-permute-start.7 = (f32[24,128]{1,0:T(8,128)S(1)}, f32[24,128]{1,0:T(8,128)S(1)}, u32[]{:S(2)}, u32[]{:S(2)}) collective-permute-start(f32[24,128]{1,0:T(8,128)S(1)} %add.7.refs_0_), channel_id=1, source_target_pairs={{0,4},{4,8},{8,12},{12,0},{1,5},{5,9},{9,13},{13,1},{2,6},{6,10},{... | collective-permute-start | bytes 36872 | tf_op jit(solution)/shard_map/ppermute | solution.py:55
  23.1 2.9 %collective-permute-start.8 = (f32[24,128]{1,0:T(8,128)S(1)}, f32[24,128]{1,0:T(8,128)S(1)}, u32[]{:S(2)}, u32[]{:S(2)}) collective-permute-start(f32[24,128]{1,0:T(8,128)S(1)} %add.7.refs_0_), channel_id=1, source_target_pairs={{0,8},{4,12},{8,0},{12,4},{1,9},{5,13},{9,1},{13,5},{2,10},{6,14},... | collective-permute-start | bytes 36872 | tf_op jit(solution)/shard_map/ppermute | solution.py:55
  26.0 0.3 collective-permute-start.9
  26.3 1.5 %collective-permute-done.7.refs_1_ = f32[24,128]{1,0:T(8,128)S(1)} collective-permute-done((f32[24,128]{1,0:T(8,128)S(1)}, f32[24,128]{1,0:T(8,128)S(1)}, u32[]{:S(2)}, u32[]{:S(2)}) %collective-permute-start.7) | collective-permute-done | bytes 12320 | tf_op jit(solution)/shard_map/ppermute | solution.py:55
  27.8 0.0 collective-permute-done.8.refs_2_
  27.8 1.9 %collective-permute-done.9.refs_3_ = f32[24,128]{1,0:T(8,128)S(1)} collective-permute-done((f32[24,128]{1,0:T(8,128)S(1)}, f32[24,128]{1,0:T(8,128)S(1)}, u32[]{:S(2)}, u32[]{:S(2)}) %collective-permute-start.9) | collective-permute-done | bytes 12320 | tf_op jit(solution)/shard_map/ppermute | solution.py:55
  29.7 1.4 %haydock.1 = (f32[1,2,2,16]{3,2,1,0:T(2,128)}, f32[2,6]{1,0:T(2,128)}) custom-call(f32[24,128]{1,0:T(8,128)S(1)} %add.7.refs_0_, f32[24,128]{1,0:T(8,128)S(1)} %collective-permute-done.7.refs_1_, f32[24,128]{1,0:T(8,128)S(1)} %collective-permute-done.8.refs_2_, f32[24,128]{1,0:T(8,128)S(1)} %collective-permute-done.9.refs_3_), custom_call_target="tpu_custom_call" | custom-call | tf_op jit(solution)/shard_map/haydock/pallas_call | solution.py:448
  (3 shorter events, 0.0 us)
Async XLA Ops:
  1.7 9.5 %collective-permute-start = (bf16[32,768]{1,0:T(8,128)(2,1)S(1)}, bf16[32,768]{1,0:T(8,128)(2,1)S(1)}, u32[]{:S(2)}, u32[]{:S(2)}) collective-permute-start(bf16[32,768]{1,0:T(8,128)(2,1)S(1)} %get-tuple-element.15), channel_id=1, source_target_pairs={{0,4},{4,8},{8,12},{12,0},{1,5},{5,9},{9,13},{13,1},{2,6},{6,10},{... | collective-permute-start | bytes 147464 | tf_op jit(solution)/shard_map/ppermute | solution.py:55
  4.8 6.4 %collective-permute-start.1 = (bf16[32,768]{1,0:T(8,128)(2,1)S(1)}, bf16[32,768]{1,0:T(8,128)(2,1)S(1)}, u32[]{:S(2)}, u32[]{:S(2)}) collective-permute-start(bf16[32,768]{1,0:T(8,128)(2,1)S(1)} %get-tuple-element.16), channel_id=1, source_target_pairs={{0,8},{4,12},{8,0},{12,4},{1,9},{5,13},{9,1},{13,5},{2,10},{6,14},... | collective-permute-start | bytes 147464 | tf_op jit(solution)/shard_map/ppermute | solution.py:55
  7.4 4.1 %collective-permute-start.2 = (bf16[32,768]{1,0:T(8,128)(2,1)S(1)}, bf16[32,768]{1,0:T(8,128)(2,1)S(1)}, u32[]{:S(2)}, u32[]{:S(2)}) collective-permute-start(bf16[32,768]{1,0:T(8,128)(2,1)S(1)} %get-tuple-element.17), channel_id=1, source_target_pairs={{0,12},{4,0},{8,4},{12,8},{1,13},{5,1},{9,5},{13,9},{2,14},{6,2},{... | collective-permute-start | bytes 147464 | tf_op jit(solution)/shard_map/ppermute | solution.py:55
  11.5 4.7 %collective-permute-start.3 = (bf16[64,768]{1,0:T(8,128)(2,1)S(1)}, bf16[64,768]{1,0:T(8,128)(2,1)S(1)}, u32[]{:S(2)}, u32[]{:S(2)}) collective-permute-start(bf16[64,768]{1,0:T(8,128)(2,1)S(1)} %get-tuple-element.18.valence), channel_id=1, source_target_pairs={{0,2},{2,0},{1,3},{3,1},{4,6},{6,4},{5,7},{7,5},{8,10},{10,8},{9,1... | collective-permute-start | bytes 294920 | tf_op jit(solution)/shard_map/ppermute | solution.py:55
  13.2 3.0 %collective-permute-start.4 = (bf16[64,768]{1,0:T(8,128)(2,1)S(1)}, bf16[64,768]{1,0:T(8,128)(2,1)S(1)}, u32[]{:S(2)}, u32[]{:S(2)}) collective-permute-start(bf16[64,768]{1,0:T(8,128)(2,1)S(1)} %get-tuple-element.19.refs_5_), channel_id=1, source_target_pairs={{0,1},{1,0},{2,3},{3,2},{4,5},{5,4},{6,7},{7,6},{8,9},{9,8},{10,11... | collective-permute-start | bytes 294920 | tf_op jit(solution)/shard_map/ppermute | solution.py:55
  17.4 1.2 %collective-permute-start.5 = (f32[24,128]{1,0:T(8,128)S(1)}, f32[24,128]{1,0:T(8,128)S(1)}, u32[]{:S(2)}, u32[]{:S(2)}) collective-permute-start(f32[24,128]{1,0:T(8,128)S(1)} %project.1), channel_id=1, source_target_pairs={{0,1},{1,0},{2,3},{3,2},{4,5},{5,4},{6,7},{7,6},{8,9},{9,8},{10,11... | collective-permute-start | bytes 36872 | tf_op jit(solution)/shard_map/ppermute | solution.py:468
  18.6 3.7 %collective-permute-start.6 = (f32[24,128]{1,0:T(8,128)S(1)}, f32[24,128]{1,0:T(8,128)S(1)}, u32[]{:S(2)}, u32[]{:S(2)}) collective-permute-start(f32[24,128]{1,0:T(8,128)S(1)} %add.6), channel_id=1, source_target_pairs={{0,2},{2,0},{1,3},{3,1},{4,6},{6,4},{5,7},{7,5},{8,10},{10,8},{9,1... | collective-permute-start | bytes 36872 | tf_op jit(solution)/shard_map/ppermute | solution.py:468
  22.3 5.5 %collective-permute-start.7 = (f32[24,128]{1,0:T(8,128)S(1)}, f32[24,128]{1,0:T(8,128)S(1)}, u32[]{:S(2)}, u32[]{:S(2)}) collective-permute-start(f32[24,128]{1,0:T(8,128)S(1)} %add.7.refs_0_), channel_id=1, source_target_pairs={{0,4},{4,8},{8,12},{12,0},{1,5},{5,9},{9,13},{13,1},{2,6},{6,10},{... | collective-permute-start | bytes 36872 | tf_op jit(solution)/shard_map/ppermute | solution.py:55
  23.1 4.7 %collective-permute-start.8 = (f32[24,128]{1,0:T(8,128)S(1)}, f32[24,128]{1,0:T(8,128)S(1)}, u32[]{:S(2)}, u32[]{:S(2)}) collective-permute-start(f32[24,128]{1,0:T(8,128)S(1)} %add.7.refs_0_), channel_id=1, source_target_pairs={{0,8},{4,12},{8,0},{12,4},{1,9},{5,13},{9,1},{13,5},{2,10},{6,14},... | collective-permute-start | bytes 36872 | tf_op jit(solution)/shard_map/ppermute | solution.py:55
  26.0 3.7 %collective-permute-start.9 = (f32[24,128]{1,0:T(8,128)S(1)}, f32[24,128]{1,0:T(8,128)S(1)}, u32[]{:S(2)}, u32[]{:S(2)}) collective-permute-start(f32[24,128]{1,0:T(8,128)S(1)} %add.7.refs_0_), channel_id=1, source_target_pairs={{0,12},{4,0},{8,4},{12,8},{1,13},{5,1},{9,5},{13,9},{2,14},{6,2},{... | collective-permute-start | bytes 36872 | tf_op jit(solution)/shard_map/ppermute | solution.py:55

commit v8 on v7

--- a/solution.py
+++ b/solution.py
@@ -17,6 +17,7 @@
 anywhere = pl.BlockSpec(memory_space=pl.ANY)
 EXTRA_ROWS = 8
 CHUNKS = 4
+TOGETHER = 4
 
 
 def in_vmem(shape, dtype):
@@ -50,14 +51,19 @@
     return lax.rem(me + size - step, size)
 
 
-def exchanged(value, axis, step):
-    size = lax.axis_size(axis)
-    return lax.ppermute(value, axis, [(i, (i + step) % size) for i in range(size)])
-
-
-def pack_kernel(ka, qmap_in, owner_in, valence_in, conduction_in, *rest):
-    outs = rest[:ka]
-    qmap, owner, partner, valence, conduction, sems = rest[ka:]
+def exchanged(value, axis, move):
+    size, cores = lax.axis_size(axis), lax.axis_size("ba")
+    pairs = [(i * cores + cores - 1, move(i, size) * cores + cores - 1) for i in range(size)]
+    return lax.ppermute(value, (axis, "ba"), pairs)
+
+
+def shifted(value, axis, step):
+    return exchanged(value, axis, lambda i, size: (i + step) % size)
+
+
+def sort_kernel(ka, qmap_in, owner_in, valence_in, conduction_in, *rest):
+    own, cond, chosen = rest[:3]
+    qmap, owner, partner, valence, conduction, sems = rest[3:]
     copies = [
         pltpu.make_async_copy(src, dst, sems.at[at])
         for at, (src, dst) in enumerate(
@@ -67,12 +73,9 @@
     for copy in copies:
         copy.start()
     me = lax.axis_index("ka")
-    half = lax.axis_index("ba")
     count, width = valence.shape[1], valence.shape[5]
-    cond_count = conduction.shape[3]
-    share = cond_count // lax.axis_size("ba")
-    val_rows = 2 * valence.shape[3] * valence.shape[4]
-    cond_rows = 2 * share * cond_count
+    val_rows = own.shape[0] // ka
+    cond_rows = cond.shape[0] // ka
 
     def note(k2, carry):
         partner[owner[qmap[me, k2]]] = k2
@@ -83,24 +86,28 @@
     lax.fori_loop(0, count, note, 0)
     copies[2].wait()
     copies[3].wait()
-    for at in range(ka):
-        k2 = partner[target(me, at, ka)]
+    for j in range(ka):
+        k2 = partner[target(me, j, ka)]
         block = valence[0, k2].astype(jnp.float32).reshape(val_rows, width)
-        outs[at][:val_rows, :] = block.astype(jnp.bfloat16)
-        block = conduction[0, k2, :, pl.ds(half * share, share)].astype(jnp.float32)
-        outs[at][val_rows:, :] = block.reshape(cond_rows, width).astype(jnp.bfloat16)
-
-
-def pack(ka, ba, qmap, owner, valence, conduction):
-    cond_count = conduction.shape[3]
-    rows = 2 * valence.shape[3] * valence.shape[4] + 2 * cond_count // ba * cond_count
-    shape = in_vmem((rows, valence.shape[5]), valence.dtype)
-    operands = [placed(x, pltpu.HBM) for x in (qmap, owner, valence, conduction)]
-    return pl.pallas_call(
-        functools.partial(pack_kernel, ka),
-        out_shape=[shape] * ka,
+        own[j * val_rows : (j + 1) * val_rows, :] = block.astype(jnp.bfloat16)
+        block = conduction[0, k2].astype(jnp.float32).reshape(cond_rows, width)
+        cond[j * cond_rows : (j + 1) * cond_rows, :] = block.astype(jnp.bfloat16)
+        chosen[j * 8 : (j + 1) * 8, :] = jnp.full((8, 128), k2.astype(jnp.float32))
+
+
+def sort(ka, qmap, owner, valence, conduction):
+    width = valence.shape[5]
+    val_rows = math.prod(valence.shape[2:5])
+    cond_rows = math.prod(conduction.shape[2:5])
+    return pl.pallas_call(
+        functools.partial(sort_kernel, ka),
+        out_shape=[
+            in_vmem((ka * val_rows, width), valence.dtype),
+            in_vmem((ka * cond_rows, width), conduction.dtype),
+            in_vmem((ka * 8, 128), jnp.float32),
+        ],
         in_specs=[anywhere] * 4,
-        out_specs=[vmem] * ka,
+        out_specs=[vmem] * 3,
         scratch_shapes=[
             pltpu.SMEM(qmap.shape, jnp.int32),
             pltpu.SMEM(owner.shape, jnp.int32),
@@ -109,17 +116,60 @@
             pltpu.VMEM(conduction.shape, conduction.dtype),
             pltpu.SemaphoreType.DMA((4,)),
         ],
+        cost_estimate=pl.CostEstimate(
+            flops=0, bytes_accessed=4 * (valence.size + conduction.size), transcendentals=0
+        ),
         compiler_params=limits(valence, conduction),
-        name="pack",
+        name="sort",
+    )(*[placed(x, pltpu.HBM) for x in (qmap, owner, valence, conduction)])
+
+
+def merge_kernel(ka, *refs):
+    own, cond, chosen = refs[:3]
+    received, outs = refs[3:-ka], refs[-ka:]
+    width = own.shape[1]
+    val_rows = own.shape[0] // ka
+    cond_rows = cond.shape[0] // ka
+    half = val_rows // 2
+    count = received[0].shape[1] if received else 0
+    others = [
+        [ref[0, k2].astype(jnp.float32).reshape(val_rows, width) for k2 in range(count)]
+        for ref in received
+    ]
+    for j in range(ka):
+        here = chosen[j * 8 : j * 8 + 1, 0:1]
+        shares = []
+        for blocks in others:
+            block = blocks[0]
+            for k2 in range(1, count):
+                block = jnp.where(here == float(k2), blocks[k2], block)
+            shares.append(block)
+        shares.append(own[j * val_rows : (j + 1) * val_rows, :].astype(jnp.float32))
+        rows = [x[part * half : (part + 1) * half] for part in range(2) for x in shares]
+        rows = jnp.concatenate(rows, 0)
+        outs[j][: rows.shape[0], :] = rows.astype(jnp.bfloat16)
+        outs[j][rows.shape[0] :, :] = cond[j * cond_rows : (j + 1) * cond_rows, :]
+
+
+def merge(ka, own, cond, chosen, received):
+    rows = (own.shape[0] * (1 + len(received)) + cond.shape[0]) // ka
+    shape = in_vmem((rows, own.shape[1]), own.dtype)
+    operands = [own, cond, chosen, *received]
+    return pl.pallas_call(
+        functools.partial(merge_kernel, ka),
+        out_shape=[shape] * ka,
+        in_specs=[vmem] * len(operands),
+        out_specs=[vmem] * ka,
+        compiler_params=limits(*operands),
+        name="merge",
     )(*operands)
 
 
 def prepare_kernel(ka, dims, *refs):
-    vloc, val_count, cond_count, npol = dims
+    val_count, cond_count, npol = dims
     ins, screening, (screen_out, table, extras), scratch = refs[:6], refs[6], refs[8:11], refs[11:]
     qmap, owner, band_pairs, val_energy, cond_energy, start, sems, screen_sems = scratch
     me = lax.axis_index("ka")
-    half = lax.axis_index("ba")
     mine = lax.axis_index("ga")
     copies = [
         pltpu.make_async_copy(src, dst, sems.at[at])
@@ -139,28 +189,26 @@
     ]
     for copy in copies + chunks:
         copy.start()
-    pairs = vloc * val_count
+    pairs = val_count * val_count
     block = 2 * pairs
-    rows = ka * block
     codes = val_count * cond_count
     mid = ka * codes
     lanes = 2 * mid
-    row = iota((2 * rows, lanes), 0)
-    col = iota((2 * rows, lanes), 1)
-    k_of_row = origin(me, row % rows // block, ka)
-    want = (
-        (row % block // pairs) * mid
-        + k_of_row * codes
-        + (half * vloc + row % pairs // val_count) * cond_count
-    )
-    joined = (col - want >= 0) & (col - want < cond_count)
-    for v2 in range(val_count):
-        pick = jnp.where(joined & (row % val_count == v2), 1.0, 0.0)
-        table[:, v2 * lanes : (v2 + 1) * lanes] = pick.astype(jnp.bfloat16)
-
+    row = iota((block, val_count * lanes), 0)
+    col = iota((block, val_count * lanes), 1)
+    same = (row // pairs == col % lanes // mid) & (row % val_count == col // lanes)
+    same = same & (row % pairs // val_count == col % codes // cond_count)
+    col_k = col % mid // codes
+
+    def fill(j, carry):
+        pick = jnp.where(same & (col_k == origin(me, j, ka)), 1.0, 0.0)
+        table[pl.ds(pl.multiple_of(j * block, block), block), :] = pick.astype(jnp.bfloat16)
+        return carry
+
+    lax.fori_loop(0, ka, fill, 0)
     for copy in copies:
         copy.wait()
-    first = jnp.where((mine == 0) & (half == 0), 1.0, 0.0)
+    first = jnp.where(mine == 0, 1.0, 0.0)
     lane = iota((1, lanes), 1)
     lane_k = lane % mid // codes
     band_row = iota((codes, lanes), 0)
@@ -196,8 +244,8 @@
 
 
 def prepare(ka, dims, qmap, owner, band_pairs, val_energy, cond_energy, start, screening, after):
-    vloc, val_count, cond_count, npol = dims
-    rows = 4 * ka * vloc * val_count
+    val_count, cond_count, npol = dims
+    rows = 2 * ka * val_count * val_count
     lanes = 2 * ka * val_count * cond_count
     operands = (qmap, owner, band_pairs, val_energy, cond_energy, start, screening)
     table = jax.ShapeDtypeStruct((rows, val_count * lanes), jnp.bfloat16)
@@ -281,52 +329,42 @@
     )(screening, valence)
 
 
-def project_kernel(ka, ga, ba, dims, *refs):
-    vloc, val_count, cond_count, npol = dims
+def project_kernel(ka, ga, dims, *refs):
+    val_count, cond_count, npol = dims
     screening, table, extras, near = refs[:4]
     val_in = refs[4 : 4 + ga - 1]
-    cond_in = refs[-1 - ba : -1]
-    out = refs[-1]
+    cond_in, out = refs[-2:]
     mine = lax.axis_index("ga")
-    half = lax.axis_index("ba")
-    pairs = vloc * val_count
+    pairs = val_count * val_count
     block = 2 * pairs
     rows = ka * block
     codes = val_count * cond_count
     lanes = 2 * ka * codes
-    share = cond_count // ba
     cond_rows = cond_count * cond_count
-    share_rows = share * cond_count
 
     fields = near[...]
     for r in range(1, ga):
         fields = fields + screened_block(screening, val_in[r - 1], pairs, origin(mine, r, ga))
     both = jnp.concatenate(split(fields), 1)
-    cond_all = jnp.concatenate([ref[...] for ref in cond_in], 0)
-    crossed = jnp.dot(cond_all, both, preferred_element_type=jnp.float32)
-    crossed = crossed[:, : 2 * rows] + crossed[:, 2 * rows :]
-    lane = iota((share_rows, 2 * rows), 1)
-    lane_j = lane % rows // block
-    turned_lane = lane // rows
-    kernel = []
-    for h in range(ba):
-        total = jnp.zeros((share_rows, 2 * rows), jnp.float32)
-        for j in range(ka):
-            base = (h * ka + j) * 2 * share_rows
-            real = crossed[base : base + share_rows]
-            imag = crossed[base + share_rows : base + 2 * share_rows]
-            value = jnp.where(turned_lane == 0, real, -imag)
-            total = jnp.where(lane_j == j, value, total)
-        kernel.append(total)
-    kernel = jnp.concatenate(kernel, 0)
+    lane_j = iota((cond_rows, rows), 1) // block
+    kernel = jnp.zeros((cond_rows, rows), jnp.float32)
+    for start in range(0, ka, TOGETHER):
+        end = min(start + TOGETHER, ka)
+        cond = cond_in[start * 2 * cond_rows : end * 2 * cond_rows, :]
+        crossed = jnp.dot(cond, both, preferred_element_type=jnp.float32)
+        crossed = crossed[:, : 2 * rows] + crossed[:, 2 * rows :]
+        for j in range(start, end):
+            base = (j - start) * 2 * cond_rows
+            real = crossed[base : base + cond_rows, :rows]
+            imag = crossed[base + cond_rows : base + 2 * cond_rows, rows:]
+            kernel = jnp.where(lane_j == j, real - imag, kernel)
 
     spread = jnp.dot(
         jnp.concatenate(split(kernel), 0), table[...], preferred_element_type=jnp.float32
     )
     spread = spread[:cond_rows] + spread[cond_rows:]
     crow = iota((cond_rows, lanes), 0)
-    c_of_row = origin(half, crow // share_rows, ba) * share + crow % share_rows // cond_count
-    same_c = c_of_row == iota((cond_rows, lanes), 1) % cond_count
+    same_c = crow // cond_count == iota((cond_rows, lanes), 1) % cond_count
     spread = jnp.concatenate(
         [
             jnp.where(same_c, spread[:, v2 * lanes : (v2 + 1) * lanes], 0.0)
@@ -345,12 +383,12 @@
     out[codes:, :] = extras[...]
 
 
-def project(ka, ga, ba, dims, screening, table, extras, near, val_far, cond_all):
-    vloc, val_count, cond_count, npol = dims
+def project(ka, ga, dims, screening, table, extras, near, val_far, cond_all):
+    val_count, cond_count, npol = dims
     codes = val_count * cond_count
-    operands = [screening, table, extras, near, *val_far, *cond_all]
-    return pl.pallas_call(
-        functools.partial(project_kernel, ka, ga, ba, dims),
+    operands = [screening, table, extras, near, *val_far, cond_all]
+    return pl.pallas_call(
+        functools.partial(project_kernel, ka, ga, dims),
         out_shape=in_vmem((codes + EXTRA_ROWS, 2 * ka * codes), jnp.float32),
         in_specs=[vmem] * len(operands),
         out_specs=vmem,
@@ -360,19 +398,22 @@
 
 
 def haydock_kernel(ka, codes, scale_count, npol, *refs):
-    pieces = refs[:-3]
+    versions = refs[:-3]
     next_out, coef_out, matrix = refs[-3:]
-    lanes = pieces[0].shape[1]
+    cores = lax.axis_size("ba")
+    gathered = versions[0][...]
+    for h in range(cores - 1):
+        gathered = jnp.where(lax.axis_index("ba") == h, versions[1 + h][...], gathered)
+    lanes = gathered.shape[1]
     mid = lanes // 2
     height = codes + EXTRA_ROWS
-    found = [(ref, at) for ref in pieces for at in range(0, ref.shape[0], height)]
     extras = None
     slots = []
-    for ref, at in found:
-        rows = ref[at + codes : at + height, :]
+    for at in range(0, gathered.shape[0], height):
+        rows = gathered[at + codes : at + height]
         extras = rows if extras is None else extras + rows
-        slots.append((ref[at : at + codes, :], rows[npol + 2 : npol + 3]))
-    own = pieces[0][codes:height, :]
+        slots.append((gathered[at : at + codes], rows[npol + 2 : npol + 3]))
+    own = gathered[codes:height]
     sign = jnp.where(iota((1, lanes), 1) < mid, -1.0, 1.0)
     for k2 in range(ka):
         block = jnp.zeros((codes, lanes), jnp.float32)
@@ -442,8 +483,8 @@
     next_out[0, :, 1, :] = picked[:, codes:]
 
 
-def haydock(ka, codes, scale_count, npol, pieces):
-    lanes = pieces[0].shape[1]
+def haydock(ka, codes, scale_count, npol, versions):
+    lanes = versions[0].shape[1]
     square = jax.ShapeDtypeStruct((lanes, lanes), jnp.float32)
     return pl.pallas_call(
         functools.partial(haydock_kernel, ka, codes, scale_count, npol),
@@ -451,27 +492,23 @@
             jax.ShapeDtypeStruct((1, npol, 2, codes), jnp.float32),
             jax.ShapeDtypeStruct((npol, 6), jnp.float32),
         ],
-        in_specs=[vmem] * len(pieces),
+        in_specs=[vmem] * len(versions),
         out_specs=[vmem, vmem],
         scratch_shapes=[pltpu.VMEM(square.shape, square.dtype)],
-        compiler_params=limits(*pieces, square),
+        compiler_params=limits(*versions, square),
         name="haydock",
-    )(*pieces)
+    )(*versions)
 
 
 def summed(value, axis):
     size = lax.axis_size(axis)
     if size & (size - 1):
-        return lax.psum(value, axis)
+        return value + sum(shifted(value, axis, step) for step in range(1, size))
     step = 1
     while step < size:
-        value = value + lax.ppermute(value, axis, [(i, i ^ step) for i in range(size)])
+        value = value + exchanged(value, axis, lambda i, size: i ^ step)
         step *= 2
     return value
-
-
-def sent(values, axis):
-    return [values[0]] + [exchanged(values[j], axis, j) for j in range(1, lax.axis_size(axis))]
 
 
 def local(
@@ -490,12 +527,15 @@
 ):
     npol = start_vector.shape[1]
     pair_count = start_vector.shape[3]
-    kcount, vloc, val_count = qpoint_map.shape[0], valence_density.shape[3], valence_density.shape[4]
+    kcount, val_count = qpoint_map.shape[0], valence_density.shape[4]
     cond_count = conduction_density.shape[3]
-    pairs = vloc * val_count
-    dims = (vloc, val_count, cond_count, npol)
-    packed = pack(ka, ba, qpoint_map, slot_owner, valence_density, conduction_density)
-    blocks = sent(packed, "ka")
+    pairs = val_count * val_count
+    dims = (val_count, cond_count, npol)
+    last = ba - 1
+    received = [lax.ppermute(valence_density, "ba", [(h, last)]) for h in range(last)]
+    own, cond, chosen = sort(ka, qpoint_map, slot_owner, valence_density, conduction_density)
+    packed = merge(ka, own, cond, chosen, received)
+    blocks = [packed[0]] + [shifted(packed[j], "ka", j) for j in range(1, ka)]
     whole, table, extras = prepare(
         ka,
         dims,
@@ -508,15 +548,16 @@
         screening,
         packed[0],
     )
-    val_all, cond_half = regroup(ka, 2 * pairs, blocks, extras)
-    val_far = [exchanged(val_all, "ga", r) for r in range(1, ga)]
-    cond_all = [cond_half] + [exchanged(cond_half, "ba", r) for r in range(1, ba)]
+    val_all, cond_all = regroup(ka, 2 * pairs, blocks, extras)
+    val_far = [shifted(val_all, "ga", r) for r in range(1, ga)]
     near = near_field(pairs, whole, val_all)
-    piece = project(ka, ga, ba, dims, whole, table, extras, near, val_far, cond_all)
-    piece = summed(summed(piece, "ba"), "ga")
-    pieces = sent([piece] * ka, "ka")
+    piece = project(ka, ga, dims, whole, table, extras, near, val_far, cond_all)
+    piece = summed(piece, "ga")
+    pieces = [piece] + [shifted(piece, "ka", j) for j in range(1, ka)]
+    gathered = jnp.concatenate(pieces, 0)
+    versions = [gathered] + [lax.ppermute(gathered, "ba", [(last, h)]) for h in range(last)]
     scale_count = float(kcount * pair_count)
-    return tuple(haydock(ka, pair_count, scale_count, npol, pieces))
+    return tuple(haydock(ka, pair_count, scale_count, npol, versions))
 
 
 def solution(mesh):

time: 31.3 us -> 47.2 us (1.51)
  waiting for transfers between devices: 9.2 us -> 29.8 us
  starting transfers between devices: 14.3 us -> 8.98 us
    ppermute x10, waiting for transfers between devices: 9.2 us -> 29.8 us  [the longest x1 29.7 us: local(): lax.ppermute(gathered, 'ba', [(last, h)])]
    ppermute x10, starting transfers between devices: 14.3 us -> 8.98 us  [the longest x8 5.33 us: exchanged(): return lax.ppermute(value, (axis, 'ba'), pairs)]
    pallas_call x2 -> x3, Pallas kernels: 2.28 us -> 2.6 us  [the longest x1 1.46 us: project(): pl.pallas_call(functools.partial(project_kernel, ka, ga, dims), out_shape...]
  transfers between devices with their start and end apart: 10 -> 10, of which waited for: 6 -> 2; matrix products, arithmetic and copies ran while one was open for 0% -> 0% of each run, Pallas kernels for 10% -> 9%
where the time goes in v8:
time: 47.2 us; the launch traced here: 46.9 us
  waiting for transfers between devices  29.8 us (63%)
  starting transfers between devices  8.98 us (19%)
  Pallas kernels  7.31 us (15%)
  between operations  0.83 us (2%)
    ppermute x1, waiting for transfers between devices, local(): lax.ppermute(gathered, 'ba', [(last, h)])  29.7 us
    ppermute x8, starting transfers between devices, exchanged(): return lax.ppermute(value, (axis, 'ba'), pairs)  5.33 us
    pallas_call x1, Pallas kernels, prepare(): pl.pallas_call(functools.partial(prepare_kernel, ka, dims), out_shape=[in...  2.46 us
    ppermute x1, starting transfers between devices, local(): lax.ppermute(valence_density, 'ba', [(h, last)])  2.36 us
    pallas_call x1, Pallas kernels, project(): pl.pallas_call(functools.partial(project_kernel, ka, ga, dims), out_shape...  1.46 us
    pallas_call x1, Pallas kernels, haydock(): pl.pallas_call(functools.partial(haydock_kernel, ka, codes, scale_count,...  1.42 us
    ppermute x1, starting transfers between devices, local(): lax.ppermute(gathered, 'ba', [(last, h)])  1.29 us
    pallas_call x1, Pallas kernels, sort(): pl.pallas_call(functools.partial(sort_kernel, ka), out_shape=[in_vmem((ka...  1.07 us
  transfers between devices with their start and end apart: 10, of which 2 were waited for; matrix products, arithmetic and copies ran while one was open for 0% of the time, Pallas kernels for 9%

profile of v8, /device:TPU:0, one launch (start us, length us, event | category | flops | bytes accessed | tf_op | source)
XLA Modules:
  0.0 46.9 jit_solution(9896761720376356069)
XLA Ops:
  0.6 2.4 %collective-permute-start = (bf16[1,4,2,2,4,768]{5,4,3,2,1,0:T(4,128)(2,1)}, bf16[1,4,2,2,4,768]{5,4,3,2,1,0:T(4,128)(2,1)S(1)}, u32[]{:S(2)}, u32[]{:S(2)}) collective-permute-start(bf16[1,4,2,2,4,768]{5,4,3,2,1,0:T(4,128)(2,1)} %valence_in.1), channel_id=1, source_target_pairs={{0,1},{2,3},{4,5},{6,7},{8,9},{10,11},{12,13},{14,15},{16,17},{18,... | collective-permute-start | bytes 294920 | tf_op jit(solution)/shard_map/ppermute | solution.py:535
  3.0 1.1 %sort.1 = (bf16[64,768]{1,0:T(8,128)(2,1)S(1)}, bf16[128,768]{1,0:T(8,128)(2,1)S(1)}, f32[32,128]{1,0:T(8,128)S(1)}) custom-call(s32[4,4]{1,0:T(4,128)} %refs_0_.1, s32[4]{0:T(128)} %refs_1_.1, bf16[1,4,2,2,4,768]{5,4,3,2,1,0:T(4,128)(2,1)} %valence_in.1, bf16[1,4,2,4,4,768]{5,4,3,2,1,0:T(4,128)(2,1)} %conduction_in.1), custom_call_target="tpu_custom_call" | custom-call | bytes 589824 | tf_op jit(solution)/shard_map/sort/pallas_call | solution.py:102
  4.1 0.1 collective-permute-done.refs_3_
  4.1 0.1 merge.1
  4.2 0.7 %collective-permute-start.1 = (bf16[64,768]{1,0:T(8,128)(2,1)S(1)}, bf16[64,768]{1,0:T(8,128)(2,1)S(1)}, u32[]{:S(2)}, u32[]{:S(2)}) collective-permute-start(bf16[64,768]{1,0:T(8,128)(2,1)S(1)} %get-tuple-element.21), channel_id=1, source_target_pairs={{1,5},{5,9},{9,13},{13,1},{3,7},{7,11},{11,15},{15,3},{17,21},{21,... | collective-permute-start | bytes 294920 | tf_op jit(solution)/shard_map/ppermute | solution.py:57
  4.9 0.7 %collective-permute-start.2 = (bf16[64,768]{1,0:T(8,128)(2,1)S(1)}, bf16[64,768]{1,0:T(8,128)(2,1)S(1)}, u32[]{:S(2)}, u32[]{:S(2)}) collective-permute-start(bf16[64,768]{1,0:T(8,128)(2,1)S(1)} %get-tuple-element.22), channel_id=1, source_target_pairs={{1,9},{5,13},{9,1},{13,5},{3,11},{7,15},{11,3},{15,7},{17,25},{21,... | collective-permute-start | bytes 294920 | tf_op jit(solution)/shard_map/ppermute | solution.py:57
  5.6 0.7 %collective-permute-start.3 = (bf16[64,768]{1,0:T(8,128)(2,1)S(1)}, bf16[64,768]{1,0:T(8,128)(2,1)S(1)}, u32[]{:S(2)}, u32[]{:S(2)}) collective-permute-start(bf16[64,768]{1,0:T(8,128)(2,1)S(1)} %get-tuple-element.23), channel_id=1, source_target_pairs={{1,13},{5,1},{9,5},{13,9},{3,15},{7,3},{11,7},{15,11},{17,29},{21,... | collective-permute-start | bytes 294920 | tf_op jit(solution)/shard_map/ppermute | solution.py:57
  6.2 2.5 %prepare.1 = (bf16[2,768,1536]{2,1,0:T(8,128)(2,1)S(1)}, bf16[128,512]{1,0:T(8,128)(2,1)S(1)}, f32[8,128]{1,0:T(8,128)S(1)}) custom-call(s32[4,4]{1,0:T(4,128)} %refs_0_.1, s32[4]{0:T(128)} %refs_1_.1, s32[16]{0:T(128)} %refs_2_.1, f32[1,4]{1,0:T(1,128)} %refs_3_.1, f32[1,4]{1,0:T(1,128)} %refs_4_.1, f32[1,2,2,16]{3,2,1,0:T(2,128)} %refs_5_.1, ...), custom_call_target="tpu_custom_call" | custom-call | bytes 9437184 | tf_op jit(solution)/shard_map/prepare/pallas_call | solution.py:252
  8.7 0.0 collective-permute-done.1.refs_1_
  8.7 0.0 collective-permute-done.2.refs_2_
  8.7 0.0 collective-permute-done.3.refs_3_
  8.8 0.7 %collective-permute-start.4 = (bf16[128,768]{1,0:T(8,128)(2,1)S(1)}, bf16[128,768]{1,0:T(8,128)(2,1)S(1)}, u32[]{:S(2)}, u32[]{:S(2)}) collective-permute-start(bf16[128,768]{1,0:T(8,128)(2,1)S(1)} %get-tuple-element.24.valence), channel_id=1, source_target_pairs={{1,3},{3,1},{5,7},{7,5},{9,11},{11,9},{13,15},{15,13},{17,19},{19,... | collective-permute-start | bytes 589832 | tf_op jit(solution)/shard_map/ppermute | solution.py:57
  9.4 0.8 %near_field.1.refs_3_ = f32[768,256]{1,0:T(8,128)S(1)} custom-call(bf16[2,768,1536]{2,1,0:T(8,128)(2,1)S(1)} %get-tuple-element.18.screening.refs_0_, bf16[128,768]{1,0:T(8,128)(2,1)S(1)} %get-tuple-element.24.valence), custom_call_target="tpu_custom_call" | custom-call | flops 603979776 | bytes 2359296 | tf_op jit(solution)/shard_map/near_field/pallas_call | solution.py:319
  10.3 0.0 collective-permute-done.4.refs_4_
  10.3 1.5 %project.1 = f32[24,128]{1,0:T(8,128)S(1)} custom-call(bf16[2,768,1536]{2,1,0:T(8,128)(2,1)S(1)} %get-tuple-element.18.screening.refs_0_, bf16[128,512]{1,0:T(8,128)(2,1)S(1)} %get-tuple-element.19.refs_1_, f32[8,128]{1,0:T(8,128)S(1)} %get-tuple-element.20.refs_4_.refs_2_, f32[768,256]{1,0:T(8,128)S(1)} %near_field.1.refs_3_, ...), custom_call_target="tpu_custom_call" | custom-call | tf_op jit(solution)/shard_map/project/pallas_call | solution.py:390
  11.7 0.7 %collective-permute-start.5 = (f32[24,128]{1,0:T(8,128)S(1)}, f32[24,128]{1,0:T(8,128)S(1)}, u32[]{:S(2)}, u32[]{:S(2)}) collective-permute-start(f32[24,128]{1,0:T(8,128)S(1)} %project.1), channel_id=1, source_target_pairs={{1,3},{3,1},{5,7},{7,5},{9,11},{11,9},{13,15},{15,13},{17,19},{19,... | collective-permute-start | bytes 36872 | tf_op jit(solution)/shard_map/ppermute | solution.py:57
  12.4 0.0 collective-permute-done.5
  12.4 0.7 %collective-permute-start.8 = (f32[24,128]{1,0:T(8,128)S(1)}, f32[24,128]{1,0:T(8,128)S(1)}, u32[]{:S(2)}, u32[]{:S(2)}) collective-permute-start(f32[24,128]{1,0:T(8,128)S(1)} %add.3), channel_id=1, source_target_pairs={{1,13},{5,1},{9,5},{13,9},{3,15},{7,3},{11,7},{15,11},{17,29},{21,... | collective-permute-start | bytes 36872 | tf_op jit(solution)/shard_map/ppermute | solution.py:57
  13.1 0.7 %collective-permute-start.7 = (f32[24,128]{1,0:T(8,128)S(1)}, f32[24,128]{1,0:T(8,128)S(1)}, u32[]{:S(2)}, u32[]{:S(2)}) collective-permute-start(f32[24,128]{1,0:T(8,128)S(1)} %add.3), channel_id=1, source_target_pairs={{1,9},{5,13},{9,1},{13,5},{3,11},{7,15},{11,3},{15,7},{17,25},{21,... | collective-permute-start | bytes 36872 | tf_op jit(solution)/shard_map/ppermute | solution.py:57
  13.8 0.7 %collective-permute-start.6 = (f32[24,128]{1,0:T(8,128)S(1)}, f32[24,128]{1,0:T(8,128)S(1)}, u32[]{:S(2)}, u32[]{:S(2)}) collective-permute-start(f32[24,128]{1,0:T(8,128)S(1)} %add.3), channel_id=1, source_target_pairs={{1,5},{5,9},{9,13},{13,1},{3,7},{7,11},{11,15},{15,3},{17,21},{21,... | collective-permute-start | bytes 36872 | tf_op jit(solution)/shard_map/ppermute | solution.py:57
  14.4 0.0 collective-permute-done.8
  14.5 0.0 collective-permute-done.7
  14.5 0.0 collective-permute-done.6
  14.5 1.3 %collective-permute-start.9 = (f32[96,128]{1,0:T(8,128)S(1)}, f32[96,128]{1,0:T(8,128)S(1)}, u32[]{:S(2)}, u32[]{:S(2)}) collective-permute-start(f32[96,128]{1,0:T(8,128)S(1)} %pad_maximum_fusion.refs_0_), channel_id=1, source_target_pairs={{1,0},{3,2},{5,4},{7,6},{9,8},{11,10},{13,12},{15,14},{17,16},{19,... | collective-permute-start | bytes 147464 | tf_op jit(solution)/shard_map/ppermute | solution.py:558
  15.8 29.7 %collective-permute-done.9.refs_1_ = f32[96,128]{1,0:T(8,128)S(1)} collective-permute-done((f32[96,128]{1,0:T(8,128)S(1)}, f32[96,128]{1,0:T(8,128)S(1)}, u32[]{:S(2)}, u32[]{:S(2)}) %collective-permute-start.9) | collective-permute-done | bytes 49184 | tf_op jit(solution)/shard_map/ppermute | solution.py:558
  45.5 1.4 %haydock.1 = (f32[1,2,2,16]{3,2,1,0:T(2,128)}, f32[2,6]{1,0:T(2,128)}) custom-call(f32[96,128]{1,0:T(8,128)S(1)} %pad_maximum_fusion.refs_0_, f32[96,128]{1,0:T(8,128)S(1)} %collective-permute-done.9.refs_1_), custom_call_target="tpu_custom_call" | custom-call | tf_op jit(solution)/shard_map/haydock/pallas_call | solution.py:489
  (3 shorter events, 0.0 us)
Async XLA Ops:
  0.6 3.5 %collective-permute-start = (bf16[1,4,2,2,4,768]{5,4,3,2,1,0:T(4,128)(2,1)}, bf16[1,4,2,2,4,768]{5,4,3,2,1,0:T(4,128)(2,1)S(1)}, u32[]{:S(2)}, u32[]{:S(2)}) collective-permute-start(bf16[1,4,2,2,4,768]{5,4,3,2,1,0:T(4,128)(2,1)} %valence_in.1), channel_id=1, source_target_pairs={{0,1},{2,3},{4,5},{6,7},{8,9},{10,11},{12,13},{14,15},{16,17},{18,... | collective-permute-start | bytes 294920 | tf_op jit(solution)/shard_map/ppermute | solution.py:535
  4.2 4.5 %collective-permute-start.1 = (bf16[64,768]{1,0:T(8,128)(2,1)S(1)}, bf16[64,768]{1,0:T(8,128)(2,1)S(1)}, u32[]{:S(2)}, u32[]{:S(2)}) collective-permute-start(bf16[64,768]{1,0:T(8,128)(2,1)S(1)} %get-tuple-element.21), channel_id=1, source_target_pairs={{1,5},{5,9},{9,13},{13,1},{3,7},{7,11},{11,15},{15,3},{17,21},{21,... | collective-permute-start | bytes 294920 | tf_op jit(solution)/shard_map/ppermute | solution.py:57
  4.9 3.8 %collective-permute-start.2 = (bf16[64,768]{1,0:T(8,128)(2,1)S(1)}, bf16[64,768]{1,0:T(8,128)(2,1)S(1)}, u32[]{:S(2)}, u32[]{:S(2)}) collective-permute-start(bf16[64,768]{1,0:T(8,128)(2,1)S(1)} %get-tuple-element.22), channel_id=1, source_target_pairs={{1,9},{5,13},{9,1},{13,5},{3,11},{7,15},{11,3},{15,7},{17,25},{21,... | collective-permute-start | bytes 294920 | tf_op jit(solution)/shard_map/ppermute | solution.py:57
  5.6 3.2 %collective-permute-start.3 = (bf16[64,768]{1,0:T(8,128)(2,1)S(1)}, bf16[64,768]{1,0:T(8,128)(2,1)S(1)}, u32[]{:S(2)}, u32[]{:S(2)}) collective-permute-start(bf16[64,768]{1,0:T(8,128)(2,1)S(1)} %get-tuple-element.23), channel_id=1, source_target_pairs={{1,13},{5,1},{9,5},{13,9},{3,15},{7,3},{11,7},{15,11},{17,29},{21,... | collective-permute-start | bytes 294920 | tf_op jit(solution)/shard_map/ppermute | solution.py:57
  8.8 1.5 %collective-permute-start.4 = (bf16[128,768]{1,0:T(8,128)(2,1)S(1)}, bf16[128,768]{1,0:T(8,128)(2,1)S(1)}, u32[]{:S(2)}, u32[]{:S(2)}) collective-permute-start(bf16[128,768]{1,0:T(8,128)(2,1)S(1)} %get-tuple-element.24.valence), channel_id=1, source_target_pairs={{1,3},{3,1},{5,7},{7,5},{9,11},{11,9},{13,15},{15,13},{17,19},{19,... | collective-permute-start | bytes 589832 | tf_op jit(solution)/shard_map/ppermute | solution.py:57
  11.7 0.7 %collective-permute-start.5 = (f32[24,128]{1,0:T(8,128)S(1)}, f32[24,128]{1,0:T(8,128)S(1)}, u32[]{:S(2)}, u32[]{:S(2)}) collective-permute-start(f32[24,128]{1,0:T(8,128)S(1)} %project.1), channel_id=1, source_target_pairs={{1,3},{3,1},{5,7},{7,5},{9,11},{11,9},{13,15},{15,13},{17,19},{19,... | collective-permute-start | bytes 36872 | tf_op jit(solution)/shard_map/ppermute | solution.py:57
  12.4 2.0 %collective-permute-start.8 = (f32[24,128]{1,0:T(8,128)S(1)}, f32[24,128]{1,0:T(8,128)S(1)}, u32[]{:S(2)}, u32[]{:S(2)}) collective-permute-start(f32[24,128]{1,0:T(8,128)S(1)} %add.3), channel_id=1, source_target_pairs={{1,13},{5,1},{9,5},{13,9},{3,15},{7,3},{11,7},{15,11},{17,29},{21,... | collective-permute-start | bytes 36872 | tf_op jit(solution)/shard_map/ppermute | solution.py:57
  13.1 1.4 %collective-permute-start.7 = (f32[24,128]{1,0:T(8,128)S(1)}, f32[24,128]{1,0:T(8,128)S(1)}, u32[]{:S(2)}, u32[]{:S(2)}) collective-permute-start(f32[24,128]{1,0:T(8,128)S(1)} %add.3), channel_id=1, source_target_pairs={{1,9},{5,13},{9,1},{13,5},{3,11},{7,15},{11,3},{15,7},{17,25},{21,... | collective-permute-start | bytes 36872 | tf_op jit(solution)/shard_map/ppermute | solution.py:57
  13.8 0.7 %collective-permute-start.6 = (f32[24,128]{1,0:T(8,128)S(1)}, f32[24,128]{1,0:T(8,128)S(1)}, u32[]{:S(2)}, u32[]{:S(2)}) collective-permute-start(f32[24,128]{1,0:T(8,128)S(1)} %add.3), channel_id=1, source_target_pairs={{1,5},{5,9},{9,13},{13,1},{3,7},{7,11},{11,15},{15,3},{17,21},{21,... | collective-permute-start | bytes 36872 | tf_op jit(solution)/shard_map/ppermute | solution.py:57
  14.5 31.0 %collective-permute-start.9 = (f32[96,128]{1,0:T(8,128)S(1)}, f32[96,128]{1,0:T(8,128)S(1)}, u32[]{:S(2)}, u32[]{:S(2)}) collective-permute-start(f32[96,128]{1,0:T(8,128)S(1)} %pad_maximum_fusion.refs_0_), channel_id=1, source_target_pairs={{1,0},{3,2},{5,4},{7,6},{9,8},{11,10},{13,12},{15,14},{17,16},{19,... | collective-permute-start | bytes 147464 | tf_op jit(solution)/shard_map/ppermute | solution.py:558

commit v9 on v8

--- a/solution.py
+++ b/solution.py
@@ -53,8 +53,16 @@
 
 def exchanged(value, axis, move):
     size, cores = lax.axis_size(axis), lax.axis_size("ba")
-    pairs = [(i * cores + cores - 1, move(i, size) * cores + cores - 1) for i in range(size)]
+    pairs = []
+    for i in range(size):
+        pairs += [(i * cores + h, i * cores + h) for h in range(cores - 1)]
+        pairs.append((i * cores + cores - 1, move(i, size) * cores + cores - 1))
     return lax.ppermute(value, (axis, "ba"), pairs)
+
+
+def handed(value, step):
+    size = lax.axis_size("ba")
+    return lax.ppermute(value, "ba", [(h, (h + step) % size) for h in range(size)])
 
 
 def shifted(value, axis, step):
@@ -532,7 +540,7 @@
     pairs = val_count * val_count
     dims = (val_count, cond_count, npol)
     last = ba - 1
-    received = [lax.ppermute(valence_density, "ba", [(h, last)]) for h in range(last)]
+    received = [handed(valence_density, last - h) for h in range(last)]
     own, cond, chosen = sort(ka, qpoint_map, slot_owner, valence_density, conduction_density)
     packed = merge(ka, own, cond, chosen, received)
     blocks = [packed[0]] + [shifted(packed[j], "ka", j) for j in range(1, ka)]
@@ -555,7 +563,7 @@
     piece = summed(piece, "ga")
     pieces = [piece] + [shifted(piece, "ka", j) for j in range(1, ka)]
     gathered = jnp.concatenate(pieces, 0)
-    versions = [gathered] + [lax.ppermute(gathered, "ba", [(last, h)]) for h in range(last)]
+    versions = [gathered] + [handed(gathered, h + 1) for h in range(last)]
     scale_count = float(kcount * pair_count)
     return tuple(haydock(ka, pair_count, scale_count, npol, versions))
 

time: 47.2 us -> 44.6 us (0.945)
  waiting for transfers between devices: 29.8 us -> 0.99 us
  starting transfers between devices: 8.98 us -> 35.2 us
    ppermute x2, waiting for transfers between devices: 29.7 us -> 0.97 us  [handed(): lax.ppermute(value, 'ba', [(h, (h + step) % size) for h in range(size)])]
    ppermute x2, starting transfers between devices: 3.65 us -> 29.8 us  [handed(): lax.ppermute(value, 'ba', [(h, (h + step) % size) for h in range(size)])]
  transfers between devices with their start and end apart: 10 -> 10, of which waited for: 2 -> 2; matrix products, arithmetic and copies ran while one was open for 0% -> 0% of each run, Pallas kernels for 9% -> 10%
where the time goes in v9:
time: 44.6 us; the launch traced here: 44.3 us
  starting transfers between devices  35.2 us (79%)
  Pallas kernels  7.3 us (16%)
  waiting for transfers between devices  0.99 us (2%)
  between operations  0.81 us (2%)
    ppermute x2, starting transfers between devices, handed(): lax.ppermute(value, 'ba', [(h, (h + step) % size) for h in range(size)])  29.8 us
    ppermute x8, starting transfers between devices, exchanged(): return lax.ppermute(value, (axis, 'ba'), pairs)  5.33 us
    pallas_call x1, Pallas kernels, prepare(): pl.pallas_call(functools.partial(prepare_kernel, ka, dims), out_shape=[in...  2.46 us
    pallas_call x1, Pallas kernels, project(): pl.pallas_call(functools.partial(project_kernel, ka, ga, dims), out_shape...  1.46 us
    pallas_call x1, Pallas kernels, haydock(): pl.pallas_call(functools.partial(haydock_kernel, ka, codes, scale_count,...  1.42 us
    pallas_call x1, Pallas kernels, sort(): pl.pallas_call(functools.partial(sort_kernel, ka), out_shape=[in_vmem((ka...  1.06 us
    ppermute x2, waiting for transfers between devices, handed(): lax.ppermute(value, 'ba', [(h, (h + step) % size) for h in range(size)])  0.97 us
  transfers between devices with their start and end apart: 10, of which 2 were waited for; matrix products, arithmetic and copies ran while one was open for 0% of the time, Pallas kernels for 10%

profile of v9, /device:TPU:0, one launch (start us, length us, event | category | flops | bytes accessed | tf_op | source)
XLA Modules:
  0.0 44.3 jit_solution(3735097741894579946)
XLA Ops:
  0.6 0.5 %collective-permute-start = (bf16[1,4,2,2,4,768]{5,4,3,2,1,0:T(4,128)(2,1)}, bf16[1,4,2,2,4,768]{5,4,3,2,1,0:T(4,128)(2,1)S(1)}, u32[]{:S(2)}, u32[]{:S(2)}) collective-permute-start(bf16[1,4,2,2,4,768]{5,4,3,2,1,0:T(4,128)(2,1)} %valence_in.1), channel_id=1, source_target_pairs={{0,1},{1,0},{2,3},{3,2},{4,5},{5,4},{6,7},{7,6},{8,9},{9,8},{10,11... | collective-permute-start | bytes 294920 | tf_op jit(solution)/shard_map/ppermute | solution.py:65
  1.1 1.1 %sort.1 = (bf16[64,768]{1,0:T(8,128)(2,1)S(1)}, bf16[128,768]{1,0:T(8,128)(2,1)S(1)}, f32[32,128]{1,0:T(8,128)S(1)}) custom-call(s32[4,4]{1,0:T(4,128)} %refs_0_.1, s32[4]{0:T(128)} %refs_1_.1, bf16[1,4,2,2,4,768]{5,4,3,2,1,0:T(4,128)(2,1)} %valence_in.1, bf16[1,4,2,4,4,768]{5,4,3,2,1,0:T(4,128)(2,1)} %conduction_in.1), custom_call_target="tpu_custom_call" | custom-call | bytes 589824 | tf_op jit(solution)/shard_map/sort/pallas_call | solution.py:110
  2.2 0.1 collective-permute-done.refs_3_
  2.3 0.1 merge.1
  2.4 0.7 %collective-permute-start.1 = (bf16[64,768]{1,0:T(8,128)(2,1)S(1)}, bf16[64,768]{1,0:T(8,128)(2,1)S(1)}, u32[]{:S(2)}, u32[]{:S(2)}) collective-permute-start(bf16[64,768]{1,0:T(8,128)(2,1)S(1)} %get-tuple-element.21), channel_id=1, source_target_pairs={{0,0},{1,5},{4,4},{5,9},{8,8},{9,13},{12,12},{13,1},{2,2},{3,7},{6... | collective-permute-start | bytes 294920 | tf_op jit(solution)/shard_map/ppermute | solution.py:60
  3.1 0.7 %collective-permute-start.2 = (bf16[64,768]{1,0:T(8,128)(2,1)S(1)}, bf16[64,768]{1,0:T(8,128)(2,1)S(1)}, u32[]{:S(2)}, u32[]{:S(2)}) collective-permute-start(bf16[64,768]{1,0:T(8,128)(2,1)S(1)} %get-tuple-element.22), channel_id=1, source_target_pairs={{0,0},{1,9},{4,4},{5,13},{8,8},{9,1},{12,12},{13,5},{2,2},{3,11},{... | collective-permute-start | bytes 294920 | tf_op jit(solution)/shard_map/ppermute | solution.py:60
  3.7 0.7 %collective-permute-start.3 = (bf16[64,768]{1,0:T(8,128)(2,1)S(1)}, bf16[64,768]{1,0:T(8,128)(2,1)S(1)}, u32[]{:S(2)}, u32[]{:S(2)}) collective-permute-start(bf16[64,768]{1,0:T(8,128)(2,1)S(1)} %get-tuple-element.23), channel_id=1, source_target_pairs={{0,0},{1,13},{4,4},{5,1},{8,8},{9,5},{12,12},{13,9},{2,2},{3,15},{... | collective-permute-start | bytes 294920 | tf_op jit(solution)/shard_map/ppermute | solution.py:60
  4.4 2.5 %prepare.1 = (bf16[2,768,1536]{2,1,0:T(8,128)(2,1)S(1)}, bf16[128,512]{1,0:T(8,128)(2,1)S(1)}, f32[8,128]{1,0:T(8,128)S(1)}) custom-call(s32[4,4]{1,0:T(4,128)} %refs_0_.1, s32[4]{0:T(128)} %refs_1_.1, s32[16]{0:T(128)} %refs_2_.1, f32[1,4]{1,0:T(1,128)} %refs_3_.1, f32[1,4]{1,0:T(1,128)} %refs_4_.1, f32[1,2,2,16]{3,2,1,0:T(2,128)} %refs_5_.1, ...), custom_call_target="tpu_custom_call" | custom-call | bytes 9437184 | tf_op jit(solution)/shard_map/prepare/pallas_call | solution.py:260
  6.9 0.0 collective-permute-done.1.refs_1_
  6.9 0.0 collective-permute-done.2.refs_2_
  6.9 0.0 collective-permute-done.3.refs_3_
  6.9 0.7 %collective-permute-start.4 = (bf16[128,768]{1,0:T(8,128)(2,1)S(1)}, bf16[128,768]{1,0:T(8,128)(2,1)S(1)}, u32[]{:S(2)}, u32[]{:S(2)}) collective-permute-start(bf16[128,768]{1,0:T(8,128)(2,1)S(1)} %get-tuple-element.24.valence), channel_id=1, source_target_pairs={{0,0},{1,3},{2,2},{3,1},{4,4},{5,7},{6,6},{7,5},{8,8},{9,11},{10,1... | collective-permute-start | bytes 589832 | tf_op jit(solution)/shard_map/ppermute | solution.py:60
  7.6 0.8 %near_field.1.refs_3_ = f32[768,256]{1,0:T(8,128)S(1)} custom-call(bf16[2,768,1536]{2,1,0:T(8,128)(2,1)S(1)} %get-tuple-element.18.screening.refs_0_, bf16[128,768]{1,0:T(8,128)(2,1)S(1)} %get-tuple-element.24.valence), custom_call_target="tpu_custom_call" | custom-call | flops 603979776 | bytes 2359296 | tf_op jit(solution)/shard_map/near_field/pallas_call | solution.py:327
  8.4 0.0 collective-permute-done.4.refs_4_
  8.4 1.5 %project.1 = f32[24,128]{1,0:T(8,128)S(1)} custom-call(bf16[2,768,1536]{2,1,0:T(8,128)(2,1)S(1)} %get-tuple-element.18.screening.refs_0_, bf16[128,512]{1,0:T(8,128)(2,1)S(1)} %get-tuple-element.19.refs_1_, f32[8,128]{1,0:T(8,128)S(1)} %get-tuple-element.20.refs_4_.refs_2_, f32[768,256]{1,0:T(8,128)S(1)} %near_field.1.refs_3_, ...), custom_call_target="tpu_custom_call" | custom-call | tf_op jit(solution)/shard_map/project/pallas_call | solution.py:398
  9.9 0.7 %collective-permute-start.5 = (f32[24,128]{1,0:T(8,128)S(1)}, f32[24,128]{1,0:T(8,128)S(1)}, u32[]{:S(2)}, u32[]{:S(2)}) collective-permute-start(f32[24,128]{1,0:T(8,128)S(1)} %project.1), channel_id=1, source_target_pairs={{0,0},{1,3},{2,2},{3,1},{4,4},{5,7},{6,6},{7,5},{8,8},{9,11},{10,1... | collective-permute-start | bytes 36872 | tf_op jit(solution)/shard_map/ppermute | solution.py:60
  10.6 0.0 collective-permute-done.5
  10.6 0.7 %collective-permute-start.8 = (f32[24,128]{1,0:T(8,128)S(1)}, f32[24,128]{1,0:T(8,128)S(1)}, u32[]{:S(2)}, u32[]{:S(2)}) collective-permute-start(f32[24,128]{1,0:T(8,128)S(1)} %add.3), channel_id=1, source_target_pairs={{0,0},{1,13},{4,4},{5,1},{8,8},{9,5},{12,12},{13,9},{2,2},{3,15},{... | collective-permute-start | bytes 36872 | tf_op jit(solution)/shard_map/ppermute | solution.py:60
  11.3 0.7 %collective-permute-start.7 = (f32[24,128]{1,0:T(8,128)S(1)}, f32[24,128]{1,0:T(8,128)S(1)}, u32[]{:S(2)}, u32[]{:S(2)}) collective-permute-start(f32[24,128]{1,0:T(8,128)S(1)} %add.3), channel_id=1, source_target_pairs={{0,0},{1,9},{4,4},{5,13},{8,8},{9,1},{12,12},{13,5},{2,2},{3,11},{... | collective-permute-start | bytes 36872 | tf_op jit(solution)/shard_map/ppermute | solution.py:60
  11.9 0.7 %collective-permute-start.6 = (f32[24,128]{1,0:T(8,128)S(1)}, f32[24,128]{1,0:T(8,128)S(1)}, u32[]{:S(2)}, u32[]{:S(2)}) collective-permute-start(f32[24,128]{1,0:T(8,128)S(1)} %add.3), channel_id=1, source_target_pairs={{0,0},{1,5},{4,4},{5,9},{8,8},{9,13},{12,12},{13,1},{2,2},{3,7},{6... | collective-permute-start | bytes 36872 | tf_op jit(solution)/shard_map/ppermute | solution.py:60
  12.6 0.0 collective-permute-done.8
  12.6 0.0 collective-permute-done.7
  12.6 0.0 collective-permute-done.6
  12.7 29.3 %collective-permute-start.9 = (f32[96,128]{1,0:T(8,128)S(1)}, f32[96,128]{1,0:T(8,128)S(1)}, u32[]{:S(2)}, u32[]{:S(2)}) collective-permute-start(f32[96,128]{1,0:T(8,128)S(1)} %pad_maximum_fusion.refs_0_), channel_id=1, source_target_pairs={{0,1},{1,0},{2,3},{3,2},{4,5},{5,4},{6,7},{7,6},{8,9},{9,8},{10,11... | collective-permute-start | bytes 147464 | tf_op jit(solution)/shard_map/ppermute | solution.py:65
  42.0 0.9 %collective-permute-done.9.refs_1_ = f32[96,128]{1,0:T(8,128)S(1)} collective-permute-done((f32[96,128]{1,0:T(8,128)S(1)}, f32[96,128]{1,0:T(8,128)S(1)}, u32[]{:S(2)}, u32[]{:S(2)}) %collective-permute-start.9) | collective-permute-done | bytes 49184 | tf_op jit(solution)/shard_map/ppermute | solution.py:65
  42.9 1.4 %haydock.1 = (f32[1,2,2,16]{3,2,1,0:T(2,128)}, f32[2,6]{1,0:T(2,128)}) custom-call(f32[96,128]{1,0:T(8,128)S(1)} %pad_maximum_fusion.refs_0_, f32[96,128]{1,0:T(8,128)S(1)} %collective-permute-done.9.refs_1_), custom_call_target="tpu_custom_call" | custom-call | tf_op jit(solution)/shard_map/haydock/pallas_call | solution.py:497
  (3 shorter events, 0.0 us)
Async XLA Ops:
  0.6 1.7 %collective-permute-start = (bf16[1,4,2,2,4,768]{5,4,3,2,1,0:T(4,128)(2,1)}, bf16[1,4,2,2,4,768]{5,4,3,2,1,0:T(4,128)(2,1)S(1)}, u32[]{:S(2)}, u32[]{:S(2)}) collective-permute-start(bf16[1,4,2,2,4,768]{5,4,3,2,1,0:T(4,128)(2,1)} %valence_in.1), channel_id=1, source_target_pairs={{0,1},{1,0},{2,3},{3,2},{4,5},{5,4},{6,7},{7,6},{8,9},{9,8},{10,11... | collective-permute-start | bytes 294920 | tf_op jit(solution)/shard_map/ppermute | solution.py:65
  2.4 4.5 %collective-permute-start.1 = (bf16[64,768]{1,0:T(8,128)(2,1)S(1)}, bf16[64,768]{1,0:T(8,128)(2,1)S(1)}, u32[]{:S(2)}, u32[]{:S(2)}) collective-permute-start(bf16[64,768]{1,0:T(8,128)(2,1)S(1)} %get-tuple-element.21), channel_id=1, source_target_pairs={{0,0},{1,5},{4,4},{5,9},{8,8},{9,13},{12,12},{13,1},{2,2},{3,7},{6... | collective-permute-start | bytes 294920 | tf_op jit(solution)/shard_map/ppermute | solution.py:60
  3.1 3.8 %collective-permute-start.2 = (bf16[64,768]{1,0:T(8,128)(2,1)S(1)}, bf16[64,768]{1,0:T(8,128)(2,1)S(1)}, u32[]{:S(2)}, u32[]{:S(2)}) collective-permute-start(bf16[64,768]{1,0:T(8,128)(2,1)S(1)} %get-tuple-element.22), channel_id=1, source_target_pairs={{0,0},{1,9},{4,4},{5,13},{8,8},{9,1},{12,12},{13,5},{2,2},{3,11},{... | collective-permute-start | bytes 294920 | tf_op jit(solution)/shard_map/ppermute | solution.py:60
  3.7 3.2 %collective-permute-start.3 = (bf16[64,768]{1,0:T(8,128)(2,1)S(1)}, bf16[64,768]{1,0:T(8,128)(2,1)S(1)}, u32[]{:S(2)}, u32[]{:S(2)}) collective-permute-start(bf16[64,768]{1,0:T(8,128)(2,1)S(1)} %get-tuple-element.23), channel_id=1, source_target_pairs={{0,0},{1,13},{4,4},{5,1},{8,8},{9,5},{12,12},{13,9},{2,2},{3,15},{... | collective-permute-start | bytes 294920 | tf_op jit(solution)/shard_map/ppermute | solution.py:60
  6.9 1.5 %collective-permute-start.4 = (bf16[128,768]{1,0:T(8,128)(2,1)S(1)}, bf16[128,768]{1,0:T(8,128)(2,1)S(1)}, u32[]{:S(2)}, u32[]{:S(2)}) collective-permute-start(bf16[128,768]{1,0:T(8,128)(2,1)S(1)} %get-tuple-element.24.valence), channel_id=1, source_target_pairs={{0,0},{1,3},{2,2},{3,1},{4,4},{5,7},{6,6},{7,5},{8,8},{9,11},{10,1... | collective-permute-start | bytes 589832 | tf_op jit(solution)/shard_map/ppermute | solution.py:60
  9.9 0.7 %collective-permute-start.5 = (f32[24,128]{1,0:T(8,128)S(1)}, f32[24,128]{1,0:T(8,128)S(1)}, u32[]{:S(2)}, u32[]{:S(2)}) collective-permute-start(f32[24,128]{1,0:T(8,128)S(1)} %project.1), channel_id=1, source_target_pairs={{0,0},{1,3},{2,2},{3,1},{4,4},{5,7},{6,6},{7,5},{8,8},{9,11},{10,1... | collective-permute-start | bytes 36872 | tf_op jit(solution)/shard_map/ppermute | solution.py:60
  10.6 2.0 %collective-permute-start.8 = (f32[24,128]{1,0:T(8,128)S(1)}, f32[24,128]{1,0:T(8,128)S(1)}, u32[]{:S(2)}, u32[]{:S(2)}) collective-permute-start(f32[24,128]{1,0:T(8,128)S(1)} %add.3), channel_id=1, source_target_pairs={{0,0},{1,13},{4,4},{5,1},{8,8},{9,5},{12,12},{13,9},{2,2},{3,15},{... | collective-permute-start | bytes 36872 | tf_op jit(solution)/shard_map/ppermute | solution.py:60
  11.3 1.4 %collective-permute-start.7 = (f32[24,128]{1,0:T(8,128)S(1)}, f32[24,128]{1,0:T(8,128)S(1)}, u32[]{:S(2)}, u32[]{:S(2)}) collective-permute-start(f32[24,128]{1,0:T(8,128)S(1)} %add.3), channel_id=1, source_target_pairs={{0,0},{1,9},{4,4},{5,13},{8,8},{9,1},{12,12},{13,5},{2,2},{3,11},{... | collective-permute-start | bytes 36872 | tf_op jit(solution)/shard_map/ppermute | solution.py:60
  11.9 0.7 %collective-permute-start.6 = (f32[24,128]{1,0:T(8,128)S(1)}, f32[24,128]{1,0:T(8,128)S(1)}, u32[]{:S(2)}, u32[]{:S(2)}) collective-permute-start(f32[24,128]{1,0:T(8,128)S(1)} %add.3), channel_id=1, source_target_pairs={{0,0},{1,5},{4,4},{5,9},{8,8},{9,13},{12,12},{13,1},{2,2},{3,7},{6... | collective-permute-start | bytes 36872 | tf_op jit(solution)/shard_map/ppermute | solution.py:60
  12.7 30.2 %collective-permute-start.9 = (f32[96,128]{1,0:T(8,128)S(1)}, f32[96,128]{1,0:T(8,128)S(1)}, u32[]{:S(2)}, u32[]{:S(2)}) collective-permute-start(f32[96,128]{1,0:T(8,128)S(1)} %pad_maximum_fusion.refs_0_), channel_id=1, source_target_pairs={{0,1},{1,0},{2,3},{3,2},{4,5},{5,4},{6,7},{7,6},{8,9},{9,8},{10,11... | collective-permute-start | bytes 147464 | tf_op jit(solution)/shard_map/ppermute | solution.py:65

commit v10 on v7

--- a/solution.py
+++ b/solution.py
@@ -50,9 +50,23 @@
     return lax.rem(me + size - step, size)
 
 
-def exchanged(value, axis, step):
-    size = lax.axis_size(axis)
-    return lax.ppermute(value, axis, [(i, (i + step) % size) for i in range(size)])
+def exchanged(value, axis, move):
+    size, cores = lax.axis_size(axis), lax.axis_size("ba")
+    pairs = [
+        (i * cores + h, move(i, size) * cores + (h + 1) % cores)
+        for i in range(size)
+        for h in range(cores)
+    ]
+    return lax.ppermute(value, (axis, "ba"), pairs)
+
+
+def shifted(value, axis, step):
+    return exchanged(value, axis, lambda i, size: (i + step) % size)
+
+
+def handed(value, step):
+    size = lax.axis_size("ba")
+    return lax.ppermute(value, "ba", [(h, (h + step) % size) for h in range(size)])
 
 
 def pack_kernel(ka, qmap_in, owner_in, valence_in, conduction_in, *rest):
@@ -87,7 +101,8 @@
         k2 = partner[target(me, at, ka)]
         block = valence[0, k2].astype(jnp.float32).reshape(val_rows, width)
         outs[at][:val_rows, :] = block.astype(jnp.bfloat16)
-        block = conduction[0, k2, :, pl.ds(half * share, share)].astype(jnp.float32)
+        to = lax.rem(half + min(at, 1), lax.axis_size("ba"))
+        block = conduction[0, k2, :, pl.ds(to * share, share)].astype(jnp.float32)
         outs[at][val_rows:, :] = block.reshape(cond_rows, width).astype(jnp.bfloat16)
 
 
@@ -116,7 +131,7 @@
 
 def prepare_kernel(ka, dims, *refs):
     vloc, val_count, cond_count, npol = dims
-    ins, screening, (screen_out, table, extras), scratch = refs[:6], refs[6], refs[8:11], refs[11:]
+    ins, screening, (screen_out, near_table, far_table, extras), scratch = refs[:6], refs[6], refs[8:12], refs[12:]
     qmap, owner, band_pairs, val_energy, cond_energy, start, sems, screen_sems = scratch
     me = lax.axis_index("ka")
     half = lax.axis_index("ba")
@@ -147,16 +162,19 @@
     lanes = 2 * mid
     row = iota((2 * rows, lanes), 0)
     col = iota((2 * rows, lanes), 1)
-    k_of_row = origin(me, row % rows // block, ka)
-    want = (
-        (row % block // pairs) * mid
-        + k_of_row * codes
-        + (half * vloc + row % pairs // val_count) * cond_count
-    )
-    joined = (col - want >= 0) & (col - want < cond_count)
-    for v2 in range(val_count):
-        pick = jnp.where(joined & (row % val_count == v2), 1.0, 0.0)
-        table[:, v2 * lanes : (v2 + 1) * lanes] = pick.astype(jnp.bfloat16)
+    j_of_row = row % rows // block
+    cores = lax.axis_size("ba")
+    for moves, table in enumerate((near_table, far_table)):
+        share = lax.rem(half + 2 * cores - moves - jnp.where(j_of_row == 0, 0, 1), cores)
+        want = (
+            (row % block // pairs) * mid
+            + origin(me, j_of_row, ka) * codes
+            + (share * vloc + row % pairs // val_count) * cond_count
+        )
+        joined = (col - want >= 0) & (col - want < cond_count)
+        for v2 in range(val_count):
+            pick = jnp.where(joined & (row % val_count == v2), 1.0, 0.0)
+            table[:, v2 * lanes : (v2 + 1) * lanes] = pick.astype(jnp.bfloat16)
 
     for copy in copies:
         copy.wait()
@@ -206,10 +224,11 @@
         out_shape=[
             in_vmem(screening.shape[1:], screening.dtype),
             in_vmem(table.shape, table.dtype),
+            in_vmem(table.shape, table.dtype),
             in_vmem((EXTRA_ROWS, lanes), jnp.float32),
         ],
         in_specs=[anywhere] * 8,
-        out_specs=[vmem] * 3,
+        out_specs=[vmem] * 4,
         scratch_shapes=[pltpu.SMEM(x.shape, x.dtype) for x in operands[:5]]
         + [
             pltpu.VMEM(start.shape, start.dtype),
@@ -261,32 +280,11 @@
     ) + lax.dot_general(screening[1, :, columns], imag, form, preferred_element_type=jnp.float32)
 
 
-def near_kernel(pairs, screening, valence, out):
-    out[...] = screened_block(screening, valence, pairs, lax.axis_index("ga"))
-
-
-def near_field(pairs, screening, valence):
-    rows, width = valence.shape
-    glocal = screening.shape[1]
-    return pl.pallas_call(
-        functools.partial(near_kernel, pairs),
-        out_shape=in_vmem((glocal, 2 * rows), jnp.float32),
-        in_specs=[vmem, vmem],
-        out_specs=vmem,
-        cost_estimate=pl.CostEstimate(
-            flops=8 * glocal * width * rows, bytes_accessed=screening.size, transcendentals=0
-        ),
-        compiler_params=limits(screening, valence),
-        name="near_field",
-    )(screening, valence)
-
-
-def project_kernel(ka, ga, ba, dims, *refs):
+def project_kernel(ka, ba, far, dims, *refs):
     vloc, val_count, cond_count, npol = dims
-    screening, table, extras, near = refs[:4]
-    val_in = refs[4 : 4 + ga - 1]
-    cond_in = refs[-1 - ba : -1]
-    out = refs[-1]
+    screening, table, held = refs[:3]
+    val_in, cond_in, out = refs[3 : -1 - ba], refs[-1 - ba : -1], refs[-1]
+    ga = lax.axis_size("ga")
     mine = lax.axis_index("ga")
     half = lax.axis_index("ba")
     pairs = vloc * val_count
@@ -298,9 +296,10 @@
     cond_rows = cond_count * cond_count
     share_rows = share * cond_count
 
-    fields = near[...]
-    for r in range(1, ga):
-        fields = fields + screened_block(screening, val_in[r - 1], pairs, origin(mine, r, ga))
+    fields = None
+    for r, valence in enumerate(val_in, far):
+        term = screened_block(screening, valence, pairs, origin(mine, r, ga))
+        fields = term if fields is None else fields + term
     both = jnp.concatenate(split(fields), 1)
     cond_all = jnp.concatenate([ref[...] for ref in cond_in], 0)
     crossed = jnp.dot(cond_all, both, preferred_element_type=jnp.float32)
@@ -341,21 +340,26 @@
     )
     fold = jnp.where(fold, 1.0, 0.0).astype(jnp.bfloat16)
     piece = jnp.dot(fold, jnp.concatenate(split(spread), 1), preferred_element_type=jnp.float32)
-    out[:codes, :] = piece[:, :lanes] + piece[:, lanes:]
-    out[codes:, :] = extras[...]
-
-
-def project(ka, ga, ba, dims, screening, table, extras, near, val_far, cond_all):
+    piece = piece[:, :lanes] + piece[:, lanes:]
+    out[:codes, :] = piece + held[:codes, :] if far else piece
+    out[codes:, :] = held[codes:, :] if far else held[...]
+
+
+def project(ka, ba, far, dims, screening, table, base, val_in, cond_all):
     vloc, val_count, cond_count, npol = dims
     codes = val_count * cond_count
-    operands = [screening, table, extras, near, *val_far, *cond_all]
+    operands = [screening, table, base, *val_in, *cond_all]
+    rows, width = val_in[0].shape
     return pl.pallas_call(
-        functools.partial(project_kernel, ka, ga, ba, dims),
+        functools.partial(project_kernel, ka, ba, far, dims),
         out_shape=in_vmem((codes + EXTRA_ROWS, 2 * ka * codes), jnp.float32),
         in_specs=[vmem] * len(operands),
         out_specs=vmem,
+        cost_estimate=pl.CostEstimate(
+            flops=8 * screening.shape[1] * width * rows, bytes_accessed=screening.size, transcendentals=0
+        ),
         compiler_params=limits(*operands),
-        name="project",
+        name="project_far" if far else "project_near",
     )(*operands)
 
 
@@ -462,16 +466,12 @@
 def summed(value, axis):
     size = lax.axis_size(axis)
     if size & (size - 1):
-        return lax.psum(value, axis)
+        return value + sum(shifted(value, axis, step) for step in range(1, size))
     step = 1
     while step < size:
-        value = value + lax.ppermute(value, axis, [(i, i ^ step) for i in range(size)])
+        value = value + exchanged(value, axis, lambda i, size: i ^ step)
         step *= 2
     return value
-
-
-def sent(values, axis):
-    return [values[0]] + [exchanged(values[j], axis, j) for j in range(1, lax.axis_size(axis))]
 
 
 def local(
@@ -495,8 +495,8 @@
     pairs = vloc * val_count
     dims = (vloc, val_count, cond_count, npol)
     packed = pack(ka, ba, qpoint_map, slot_owner, valence_density, conduction_density)
-    blocks = sent(packed, "ka")
-    whole, table, extras = prepare(
+    blocks = [packed[0]] + [shifted(packed[j], "ka", j) for j in range(1, ka)]
+    whole, near_table, far_table, extras = prepare(
         ka,
         dims,
         qpoint_map,
@@ -509,12 +509,14 @@
         packed[0],
     )
     val_all, cond_half = regroup(ka, 2 * pairs, blocks, extras)
-    val_far = [exchanged(val_all, "ga", r) for r in range(1, ga)]
-    cond_all = [cond_half] + [exchanged(cond_half, "ba", r) for r in range(1, ba)]
-    near = near_field(pairs, whole, val_all)
-    piece = project(ka, ga, ba, dims, whole, table, extras, near, val_far, cond_all)
-    piece = summed(summed(piece, "ba"), "ga")
-    pieces = sent([piece] * ka, "ka")
+    val_far = [shifted(val_all, "ga", r) for r in range(1, ga)]
+    cond_all = [cond_half] + [handed(cond_half, r) for r in range(1, ba)]
+    piece = project(ka, ba, 0, dims, whole, near_table, extras, [val_all], cond_all)
+    if val_far:
+        piece = project(ka, ba, 1, dims, whole, far_table, piece, val_far, cond_all)
+    piece = piece + sum(handed(piece, r) for r in range(1, ba))
+    piece = summed(piece, "ga")
+    pieces = [piece] + [shifted(piece, "ka", j) for j in range(1, ka)]
     scale_count = float(kcount * pair_count)
     return tuple(haydock(ka, pair_count, scale_count, npol, pieces))
 

time: 31.3 us -> 29.7 us (0.949)
  waiting for transfers between devices: 9.2 us -> 7.93 us
  starting transfers between devices: 14.3 us -> 13.5 us
  Pallas kernels: 6.92 us -> 7.43 us
    ppermute x10, waiting for transfers between devices: 9.2 us -> 7.93 us  [the longest x8 7.04 us: exchanged(): return lax.ppermute(value, (axis, 'ba'), pairs)]
    ppermute x10, starting transfers between devices: 14.3 us -> 13.5 us  [the longest x8 13 us: exchanged(): return lax.ppermute(value, (axis, 'ba'), pairs)]
    pallas_call x2, Pallas kernels: 2 us -> 2.51 us  [project(): pl.pallas_call(functools.partial(project_kernel, ka, ba, far, dims), out_...]
  transfers between devices with their start and end apart: 10 -> 10, of which waited for: 6 -> 7; matrix products, arithmetic and copies ran while one was open for 0% -> 0% of each run, Pallas kernels for 10% -> 13%
where the time goes in v10:
time: 29.7 us; the launch traced here: 29.5 us
  starting transfers between devices  13.5 us (45%)
  waiting for transfers between devices  7.93 us (27%)
  Pallas kernels  7.43 us (25%)
  between operations  0.67 us (2%)
    ppermute x8, starting transfers between devices, exchanged(): return lax.ppermute(value, (axis, 'ba'), pairs)  13 us
    ppermute x8, waiting for transfers between devices, exchanged(): return lax.ppermute(value, (axis, 'ba'), pairs)  7.04 us
    pallas_call x2, Pallas kernels, project(): pl.pallas_call(functools.partial(project_kernel, ka, ba, far, dims), out_...  2.51 us
    pallas_call x1, Pallas kernels, prepare(): pl.pallas_call(functools.partial(prepare_kernel, ka, dims), out_shape=[in...  2.45 us
    pallas_call x1, Pallas kernels, haydock(): pl.pallas_call(functools.partial(haydock_kernel, ka, codes, scale_count,...  1.41 us
    pallas_call x1, Pallas kernels, pack(): pl.pallas_call(functools.partial(pack_kernel, ka), out_shape=[shape] * ka...  1.05 us
    ppermute x2, waiting for transfers between devices, handed(): lax.ppermute(value, 'ba', [(h, (h + step) % size) for h in range(size)])  0.88 us
  transfers between devices with their start and end apart: 10, of which 7 were waited for; matrix products, arithmetic and copies ran while one was open for 0% of the time, Pallas kernels for 13%

profile of v10, /device:TPU:0, one launch (start us, length us, event | category | flops | bytes accessed | tf_op | source)
XLA Modules:
  0.0 29.5 jit_solution(8251519861202624053)
XLA Ops:
  0.6 1.0 %pack.1 = (bf16[32,768]{1,0:T(8,128)(2,1)S(1)}, bf16[32,768]{1,0:T(8,128)(2,1)S(1)}, bf16[32,768]{1,0:T(8,128)(2,1)S(1)}, bf16[32,768]{1,0:T(8,128)(2,1)S(1)}) custom-call(s32[4,4]{1,0:T(4,128)} %refs_0_.1, s32[4]{0:T(128)} %refs_1_.1, bf16[1,4,2,2,4,768]{5,4,3,2,1,0:T(4,128)(2,1)} %valence_in.1, bf16[1,4,2,4,4,768]{5,4,3,2,1,0:T(4,128)(2,1)} %conduction_in.1), custom_call_target="tpu_custom_call" | custom-call | tf_op jit(solution)/shard_map/pack/pallas_call | solution.py:114
  1.7 2.5 %collective-permute-start = (bf16[32,768]{1,0:T(8,128)(2,1)S(1)}, bf16[32,768]{1,0:T(8,128)(2,1)S(1)}, u32[]{:S(2)}, u32[]{:S(2)}) collective-permute-start(bf16[32,768]{1,0:T(8,128)(2,1)S(1)} %get-tuple-element.17), channel_id=1, source_target_pairs={{0,5},{1,4},{4,9},{5,8},{8,13},{9,12},{12,1},{13,0},{2,7},{3,6},{6... | collective-permute-start | bytes 147464 | tf_op jit(solution)/shard_map/ppermute | solution.py:60
  4.2 2.9 %collective-permute-start.1 = (bf16[32,768]{1,0:T(8,128)(2,1)S(1)}, bf16[32,768]{1,0:T(8,128)(2,1)S(1)}, u32[]{:S(2)}, u32[]{:S(2)}) collective-permute-start(bf16[32,768]{1,0:T(8,128)(2,1)S(1)} %get-tuple-element.18), channel_id=1, source_target_pairs={{0,9},{1,8},{4,13},{5,12},{8,1},{9,0},{12,5},{13,4},{2,11},{3,10},... | collective-permute-start | bytes 147464 | tf_op jit(solution)/shard_map/ppermute | solution.py:60
  7.1 0.8 %collective-permute-start.2 = (bf16[32,768]{1,0:T(8,128)(2,1)S(1)}, bf16[32,768]{1,0:T(8,128)(2,1)S(1)}, u32[]{:S(2)}, u32[]{:S(2)}) collective-permute-start(bf16[32,768]{1,0:T(8,128)(2,1)S(1)} %get-tuple-element.19), channel_id=1, source_target_pairs={{0,13},{1,12},{4,1},{5,0},{8,5},{9,4},{12,9},{13,8},{2,15},{3,14},... | collective-permute-start | bytes 147464 | tf_op jit(solution)/shard_map/ppermute | solution.py:60
  7.9 2.5 %prepare.1 = (bf16[2,768,1536]{2,1,0:T(8,128)(2,1)S(1)}, bf16[128,512]{1,0:T(8,128)(2,1)S(1)}, bf16[128,512]{1,0:T(8,128)(2,1)S(1)}, f32[8,128]{1,0:T(8,128)S(1)}) custom-call(s32[4,4]{1,0:T(4,128)} %refs_0_.1, s32[4]{0:T(128)} %refs_1_.1, s32[16]{0:T(128)} %refs_2_.1, f32[1,4]{1,0:T(1,128)} %refs_3_.1, f32[1,4]{1,0:T(1,128)} %refs_4_.1, ...), custom_call_target="tpu_custom_call" | custom-call | bytes 9437184 | tf_op jit(solution)/shard_map/prepare/pallas_call | solution.py:222
  10.3 0.0 collective-permute-done.refs_1_
  10.3 0.3 %collective-permute-done.1.refs_2_ = bf16[32,768]{1,0:T(8,128)(2,1)S(1)} collective-permute-done((bf16[32,768]{1,0:T(8,128)(2,1)S(1)}, bf16[32,768]{1,0:T(8,128)(2,1)S(1)}, u32[]{:S(2)}, u32[]{:S(2)}) %collective-permute-start.1) | collective-permute-done | bytes 49184 | tf_op jit(solution)/shard_map/ppermute | solution.py:60
  10.7 0.9 %collective-permute-done.2.refs_3_ = bf16[32,768]{1,0:T(8,128)(2,1)S(1)} collective-permute-done((bf16[32,768]{1,0:T(8,128)(2,1)S(1)}, bf16[32,768]{1,0:T(8,128)(2,1)S(1)}, u32[]{:S(2)}, u32[]{:S(2)}) %collective-permute-start.2) | collective-permute-done | bytes 49184 | tf_op jit(solution)/shard_map/ppermute | solution.py:60
  11.5 0.2 collective-permute-start.3
  11.7 1.7 %collective-permute-start.4 = (bf16[64,768]{1,0:T(8,128)(2,1)S(1)}, bf16[64,768]{1,0:T(8,128)(2,1)S(1)}, u32[]{:S(2)}, u32[]{:S(2)}) collective-permute-start(bf16[64,768]{1,0:T(8,128)(2,1)S(1)} %get-tuple-element.20.refs_3_), channel_id=1, source_target_pairs={{0,3},{1,2},{2,1},{3,0},{4,7},{5,6},{6,5},{7,4},{8,11},{9,10},{10,... | collective-permute-start | bytes 294920 | tf_op jit(solution)/shard_map/ppermute | solution.py:60
  13.4 0.0 collective-permute-done.3.refs_5_
  13.4 1.3 %project_near.1.refs_2_ = f32[24,128]{1,0:T(8,128)S(1)} custom-call(bf16[2,768,1536]{2,1,0:T(8,128)(2,1)S(1)} %get-tuple-element.13.refs_0_, bf16[128,512]{1,0:T(8,128)(2,1)S(1)} %get-tuple-element.15.refs_1_, f32[8,128]{1,0:T(8,128)S(1)} %get-tuple-element.16.refs_4_.refs_2_, bf16[64,768]{1,0:T(8,128)(2,1)S(1)} %get-tuple-element.20.refs_3_, ...), custom_call_target="tpu_custom_call" | custom-call | flops 301989888 | bytes 2359296 | tf_op jit(solution)/shard_map/project_near/pallas_call | solution.py:353
  14.6 1.7 %collective-permute-done.4.refs_3_ = bf16[64,768]{1,0:T(8,128)(2,1)S(1)} collective-permute-done((bf16[64,768]{1,0:T(8,128)(2,1)S(1)}, bf16[64,768]{1,0:T(8,128)(2,1)S(1)}, u32[]{:S(2)}, u32[]{:S(2)}) %collective-permute-start.4) | collective-permute-done | bytes 98336 | tf_op jit(solution)/shard_map/ppermute | solution.py:60
  16.4 1.3 %project_far.1 = f32[24,128]{1,0:T(8,128)S(1)} custom-call(bf16[2,768,1536]{2,1,0:T(8,128)(2,1)S(1)} %get-tuple-element.13.refs_0_, bf16[128,512]{1,0:T(8,128)(2,1)S(1)} %get-tuple-element.14.refs_1_, f32[24,128]{1,0:T(8,128)S(1)} %project_near.1.refs_2_, bf16[64,768]{1,0:T(8,128)(2,1)S(1)} %collective-permute-done.4.refs_3_, ...), custom_call_target="tpu_custom_call" | custom-call | flops 301989888 | bytes 2359296 | tf_op jit(solution)/shard_map/project_far/pallas_call | solution.py:353
  17.6 0.3 %collective-permute-start.5 = (f32[24,128]{1,0:T(8,128)S(1)}, f32[24,128]{1,0:T(8,128)S(1)}, u32[]{:S(2)}, u32[]{:S(2)}) collective-permute-start(f32[24,128]{1,0:T(8,128)S(1)} %project_far.1), channel_id=1, source_target_pairs={{0,1},{1,0},{2,3},{3,2},{4,5},{5,4},{6,7},{7,6},{8,9},{9,8},{10,11... | collective-permute-start | bytes 36872 | tf_op jit(solution)/shard_map/ppermute | solution.py:69
  17.9 0.9 %collective-permute-done.5 = f32[24,128]{1,0:T(8,128)S(1)} collective-permute-done((f32[24,128]{1,0:T(8,128)S(1)}, f32[24,128]{1,0:T(8,128)S(1)}, u32[]{:S(2)}, u32[]{:S(2)}) %collective-permute-start.5) | collective-permute-done | bytes 12320 | tf_op jit(solution)/shard_map/ppermute | solution.py:69
  18.8 1.6 %collective-permute-start.6 = (f32[24,128]{1,0:T(8,128)S(1)}, f32[24,128]{1,0:T(8,128)S(1)}, u32[]{:S(2)}, u32[]{:S(2)}) collective-permute-start(f32[24,128]{1,0:T(8,128)S(1)} %add.6), channel_id=1, source_target_pairs={{0,3},{1,2},{2,1},{3,0},{4,7},{5,6},{6,5},{7,4},{8,11},{9,10},{10,... | collective-permute-start | bytes 36872 | tf_op jit(solution)/shard_map/ppermute | solution.py:60
  20.4 1.5 %collective-permute-done.6 = f32[24,128]{1,0:T(8,128)S(1)} collective-permute-done((f32[24,128]{1,0:T(8,128)S(1)}, f32[24,128]{1,0:T(8,128)S(1)}, u32[]{:S(2)}, u32[]{:S(2)}) %collective-permute-start.6) | collective-permute-done | bytes 12320 | tf_op jit(solution)/shard_map/ppermute | solution.py:60
  21.9 0.8 %collective-permute-start.7 = (f32[24,128]{1,0:T(8,128)S(1)}, f32[24,128]{1,0:T(8,128)S(1)}, u32[]{:S(2)}, u32[]{:S(2)}) collective-permute-start(f32[24,128]{1,0:T(8,128)S(1)} %add.7.refs_0_), channel_id=1, source_target_pairs={{0,5},{1,4},{4,9},{5,8},{8,13},{9,12},{12,1},{13,0},{2,7},{3,6},{6... | collective-permute-start | bytes 36872 | tf_op jit(solution)/shard_map/ppermute | solution.py:60
  22.8 2.2 %collective-permute-start.8 = (f32[24,128]{1,0:T(8,128)S(1)}, f32[24,128]{1,0:T(8,128)S(1)}, u32[]{:S(2)}, u32[]{:S(2)}) collective-permute-start(f32[24,128]{1,0:T(8,128)S(1)} %add.7.refs_0_), channel_id=1, source_target_pairs={{0,9},{1,8},{4,13},{5,12},{8,1},{9,0},{12,5},{13,4},{2,11},{3,10},... | collective-permute-start | bytes 36872 | tf_op jit(solution)/shard_map/ppermute | solution.py:60
  25.0 0.5 %collective-permute-start.9 = (f32[24,128]{1,0:T(8,128)S(1)}, f32[24,128]{1,0:T(8,128)S(1)}, u32[]{:S(2)}, u32[]{:S(2)}) collective-permute-start(f32[24,128]{1,0:T(8,128)S(1)} %add.7.refs_0_), channel_id=1, source_target_pairs={{0,13},{1,12},{4,1},{5,0},{8,5},{9,4},{12,9},{13,8},{2,15},{3,14},... | collective-permute-start | bytes 36872 | tf_op jit(solution)/shard_map/ppermute | solution.py:60
  25.5 1.4 %collective-permute-done.7.refs_1_ = f32[24,128]{1,0:T(8,128)S(1)} collective-permute-done((f32[24,128]{1,0:T(8,128)S(1)}, f32[24,128]{1,0:T(8,128)S(1)}, u32[]{:S(2)}, u32[]{:S(2)}) %collective-permute-start.7) | collective-permute-done | bytes 12320 | tf_op jit(solution)/shard_map/ppermute | solution.py:60
  26.9 0.0 collective-permute-done.8.refs_2_
  26.9 1.1 %collective-permute-done.9.refs_3_ = f32[24,128]{1,0:T(8,128)S(1)} collective-permute-done((f32[24,128]{1,0:T(8,128)S(1)}, f32[24,128]{1,0:T(8,128)S(1)}, u32[]{:S(2)}, u32[]{:S(2)}) %collective-permute-start.9) | collective-permute-done | bytes 12320 | tf_op jit(solution)/shard_map/ppermute | solution.py:60
  28.1 1.4 %haydock.1 = (f32[1,2,2,16]{3,2,1,0:T(2,128)}, f32[2,6]{1,0:T(2,128)}) custom-call(f32[24,128]{1,0:T(8,128)S(1)} %add.7.refs_0_, f32[24,128]{1,0:T(8,128)S(1)} %collective-permute-done.7.refs_1_, f32[24,128]{1,0:T(8,128)S(1)} %collective-permute-done.8.refs_2_, f32[24,128]{1,0:T(8,128)S(1)} %collective-permute-done.9.refs_3_), custom_call_target="tpu_custom_call" | custom-call | tf_op jit(solution)/shard_map/haydock/pallas_call | solution.py:452
  (3 shorter events, 0.0 us)
Async XLA Ops:
  1.7 8.6 %collective-permute-start = (bf16[32,768]{1,0:T(8,128)(2,1)S(1)}, bf16[32,768]{1,0:T(8,128)(2,1)S(1)}, u32[]{:S(2)}, u32[]{:S(2)}) collective-permute-start(bf16[32,768]{1,0:T(8,128)(2,1)S(1)} %get-tuple-element.17), channel_id=1, source_target_pairs={{0,5},{1,4},{4,9},{5,8},{8,13},{9,12},{12,1},{13,0},{2,7},{3,6},{6... | collective-permute-start | bytes 147464 | tf_op jit(solution)/shard_map/ppermute | solution.py:60
  4.2 6.5 %collective-permute-start.1 = (bf16[32,768]{1,0:T(8,128)(2,1)S(1)}, bf16[32,768]{1,0:T(8,128)(2,1)S(1)}, u32[]{:S(2)}, u32[]{:S(2)}) collective-permute-start(bf16[32,768]{1,0:T(8,128)(2,1)S(1)} %get-tuple-element.18), channel_id=1, source_target_pairs={{0,9},{1,8},{4,13},{5,12},{8,1},{9,0},{12,5},{13,4},{2,11},{3,10},... | collective-permute-start | bytes 147464 | tf_op jit(solution)/shard_map/ppermute | solution.py:60
  7.1 4.4 %collective-permute-start.2 = (bf16[32,768]{1,0:T(8,128)(2,1)S(1)}, bf16[32,768]{1,0:T(8,128)(2,1)S(1)}, u32[]{:S(2)}, u32[]{:S(2)}) collective-permute-start(bf16[32,768]{1,0:T(8,128)(2,1)S(1)} %get-tuple-element.19), channel_id=1, source_target_pairs={{0,13},{1,12},{4,1},{5,0},{8,5},{9,4},{12,9},{13,8},{2,15},{3,14},... | collective-permute-start | bytes 147464 | tf_op jit(solution)/shard_map/ppermute | solution.py:60
  11.5 1.9 %collective-permute-start.3 = (bf16[64,768]{1,0:T(8,128)(2,1)S(1)}, bf16[64,768]{1,0:T(8,128)(2,1)S(1)}, u32[]{:S(2)}, u32[]{:S(2)}) collective-permute-start(bf16[64,768]{1,0:T(8,128)(2,1)S(1)} %get-tuple-element.21.refs_4_), channel_id=1, source_target_pairs={{0,1},{1,0},{2,3},{3,2},{4,5},{5,4},{6,7},{7,6},{8,9},{9,8},{10,11... | collective-permute-start | bytes 294920 | tf_op jit(solution)/shard_map/ppermute | solution.py:69
  11.7 4.7 %collective-permute-start.4 = (bf16[64,768]{1,0:T(8,128)(2,1)S(1)}, bf16[64,768]{1,0:T(8,128)(2,1)S(1)}, u32[]{:S(2)}, u32[]{:S(2)}) collective-permute-start(bf16[64,768]{1,0:T(8,128)(2,1)S(1)} %get-tuple-element.20.refs_3_), channel_id=1, source_target_pairs={{0,3},{1,2},{2,1},{3,0},{4,7},{5,6},{6,5},{7,4},{8,11},{9,10},{10,... | collective-permute-start | bytes 294920 | tf_op jit(solution)/shard_map/ppermute | solution.py:60
  17.6 1.2 %collective-permute-start.5 = (f32[24,128]{1,0:T(8,128)S(1)}, f32[24,128]{1,0:T(8,128)S(1)}, u32[]{:S(2)}, u32[]{:S(2)}) collective-permute-start(f32[24,128]{1,0:T(8,128)S(1)} %project_far.1), channel_id=1, source_target_pairs={{0,1},{1,0},{2,3},{3,2},{4,5},{5,4},{6,7},{7,6},{8,9},{9,8},{10,11... | collective-permute-start | bytes 36872 | tf_op jit(solution)/shard_map/ppermute | solution.py:69
  18.8 3.1 %collective-permute-start.6 = (f32[24,128]{1,0:T(8,128)S(1)}, f32[24,128]{1,0:T(8,128)S(1)}, u32[]{:S(2)}, u32[]{:S(2)}) collective-permute-start(f32[24,128]{1,0:T(8,128)S(1)} %add.6), channel_id=1, source_target_pairs={{0,3},{1,2},{2,1},{3,0},{4,7},{5,6},{6,5},{7,4},{8,11},{9,10},{10,... | collective-permute-start | bytes 36872 | tf_op jit(solution)/shard_map/ppermute | solution.py:60
  21.9 5.0 %collective-permute-start.7 = (f32[24,128]{1,0:T(8,128)S(1)}, f32[24,128]{1,0:T(8,128)S(1)}, u32[]{:S(2)}, u32[]{:S(2)}) collective-permute-start(f32[24,128]{1,0:T(8,128)S(1)} %add.7.refs_0_), channel_id=1, source_target_pairs={{0,5},{1,4},{4,9},{5,8},{8,13},{9,12},{12,1},{13,0},{2,7},{3,6},{6... | collective-permute-start | bytes 36872 | tf_op jit(solution)/shard_map/ppermute | solution.py:60
  22.8 4.2 %collective-permute-start.8 = (f32[24,128]{1,0:T(8,128)S(1)}, f32[24,128]{1,0:T(8,128)S(1)}, u32[]{:S(2)}, u32[]{:S(2)}) collective-permute-start(f32[24,128]{1,0:T(8,128)S(1)} %add.7.refs_0_), channel_id=1, source_target_pairs={{0,9},{1,8},{4,13},{5,12},{8,1},{9,0},{12,5},{13,4},{2,11},{3,10},... | collective-permute-start | bytes 36872 | tf_op jit(solution)/shard_map/ppermute | solution.py:60
  25.0 3.1 %collective-permute-start.9 = (f32[24,128]{1,0:T(8,128)S(1)}, f32[24,128]{1,0:T(8,128)S(1)}, u32[]{:S(2)}, u32[]{:S(2)}) collective-permute-start(f32[24,128]{1,0:T(8,128)S(1)} %add.7.refs_0_), channel_id=1, source_target_pairs={{0,13},{1,12},{4,1},{5,0},{8,5},{9,4},{12,9},{13,8},{2,15},{3,14},... | collective-permute-start | bytes 36872 | tf_op jit(solution)/shard_map/ppermute | solution.py:60

commit v11 on v10

--- a/solution.py
+++ b/solution.py
@@ -264,66 +264,31 @@
     )(*blocks, after)
 
 
-def screened_block(screening, valence, pairs, place):
+def with_turned(valence, pairs):
     wide = valence[...].astype(jnp.float32)
     parts = []
     for at in range(0, wide.shape[0], 2 * pairs):
         parts += [-wide[at + pairs : at + 2 * pairs], wide[at : at + pairs]]
-    turned = jnp.concatenate(parts, 0)
-    real = jnp.concatenate([wide, turned], 0).astype(jnp.bfloat16)
-    imag = jnp.concatenate([turned, -wide], 0).astype(jnp.bfloat16)
-    width = wide.shape[1]
-    columns = pl.ds(pl.multiple_of(place * width, 128), width)
-    form = (((1,), (1,)), ((), ()))
-    return lax.dot_general(
-        screening[0, :, columns], real, form, preferred_element_type=jnp.float32
-    ) + lax.dot_general(screening[1, :, columns], imag, form, preferred_element_type=jnp.float32)
-
-
-def project_kernel(ka, ba, far, dims, *refs):
+    return wide, jnp.concatenate(parts, 0)
+
+
+def columns_of(place, width):
+    return pl.ds(pl.multiple_of(place * width, 128), width)
+
+
+def placed_piece(kernel, table, dims, ba):
     vloc, val_count, cond_count, npol = dims
-    screening, table, held = refs[:3]
-    val_in, cond_in, out = refs[3 : -1 - ba], refs[-1 - ba : -1], refs[-1]
-    ga = lax.axis_size("ga")
-    mine = lax.axis_index("ga")
     half = lax.axis_index("ba")
-    pairs = vloc * val_count
-    block = 2 * pairs
-    rows = ka * block
     codes = val_count * cond_count
-    lanes = 2 * ka * codes
+    lanes = table.shape[1] // val_count
     share = cond_count // ba
     cond_rows = cond_count * cond_count
-    share_rows = share * cond_count
-
-    fields = None
-    for r, valence in enumerate(val_in, far):
-        term = screened_block(screening, valence, pairs, origin(mine, r, ga))
-        fields = term if fields is None else fields + term
-    both = jnp.concatenate(split(fields), 1)
-    cond_all = jnp.concatenate([ref[...] for ref in cond_in], 0)
-    crossed = jnp.dot(cond_all, both, preferred_element_type=jnp.float32)
-    crossed = crossed[:, : 2 * rows] + crossed[:, 2 * rows :]
-    lane = iota((share_rows, 2 * rows), 1)
-    lane_j = lane % rows // block
-    turned_lane = lane // rows
-    kernel = []
-    for h in range(ba):
-        total = jnp.zeros((share_rows, 2 * rows), jnp.float32)
-        for j in range(ka):
-            base = (h * ka + j) * 2 * share_rows
-            real = crossed[base : base + share_rows]
-            imag = crossed[base + share_rows : base + 2 * share_rows]
-            value = jnp.where(turned_lane == 0, real, -imag)
-            total = jnp.where(lane_j == j, value, total)
-        kernel.append(total)
-    kernel = jnp.concatenate(kernel, 0)
-
     spread = jnp.dot(
         jnp.concatenate(split(kernel), 0), table[...], preferred_element_type=jnp.float32
     )
     spread = spread[:cond_rows] + spread[cond_rows:]
     crow = iota((cond_rows, lanes), 0)
+    share_rows = share * cond_count
     c_of_row = origin(half, crow // share_rows, ba) * share + crow % share_rows // cond_count
     same_c = c_of_row == iota((cond_rows, lanes), 1) % cond_count
     spread = jnp.concatenate(
@@ -340,18 +305,56 @@
     )
     fold = jnp.where(fold, 1.0, 0.0).astype(jnp.bfloat16)
     piece = jnp.dot(fold, jnp.concatenate(split(spread), 1), preferred_element_type=jnp.float32)
-    piece = piece[:, :lanes] + piece[:, lanes:]
-    out[:codes, :] = piece + held[:codes, :] if far else piece
-    out[codes:, :] = held[codes:, :] if far else held[...]
-
-
-def project(ka, ba, far, dims, screening, table, base, val_in, cond_all):
+    return piece[:, :lanes] + piece[:, lanes:]
+
+
+def diagonal(crossed, ka, ba, share_rows, sign):
+    rows = crossed.shape[1] // 2
+    lane = iota((share_rows, 2 * rows), 1)
+    lane_j = lane % rows // (rows // ka)
+    straight = lane < rows
+    kernel = []
+    for h in range(ba):
+        total = jnp.zeros((share_rows, 2 * rows), jnp.float32)
+        for j in range(ka):
+            at = (h * ka + j) * 2 * share_rows
+            real = crossed[at : at + share_rows]
+            imag = crossed[at + share_rows : at + 2 * share_rows]
+            total = jnp.where(lane_j == j, jnp.where(straight, real, sign * imag), total)
+        kernel.append(total)
+    return jnp.concatenate(kernel, 0)
+
+
+def near_kernel(ka, ba, dims, *refs):
+    vloc, val_count, cond_count, npol = dims
+    screening, table, extras, valence = refs[:4]
+    cond_in, out = refs[4 : 4 + ba], refs[-1]
+    codes = val_count * cond_count
+    columns = columns_of(lax.axis_index("ga"), valence.shape[1])
+    wide, turned = with_turned(valence, vloc * val_count)
+    real = jnp.concatenate([wide, turned], 0).astype(jnp.bfloat16)
+    imag = jnp.concatenate([turned, -wide], 0).astype(jnp.bfloat16)
+    form = (((1,), (1,)), ((), ()))
+    fields = lax.dot_general(
+        screening[0, :, columns], real, form, preferred_element_type=jnp.float32
+    ) + lax.dot_general(screening[1, :, columns], imag, form, preferred_element_type=jnp.float32)
+    both = jnp.concatenate(split(fields), 1)
+    cond = jnp.concatenate([ref[...] for ref in cond_in], 0)
+    crossed = jnp.dot(cond, both, preferred_element_type=jnp.float32)
+    half = crossed.shape[1] // 2
+    crossed = crossed[:, :half] + crossed[:, half:]
+    kernel = diagonal(crossed, ka, ba, cond_count // ba * cond_count, -1.0)
+    out[:codes, :] = placed_piece(kernel, table, dims, ba)
+    out[codes:, :] = extras[...]
+
+
+def near(ka, ba, dims, screening, table, extras, valence, cond_all):
     vloc, val_count, cond_count, npol = dims
     codes = val_count * cond_count
-    operands = [screening, table, base, *val_in, *cond_all]
-    rows, width = val_in[0].shape
+    operands = [screening, table, extras, valence, *cond_all]
+    rows, width = valence.shape
     return pl.pallas_call(
-        functools.partial(project_kernel, ka, ba, far, dims),
+        functools.partial(near_kernel, ka, ba, dims),
         out_shape=in_vmem((codes + EXTRA_ROWS, 2 * ka * codes), jnp.float32),
         in_specs=[vmem] * len(operands),
         out_specs=vmem,
@@ -359,7 +362,78 @@
             flops=8 * screening.shape[1] * width * rows, bytes_accessed=screening.size, transcendentals=0
         ),
         compiler_params=limits(*operands),
-        name="project_far" if far else "project_near",
+        name="near",
+    )(*operands)
+
+
+def couple_kernel(ka, ga, ba, share_rows, screening, *refs):
+    cond_in, outs = refs[:ba], refs[ba:]
+    mine = lax.axis_index("ga")
+    wide = jnp.concatenate([ref[...].astype(jnp.float32) for ref in cond_in], 0)
+    straight, turned = [], []
+    for at in range(0, wide.shape[0], 2 * share_rows):
+        real, imag = wide[at : at + share_rows], wide[at + share_rows : at + 2 * share_rows]
+        straight += [real, -imag]
+        turned += [imag, real]
+    straight = jnp.concatenate(straight, 0).astype(jnp.bfloat16)
+    turned = jnp.concatenate(turned, 0).astype(jnp.bfloat16)
+    width = screening.shape[2] // ga
+    for r in range(1, ga):
+        columns = columns_of(origin(mine, r, ga), width)
+        coupled = jnp.dot(
+            straight, screening[0, :, columns], preferred_element_type=jnp.float32
+        ) + jnp.dot(turned, screening[1, :, columns], preferred_element_type=jnp.float32)
+        high, low = split(coupled)
+        outs[r - 1][: coupled.shape[0], :] = high
+        outs[r - 1][coupled.shape[0] :, :] = low
+
+
+def couple(ka, ga, ba, dims, screening, cond_all):
+    share_rows = dims[2] // ba * dims[2]
+    rows = 2 * sum(x.shape[0] for x in cond_all)
+    width = screening.shape[2] // ga
+    operands = [screening, *cond_all]
+    return pl.pallas_call(
+        functools.partial(couple_kernel, ka, ga, ba, share_rows),
+        out_shape=[in_vmem((rows, width), jnp.bfloat16)] * (ga - 1),
+        in_specs=[vmem] * len(operands),
+        out_specs=[vmem] * (ga - 1),
+        cost_estimate=pl.CostEstimate(
+            flops=2 * screening.size * rows, bytes_accessed=screening.size, transcendentals=0
+        ),
+        compiler_params=limits(*operands),
+        name="couple",
+    )(*operands)
+
+
+def far_kernel(ka, ba, dims, *refs):
+    vloc, val_count, cond_count, npol = dims
+    table, held, out = refs[0], refs[1], refs[-1]
+    count = (len(refs) - 3) // 2
+    codes = val_count * cond_count
+    crossed = None
+    for coupled, valence in zip(refs[2 : 2 + count], refs[2 + count : -1]):
+        rows = jnp.concatenate(with_turned(valence, vloc * val_count), 0).astype(jnp.bfloat16)
+        term = lax.dot_general(
+            coupled[...], rows, (((1,), (1,)), ((), ())), preferred_element_type=jnp.float32
+        )
+        crossed = term if crossed is None else crossed + term
+    half = crossed.shape[0] // 2
+    crossed = crossed[:half] + crossed[half:]
+    kernel = diagonal(crossed, ka, ba, cond_count // ba * cond_count, 1.0)
+    out[:codes, :] = held[:codes, :] + placed_piece(kernel, table, dims, ba)
+    out[codes:, :] = held[codes:, :]
+
+
+def far(ka, ba, dims, table, held, coupled, val_far):
+    operands = [table, held, *coupled, *val_far]
+    return pl.pallas_call(
+        functools.partial(far_kernel, ka, ba, dims),
+        out_shape=in_vmem(held.shape, jnp.float32),
+        in_specs=[vmem] * len(operands),
+        out_specs=vmem,
+        compiler_params=limits(*operands),
+        name="far",
     )(*operands)
 
 
@@ -511,9 +585,10 @@
     val_all, cond_half = regroup(ka, 2 * pairs, blocks, extras)
     val_far = [shifted(val_all, "ga", r) for r in range(1, ga)]
     cond_all = [cond_half] + [handed(cond_half, r) for r in range(1, ba)]
-    piece = project(ka, ba, 0, dims, whole, near_table, extras, [val_all], cond_all)
+    piece = near(ka, ba, dims, whole, near_table, extras, val_all, cond_all)
     if val_far:
-        piece = project(ka, ba, 1, dims, whole, far_table, piece, val_far, cond_all)
+        coupled = couple(ka, ga, ba, dims, whole, cond_all)
+        piece = far(ka, ba, dims, far_table, piece, coupled, val_far)
     piece = piece + sum(handed(piece, r) for r in range(1, ba))
     piece = summed(piece, "ga")
     pieces = [piece] + [shifted(piece, "ka", j) for j in range(1, ka)]

time: 29.7 us -> 30.4 us (1.024)
  waiting for transfers between devices: 7.93 us -> 9.36 us
  starting transfers between devices: 13.5 us -> 12.9 us
    ppermute x8, waiting for transfers between devices: 7.04 us -> 8.47 us  [exchanged(): return lax.ppermute(value, (axis, 'ba'), pairs)]
    ppermute x8, starting transfers between devices: 13 us -> 12.4 us  [exchanged(): return lax.ppermute(value, (axis, 'ba'), pairs)]
    pallas_call x2 -> x3, Pallas kernels: 2.51 us -> 2.3 us  [the longest x1 1.26 us: near(): pl.pallas_call(functools.partial(near_kernel, ka, ba, dims), out_shape=in...]
  transfers between devices with their start and end apart: 10 -> 10, of which waited for: 7 -> 8; matrix products, arithmetic and copies ran while one was open for 0% -> 0% of each run, Pallas kernels for 13% -> 14%
where the time goes in v11:
time: 30.4 us; the launch traced here: 30.2 us
  starting transfers between devices  12.9 us (42%)
  waiting for transfers between devices  9.36 us (31%)
  Pallas kernels  7.22 us (24%)
  between operations  0.68 us (2%)
    ppermute x8, starting transfers between devices, exchanged(): return lax.ppermute(value, (axis, 'ba'), pairs)  12.4 us
    ppermute x8, waiting for transfers between devices, exchanged(): return lax.ppermute(value, (axis, 'ba'), pairs)  8.47 us
    pallas_call x1, Pallas kernels, prepare(): pl.pallas_call(functools.partial(prepare_kernel, ka, dims), out_shape=[in...  2.45 us
    pallas_call x1, Pallas kernels, haydock(): pl.pallas_call(functools.partial(haydock_kernel, ka, codes, scale_count,...  1.41 us
    pallas_call x1, Pallas kernels, near(): pl.pallas_call(functools.partial(near_kernel, ka, ba, dims), out_shape=in...  1.26 us
    pallas_call x1, Pallas kernels, pack(): pl.pallas_call(functools.partial(pack_kernel, ka), out_shape=[shape] * ka...  1.05 us
    ppermute x2, waiting for transfers between devices, handed(): lax.ppermute(value, 'ba', [(h, (h + step) % size) for h in range(size)])  0.88 us
  transfers between devices with their start and end apart: 10, of which 8 were waited for; matrix products, arithmetic and copies ran while one was open for 0% of the time, Pallas kernels for 14%

profile of v11, /device:TPU:0, one launch (start us, length us, event | category | flops | bytes accessed | tf_op | source)
XLA Modules:
  0.0 30.2 jit_solution(6822819331489983997)
XLA Ops:
  0.6 1.0 %pack.1 = (bf16[32,768]{1,0:T(8,128)(2,1)S(1)}, bf16[32,768]{1,0:T(8,128)(2,1)S(1)}, bf16[32,768]{1,0:T(8,128)(2,1)S(1)}, bf16[32,768]{1,0:T(8,128)(2,1)S(1)}) custom-call(s32[4,4]{1,0:T(4,128)} %refs_0_.1, s32[4]{0:T(128)} %refs_1_.1, bf16[1,4,2,2,4,768]{5,4,3,2,1,0:T(4,128)(2,1)} %valence_in.1, bf16[1,4,2,4,4,768]{5,4,3,2,1,0:T(4,128)(2,1)} %conduction_in.1), custom_call_target="tpu_custom_call" | custom-call | tf_op jit(solution)/shard_map/pack/pallas_call | solution.py:114
  1.7 2.5 %collective-permute-start = (bf16[32,768]{1,0:T(8,128)(2,1)S(1)}, bf16[32,768]{1,0:T(8,128)(2,1)S(1)}, u32[]{:S(2)}, u32[]{:S(2)}) collective-permute-start(bf16[32,768]{1,0:T(8,128)(2,1)S(1)} %get-tuple-element.17), channel_id=1, source_target_pairs={{0,5},{1,4},{4,9},{5,8},{8,13},{9,12},{12,1},{13,0},{2,7},{3,6},{6... | collective-permute-start | bytes 147464 | tf_op jit(solution)/shard_map/ppermute | solution.py:60
  4.2 2.9 %collective-permute-start.1 = (bf16[32,768]{1,0:T(8,128)(2,1)S(1)}, bf16[32,768]{1,0:T(8,128)(2,1)S(1)}, u32[]{:S(2)}, u32[]{:S(2)}) collective-permute-start(bf16[32,768]{1,0:T(8,128)(2,1)S(1)} %get-tuple-element.18), channel_id=1, source_target_pairs={{0,9},{1,8},{4,13},{5,12},{8,1},{9,0},{12,5},{13,4},{2,11},{3,10},... | collective-permute-start | bytes 147464 | tf_op jit(solution)/shard_map/ppermute | solution.py:60
  7.1 0.8 %collective-permute-start.2 = (bf16[32,768]{1,0:T(8,128)(2,1)S(1)}, bf16[32,768]{1,0:T(8,128)(2,1)S(1)}, u32[]{:S(2)}, u32[]{:S(2)}) collective-permute-start(bf16[32,768]{1,0:T(8,128)(2,1)S(1)} %get-tuple-element.19), channel_id=1, source_target_pairs={{0,13},{1,12},{4,1},{5,0},{8,5},{9,4},{12,9},{13,8},{2,15},{3,14},... | collective-permute-start | bytes 147464 | tf_op jit(solution)/shard_map/ppermute | solution.py:60
  7.9 2.5 %prepare.1 = (bf16[2,768,1536]{2,1,0:T(8,128)(2,1)S(1)}, bf16[128,512]{1,0:T(8,128)(2,1)S(1)}, bf16[128,512]{1,0:T(8,128)(2,1)S(1)}, f32[8,128]{1,0:T(8,128)S(1)}) custom-call(s32[4,4]{1,0:T(4,128)} %refs_0_.1, s32[4]{0:T(128)} %refs_1_.1, s32[16]{0:T(128)} %refs_2_.1, f32[1,4]{1,0:T(1,128)} %refs_3_.1, f32[1,4]{1,0:T(1,128)} %refs_4_.1, ...), custom_call_target="tpu_custom_call" | custom-call | bytes 9437184 | tf_op jit(solution)/shard_map/prepare/pallas_call | solution.py:222
  10.3 0.0 collective-permute-done.refs_1_
  10.3 0.3 %collective-permute-done.1.refs_2_ = bf16[32,768]{1,0:T(8,128)(2,1)S(1)} collective-permute-done((bf16[32,768]{1,0:T(8,128)(2,1)S(1)}, bf16[32,768]{1,0:T(8,128)(2,1)S(1)}, u32[]{:S(2)}, u32[]{:S(2)}) %collective-permute-start.1) | collective-permute-done | bytes 49184 | tf_op jit(solution)/shard_map/ppermute | solution.py:60
  10.7 0.9 %collective-permute-done.2.refs_3_ = bf16[32,768]{1,0:T(8,128)(2,1)S(1)} collective-permute-done((bf16[32,768]{1,0:T(8,128)(2,1)S(1)}, bf16[32,768]{1,0:T(8,128)(2,1)S(1)}, u32[]{:S(2)}, u32[]{:S(2)}) %collective-permute-start.2) | collective-permute-done | bytes 49184 | tf_op jit(solution)/shard_map/ppermute | solution.py:60
  11.5 0.2 collective-permute-start.3
  11.7 1.7 %collective-permute-start.4 = (bf16[64,768]{1,0:T(8,128)(2,1)S(1)}, bf16[64,768]{1,0:T(8,128)(2,1)S(1)}, u32[]{:S(2)}, u32[]{:S(2)}) collective-permute-start(bf16[64,768]{1,0:T(8,128)(2,1)S(1)} %get-tuple-element.20.refs_3_), channel_id=1, source_target_pairs={{0,3},{1,2},{2,1},{3,0},{4,7},{5,6},{6,5},{7,4},{8,11},{9,10},{10,... | collective-permute-start | bytes 294920 | tf_op jit(solution)/shard_map/ppermute | solution.py:60
  13.4 0.0 collective-permute-done.3.refs_5_.refs_1_
  13.4 1.3 %near.1.refs_1_ = f32[24,128]{1,0:T(8,128)S(1)} custom-call(bf16[2,768,1536]{2,1,0:T(8,128)(2,1)S(1)} %get-tuple-element.14.refs_0_.screening, bf16[128,512]{1,0:T(8,128)(2,1)S(1)} %get-tuple-element.15.refs_1_, f32[8,128]{1,0:T(8,128)S(1)} %get-tuple-element.16.refs_4_.refs_2_, bf16[64,768]{1,0:T(8,128)(2,1)S(1)} %get-tuple-element.20.refs_3_, ...), custom_call_target="tpu_custom_call" | custom-call | flops 301989888 | bytes 2359296 | tf_op jit(solution)/shard_map/near/pallas_call | solution.py:356
  14.6 0.5 %couple.1.refs_2_ = bf16[256,768]{1,0:T(8,128)(2,1)S(1)} custom-call(bf16[2,768,1536]{2,1,0:T(8,128)(2,1)S(1)} %get-tuple-element.14.refs_0_.screening, bf16[64,768]{1,0:T(8,128)(2,1)S(1)} %get-tuple-element.21.refs_4_.refs_0_, bf16[64,768]{1,0:T(8,128)(2,1)S(1)} %collective-permute-done.3.refs_5_.refs_1_), custom_call_target="tpu_custom_call" | custom-call | flops 1207959552 | bytes 2359296 | tf_op jit(solution)/shard_map/couple/pallas_call | solution.py:396
  15.2 1.2 %collective-permute-done.4.refs_3_ = bf16[64,768]{1,0:T(8,128)(2,1)S(1)} collective-permute-done((bf16[64,768]{1,0:T(8,128)(2,1)S(1)}, bf16[64,768]{1,0:T(8,128)(2,1)S(1)}, u32[]{:S(2)}, u32[]{:S(2)}) %collective-permute-start.4) | collective-permute-done | bytes 98336 | tf_op jit(solution)/shard_map/ppermute | solution.py:60
  16.4 0.5 %far.1 = f32[24,128]{1,0:T(8,128)S(1)} custom-call(bf16[128,512]{1,0:T(8,128)(2,1)S(1)} %get-tuple-element.13.refs_0_, f32[24,128]{1,0:T(8,128)S(1)} %near.1.refs_1_, bf16[256,768]{1,0:T(8,128)(2,1)S(1)} %couple.1.refs_2_, bf16[64,768]{1,0:T(8,128)(2,1)S(1)} %collective-permute-done.4.refs_3_), custom_call_target="tpu_custom_call" | custom-call | tf_op jit(solution)/shard_map/far/pallas_call | solution.py:430
  16.9 0.3 %collective-permute-start.5 = (f32[24,128]{1,0:T(8,128)S(1)}, f32[24,128]{1,0:T(8,128)S(1)}, u32[]{:S(2)}, u32[]{:S(2)}) collective-permute-start(f32[24,128]{1,0:T(8,128)S(1)} %far.1), channel_id=1, source_target_pairs={{0,1},{1,0},{2,3},{3,2},{4,5},{5,4},{6,7},{7,6},{8,9},{9,8},{10,11... | collective-permute-start | bytes 36872 | tf_op jit(solution)/shard_map/ppermute | solution.py:69
  17.2 0.9 %collective-permute-done.5 = f32[24,128]{1,0:T(8,128)S(1)} collective-permute-done((f32[24,128]{1,0:T(8,128)S(1)}, f32[24,128]{1,0:T(8,128)S(1)}, u32[]{:S(2)}, u32[]{:S(2)}) %collective-permute-start.5) | collective-permute-done | bytes 12320 | tf_op jit(solution)/shard_map/ppermute | solution.py:69
  18.1 1.6 %collective-permute-start.6 = (f32[24,128]{1,0:T(8,128)S(1)}, f32[24,128]{1,0:T(8,128)S(1)}, u32[]{:S(2)}, u32[]{:S(2)}) collective-permute-start(f32[24,128]{1,0:T(8,128)S(1)} %add.6), channel_id=1, source_target_pairs={{0,3},{1,2},{2,1},{3,0},{4,7},{5,6},{6,5},{7,4},{8,11},{9,10},{10,... | collective-permute-start | bytes 36872 | tf_op jit(solution)/shard_map/ppermute | solution.py:60
  19.7 1.5 %collective-permute-done.6 = f32[24,128]{1,0:T(8,128)S(1)} collective-permute-done((f32[24,128]{1,0:T(8,128)S(1)}, f32[24,128]{1,0:T(8,128)S(1)}, u32[]{:S(2)}, u32[]{:S(2)}) %collective-permute-start.6) | collective-permute-done | bytes 12320 | tf_op jit(solution)/shard_map/ppermute | solution.py:60
  21.2 2.6 %collective-permute-start.9 = (f32[24,128]{1,0:T(8,128)S(1)}, f32[24,128]{1,0:T(8,128)S(1)}, u32[]{:S(2)}, u32[]{:S(2)}) collective-permute-start(f32[24,128]{1,0:T(8,128)S(1)} %add.7.refs_0_), channel_id=1, source_target_pairs={{0,13},{1,12},{4,1},{5,0},{8,5},{9,4},{12,9},{13,8},{2,15},{3,14},... | collective-permute-start | bytes 36872 | tf_op jit(solution)/shard_map/ppermute | solution.py:60
  23.9 0.0 collective-permute-start.8
  23.9 0.4 %collective-permute-start.7 = (f32[24,128]{1,0:T(8,128)S(1)}, f32[24,128]{1,0:T(8,128)S(1)}, u32[]{:S(2)}, u32[]{:S(2)}) collective-permute-start(f32[24,128]{1,0:T(8,128)S(1)} %add.7.refs_0_), channel_id=1, source_target_pairs={{0,5},{1,4},{4,9},{5,8},{8,13},{9,12},{12,1},{13,0},{2,7},{3,6},{6... | collective-permute-start | bytes 36872 | tf_op jit(solution)/shard_map/ppermute | solution.py:60
  24.2 1.0 %collective-permute-done.9.refs_3_ = f32[24,128]{1,0:T(8,128)S(1)} collective-permute-done((f32[24,128]{1,0:T(8,128)S(1)}, f32[24,128]{1,0:T(8,128)S(1)}, u32[]{:S(2)}, u32[]{:S(2)}) %collective-permute-start.9) | collective-permute-done | bytes 12320 | tf_op jit(solution)/shard_map/ppermute | solution.py:60
  25.3 2.6 %collective-permute-done.8.refs_2_ = f32[24,128]{1,0:T(8,128)S(1)} collective-permute-done((f32[24,128]{1,0:T(8,128)S(1)}, f32[24,128]{1,0:T(8,128)S(1)}, u32[]{:S(2)}, u32[]{:S(2)}) %collective-permute-start.8) | collective-permute-done | bytes 12320 | tf_op jit(solution)/shard_map/ppermute | solution.py:60
  27.9 0.9 %collective-permute-done.7.refs_1_ = f32[24,128]{1,0:T(8,128)S(1)} collective-permute-done((f32[24,128]{1,0:T(8,128)S(1)}, f32[24,128]{1,0:T(8,128)S(1)}, u32[]{:S(2)}, u32[]{:S(2)}) %collective-permute-start.7) | collective-permute-done | bytes 12320 | tf_op jit(solution)/shard_map/ppermute | solution.py:60
  28.8 1.4 %haydock.1 = (f32[1,2,2,16]{3,2,1,0:T(2,128)}, f32[2,6]{1,0:T(2,128)}) custom-call(f32[24,128]{1,0:T(8,128)S(1)} %add.7.refs_0_, f32[24,128]{1,0:T(8,128)S(1)} %collective-permute-done.7.refs_1_, f32[24,128]{1,0:T(8,128)S(1)} %collective-permute-done.8.refs_2_, f32[24,128]{1,0:T(8,128)S(1)} %collective-permute-done.9.refs_3_), custom_call_target="tpu_custom_call" | custom-call | tf_op jit(solution)/shard_map/haydock/pallas_call | solution.py:526
  (3 shorter events, 0.0 us)
Async XLA Ops:
  1.7 8.6 %collective-permute-start = (bf16[32,768]{1,0:T(8,128)(2,1)S(1)}, bf16[32,768]{1,0:T(8,128)(2,1)S(1)}, u32[]{:S(2)}, u32[]{:S(2)}) collective-permute-start(bf16[32,768]{1,0:T(8,128)(2,1)S(1)} %get-tuple-element.17), channel_id=1, source_target_pairs={{0,5},{1,4},{4,9},{5,8},{8,13},{9,12},{12,1},{13,0},{2,7},{3,6},{6... | collective-permute-start | bytes 147464 | tf_op jit(solution)/shard_map/ppermute | solution.py:60
  4.2 6.5 %collective-permute-start.1 = (bf16[32,768]{1,0:T(8,128)(2,1)S(1)}, bf16[32,768]{1,0:T(8,128)(2,1)S(1)}, u32[]{:S(2)}, u32[]{:S(2)}) collective-permute-start(bf16[32,768]{1,0:T(8,128)(2,1)S(1)} %get-tuple-element.18), channel_id=1, source_target_pairs={{0,9},{1,8},{4,13},{5,12},{8,1},{9,0},{12,5},{13,4},{2,11},{3,10},... | collective-permute-start | bytes 147464 | tf_op jit(solution)/shard_map/ppermute | solution.py:60
  7.1 4.4 %collective-permute-start.2 = (bf16[32,768]{1,0:T(8,128)(2,1)S(1)}, bf16[32,768]{1,0:T(8,128)(2,1)S(1)}, u32[]{:S(2)}, u32[]{:S(2)}) collective-permute-start(bf16[32,768]{1,0:T(8,128)(2,1)S(1)} %get-tuple-element.19), channel_id=1, source_target_pairs={{0,13},{1,12},{4,1},{5,0},{8,5},{9,4},{12,9},{13,8},{2,15},{3,14},... | collective-permute-start | bytes 147464 | tf_op jit(solution)/shard_map/ppermute | solution.py:60
  11.5 1.9 %collective-permute-start.3 = (bf16[64,768]{1,0:T(8,128)(2,1)S(1)}, bf16[64,768]{1,0:T(8,128)(2,1)S(1)}, u32[]{:S(2)}, u32[]{:S(2)}) collective-permute-start(bf16[64,768]{1,0:T(8,128)(2,1)S(1)} %get-tuple-element.21.refs_4_.refs_0_), channel_id=1, source_target_pairs={{0,1},{1,0},{2,3},{3,2},{4,5},{5,4},{6,7},{7,6},{8,9},{9,8},{10,11... | collective-permute-start | bytes 294920 | tf_op jit(solution)/shard_map/ppermute | solution.py:69
  11.7 4.7 %collective-permute-start.4 = (bf16[64,768]{1,0:T(8,128)(2,1)S(1)}, bf16[64,768]{1,0:T(8,128)(2,1)S(1)}, u32[]{:S(2)}, u32[]{:S(2)}) collective-permute-start(bf16[64,768]{1,0:T(8,128)(2,1)S(1)} %get-tuple-element.20.refs_3_), channel_id=1, source_target_pairs={{0,3},{1,2},{2,1},{3,0},{4,7},{5,6},{6,5},{7,4},{8,11},{9,10},{10,... | collective-permute-start | bytes 294920 | tf_op jit(solution)/shard_map/ppermute | solution.py:60
  16.9 1.2 %collective-permute-start.5 = (f32[24,128]{1,0:T(8,128)S(1)}, f32[24,128]{1,0:T(8,128)S(1)}, u32[]{:S(2)}, u32[]{:S(2)}) collective-permute-start(f32[24,128]{1,0:T(8,128)S(1)} %far.1), channel_id=1, source_target_pairs={{0,1},{1,0},{2,3},{3,2},{4,5},{5,4},{6,7},{7,6},{8,9},{9,8},{10,11... | collective-permute-start | bytes 36872 | tf_op jit(solution)/shard_map/ppermute | solution.py:69
  18.1 3.1 %collective-permute-start.6 = (f32[24,128]{1,0:T(8,128)S(1)}, f32[24,128]{1,0:T(8,128)S(1)}, u32[]{:S(2)}, u32[]{:S(2)}) collective-permute-start(f32[24,128]{1,0:T(8,128)S(1)} %add.6), channel_id=1, source_target_pairs={{0,3},{1,2},{2,1},{3,0},{4,7},{5,6},{6,5},{7,4},{8,11},{9,10},{10,... | collective-permute-start | bytes 36872 | tf_op jit(solution)/shard_map/ppermute | solution.py:60
  21.2 4.0 %collective-permute-start.9 = (f32[24,128]{1,0:T(8,128)S(1)}, f32[24,128]{1,0:T(8,128)S(1)}, u32[]{:S(2)}, u32[]{:S(2)}) collective-permute-start(f32[24,128]{1,0:T(8,128)S(1)} %add.7.refs_0_), channel_id=1, source_target_pairs={{0,13},{1,12},{4,1},{5,0},{8,5},{9,4},{12,9},{13,8},{2,15},{3,14},... | collective-permute-start | bytes 36872 | tf_op jit(solution)/shard_map/ppermute | solution.py:60
  23.9 4.0 %collective-permute-start.8 = (f32[24,128]{1,0:T(8,128)S(1)}, f32[24,128]{1,0:T(8,128)S(1)}, u32[]{:S(2)}, u32[]{:S(2)}) collective-permute-start(f32[24,128]{1,0:T(8,128)S(1)} %add.7.refs_0_), channel_id=1, source_target_pairs={{0,9},{1,8},{4,13},{5,12},{8,1},{9,0},{12,5},{13,4},{2,11},{3,10},... | collective-permute-start | bytes 36872 | tf_op jit(solution)/shard_map/ppermute | solution.py:60
  23.9 4.9 %collective-permute-start.7 = (f32[24,128]{1,0:T(8,128)S(1)}, f32[24,128]{1,0:T(8,128)S(1)}, u32[]{:S(2)}, u32[]{:S(2)}) collective-permute-start(f32[24,128]{1,0:T(8,128)S(1)} %add.7.refs_0_), channel_id=1, source_target_pairs={{0,5},{1,4},{4,9},{5,8},{8,13},{9,12},{12,1},{13,0},{2,7},{3,6},{6... | collective-permute-start | bytes 36872 | tf_op jit(solution)/shard_map/ppermute | solution.py:60

commit v12 on v11

--- a/solution.py
+++ b/solution.py
@@ -243,29 +243,42 @@
     )(*[placed(x, pltpu.HBM) for x in operands], after)
 
 
-def regroup_kernel(ka, val_rows, *refs):
-    blocks, (val_all, cond_half) = refs[:ka], refs[-2:]
-    cond_rows = blocks[0].shape[0] - val_rows
-    for j in range(ka):
-        val_all[j * val_rows : (j + 1) * val_rows, :] = blocks[j][:val_rows, :]
-        cond_half[j * cond_rows : (j + 1) * cond_rows, :] = blocks[j][val_rows:, :]
-
-
-def regroup(ka, val_rows, blocks, after):
-    rows, width = blocks[0].shape
-    kind = blocks[0].dtype
-    return pl.pallas_call(
-        functools.partial(regroup_kernel, ka, val_rows),
-        out_shape=[in_vmem((ka * val_rows, width), kind), in_vmem((ka * (rows - val_rows), width), kind)],
-        in_specs=[vmem] * ka + [anywhere],
-        out_specs=[vmem] * 2,
+def hold_kernel(value, token, out):
+    out[...] = value[...]
+
+
+def hold(value, token):
+    return pl.pallas_call(
+        hold_kernel,
+        out_shape=in_vmem(value.shape, value.dtype),
+        in_specs=[vmem, anywhere],
+        out_specs=vmem,
+        compiler_params=limits(value),
+        name="hold",
+    )(value, token)
+
+
+def regroup_kernel(count, first, last, *refs):
+    blocks, out = refs[:count], refs[-1]
+    rows = last - first
+    for at in range(count):
+        out[at * rows : (at + 1) * rows, :] = blocks[at][first:last, :]
+
+
+def regroup(blocks, first, last, after=()):
+    shape = (len(blocks) * (last - first), blocks[0].shape[1])
+    return pl.pallas_call(
+        functools.partial(regroup_kernel, len(blocks), first, last),
+        out_shape=in_vmem(shape, blocks[0].dtype),
+        in_specs=[vmem] * len(blocks) + [anywhere] * len(after),
+        out_specs=vmem,
         compiler_params=limits(*blocks),
         name="regroup",
-    )(*blocks, after)
-
-
-def with_turned(valence, pairs):
-    wide = valence[...].astype(jnp.float32)
+    )(*blocks, *after)
+
+
+def with_turned(halves, pairs):
+    wide = jnp.concatenate([half[...].astype(jnp.float32) for half in halves], 0)
     parts = []
     for at in range(0, wide.shape[0], 2 * pairs):
         parts += [-wide[at + pairs : at + 2 * pairs], wide[at : at + pairs]]
@@ -327,11 +340,11 @@
 
 def near_kernel(ka, ba, dims, *refs):
     vloc, val_count, cond_count, npol = dims
-    screening, table, extras, valence = refs[:4]
-    cond_in, out = refs[4 : 4 + ba], refs[-1]
+    screening, table, extras = refs[:3]
+    halves, cond_in, out = refs[3 : -1 - ba], refs[-1 - ba : -1], refs[-1]
     codes = val_count * cond_count
-    columns = columns_of(lax.axis_index("ga"), valence.shape[1])
-    wide, turned = with_turned(valence, vloc * val_count)
+    columns = columns_of(lax.axis_index("ga"), halves[0].shape[1])
+    wide, turned = with_turned(halves, vloc * val_count)
     real = jnp.concatenate([wide, turned], 0).astype(jnp.bfloat16)
     imag = jnp.concatenate([turned, -wide], 0).astype(jnp.bfloat16)
     form = (((1,), (1,)), ((), ()))
@@ -348,11 +361,11 @@
     out[codes:, :] = extras[...]
 
 
-def near(ka, ba, dims, screening, table, extras, valence, cond_all):
+def near(ka, ba, dims, screening, table, extras, halves, cond_all):
     vloc, val_count, cond_count, npol = dims
     codes = val_count * cond_count
-    operands = [screening, table, extras, valence, *cond_all]
-    rows, width = valence.shape
+    operands = [screening, table, extras, *halves, *cond_all]
+    rows, width = sum(half.shape[0] for half in halves), halves[0].shape[1]
     return pl.pallas_call(
         functools.partial(near_kernel, ka, ba, dims),
         out_shape=in_vmem((codes + EXTRA_ROWS, 2 * ka * codes), jnp.float32),
@@ -409,11 +422,14 @@
 def far_kernel(ka, ba, dims, *refs):
     vloc, val_count, cond_count, npol = dims
     table, held, out = refs[0], refs[1], refs[-1]
-    count = (len(refs) - 3) // 2
+    count = lax.axis_size("ga") - 1
+    each = (len(refs) - 3 - count) // count
     codes = val_count * cond_count
     crossed = None
-    for coupled, valence in zip(refs[2 : 2 + count], refs[2 + count : -1]):
-        rows = jnp.concatenate(with_turned(valence, vloc * val_count), 0).astype(jnp.bfloat16)
+    for r in range(count):
+        coupled = refs[2 + r]
+        halves = refs[2 + count + r * each : 2 + count + (r + 1) * each]
+        rows = jnp.concatenate(with_turned(halves, vloc * val_count), 0).astype(jnp.bfloat16)
         term = lax.dot_general(
             coupled[...], rows, (((1,), (1,)), ((), ())), preferred_element_type=jnp.float32
         )
@@ -570,6 +586,9 @@
     dims = (vloc, val_count, cond_count, npol)
     packed = pack(ka, ba, qpoint_map, slot_owner, valence_density, conduction_density)
     blocks = [packed[0]] + [shifted(packed[j], "ka", j) for j in range(1, ka)]
+    early = ka // 2
+    val_early = regroup(blocks[:early], 0, 2 * pairs)
+    far_early = [shifted(val_early, "ga", r) for r in range(1, ga)]
     whole, near_table, far_table, extras = prepare(
         ka,
         dims,
@@ -580,18 +599,23 @@
         conduction_energy,
         start_vector,
         screening,
-        packed[0],
+        val_early,
     )
-    val_all, cond_half = regroup(ka, 2 * pairs, blocks, extras)
-    val_far = [shifted(val_all, "ga", r) for r in range(1, ga)]
+    val_late = regroup(blocks[early:], 0, 2 * pairs, (extras,))
+    far_late = [shifted(val_late, "ga", r) for r in range(1, ga)]
+    cond_half = regroup(blocks, 2 * pairs, blocks[0].shape[0], (val_late, *far_early))
     cond_all = [cond_half] + [handed(cond_half, r) for r in range(1, ba)]
-    piece = near(ka, ba, dims, whole, near_table, extras, val_all, cond_all)
-    if val_far:
+    piece = near(ka, ba, dims, whole, near_table, extras, [val_early, val_late], cond_all)
+    if ga > 1:
         coupled = couple(ka, ga, ba, dims, whole, cond_all)
+        val_far = [half for both in zip(far_early, far_late) for half in both]
         piece = far(ka, ba, dims, far_table, piece, coupled, val_far)
     piece = piece + sum(handed(piece, r) for r in range(1, ba))
     piece = summed(piece, "ga")
-    pieces = [piece] + [shifted(piece, "ka", j) for j in range(1, ka)]
+    pieces, token = [piece], piece
+    for j in range(1, ka):
+        pieces.append(shifted(token, "ka", j))
+        token = hold(piece, token)
     scale_count = float(kcount * pair_count)
     return tuple(haydock(ka, pair_count, scale_count, npol, pieces))
 

time: 30.4 us -> 29.9 us (0.984)
  waiting for transfers between devices: 9.36 us -> 8.28 us
  starting transfers between devices: 12.9 us -> 13.6 us
    ppermute x8 -> x9, waiting for transfers between devices: 8.47 us -> 7.23 us  [exchanged(): return lax.ppermute(value, (axis, 'ba'), pairs)]
    ppermute x8 -> x9, starting transfers between devices: 12.4 us -> 13 us  [exchanged(): return lax.ppermute(value, (axis, 'ba'), pairs)]
  transfers between devices with their start and end apart: 10 -> 11, of which waited for: 8 -> 7; matrix products, arithmetic and copies ran while one was open for 0% -> 0% of each run, Pallas kernels for 14% -> 14%
where the time goes in v12:
time: 29.9 us; the launch traced here: 29.8 us
  starting transfers between devices  13.6 us (45%)
  waiting for transfers between devices  8.28 us (28%)
  Pallas kernels  7.22 us (24%)
  between operations  0.71 us (2%)
    ppermute x9, starting transfers between devices, exchanged(): return lax.ppermute(value, (axis, 'ba'), pairs)  13 us
    ppermute x9, waiting for transfers between devices, exchanged(): return lax.ppermute(value, (axis, 'ba'), pairs)  7.23 us
    pallas_call x1, Pallas kernels, prepare(): pl.pallas_call(functools.partial(prepare_kernel, ka, dims), out_shape=[in...  2.45 us
    pallas_call x1, Pallas kernels, haydock(): pl.pallas_call(functools.partial(haydock_kernel, ka, codes, scale_count,...  1.41 us
    pallas_call x1, Pallas kernels, near(): pl.pallas_call(functools.partial(near_kernel, ka, ba, dims), out_shape=in...  1.26 us
    ppermute x2, waiting for transfers between devices, handed(): lax.ppermute(value, 'ba', [(h, (h + step) % size) for h in range(size)])  1.06 us
    pallas_call x1, Pallas kernels, pack(): pl.pallas_call(functools.partial(pack_kernel, ka), out_shape=[shape] * ka...  1.05 us
  transfers between devices with their start and end apart: 11, of which 7 were waited for; matrix products, arithmetic and copies ran while one was open for 0% of the time, Pallas kernels for 14%

profile of v12, /device:TPU:0, one launch (start us, length us, event | category | flops | bytes accessed | tf_op | source)
XLA Modules:
  0.0 29.8 jit_solution(3434125262395271661)
XLA Ops:
  0.6 1.0 %pack.1 = (bf16[32,768]{1,0:T(8,128)(2,1)S(1)}, bf16[32,768]{1,0:T(8,128)(2,1)S(1)}, bf16[32,768]{1,0:T(8,128)(2,1)S(1)}, bf16[32,768]{1,0:T(8,128)(2,1)S(1)}) custom-call(s32[4,4]{1,0:T(4,128)} %refs_0_.1, s32[4]{0:T(128)} %refs_1_.1, bf16[1,4,2,2,4,768]{5,4,3,2,1,0:T(4,128)(2,1)} %valence_in.1, bf16[1,4,2,4,4,768]{5,4,3,2,1,0:T(4,128)(2,1)} %conduction_in.1), custom_call_target="tpu_custom_call" | custom-call | tf_op jit(solution)/shard_map/pack/pallas_call | solution.py:114
  1.7 2.5 %collective-permute-start = (bf16[32,768]{1,0:T(8,128)(2,1)S(1)}, bf16[32,768]{1,0:T(8,128)(2,1)S(1)}, u32[]{:S(2)}, u32[]{:S(2)}) collective-permute-start(bf16[32,768]{1,0:T(8,128)(2,1)S(1)} %get-tuple-element.11), channel_id=1, source_target_pairs={{0,5},{1,4},{4,9},{5,8},{8,13},{9,12},{12,1},{13,0},{2,7},{3,6},{6... | collective-permute-start | bytes 147464 | tf_op jit(solution)/shard_map/ppermute | solution.py:60
  4.2 2.9 %collective-permute-start.1 = (bf16[32,768]{1,0:T(8,128)(2,1)S(1)}, bf16[32,768]{1,0:T(8,128)(2,1)S(1)}, u32[]{:S(2)}, u32[]{:S(2)}) collective-permute-start(bf16[32,768]{1,0:T(8,128)(2,1)S(1)} %get-tuple-element.16), channel_id=1, source_target_pairs={{0,9},{1,8},{4,13},{5,12},{8,1},{9,0},{12,5},{13,4},{2,11},{3,10},... | collective-permute-start | bytes 147464 | tf_op jit(solution)/shard_map/ppermute | solution.py:60
  7.1 0.8 %collective-permute-start.2 = (bf16[32,768]{1,0:T(8,128)(2,1)S(1)}, bf16[32,768]{1,0:T(8,128)(2,1)S(1)}, u32[]{:S(2)}, u32[]{:S(2)}) collective-permute-start(bf16[32,768]{1,0:T(8,128)(2,1)S(1)} %get-tuple-element.17), channel_id=1, source_target_pairs={{0,13},{1,12},{4,1},{5,0},{8,5},{9,4},{12,9},{13,8},{2,15},{3,14},... | collective-permute-start | bytes 147464 | tf_op jit(solution)/shard_map/ppermute | solution.py:60
  7.9 0.1 collective-permute-done.refs_1_
  8.0 2.0 %collective-permute-start.3 = (bf16[32,768]{1,0:T(8,128)(2,1)S(1)}, bf16[32,768]{1,0:T(8,128)(2,1)S(1)}, u32[]{:S(2)}, u32[]{:S(2)}) collective-permute-start(bf16[32,768]{1,0:T(8,128)(2,1)S(1)} %regroup.3.refs_7_.refs_3_), channel_id=1, source_target_pairs={{0,3},{1,2},{2,1},{3,0},{4,7},{5,6},{6,5},{7,4},{8,11},{9,10},{10,... | collective-permute-start | bytes 147464 | tf_op jit(solution)/shard_map/ppermute | solution.py:60
  10.0 2.5 %prepare.1 = (bf16[2,768,1536]{2,1,0:T(8,128)(2,1)S(1)}, bf16[128,512]{1,0:T(8,128)(2,1)S(1)}, bf16[128,512]{1,0:T(8,128)(2,1)S(1)}, f32[8,128]{1,0:T(8,128)S(1)}) custom-call(s32[4,4]{1,0:T(4,128)} %refs_0_.1, s32[4]{0:T(128)} %refs_1_.1, s32[16]{0:T(128)} %refs_2_.1, f32[1,4]{1,0:T(1,128)} %refs_3_.1, f32[1,4]{1,0:T(1,128)} %refs_4_.1, ...), custom_call_target="tpu_custom_call" | custom-call | bytes 9437184 | tf_op jit(solution)/shard_map/prepare/pallas_call | solution.py:222
  12.5 0.0 collective-permute-done.1.refs_0_.refs_2_
  12.5 0.0 collective-permute-done.2.refs_1_.refs_3_
  12.5 0.0 collective-permute-done.3.refs_5_.refs_3_
  12.5 0.5 %collective-permute-start.4 = (bf16[64,768]{1,0:T(8,128)(2,1)S(1)}, bf16[64,768]{1,0:T(8,128)(2,1)S(1)}, u32[]{:S(2)}, u32[]{:S(2)}) collective-permute-start(bf16[64,768]{1,0:T(8,128)(2,1)S(1)} %regroup.5.refs_5_.refs_0_), channel_id=1, source_target_pairs={{0,1},{1,0},{2,3},{3,2},{4,5},{5,4},{6,7},{7,6},{8,9},{9,8},{10,11... | collective-permute-start | bytes 294920 | tf_op jit(solution)/shard_map/ppermute | solution.py:69
  13.0 1.2 %collective-permute-start.5 = (bf16[32,768]{1,0:T(8,128)(2,1)S(1)}, bf16[32,768]{1,0:T(8,128)(2,1)S(1)}, u32[]{:S(2)}, u32[]{:S(2)}) collective-permute-start(bf16[32,768]{1,0:T(8,128)(2,1)S(1)} %regroup.4.refs_4_), channel_id=1, source_target_pairs={{0,3},{1,2},{2,1},{3,0},{4,7},{5,6},{6,5},{7,4},{8,11},{9,10},{10,... | collective-permute-start | bytes 147464 | tf_op jit(solution)/shard_map/ppermute | solution.py:60
  14.2 0.0 collective-permute-done.4.refs_6_.refs_1_
  14.2 0.5 %couple.1.refs_2_ = bf16[256,768]{1,0:T(8,128)(2,1)S(1)} custom-call(bf16[2,768,1536]{2,1,0:T(8,128)(2,1)S(1)} %get-tuple-element.13.refs_0_.screening, bf16[64,768]{1,0:T(8,128)(2,1)S(1)} %regroup.5.refs_5_.refs_0_, bf16[64,768]{1,0:T(8,128)(2,1)S(1)} %collective-permute-done.4.refs_6_.refs_1_), custom_call_target="tpu_custom_call" | custom-call | flops 1207959552 | bytes 2359296 | tf_op jit(solution)/shard_map/couple/pallas_call | solution.py:409
  14.7 1.3 %near.1.refs_1_ = f32[24,128]{1,0:T(8,128)S(1)} custom-call(bf16[2,768,1536]{2,1,0:T(8,128)(2,1)S(1)} %get-tuple-element.13.refs_0_.screening, bf16[128,512]{1,0:T(8,128)(2,1)S(1)} %get-tuple-element.14.refs_1_, f32[8,128]{1,0:T(8,128)S(1)} %get-tuple-element.15.refs_2_, bf16[32,768]{1,0:T(8,128)(2,1)S(1)} %regroup.3.refs_7_.refs_3_, ...), custom_call_target="tpu_custom_call" | custom-call | flops 301989888 | bytes 2359296 | tf_op jit(solution)/shard_map/near/pallas_call | solution.py:369
  16.0 0.8 %collective-permute-done.5.refs_4_ = bf16[32,768]{1,0:T(8,128)(2,1)S(1)} collective-permute-done((bf16[32,768]{1,0:T(8,128)(2,1)S(1)}, bf16[32,768]{1,0:T(8,128)(2,1)S(1)}, u32[]{:S(2)}, u32[]{:S(2)}) %collective-permute-start.5) | collective-permute-done | bytes 49184 | tf_op jit(solution)/shard_map/ppermute | solution.py:60
  16.7 0.5 %far.1 = f32[24,128]{1,0:T(8,128)S(1)} custom-call(bf16[128,512]{1,0:T(8,128)(2,1)S(1)} %get-tuple-element.12.refs_0_, f32[24,128]{1,0:T(8,128)S(1)} %near.1.refs_1_, bf16[256,768]{1,0:T(8,128)(2,1)S(1)} %couple.1.refs_2_, bf16[32,768]{1,0:T(8,128)(2,1)S(1)} %collective-permute-done.3.refs_5_.refs_3_, bf16[32,768]{1,0:T(8,128)(2,1)S(1)} %collective-permute-done.5.refs_4_), custom_call_target="tpu_custom_call" | custom-call | tf_op jit(solution)/shard_map/far/pallas_call | solution.py:446
  17.3 0.1 collective-permute-start.6
  17.4 1.1 %collective-permute-done.6 = f32[24,128]{1,0:T(8,128)S(1)} collective-permute-done((f32[24,128]{1,0:T(8,128)S(1)}, f32[24,128]{1,0:T(8,128)S(1)}, u32[]{:S(2)}, u32[]{:S(2)}) %collective-permute-start.6) | collective-permute-done | bytes 12320 | tf_op jit(solution)/shard_map/ppermute | solution.py:69
  18.5 1.0 %collective-permute-start.7 = (f32[24,128]{1,0:T(8,128)S(1)}, f32[24,128]{1,0:T(8,128)S(1)}, u32[]{:S(2)}, u32[]{:S(2)}) collective-permute-start(f32[24,128]{1,0:T(8,128)S(1)} %add.6), channel_id=1, source_target_pairs={{0,3},{1,2},{2,1},{3,0},{4,7},{5,6},{6,5},{7,4},{8,11},{9,10},{10,... | collective-permute-start | bytes 36872 | tf_op jit(solution)/shard_map/ppermute | solution.py:60
  19.5 2.1 %collective-permute-done.7 = f32[24,128]{1,0:T(8,128)S(1)} collective-permute-done((f32[24,128]{1,0:T(8,128)S(1)}, f32[24,128]{1,0:T(8,128)S(1)}, u32[]{:S(2)}, u32[]{:S(2)}) %collective-permute-start.7) | collective-permute-done | bytes 12320 | tf_op jit(solution)/shard_map/ppermute | solution.py:60
  21.6 1.8 %collective-permute-start.10 = (f32[24,128]{1,0:T(8,128)S(1)}, f32[24,128]{1,0:T(8,128)S(1)}, u32[]{:S(2)}, u32[]{:S(2)}) collective-permute-start(f32[24,128]{1,0:T(8,128)S(1)} %hold.3), channel_id=1, source_target_pairs={{0,13},{1,12},{4,1},{5,0},{8,5},{9,4},{12,9},{13,8},{2,15},{3,14},... | collective-permute-start | bytes 36872 | tf_op jit(solution)/shard_map/ppermute | solution.py:60
  23.4 0.0 collective-permute-start.9
  23.4 0.7 %collective-permute-start.8 = (f32[24,128]{1,0:T(8,128)S(1)}, f32[24,128]{1,0:T(8,128)S(1)}, u32[]{:S(2)}, u32[]{:S(2)}) collective-permute-start(f32[24,128]{1,0:T(8,128)S(1)} %add.7.value.token.refs_0_), channel_id=1, source_target_pairs={{0,5},{1,4},{4,9},{5,8},{8,13},{9,12},{12,1},{13,0},{2,7},{3,6},{6... | collective-permute-start | bytes 36872 | tf_op jit(solution)/shard_map/ppermute | solution.py:60
  24.2 0.7 %collective-permute-done.10.refs_3_ = f32[24,128]{1,0:T(8,128)S(1)} collective-permute-done((f32[24,128]{1,0:T(8,128)S(1)}, f32[24,128]{1,0:T(8,128)S(1)}, u32[]{:S(2)}, u32[]{:S(2)}) %collective-permute-start.10) | collective-permute-done | bytes 12320 | tf_op jit(solution)/shard_map/ppermute | solution.py:60
  24.8 2.7 %collective-permute-done.9.refs_2_ = f32[24,128]{1,0:T(8,128)S(1)} collective-permute-done((f32[24,128]{1,0:T(8,128)S(1)}, f32[24,128]{1,0:T(8,128)S(1)}, u32[]{:S(2)}, u32[]{:S(2)}) %collective-permute-start.9) | collective-permute-done | bytes 12320 | tf_op jit(solution)/shard_map/ppermute | solution.py:60
  27.6 0.8 %collective-permute-done.8.refs_1_ = f32[24,128]{1,0:T(8,128)S(1)} collective-permute-done((f32[24,128]{1,0:T(8,128)S(1)}, f32[24,128]{1,0:T(8,128)S(1)}, u32[]{:S(2)}, u32[]{:S(2)}) %collective-permute-start.8) | collective-permute-done | bytes 12320 | tf_op jit(solution)/shard_map/ppermute | solution.py:60
  28.4 1.4 %haydock.1 = (f32[1,2,2,16]{3,2,1,0:T(2,128)}, f32[2,6]{1,0:T(2,128)}) custom-call(f32[24,128]{1,0:T(8,128)S(1)} %add.7.value.token.refs_0_, f32[24,128]{1,0:T(8,128)S(1)} %collective-permute-done.8.refs_1_, f32[24,128]{1,0:T(8,128)S(1)} %collective-permute-done.9.refs_2_, f32[24,128]{1,0:T(8,128)S(1)} %collective-permute-done.10.refs_3_), custom_call_target="tpu_custom_call" | custom-call | tf_op jit(solution)/shard_map/haydock/pallas_call | solution.py:542
  (7 shorter events, 0.0 us)
Async XLA Ops:
  1.7 6.3 %collective-permute-start = (bf16[32,768]{1,0:T(8,128)(2,1)S(1)}, bf16[32,768]{1,0:T(8,128)(2,1)S(1)}, u32[]{:S(2)}, u32[]{:S(2)}) collective-permute-start(bf16[32,768]{1,0:T(8,128)(2,1)S(1)} %get-tuple-element.11), channel_id=1, source_target_pairs={{0,5},{1,4},{4,9},{5,8},{8,13},{9,12},{12,1},{13,0},{2,7},{3,6},{6... | collective-permute-start | bytes 147464 | tf_op jit(solution)/shard_map/ppermute | solution.py:60
  4.2 8.3 %collective-permute-start.1 = (bf16[32,768]{1,0:T(8,128)(2,1)S(1)}, bf16[32,768]{1,0:T(8,128)(2,1)S(1)}, u32[]{:S(2)}, u32[]{:S(2)}) collective-permute-start(bf16[32,768]{1,0:T(8,128)(2,1)S(1)} %get-tuple-element.16), channel_id=1, source_target_pairs={{0,9},{1,8},{4,13},{5,12},{8,1},{9,0},{12,5},{13,4},{2,11},{3,10},... | collective-permute-start | bytes 147464 | tf_op jit(solution)/shard_map/ppermute | solution.py:60
  7.1 5.4 %collective-permute-start.2 = (bf16[32,768]{1,0:T(8,128)(2,1)S(1)}, bf16[32,768]{1,0:T(8,128)(2,1)S(1)}, u32[]{:S(2)}, u32[]{:S(2)}) collective-permute-start(bf16[32,768]{1,0:T(8,128)(2,1)S(1)} %get-tuple-element.17), channel_id=1, source_target_pairs={{0,13},{1,12},{4,1},{5,0},{8,5},{9,4},{12,9},{13,8},{2,15},{3,14},... | collective-permute-start | bytes 147464 | tf_op jit(solution)/shard_map/ppermute | solution.py:60
  8.0 4.5 %collective-permute-start.3 = (bf16[32,768]{1,0:T(8,128)(2,1)S(1)}, bf16[32,768]{1,0:T(8,128)(2,1)S(1)}, u32[]{:S(2)}, u32[]{:S(2)}) collective-permute-start(bf16[32,768]{1,0:T(8,128)(2,1)S(1)} %regroup.3.refs_7_.refs_3_), channel_id=1, source_target_pairs={{0,3},{1,2},{2,1},{3,0},{4,7},{5,6},{6,5},{7,4},{8,11},{9,10},{10,... | collective-permute-start | bytes 147464 | tf_op jit(solution)/shard_map/ppermute | solution.py:60
  12.5 1.7 %collective-permute-start.4 = (bf16[64,768]{1,0:T(8,128)(2,1)S(1)}, bf16[64,768]{1,0:T(8,128)(2,1)S(1)}, u32[]{:S(2)}, u32[]{:S(2)}) collective-permute-start(bf16[64,768]{1,0:T(8,128)(2,1)S(1)} %regroup.5.refs_5_.refs_0_), channel_id=1, source_target_pairs={{0,1},{1,0},{2,3},{3,2},{4,5},{5,4},{6,7},{7,6},{8,9},{9,8},{10,11... | collective-permute-start | bytes 294920 | tf_op jit(solution)/shard_map/ppermute | solution.py:69
  13.0 3.7 %collective-permute-start.5 = (bf16[32,768]{1,0:T(8,128)(2,1)S(1)}, bf16[32,768]{1,0:T(8,128)(2,1)S(1)}, u32[]{:S(2)}, u32[]{:S(2)}) collective-permute-start(bf16[32,768]{1,0:T(8,128)(2,1)S(1)} %regroup.4.refs_4_), channel_id=1, source_target_pairs={{0,3},{1,2},{2,1},{3,0},{4,7},{5,6},{6,5},{7,4},{8,11},{9,10},{10,... | collective-permute-start | bytes 147464 | tf_op jit(solution)/shard_map/ppermute | solution.py:60
  17.3 1.2 %collective-permute-start.6 = (f32[24,128]{1,0:T(8,128)S(1)}, f32[24,128]{1,0:T(8,128)S(1)}, u32[]{:S(2)}, u32[]{:S(2)}) collective-permute-start(f32[24,128]{1,0:T(8,128)S(1)} %far.1), channel_id=1, source_target_pairs={{0,1},{1,0},{2,3},{3,2},{4,5},{5,4},{6,7},{7,6},{8,9},{9,8},{10,11... | collective-permute-start | bytes 36872 | tf_op jit(solution)/shard_map/ppermute | solution.py:69
  18.5 3.1 %collective-permute-start.7 = (f32[24,128]{1,0:T(8,128)S(1)}, f32[24,128]{1,0:T(8,128)S(1)}, u32[]{:S(2)}, u32[]{:S(2)}) collective-permute-start(f32[24,128]{1,0:T(8,128)S(1)} %add.6), channel_id=1, source_target_pairs={{0,3},{1,2},{2,1},{3,0},{4,7},{5,6},{6,5},{7,4},{8,11},{9,10},{10,... | collective-permute-start | bytes 36872 | tf_op jit(solution)/shard_map/ppermute | solution.py:60
  21.6 3.2 %collective-permute-start.10 = (f32[24,128]{1,0:T(8,128)S(1)}, f32[24,128]{1,0:T(8,128)S(1)}, u32[]{:S(2)}, u32[]{:S(2)}) collective-permute-start(f32[24,128]{1,0:T(8,128)S(1)} %hold.3), channel_id=1, source_target_pairs={{0,13},{1,12},{4,1},{5,0},{8,5},{9,4},{12,9},{13,8},{2,15},{3,14},... | collective-permute-start | bytes 36872 | tf_op jit(solution)/shard_map/ppermute | solution.py:60
  23.4 4.1 %collective-permute-start.9 = (f32[24,128]{1,0:T(8,128)S(1)}, f32[24,128]{1,0:T(8,128)S(1)}, u32[]{:S(2)}, u32[]{:S(2)}) collective-permute-start(f32[24,128]{1,0:T(8,128)S(1)} %hold.2.token), channel_id=1, source_target_pairs={{0,9},{1,8},{4,13},{5,12},{8,1},{9,0},{12,5},{13,4},{2,11},{3,10},... | collective-permute-start | bytes 36872 | tf_op jit(solution)/shard_map/ppermute | solution.py:60
  23.4 4.9 %collective-permute-start.8 = (f32[24,128]{1,0:T(8,128)S(1)}, f32[24,128]{1,0:T(8,128)S(1)}, u32[]{:S(2)}, u32[]{:S(2)}) collective-permute-start(f32[24,128]{1,0:T(8,128)S(1)} %add.7.value.token.refs_0_), channel_id=1, source_target_pairs={{0,5},{1,4},{4,9},{5,8},{8,13},{9,12},{12,1},{13,0},{2,7},{3,6},{6... | collective-permute-start | bytes 36872 | tf_op jit(solution)/shard_map/ppermute | solution.py:60

commit v13 on v12

--- a/solution.py
+++ b/solution.py
@@ -16,7 +16,6 @@
 vmem = pl.BlockSpec(memory_space=pltpu.VMEM)
 anywhere = pl.BlockSpec(memory_space=pl.ANY)
 EXTRA_ROWS = 8
-CHUNKS = 4
 
 
 def in_vmem(shape, dtype):
@@ -132,7 +131,7 @@
 def prepare_kernel(ka, dims, *refs):
     vloc, val_count, cond_count, npol = dims
     ins, screening, (screen_out, near_table, far_table, extras), scratch = refs[:6], refs[6], refs[8:12], refs[12:]
-    qmap, owner, band_pairs, val_energy, cond_energy, start, sems, screen_sems = scratch
+    qmap, owner, band_pairs, val_energy, cond_energy, start, sems, screen_sem = scratch
     me = lax.axis_index("ka")
     half = lax.axis_index("ba")
     mine = lax.axis_index("ga")
@@ -142,17 +141,8 @@
             zip(ins, (qmap, owner, band_pairs, val_energy, cond_energy, start))
         )
     ]
-    height = screening.shape[2] // CHUNKS
-    chunks = [
-        pltpu.make_async_copy(
-            screening.at[0, part, pl.ds(c * height, height)],
-            screen_out.at[part, pl.ds(c * height, height)],
-            screen_sems.at[part, c],
-        )
-        for part in range(2)
-        for c in range(CHUNKS)
-    ]
-    for copy in copies + chunks:
+    load = pltpu.make_async_copy(screening.at[0, 0], screen_out, screen_sem)
+    for copy in copies + [load]:
         copy.start()
     pairs = vloc * val_count
     block = 2 * pairs
@@ -209,8 +199,7 @@
     second = jnp.where(second >= kcount, second - kcount, second).astype(jnp.float32) * first
     rest = jnp.zeros((EXTRA_ROWS - 3 - npol, lanes), jnp.float32)
     extras[...] = jnp.concatenate([vectors, energy, bands * first, second, rest], 0)
-    for copy in chunks:
-        copy.wait()
+    load.wait()
 
 
 def prepare(ka, dims, qmap, owner, band_pairs, val_energy, cond_energy, start, screening, after):
@@ -222,7 +211,7 @@
     return pl.pallas_call(
         functools.partial(prepare_kernel, ka, dims),
         out_shape=[
-            in_vmem(screening.shape[1:], screening.dtype),
+            in_vmem(screening.shape[2:], screening.dtype),
             in_vmem(table.shape, table.dtype),
             in_vmem(table.shape, table.dtype),
             in_vmem((EXTRA_ROWS, lanes), jnp.float32),
@@ -233,29 +222,35 @@
         + [
             pltpu.VMEM(start.shape, start.dtype),
             pltpu.SemaphoreType.DMA((6,)),
-            pltpu.SemaphoreType.DMA((2, CHUNKS)),
+            pltpu.SemaphoreType.DMA,
         ],
         cost_estimate=pl.CostEstimate(
-            flops=0, bytes_accessed=4 * screening.size, transcendentals=0
+            flops=0, bytes_accessed=2 * screening.size, transcendentals=0
         ),
         compiler_params=limits(table),
         name="prepare",
     )(*[placed(x, pltpu.HBM) for x in operands], after)
 
 
-def hold_kernel(value, token, out):
-    out[...] = value[...]
-
-
-def hold(value, token):
-    return pl.pallas_call(
-        hold_kernel,
-        out_shape=in_vmem(value.shape, value.dtype),
-        in_specs=[vmem, anywhere],
+def load_kernel(screening, after, out, sem):
+    load = pltpu.make_async_copy(screening.at[0, 1], out, sem)
+    load.start()
+    load.wait()
+
+
+def load_imaginary(screening, after):
+    return pl.pallas_call(
+        load_kernel,
+        out_shape=in_vmem(screening.shape[2:], screening.dtype),
+        in_specs=[anywhere, anywhere],
         out_specs=vmem,
-        compiler_params=limits(value),
-        name="hold",
-    )(value, token)
+        scratch_shapes=[pltpu.SemaphoreType.DMA],
+        cost_estimate=pl.CostEstimate(
+            flops=0, bytes_accessed=2 * screening.size, transcendentals=0
+        ),
+        compiler_params=limits(),
+        name="load_imaginary",
+    )(placed(screening, pltpu.HBM), after)
 
 
 def regroup_kernel(count, first, last, *refs):
@@ -340,8 +335,8 @@
 
 def near_kernel(ka, ba, dims, *refs):
     vloc, val_count, cond_count, npol = dims
-    screening, table, extras = refs[:3]
-    halves, cond_in, out = refs[3 : -1 - ba], refs[-1 - ba : -1], refs[-1]
+    screen_real, screen_imag, table, extras = refs[:4]
+    halves, cond_in, out = refs[4 : -1 - ba], refs[-1 - ba : -1], refs[-1]
     codes = val_count * cond_count
     columns = columns_of(lax.axis_index("ga"), halves[0].shape[1])
     wide, turned = with_turned(halves, vloc * val_count)
@@ -349,8 +344,8 @@
     imag = jnp.concatenate([turned, -wide], 0).astype(jnp.bfloat16)
     form = (((1,), (1,)), ((), ()))
     fields = lax.dot_general(
-        screening[0, :, columns], real, form, preferred_element_type=jnp.float32
-    ) + lax.dot_general(screening[1, :, columns], imag, form, preferred_element_type=jnp.float32)
+        screen_real[:, columns], real, form, preferred_element_type=jnp.float32
+    ) + lax.dot_general(screen_imag[:, columns], imag, form, preferred_element_type=jnp.float32)
     both = jnp.concatenate(split(fields), 1)
     cond = jnp.concatenate([ref[...] for ref in cond_in], 0)
     crossed = jnp.dot(cond, both, preferred_element_type=jnp.float32)
@@ -364,7 +359,7 @@
 def near(ka, ba, dims, screening, table, extras, halves, cond_all):
     vloc, val_count, cond_count, npol = dims
     codes = val_count * cond_count
-    operands = [screening, table, extras, *halves, *cond_all]
+    operands = [*screening, table, extras, *halves, *cond_all]
     rows, width = sum(half.shape[0] for half in halves), halves[0].shape[1]
     return pl.pallas_call(
         functools.partial(near_kernel, ka, ba, dims),
@@ -372,14 +367,14 @@
         in_specs=[vmem] * len(operands),
         out_specs=vmem,
         cost_estimate=pl.CostEstimate(
-            flops=8 * screening.shape[1] * width * rows, bytes_accessed=screening.size, transcendentals=0
+            flops=8 * screening[0].shape[0] * width * rows, bytes_accessed=screening[0].size, transcendentals=0
         ),
         compiler_params=limits(*operands),
         name="near",
     )(*operands)
 
 
-def couple_kernel(ka, ga, ba, share_rows, screening, *refs):
+def couple_kernel(ka, ga, ba, share_rows, screen_real, screen_imag, *refs):
     cond_in, outs = refs[:ba], refs[ba:]
     mine = lax.axis_index("ga")
     wide = jnp.concatenate([ref[...].astype(jnp.float32) for ref in cond_in], 0)
@@ -390,12 +385,12 @@
         turned += [imag, real]
     straight = jnp.concatenate(straight, 0).astype(jnp.bfloat16)
     turned = jnp.concatenate(turned, 0).astype(jnp.bfloat16)
-    width = screening.shape[2] // ga
+    width = screen_real.shape[1] // ga
     for r in range(1, ga):
         columns = columns_of(origin(mine, r, ga), width)
         coupled = jnp.dot(
-            straight, screening[0, :, columns], preferred_element_type=jnp.float32
-        ) + jnp.dot(turned, screening[1, :, columns], preferred_element_type=jnp.float32)
+            straight, screen_real[:, columns], preferred_element_type=jnp.float32
+        ) + jnp.dot(turned, screen_imag[:, columns], preferred_element_type=jnp.float32)
         high, low = split(coupled)
         outs[r - 1][: coupled.shape[0], :] = high
         outs[r - 1][coupled.shape[0] :, :] = low
@@ -404,15 +399,15 @@
 def couple(ka, ga, ba, dims, screening, cond_all):
     share_rows = dims[2] // ba * dims[2]
     rows = 2 * sum(x.shape[0] for x in cond_all)
-    width = screening.shape[2] // ga
-    operands = [screening, *cond_all]
+    width = screening[0].shape[1] // ga
+    operands = [*screening, *cond_all]
     return pl.pallas_call(
         functools.partial(couple_kernel, ka, ga, ba, share_rows),
         out_shape=[in_vmem((rows, width), jnp.bfloat16)] * (ga - 1),
         in_specs=[vmem] * len(operands),
         out_specs=[vmem] * (ga - 1),
         cost_estimate=pl.CostEstimate(
-            flops=2 * screening.size * rows, bytes_accessed=screening.size, transcendentals=0
+            flops=4 * screening[0].size * rows, bytes_accessed=screening[0].size, transcendentals=0
         ),
         compiler_params=limits(*operands),
         name="couple",
@@ -586,10 +581,7 @@
     dims = (vloc, val_count, cond_count, npol)
     packed = pack(ka, ba, qpoint_map, slot_owner, valence_density, conduction_density)
     blocks = [packed[0]] + [shifted(packed[j], "ka", j) for j in range(1, ka)]
-    early = ka // 2
-    val_early = regroup(blocks[:early], 0, 2 * pairs)
-    far_early = [shifted(val_early, "ga", r) for r in range(1, ga)]
-    whole, near_table, far_table, extras = prepare(
+    real, near_table, far_table, extras = prepare(
         ka,
         dims,
         qpoint_map,
@@ -599,9 +591,14 @@
         conduction_energy,
         start_vector,
         screening,
-        val_early,
+        packed[0],
     )
-    val_late = regroup(blocks[early:], 0, 2 * pairs, (extras,))
+    early = ka // 2
+    val_early = regroup(blocks[:early], 0, 2 * pairs, (extras,))
+    far_early = [shifted(val_early, "ga", r) for r in range(1, ga)]
+    imag = load_imaginary(screening, val_early)
+    whole = (real, imag)
+    val_late = regroup(blocks[early:], 0, 2 * pairs, (imag,))
     far_late = [shifted(val_late, "ga", r) for r in range(1, ga)]
     cond_half = regroup(blocks, 2 * pairs, blocks[0].shape[0], (val_late, *far_early))
     cond_all = [cond_half] + [handed(cond_half, r) for r in range(1, ba)]
@@ -612,10 +609,7 @@
         piece = far(ka, ba, dims, far_table, piece, coupled, val_far)
     piece = piece + sum(handed(piece, r) for r in range(1, ba))
     piece = summed(piece, "ga")
-    pieces, token = [piece], piece
-    for j in range(1, ka):
-        pieces.append(shifted(token, "ka", j))
-        token = hold(piece, token)
+    pieces = [piece] + [shifted(piece, "ka", j) for j in reversed(range(1, ka))]
     scale_count = float(kcount * pair_count)
     return tuple(haydock(ka, pair_count, scale_count, npol, pieces))
 

time: 29.9 us -> 29.6 us (0.990)
  waiting for transfers between devices: 8.28 us -> 5.69 us
  starting transfers between devices: 13.6 us -> 14.8 us
  Pallas kernels: 7.22 us -> 8.19 us
    ppermute x9, waiting for transfers between devices: 7.23 us -> 4.63 us  [exchanged(): return lax.ppermute(value, (axis, 'ba'), pairs)]
    pallas_call x2 -> x1, Pallas kernels: 0.01 us -> 1.67 us  [load_imaginary(): pl.pallas_call(load_kernel, out_shape=in_vmem(screening.shape[2:], screen...]
    ppermute x9, starting transfers between devices: 13 us -> 14 us  [exchanged(): return lax.ppermute(value, (axis, 'ba'), pairs)]
    pallas_call x1, Pallas kernels: 2.45 us -> 1.75 us  [prepare(): pl.pallas_call(functools.partial(prepare_kernel, ka, dims), out_shape=[in...]
  transfers between devices with their start and end apart: 11 -> 11, of which waited for: 7 -> 6; matrix products, arithmetic and copies ran while one was open for 0% -> 0% of each run, Pallas kernels for 14% -> 18%
where the time goes in v13:
time: 29.6 us; the launch traced here: 29.4 us
  starting transfers between devices  14.8 us (50%)
  Pallas kernels  8.19 us (28%)
  waiting for transfers between devices  5.69 us (19%)
  between operations  0.72 us (2%)
    ppermute x9, starting transfers between devices, exchanged(): return lax.ppermute(value, (axis, 'ba'), pairs)  14 us
    ppermute x9, waiting for transfers between devices, exchanged(): return lax.ppermute(value, (axis, 'ba'), pairs)  4.63 us
    pallas_call x1, Pallas kernels, prepare(): pl.pallas_call(functools.partial(prepare_kernel, ka, dims), out_shape=[in...  1.75 us
    pallas_call x1, Pallas kernels, load_imaginary(): pl.pallas_call(load_kernel, out_shape=in_vmem(screening.shape[2:], screen...  1.67 us
    pallas_call x1, Pallas kernels, haydock(): pl.pallas_call(functools.partial(haydock_kernel, ka, codes, scale_count,...  1.41 us
    pallas_call x1, Pallas kernels, near(): pl.pallas_call(functools.partial(near_kernel, ka, ba, dims), out_shape=in...  1.26 us
    ppermute x2, waiting for transfers between devices, handed(): lax.ppermute(value, 'ba', [(h, (h + step) % size) for h in range(size)])  1.07 us
    pallas_call x1, Pallas kernels, pack(): pl.pallas_call(functools.partial(pack_kernel, ka), out_shape=[shape] * ka...  1.05 us
  transfers between devices with their start and end apart: 11, of which 6 were waited for; matrix products, arithmetic and copies ran while one was open for 0% of the time, Pallas kernels for 18%

profile of v13, /device:TPU:0, one launch (start us, length us, event | category | flops | bytes accessed | tf_op | source)
XLA Modules:
  0.0 29.4 jit_solution(10582204410365008895)
XLA Ops:
  0.6 1.0 %pack.1 = (bf16[32,768]{1,0:T(8,128)(2,1)S(1)}, bf16[32,768]{1,0:T(8,128)(2,1)S(1)}, bf16[32,768]{1,0:T(8,128)(2,1)S(1)}, bf16[32,768]{1,0:T(8,128)(2,1)S(1)}) custom-call(s32[4,4]{1,0:T(4,128)} %refs_0_.1, s32[4]{0:T(128)} %refs_1_.1, bf16[1,4,2,2,4,768]{5,4,3,2,1,0:T(4,128)(2,1)} %valence_in.1, bf16[1,4,2,4,4,768]{5,4,3,2,1,0:T(4,128)(2,1)} %conduction_in.1), custom_call_target="tpu_custom_call" | custom-call | tf_op jit(solution)/shard_map/pack/pallas_call | solution.py:113
  1.7 2.5 %collective-permute-start = (bf16[32,768]{1,0:T(8,128)(2,1)S(1)}, bf16[32,768]{1,0:T(8,128)(2,1)S(1)}, u32[]{:S(2)}, u32[]{:S(2)}) collective-permute-start(bf16[32,768]{1,0:T(8,128)(2,1)S(1)} %get-tuple-element.13), channel_id=1, source_target_pairs={{0,5},{1,4},{4,9},{5,8},{8,13},{9,12},{12,1},{13,0},{2,7},{3,6},{6... | collective-permute-start | bytes 147464 | tf_op jit(solution)/shard_map/ppermute | solution.py:59
  4.2 2.9 %collective-permute-start.1 = (bf16[32,768]{1,0:T(8,128)(2,1)S(1)}, bf16[32,768]{1,0:T(8,128)(2,1)S(1)}, u32[]{:S(2)}, u32[]{:S(2)}) collective-permute-start(bf16[32,768]{1,0:T(8,128)(2,1)S(1)} %get-tuple-element.16), channel_id=1, source_target_pairs={{0,9},{1,8},{4,13},{5,12},{8,1},{9,0},{12,5},{13,4},{2,11},{3,10},... | collective-permute-start | bytes 147464 | tf_op jit(solution)/shard_map/ppermute | solution.py:59
  7.1 0.8 %collective-permute-start.2 = (bf16[32,768]{1,0:T(8,128)(2,1)S(1)}, bf16[32,768]{1,0:T(8,128)(2,1)S(1)}, u32[]{:S(2)}, u32[]{:S(2)}) collective-permute-start(bf16[32,768]{1,0:T(8,128)(2,1)S(1)} %get-tuple-element.17), channel_id=1, source_target_pairs={{0,13},{1,12},{4,1},{5,0},{8,5},{9,4},{12,9},{13,8},{2,15},{3,14},... | collective-permute-start | bytes 147464 | tf_op jit(solution)/shard_map/ppermute | solution.py:59
  7.9 1.7 %prepare.1 = (bf16[768,1536]{1,0:T(8,128)(2,1)S(1)}, bf16[128,512]{1,0:T(8,128)(2,1)S(1)}, bf16[128,512]{1,0:T(8,128)(2,1)S(1)}, f32[8,128]{1,0:T(8,128)S(1)}) custom-call(s32[4,4]{1,0:T(4,128)} %refs_0_.1, s32[4]{0:T(128)} %refs_1_.1, s32[16]{0:T(128)} %refs_2_.1, f32[1,4]{1,0:T(1,128)} %refs_3_.1, f32[1,4]{1,0:T(1,128)} %refs_4_.1, ...), custom_call_target="tpu_custom_call" | custom-call | bytes 4718592 | tf_op jit(solution)/shard_map/prepare/pallas_call | solution.py:211
  9.6 0.0 collective-permute-done.refs_1_
  9.6 1.8 %collective-permute-start.3 = (bf16[32,768]{1,0:T(8,128)(2,1)S(1)}, bf16[32,768]{1,0:T(8,128)(2,1)S(1)}, u32[]{:S(2)}, u32[]{:S(2)}) collective-permute-start(bf16[32,768]{1,0:T(8,128)(2,1)S(1)} %regroup.3.after.refs_4_), channel_id=1, source_target_pairs={{0,3},{1,2},{2,1},{3,0},{4,7},{5,6},{6,5},{7,4},{8,11},{9,10},{10,... | collective-permute-start | bytes 147464 | tf_op jit(solution)/shard_map/ppermute | solution.py:59
  11.5 1.7 %load_imaginary.1.refs_2_.refs_1_.screen_imag = bf16[768,1536]{1,0:T(8,128)(2,1)S(1)} custom-call(bf16[1,2,768,1536]{3,2,1,0:T(8,128)(2,1)} %screening.1, bf16[32,768]{1,0:T(8,128)(2,1)S(1)} %regroup.3.after.refs_4_), custom_call_target="tpu_custom_call" | custom-call | bytes 4718592 | tf_op jit(solution)/shard_map/load_imaginary/pallas_call | solution.py:242
  13.2 0.0 collective-permute-done.1.refs_0_.refs_2_
  13.2 0.0 collective-permute-done.2.refs_1_.refs_3_
  13.2 0.1 collective-permute-done.3.refs_5_.refs_3_
  13.3 0.7 %collective-permute-start.4 = (bf16[64,768]{1,0:T(8,128)(2,1)S(1)}, bf16[64,768]{1,0:T(8,128)(2,1)S(1)}, u32[]{:S(2)}, u32[]{:S(2)}) collective-permute-start(bf16[64,768]{1,0:T(8,128)(2,1)S(1)} %regroup.5.refs_6_.refs_0_), channel_id=1, source_target_pairs={{0,1},{1,0},{2,3},{3,2},{4,5},{5,4},{6,7},{7,6},{8,9},{9,8},{10,11... | collective-permute-start | bytes 294920 | tf_op jit(solution)/shard_map/ppermute | solution.py:68
  14.0 1.2 %collective-permute-start.5 = (bf16[32,768]{1,0:T(8,128)(2,1)S(1)}, bf16[32,768]{1,0:T(8,128)(2,1)S(1)}, u32[]{:S(2)}, u32[]{:S(2)}) collective-permute-start(bf16[32,768]{1,0:T(8,128)(2,1)S(1)} %regroup.4.refs_4_.refs_5_), channel_id=1, source_target_pairs={{0,3},{1,2},{2,1},{3,0},{4,7},{5,6},{6,5},{7,4},{8,11},{9,10},{10,... | collective-permute-start | bytes 147464 | tf_op jit(solution)/shard_map/ppermute | solution.py:59
  15.1 0.0 collective-permute-done.4.refs_7_.refs_1_
  15.2 0.5 %couple.1.refs_2_ = bf16[256,768]{1,0:T(8,128)(2,1)S(1)} custom-call(bf16[768,1536]{1,0:T(8,128)(2,1)S(1)} %get-tuple-element.12.refs_0_.screen_real, bf16[768,1536]{1,0:T(8,128)(2,1)S(1)} %load_imaginary.1.refs_2_.refs_1_.screen_imag, bf16[64,768]{1,0:T(8,128)(2,1)S(1)} %regroup.5.refs_6_.refs_0_, bf16[64,768]{1,0:T(8,128)(2,1)S(1)} %collective-permute-done.4.refs_7_.refs_1_), custom_call_target="tpu_custom_call" | custom-call | flops 1207959552 | bytes 1179648 | tf_op jit(solution)/shard_map/couple/pallas_call | solution.py:404
  15.7 1.3 %near.1.refs_1_ = f32[24,128]{1,0:T(8,128)S(1)} custom-call(bf16[768,1536]{1,0:T(8,128)(2,1)S(1)} %get-tuple-element.12.refs_0_.screen_real, bf16[768,1536]{1,0:T(8,128)(2,1)S(1)} %load_imaginary.1.refs_2_.refs_1_.screen_imag, bf16[128,512]{1,0:T(8,128)(2,1)S(1)} %get-tuple-element.15.refs_2_, f32[8,128]{1,0:T(8,128)S(1)} %get-tuple-element.14.refs_2_.refs_3_, ...), custom_call_target="tpu_custom_call" | custom-call | flops 301989888 | bytes 1179648 | tf_op jit(solution)/shard_map/near/pallas_call | solution.py:364
  16.9 0.8 %collective-permute-done.5.refs_4_ = bf16[32,768]{1,0:T(8,128)(2,1)S(1)} collective-permute-done((bf16[32,768]{1,0:T(8,128)(2,1)S(1)}, bf16[32,768]{1,0:T(8,128)(2,1)S(1)}, u32[]{:S(2)}, u32[]{:S(2)}) %collective-permute-start.5) | collective-permute-done | bytes 49184 | tf_op jit(solution)/shard_map/ppermute | solution.py:59
  17.8 0.5 %far.1 = f32[24,128]{1,0:T(8,128)S(1)} custom-call(bf16[128,512]{1,0:T(8,128)(2,1)S(1)} %get-tuple-element.11.refs_0_, f32[24,128]{1,0:T(8,128)S(1)} %near.1.refs_1_, bf16[256,768]{1,0:T(8,128)(2,1)S(1)} %couple.1.refs_2_, bf16[32,768]{1,0:T(8,128)(2,1)S(1)} %collective-permute-done.3.refs_5_.refs_3_, bf16[32,768]{1,0:T(8,128)(2,1)S(1)} %collective-permute-done.5.refs_4_), custom_call_target="tpu_custom_call" | custom-call | tf_op jit(solution)/shard_map/far/pallas_call | solution.py:441
  18.3 0.1 collective-permute-start.6
  18.4 1.1 %collective-permute-done.6 = f32[24,128]{1,0:T(8,128)S(1)} collective-permute-done((f32[24,128]{1,0:T(8,128)S(1)}, f32[24,128]{1,0:T(8,128)S(1)}, u32[]{:S(2)}, u32[]{:S(2)}) %collective-permute-start.6) | collective-permute-done | bytes 12320 | tf_op jit(solution)/shard_map/ppermute | solution.py:68
  19.5 1.3 %collective-permute-start.7 = (f32[24,128]{1,0:T(8,128)S(1)}, f32[24,128]{1,0:T(8,128)S(1)}, u32[]{:S(2)}, u32[]{:S(2)}) collective-permute-start(f32[24,128]{1,0:T(8,128)S(1)} %add.6), channel_id=1, source_target_pairs={{0,3},{1,2},{2,1},{3,0},{4,7},{5,6},{6,5},{7,4},{8,11},{9,10},{10,... | collective-permute-start | bytes 36872 | tf_op jit(solution)/shard_map/ppermute | solution.py:59
  20.7 1.9 %collective-permute-done.7 = f32[24,128]{1,0:T(8,128)S(1)} collective-permute-done((f32[24,128]{1,0:T(8,128)S(1)}, f32[24,128]{1,0:T(8,128)S(1)}, u32[]{:S(2)}, u32[]{:S(2)}) %collective-permute-start.7) | collective-permute-done | bytes 12320 | tf_op jit(solution)/shard_map/ppermute | solution.py:59
  22.6 0.4 %collective-permute-start.10 = (f32[24,128]{1,0:T(8,128)S(1)}, f32[24,128]{1,0:T(8,128)S(1)}, u32[]{:S(2)}, u32[]{:S(2)}) collective-permute-start(f32[24,128]{1,0:T(8,128)S(1)} %add.7.refs_0_), channel_id=1, source_target_pairs={{0,5},{1,4},{4,9},{5,8},{8,13},{9,12},{12,1},{13,0},{2,7},{3,6},{6... | collective-permute-start | bytes 36872 | tf_op jit(solution)/shard_map/ppermute | solution.py:59
  23.1 0.4 %collective-permute-start.9 = (f32[24,128]{1,0:T(8,128)S(1)}, f32[24,128]{1,0:T(8,128)S(1)}, u32[]{:S(2)}, u32[]{:S(2)}) collective-permute-start(f32[24,128]{1,0:T(8,128)S(1)} %add.7.refs_0_), channel_id=1, source_target_pairs={{0,9},{1,8},{4,13},{5,12},{8,1},{9,0},{12,5},{13,4},{2,11},{3,10},... | collective-permute-start | bytes 36872 | tf_op jit(solution)/shard_map/ppermute | solution.py:59
  23.5 2.7 %collective-permute-start.8 = (f32[24,128]{1,0:T(8,128)S(1)}, f32[24,128]{1,0:T(8,128)S(1)}, u32[]{:S(2)}, u32[]{:S(2)}) collective-permute-start(f32[24,128]{1,0:T(8,128)S(1)} %add.7.refs_0_), channel_id=1, source_target_pairs={{0,13},{1,12},{4,1},{5,0},{8,5},{9,4},{12,9},{13,8},{2,15},{3,14},... | collective-permute-start | bytes 36872 | tf_op jit(solution)/shard_map/ppermute | solution.py:59
  26.2 1.4 %collective-permute-done.10.refs_3_ = f32[24,128]{1,0:T(8,128)S(1)} collective-permute-done((f32[24,128]{1,0:T(8,128)S(1)}, f32[24,128]{1,0:T(8,128)S(1)}, u32[]{:S(2)}, u32[]{:S(2)}) %collective-permute-start.10) | collective-permute-done | bytes 12320 | tf_op jit(solution)/shard_map/ppermute | solution.py:59
  27.5 0.0 collective-permute-done.9.refs_2_
  27.5 0.5 %collective-permute-done.8.refs_1_ = f32[24,128]{1,0:T(8,128)S(1)} collective-permute-done((f32[24,128]{1,0:T(8,128)S(1)}, f32[24,128]{1,0:T(8,128)S(1)}, u32[]{:S(2)}, u32[]{:S(2)}) %collective-permute-start.8) | collective-permute-done | bytes 12320 | tf_op jit(solution)/shard_map/ppermute | solution.py:59
  28.0 1.4 %haydock.1 = (f32[1,2,2,16]{3,2,1,0:T(2,128)}, f32[2,6]{1,0:T(2,128)}) custom-call(f32[24,128]{1,0:T(8,128)S(1)} %add.7.refs_0_, f32[24,128]{1,0:T(8,128)S(1)} %collective-permute-done.8.refs_1_, f32[24,128]{1,0:T(8,128)S(1)} %collective-permute-done.9.refs_2_, f32[24,128]{1,0:T(8,128)S(1)} %collective-permute-done.10.refs_3_), custom_call_target="tpu_custom_call" | custom-call | tf_op jit(solution)/shard_map/haydock/pallas_call | solution.py:537
  (5 shorter events, 0.0 us)
Async XLA Ops:
  1.7 7.9 %collective-permute-start = (bf16[32,768]{1,0:T(8,128)(2,1)S(1)}, bf16[32,768]{1,0:T(8,128)(2,1)S(1)}, u32[]{:S(2)}, u32[]{:S(2)}) collective-permute-start(bf16[32,768]{1,0:T(8,128)(2,1)S(1)} %get-tuple-element.13), channel_id=1, source_target_pairs={{0,5},{1,4},{4,9},{5,8},{8,13},{9,12},{12,1},{13,0},{2,7},{3,6},{6... | collective-permute-start | bytes 147464 | tf_op jit(solution)/shard_map/ppermute | solution.py:59
  4.2 9.0 %collective-permute-start.1 = (bf16[32,768]{1,0:T(8,128)(2,1)S(1)}, bf16[32,768]{1,0:T(8,128)(2,1)S(1)}, u32[]{:S(2)}, u32[]{:S(2)}) collective-permute-start(bf16[32,768]{1,0:T(8,128)(2,1)S(1)} %get-tuple-element.16), channel_id=1, source_target_pairs={{0,9},{1,8},{4,13},{5,12},{8,1},{9,0},{12,5},{13,4},{2,11},{3,10},... | collective-permute-start | bytes 147464 | tf_op jit(solution)/shard_map/ppermute | solution.py:59
  7.1 6.1 %collective-permute-start.2 = (bf16[32,768]{1,0:T(8,128)(2,1)S(1)}, bf16[32,768]{1,0:T(8,128)(2,1)S(1)}, u32[]{:S(2)}, u32[]{:S(2)}) collective-permute-start(bf16[32,768]{1,0:T(8,128)(2,1)S(1)} %get-tuple-element.17), channel_id=1, source_target_pairs={{0,13},{1,12},{4,1},{5,0},{8,5},{9,4},{12,9},{13,8},{2,15},{3,14},... | collective-permute-start | bytes 147464 | tf_op jit(solution)/shard_map/ppermute | solution.py:59
  9.6 3.6 %collective-permute-start.3 = (bf16[32,768]{1,0:T(8,128)(2,1)S(1)}, bf16[32,768]{1,0:T(8,128)(2,1)S(1)}, u32[]{:S(2)}, u32[]{:S(2)}) collective-permute-start(bf16[32,768]{1,0:T(8,128)(2,1)S(1)} %regroup.3.after.refs_4_), channel_id=1, source_target_pairs={{0,3},{1,2},{2,1},{3,0},{4,7},{5,6},{6,5},{7,4},{8,11},{9,10},{10,... | collective-permute-start | bytes 147464 | tf_op jit(solution)/shard_map/ppermute | solution.py:59
  13.3 1.9 %collective-permute-start.4 = (bf16[64,768]{1,0:T(8,128)(2,1)S(1)}, bf16[64,768]{1,0:T(8,128)(2,1)S(1)}, u32[]{:S(2)}, u32[]{:S(2)}) collective-permute-start(bf16[64,768]{1,0:T(8,128)(2,1)S(1)} %regroup.5.refs_6_.refs_0_), channel_id=1, source_target_pairs={{0,1},{1,0},{2,3},{3,2},{4,5},{5,4},{6,7},{7,6},{8,9},{9,8},{10,11... | collective-permute-start | bytes 294920 | tf_op jit(solution)/shard_map/ppermute | solution.py:68
  14.0 3.8 %collective-permute-start.5 = (bf16[32,768]{1,0:T(8,128)(2,1)S(1)}, bf16[32,768]{1,0:T(8,128)(2,1)S(1)}, u32[]{:S(2)}, u32[]{:S(2)}) collective-permute-start(bf16[32,768]{1,0:T(8,128)(2,1)S(1)} %regroup.4.refs_4_.refs_5_), channel_id=1, source_target_pairs={{0,3},{1,2},{2,1},{3,0},{4,7},{5,6},{6,5},{7,4},{8,11},{9,10},{10,... | collective-permute-start | bytes 147464 | tf_op jit(solution)/shard_map/ppermute | solution.py:59
  18.3 1.2 %collective-permute-start.6 = (f32[24,128]{1,0:T(8,128)S(1)}, f32[24,128]{1,0:T(8,128)S(1)}, u32[]{:S(2)}, u32[]{:S(2)}) collective-permute-start(f32[24,128]{1,0:T(8,128)S(1)} %far.1), channel_id=1, source_target_pairs={{0,1},{1,0},{2,3},{3,2},{4,5},{5,4},{6,7},{7,6},{8,9},{9,8},{10,11... | collective-permute-start | bytes 36872 | tf_op jit(solution)/shard_map/ppermute | solution.py:68
  19.5 3.1 %collective-permute-start.7 = (f32[24,128]{1,0:T(8,128)S(1)}, f32[24,128]{1,0:T(8,128)S(1)}, u32[]{:S(2)}, u32[]{:S(2)}) collective-permute-start(f32[24,128]{1,0:T(8,128)S(1)} %add.6), channel_id=1, source_target_pairs={{0,3},{1,2},{2,1},{3,0},{4,7},{5,6},{6,5},{7,4},{8,11},{9,10},{10,... | collective-permute-start | bytes 36872 | tf_op jit(solution)/shard_map/ppermute | solution.py:59
  22.6 4.9 %collective-permute-start.10 = (f32[24,128]{1,0:T(8,128)S(1)}, f32[24,128]{1,0:T(8,128)S(1)}, u32[]{:S(2)}, u32[]{:S(2)}) collective-permute-start(f32[24,128]{1,0:T(8,128)S(1)} %add.7.refs_0_), channel_id=1, source_target_pairs={{0,5},{1,4},{4,9},{5,8},{8,13},{9,12},{12,1},{13,0},{2,7},{3,6},{6... | collective-permute-start | bytes 36872 | tf_op jit(solution)/shard_map/ppermute | solution.py:59
  23.1 4.5 %collective-permute-start.9 = (f32[24,128]{1,0:T(8,128)S(1)}, f32[24,128]{1,0:T(8,128)S(1)}, u32[]{:S(2)}, u32[]{:S(2)}) collective-permute-start(f32[24,128]{1,0:T(8,128)S(1)} %add.7.refs_0_), channel_id=1, source_target_pairs={{0,9},{1,8},{4,13},{5,12},{8,1},{9,0},{12,5},{13,4},{2,11},{3,10},... | collective-permute-start | bytes 36872 | tf_op jit(solution)/shard_map/ppermute | solution.py:59
  23.5 4.6 %collective-permute-start.8 = (f32[24,128]{1,0:T(8,128)S(1)}, f32[24,128]{1,0:T(8,128)S(1)}, u32[]{:S(2)}, u32[]{:S(2)}) collective-permute-start(f32[24,128]{1,0:T(8,128)S(1)} %add.7.refs_0_), channel_id=1, source_target_pairs={{0,13},{1,12},{4,1},{5,0},{8,5},{9,4},{12,9},{13,8},{2,15},{3,14},... | collective-permute-start | bytes 36872 | tf_op jit(solution)/shard_map/ppermute | solution.py:59

commit v14 on v12

--- a/solution.py
+++ b/solution.py
@@ -16,6 +16,7 @@
 vmem = pl.BlockSpec(memory_space=pltpu.VMEM)
 anywhere = pl.BlockSpec(memory_space=pl.ANY)
 EXTRA_ROWS = 8
+LIGHT = pl.CostEstimate(flops=1, bytes_accessed=1, transcendentals=0)
 CHUNKS = 4
 
 
@@ -243,21 +244,6 @@
     )(*[placed(x, pltpu.HBM) for x in operands], after)
 
 
-def hold_kernel(value, token, out):
-    out[...] = value[...]
-
-
-def hold(value, token):
-    return pl.pallas_call(
-        hold_kernel,
-        out_shape=in_vmem(value.shape, value.dtype),
-        in_specs=[vmem, anywhere],
-        out_specs=vmem,
-        compiler_params=limits(value),
-        name="hold",
-    )(value, token)
-
-
 def regroup_kernel(count, first, last, *refs):
     blocks, out = refs[:count], refs[-1]
     rows = last - first
@@ -365,15 +351,12 @@
     vloc, val_count, cond_count, npol = dims
     codes = val_count * cond_count
     operands = [screening, table, extras, *halves, *cond_all]
-    rows, width = sum(half.shape[0] for half in halves), halves[0].shape[1]
     return pl.pallas_call(
         functools.partial(near_kernel, ka, ba, dims),
         out_shape=in_vmem((codes + EXTRA_ROWS, 2 * ka * codes), jnp.float32),
         in_specs=[vmem] * len(operands),
         out_specs=vmem,
-        cost_estimate=pl.CostEstimate(
-            flops=8 * screening.shape[1] * width * rows, bytes_accessed=screening.size, transcendentals=0
-        ),
+        cost_estimate=LIGHT,
         compiler_params=limits(*operands),
         name="near",
     )(*operands)
@@ -411,9 +394,7 @@
         out_shape=[in_vmem((rows, width), jnp.bfloat16)] * (ga - 1),
         in_specs=[vmem] * len(operands),
         out_specs=[vmem] * (ga - 1),
-        cost_estimate=pl.CostEstimate(
-            flops=2 * screening.size * rows, bytes_accessed=screening.size, transcendentals=0
-        ),
+        cost_estimate=LIGHT,
         compiler_params=limits(*operands),
         name="couple",
     )(*operands)
@@ -612,10 +593,7 @@
         piece = far(ka, ba, dims, far_table, piece, coupled, val_far)
     piece = piece + sum(handed(piece, r) for r in range(1, ba))
     piece = summed(piece, "ga")
-    pieces, token = [piece], piece
-    for j in range(1, ka):
-        pieces.append(shifted(token, "ka", j))
-        token = hold(piece, token)
+    pieces = [piece] + [shifted(piece, "ka", j) for j in reversed(range(1, ka))]
     scale_count = float(kcount * pair_count)
     return tuple(haydock(ka, pair_count, scale_count, npol, pieces))
 

time: 29.9 us -> 28.6 us (0.957)
  waiting for transfers between devices: 8.28 us -> 6 us
  starting transfers between devices: 13.6 us -> 14.6 us
    ppermute x9, waiting for transfers between devices: 7.23 us -> 4.95 us  [exchanged(): return lax.ppermute(value, (axis, 'ba'), pairs)]
    ppermute x9, starting transfers between devices: 13 us -> 14 us  [exchanged(): return lax.ppermute(value, (axis, 'ba'), pairs)]
  transfers between devices with their start and end apart: 11 -> 11, of which waited for: 7 -> 6; matrix products, arithmetic and copies ran while one was open for 0% -> 0% of each run, Pallas kernels for 14% -> 15%
where the time goes in v14:
time: 28.6 us; the launch traced here: 28.5 us
  starting transfers between devices  14.6 us (51%)
  Pallas kernels  7.21 us (25%)
  waiting for transfers between devices  6 us (21%)
  between operations  0.71 us (2%)
    ppermute x9, starting transfers between devices, exchanged(): return lax.ppermute(value, (axis, 'ba'), pairs)  14 us
    ppermute x9, waiting for transfers between devices, exchanged(): return lax.ppermute(value, (axis, 'ba'), pairs)  4.95 us
    pallas_call x1, Pallas kernels, prepare(): pl.pallas_call(functools.partial(prepare_kernel, ka, dims), out_shape=[in...  2.45 us
    pallas_call x1, Pallas kernels, haydock(): pl.pallas_call(functools.partial(haydock_kernel, ka, codes, scale_count,...  1.41 us
    pallas_call x1, Pallas kernels, near(): pl.pallas_call(functools.partial(near_kernel, ka, ba, dims), out_shape=in...  1.26 us
    ppermute x2, waiting for transfers between devices, handed(): lax.ppermute(value, 'ba', [(h, (h + step) % size) for h in range(size)])  1.06 us
    pallas_call x1, Pallas kernels, pack(): pl.pallas_call(functools.partial(pack_kernel, ka), out_shape=[shape] * ka...  1.05 us
    ppermute x2, starting transfers between devices, handed(): lax.ppermute(value, 'ba', [(h, (h + step) % size) for h in range(size)])  0.59 us
  transfers between devices with their start and end apart: 11, of which 6 were waited for; matrix products, arithmetic and copies ran while one was open for 0% of the time, Pallas kernels for 15%

profile of v14, /device:TPU:0, one launch (start us, length us, event | category | flops | bytes accessed | tf_op | source)
XLA Modules:
  0.0 28.5 jit_solution(13215982272860385579)
XLA Ops:
  0.6 1.0 %pack.1 = (bf16[32,768]{1,0:T(8,128)(2,1)S(1)}, bf16[32,768]{1,0:T(8,128)(2,1)S(1)}, bf16[32,768]{1,0:T(8,128)(2,1)S(1)}, bf16[32,768]{1,0:T(8,128)(2,1)S(1)}) custom-call(s32[4,4]{1,0:T(4,128)} %refs_0_.1, s32[4]{0:T(128)} %refs_1_.1, bf16[1,4,2,2,4,768]{5,4,3,2,1,0:T(4,128)(2,1)} %valence_in.1, bf16[1,4,2,4,4,768]{5,4,3,2,1,0:T(4,128)(2,1)} %conduction_in.1), custom_call_target="tpu_custom_call" | custom-call | tf_op jit(solution)/shard_map/pack/pallas_call | solution.py:115
  1.7 2.5 %collective-permute-start = (bf16[32,768]{1,0:T(8,128)(2,1)S(1)}, bf16[32,768]{1,0:T(8,128)(2,1)S(1)}, u32[]{:S(2)}, u32[]{:S(2)}) collective-permute-start(bf16[32,768]{1,0:T(8,128)(2,1)S(1)} %get-tuple-element.11), channel_id=1, source_target_pairs={{0,5},{1,4},{4,9},{5,8},{8,13},{9,12},{12,1},{13,0},{2,7},{3,6},{6... | collective-permute-start | bytes 147464 | tf_op jit(solution)/shard_map/ppermute | solution.py:61
  4.2 2.9 %collective-permute-start.1 = (bf16[32,768]{1,0:T(8,128)(2,1)S(1)}, bf16[32,768]{1,0:T(8,128)(2,1)S(1)}, u32[]{:S(2)}, u32[]{:S(2)}) collective-permute-start(bf16[32,768]{1,0:T(8,128)(2,1)S(1)} %get-tuple-element.16), channel_id=1, source_target_pairs={{0,9},{1,8},{4,13},{5,12},{8,1},{9,0},{12,5},{13,4},{2,11},{3,10},... | collective-permute-start | bytes 147464 | tf_op jit(solution)/shard_map/ppermute | solution.py:61
  7.1 0.8 %collective-permute-start.2 = (bf16[32,768]{1,0:T(8,128)(2,1)S(1)}, bf16[32,768]{1,0:T(8,128)(2,1)S(1)}, u32[]{:S(2)}, u32[]{:S(2)}) collective-permute-start(bf16[32,768]{1,0:T(8,128)(2,1)S(1)} %get-tuple-element.17), channel_id=1, source_target_pairs={{0,13},{1,12},{4,1},{5,0},{8,5},{9,4},{12,9},{13,8},{2,15},{3,14},... | collective-permute-start | bytes 147464 | tf_op jit(solution)/shard_map/ppermute | solution.py:61
  7.9 0.1 collective-permute-done.refs_1_
  8.0 2.0 %collective-permute-start.3 = (bf16[32,768]{1,0:T(8,128)(2,1)S(1)}, bf16[32,768]{1,0:T(8,128)(2,1)S(1)}, u32[]{:S(2)}, u32[]{:S(2)}) collective-permute-start(bf16[32,768]{1,0:T(8,128)(2,1)S(1)} %regroup.3.refs_7_.refs_3_), channel_id=1, source_target_pairs={{0,3},{1,2},{2,1},{3,0},{4,7},{5,6},{6,5},{7,4},{8,11},{9,10},{10,... | collective-permute-start | bytes 147464 | tf_op jit(solution)/shard_map/ppermute | solution.py:61
  10.0 2.5 %prepare.1 = (bf16[2,768,1536]{2,1,0:T(8,128)(2,1)S(1)}, bf16[128,512]{1,0:T(8,128)(2,1)S(1)}, bf16[128,512]{1,0:T(8,128)(2,1)S(1)}, f32[8,128]{1,0:T(8,128)S(1)}) custom-call(s32[4,4]{1,0:T(4,128)} %refs_0_.1, s32[4]{0:T(128)} %refs_1_.1, s32[16]{0:T(128)} %refs_2_.1, f32[1,4]{1,0:T(1,128)} %refs_3_.1, f32[1,4]{1,0:T(1,128)} %refs_4_.1, ...), custom_call_target="tpu_custom_call" | custom-call | bytes 9437184 | tf_op jit(solution)/shard_map/prepare/pallas_call | solution.py:223
  12.5 0.0 collective-permute-done.1.refs_0_.refs_2_
  12.5 0.0 collective-permute-done.2.refs_1_.refs_3_
  12.5 0.0 collective-permute-done.3.refs_5_.refs_3_
  12.5 0.5 %collective-permute-start.4 = (bf16[64,768]{1,0:T(8,128)(2,1)S(1)}, bf16[64,768]{1,0:T(8,128)(2,1)S(1)}, u32[]{:S(2)}, u32[]{:S(2)}) collective-permute-start(bf16[64,768]{1,0:T(8,128)(2,1)S(1)} %regroup.5.refs_5_.refs_0_), channel_id=1, source_target_pairs={{0,1},{1,0},{2,3},{3,2},{4,5},{5,4},{6,7},{7,6},{8,9},{9,8},{10,11... | collective-permute-start | bytes 294920 | tf_op jit(solution)/shard_map/ppermute | solution.py:70
  13.0 1.2 %collective-permute-start.5 = (bf16[32,768]{1,0:T(8,128)(2,1)S(1)}, bf16[32,768]{1,0:T(8,128)(2,1)S(1)}, u32[]{:S(2)}, u32[]{:S(2)}) collective-permute-start(bf16[32,768]{1,0:T(8,128)(2,1)S(1)} %regroup.4.refs_4_), channel_id=1, source_target_pairs={{0,3},{1,2},{2,1},{3,0},{4,7},{5,6},{6,5},{7,4},{8,11},{9,10},{10,... | collective-permute-start | bytes 147464 | tf_op jit(solution)/shard_map/ppermute | solution.py:61
  14.2 0.0 collective-permute-done.4.refs_6_.refs_1_
  14.2 0.5 %couple.1.refs_2_ = bf16[256,768]{1,0:T(8,128)(2,1)S(1)} custom-call(bf16[2,768,1536]{2,1,0:T(8,128)(2,1)S(1)} %get-tuple-element.13.refs_0_.screening, bf16[64,768]{1,0:T(8,128)(2,1)S(1)} %regroup.5.refs_5_.refs_0_, bf16[64,768]{1,0:T(8,128)(2,1)S(1)} %collective-permute-done.4.refs_6_.refs_1_), custom_call_target="tpu_custom_call" | custom-call | flops 1 | bytes 1 | tf_op jit(solution)/shard_map/couple/pallas_call | solution.py:392
  14.7 1.3 %near.1.refs_1_ = f32[24,128]{1,0:T(8,128)S(1)} custom-call(bf16[2,768,1536]{2,1,0:T(8,128)(2,1)S(1)} %get-tuple-element.13.refs_0_.screening, bf16[128,512]{1,0:T(8,128)(2,1)S(1)} %get-tuple-element.14.refs_1_, f32[8,128]{1,0:T(8,128)S(1)} %get-tuple-element.15.refs_2_, bf16[32,768]{1,0:T(8,128)(2,1)S(1)} %regroup.3.refs_7_.refs_3_, ...), custom_call_target="tpu_custom_call" | custom-call | flops 1 | bytes 1 | tf_op jit(solution)/shard_map/near/pallas_call | solution.py:354
  16.0 0.8 %collective-permute-done.5.refs_4_ = bf16[32,768]{1,0:T(8,128)(2,1)S(1)} collective-permute-done((bf16[32,768]{1,0:T(8,128)(2,1)S(1)}, bf16[32,768]{1,0:T(8,128)(2,1)S(1)}, u32[]{:S(2)}, u32[]{:S(2)}) %collective-permute-start.5) | collective-permute-done | bytes 49184 | tf_op jit(solution)/shard_map/ppermute | solution.py:61
  16.7 0.5 %far.1 = f32[24,128]{1,0:T(8,128)S(1)} custom-call(bf16[128,512]{1,0:T(8,128)(2,1)S(1)} %get-tuple-element.12.refs_0_, f32[24,128]{1,0:T(8,128)S(1)} %near.1.refs_1_, bf16[256,768]{1,0:T(8,128)(2,1)S(1)} %couple.1.refs_2_, bf16[32,768]{1,0:T(8,128)(2,1)S(1)} %collective-permute-done.3.refs_5_.refs_3_, bf16[32,768]{1,0:T(8,128)(2,1)S(1)} %collective-permute-done.5.refs_4_), custom_call_target="tpu_custom_call" | custom-call | tf_op jit(solution)/shard_map/far/pallas_call | solution.py:427
  17.3 0.1 collective-permute-start.6
  17.4 1.1 %collective-permute-done.6 = f32[24,128]{1,0:T(8,128)S(1)} collective-permute-done((f32[24,128]{1,0:T(8,128)S(1)}, f32[24,128]{1,0:T(8,128)S(1)}, u32[]{:S(2)}, u32[]{:S(2)}) %collective-permute-start.6) | collective-permute-done | bytes 12320 | tf_op jit(solution)/shard_map/ppermute | solution.py:70
  18.5 1.0 %collective-permute-start.7 = (f32[24,128]{1,0:T(8,128)S(1)}, f32[24,128]{1,0:T(8,128)S(1)}, u32[]{:S(2)}, u32[]{:S(2)}) collective-permute-start(f32[24,128]{1,0:T(8,128)S(1)} %add.6), channel_id=1, source_target_pairs={{0,3},{1,2},{2,1},{3,0},{4,7},{5,6},{6,5},{7,4},{8,11},{9,10},{10,... | collective-permute-start | bytes 36872 | tf_op jit(solution)/shard_map/ppermute | solution.py:61
  19.5 2.1 %collective-permute-done.7 = f32[24,128]{1,0:T(8,128)S(1)} collective-permute-done((f32[24,128]{1,0:T(8,128)S(1)}, f32[24,128]{1,0:T(8,128)S(1)}, u32[]{:S(2)}, u32[]{:S(2)}) %collective-permute-start.7) | collective-permute-done | bytes 12320 | tf_op jit(solution)/shard_map/ppermute | solution.py:61
  21.6 0.0 collective-permute-start.10
  21.6 2.3 %collective-permute-start.9 = (f32[24,128]{1,0:T(8,128)S(1)}, f32[24,128]{1,0:T(8,128)S(1)}, u32[]{:S(2)}, u32[]{:S(2)}) collective-permute-start(f32[24,128]{1,0:T(8,128)S(1)} %add.7.refs_0_), channel_id=1, source_target_pairs={{0,9},{1,8},{4,13},{5,12},{8,1},{9,0},{12,5},{13,4},{2,11},{3,10},... | collective-permute-start | bytes 36872 | tf_op jit(solution)/shard_map/ppermute | solution.py:61
  23.9 1.2 %collective-permute-start.8 = (f32[24,128]{1,0:T(8,128)S(1)}, f32[24,128]{1,0:T(8,128)S(1)}, u32[]{:S(2)}, u32[]{:S(2)}) collective-permute-start(f32[24,128]{1,0:T(8,128)S(1)} %add.7.refs_0_), channel_id=1, source_target_pairs={{0,13},{1,12},{4,1},{5,0},{8,5},{9,4},{12,9},{13,8},{2,15},{3,14},... | collective-permute-start | bytes 36872 | tf_op jit(solution)/shard_map/ppermute | solution.py:61
  25.1 1.4 %collective-permute-done.10.refs_3_ = f32[24,128]{1,0:T(8,128)S(1)} collective-permute-done((f32[24,128]{1,0:T(8,128)S(1)}, f32[24,128]{1,0:T(8,128)S(1)}, u32[]{:S(2)}, u32[]{:S(2)}) %collective-permute-start.10) | collective-permute-done | bytes 12320 | tf_op jit(solution)/shard_map/ppermute | solution.py:61
  26.5 0.0 collective-permute-done.9.refs_2_
  26.5 0.6 %collective-permute-done.8.refs_1_ = f32[24,128]{1,0:T(8,128)S(1)} collective-permute-done((f32[24,128]{1,0:T(8,128)S(1)}, f32[24,128]{1,0:T(8,128)S(1)}, u32[]{:S(2)}, u32[]{:S(2)}) %collective-permute-start.8) | collective-permute-done | bytes 12320 | tf_op jit(solution)/shard_map/ppermute | solution.py:61
  27.1 1.4 %haydock.1 = (f32[1,2,2,16]{3,2,1,0:T(2,128)}, f32[2,6]{1,0:T(2,128)}) custom-call(f32[24,128]{1,0:T(8,128)S(1)} %add.7.refs_0_, f32[24,128]{1,0:T(8,128)S(1)} %collective-permute-done.8.refs_1_, f32[24,128]{1,0:T(8,128)S(1)} %collective-permute-done.9.refs_2_, f32[24,128]{1,0:T(8,128)S(1)} %collective-permute-done.10.refs_3_), custom_call_target="tpu_custom_call" | custom-call | tf_op jit(solution)/shard_map/haydock/pallas_call | solution.py:523
  (5 shorter events, 0.0 us)
Async XLA Ops:
  1.7 6.3 %collective-permute-start = (bf16[32,768]{1,0:T(8,128)(2,1)S(1)}, bf16[32,768]{1,0:T(8,128)(2,1)S(1)}, u32[]{:S(2)}, u32[]{:S(2)}) collective-permute-start(bf16[32,768]{1,0:T(8,128)(2,1)S(1)} %get-tuple-element.11), channel_id=1, source_target_pairs={{0,5},{1,4},{4,9},{5,8},{8,13},{9,12},{12,1},{13,0},{2,7},{3,6},{6... | collective-permute-start | bytes 147464 | tf_op jit(solution)/shard_map/ppermute | solution.py:61
  4.2 8.3 %collective-permute-start.1 = (bf16[32,768]{1,0:T(8,128)(2,1)S(1)}, bf16[32,768]{1,0:T(8,128)(2,1)S(1)}, u32[]{:S(2)}, u32[]{:S(2)}) collective-permute-start(bf16[32,768]{1,0:T(8,128)(2,1)S(1)} %get-tuple-element.16), channel_id=1, source_target_pairs={{0,9},{1,8},{4,13},{5,12},{8,1},{9,0},{12,5},{13,4},{2,11},{3,10},... | collective-permute-start | bytes 147464 | tf_op jit(solution)/shard_map/ppermute | solution.py:61
  7.1 5.4 %collective-permute-start.2 = (bf16[32,768]{1,0:T(8,128)(2,1)S(1)}, bf16[32,768]{1,0:T(8,128)(2,1)S(1)}, u32[]{:S(2)}, u32[]{:S(2)}) collective-permute-start(bf16[32,768]{1,0:T(8,128)(2,1)S(1)} %get-tuple-element.17), channel_id=1, source_target_pairs={{0,13},{1,12},{4,1},{5,0},{8,5},{9,4},{12,9},{13,8},{2,15},{3,14},... | collective-permute-start | bytes 147464 | tf_op jit(solution)/shard_map/ppermute | solution.py:61
  8.0 4.5 %collective-permute-start.3 = (bf16[32,768]{1,0:T(8,128)(2,1)S(1)}, bf16[32,768]{1,0:T(8,128)(2,1)S(1)}, u32[]{:S(2)}, u32[]{:S(2)}) collective-permute-start(bf16[32,768]{1,0:T(8,128)(2,1)S(1)} %regroup.3.refs_7_.refs_3_), channel_id=1, source_target_pairs={{0,3},{1,2},{2,1},{3,0},{4,7},{5,6},{6,5},{7,4},{8,11},{9,10},{10,... | collective-permute-start | bytes 147464 | tf_op jit(solution)/shard_map/ppermute | solution.py:61
  12.5 1.7 %collective-permute-start.4 = (bf16[64,768]{1,0:T(8,128)(2,1)S(1)}, bf16[64,768]{1,0:T(8,128)(2,1)S(1)}, u32[]{:S(2)}, u32[]{:S(2)}) collective-permute-start(bf16[64,768]{1,0:T(8,128)(2,1)S(1)} %regroup.5.refs_5_.refs_0_), channel_id=1, source_target_pairs={{0,1},{1,0},{2,3},{3,2},{4,5},{5,4},{6,7},{7,6},{8,9},{9,8},{10,11... | collective-permute-start | bytes 294920 | tf_op jit(solution)/shard_map/ppermute | solution.py:70
  13.0 3.7 %collective-permute-start.5 = (bf16[32,768]{1,0:T(8,128)(2,1)S(1)}, bf16[32,768]{1,0:T(8,128)(2,1)S(1)}, u32[]{:S(2)}, u32[]{:S(2)}) collective-permute-start(bf16[32,768]{1,0:T(8,128)(2,1)S(1)} %regroup.4.refs_4_), channel_id=1, source_target_pairs={{0,3},{1,2},{2,1},{3,0},{4,7},{5,6},{6,5},{7,4},{8,11},{9,10},{10,... | collective-permute-start | bytes 147464 | tf_op jit(solution)/shard_map/ppermute | solution.py:61
  17.3 1.2 %collective-permute-start.6 = (f32[24,128]{1,0:T(8,128)S(1)}, f32[24,128]{1,0:T(8,128)S(1)}, u32[]{:S(2)}, u32[]{:S(2)}) collective-permute-start(f32[24,128]{1,0:T(8,128)S(1)} %far.1), channel_id=1, source_target_pairs={{0,1},{1,0},{2,3},{3,2},{4,5},{5,4},{6,7},{7,6},{8,9},{9,8},{10,11... | collective-permute-start | bytes 36872 | tf_op jit(solution)/shard_map/ppermute | solution.py:70
  18.5 3.1 %collective-permute-start.7 = (f32[24,128]{1,0:T(8,128)S(1)}, f32[24,128]{1,0:T(8,128)S(1)}, u32[]{:S(2)}, u32[]{:S(2)}) collective-permute-start(f32[24,128]{1,0:T(8,128)S(1)} %add.6), channel_id=1, source_target_pairs={{0,3},{1,2},{2,1},{3,0},{4,7},{5,6},{6,5},{7,4},{8,11},{9,10},{10,... | collective-permute-start | bytes 36872 | tf_op jit(solution)/shard_map/ppermute | solution.py:61
  21.6 4.9 %collective-permute-start.10 = (f32[24,128]{1,0:T(8,128)S(1)}, f32[24,128]{1,0:T(8,128)S(1)}, u32[]{:S(2)}, u32[]{:S(2)}) collective-permute-start(f32[24,128]{1,0:T(8,128)S(1)} %add.7.refs_0_), channel_id=1, source_target_pairs={{0,5},{1,4},{4,9},{5,8},{8,13},{9,12},{12,1},{13,0},{2,7},{3,6},{6... | collective-permute-start | bytes 36872 | tf_op jit(solution)/shard_map/ppermute | solution.py:61
  21.6 4.9 %collective-permute-start.9 = (f32[24,128]{1,0:T(8,128)S(1)}, f32[24,128]{1,0:T(8,128)S(1)}, u32[]{:S(2)}, u32[]{:S(2)}) collective-permute-start(f32[24,128]{1,0:T(8,128)S(1)} %add.7.refs_0_), channel_id=1, source_target_pairs={{0,9},{1,8},{4,13},{5,12},{8,1},{9,0},{12,5},{13,4},{2,11},{3,10},... | collective-permute-start | bytes 36872 | tf_op jit(solution)/shard_map/ppermute | solution.py:61
  23.9 3.2 %collective-permute-start.8 = (f32[24,128]{1,0:T(8,128)S(1)}, f32[24,128]{1,0:T(8,128)S(1)}, u32[]{:S(2)}, u32[]{:S(2)}) collective-permute-start(f32[24,128]{1,0:T(8,128)S(1)} %add.7.refs_0_), channel_id=1, source_target_pairs={{0,13},{1,12},{4,1},{5,0},{8,5},{9,4},{12,9},{13,8},{2,15},{3,14},... | collective-permute-start | bytes 36872 | tf_op jit(solution)/shard_map/ppermute | solution.py:61

commit v15 on v14

--- a/solution.py
+++ b/solution.py
@@ -17,7 +17,7 @@
 anywhere = pl.BlockSpec(memory_space=pl.ANY)
 EXTRA_ROWS = 8
 LIGHT = pl.CostEstimate(flops=1, bytes_accessed=1, transcendentals=0)
-CHUNKS = 4
+CHUNKS = 3
 
 
 def in_vmem(shape, dtype):
@@ -133,7 +133,7 @@
 def prepare_kernel(ka, dims, *refs):
     vloc, val_count, cond_count, npol = dims
     ins, screening, (screen_out, near_table, far_table, extras), scratch = refs[:6], refs[6], refs[8:12], refs[12:]
-    qmap, owner, band_pairs, val_energy, cond_energy, start, sems, screen_sems = scratch
+    qmap, owner, band_pairs, val_energy, cond_energy, start, sems, screen_sem = scratch
     me = lax.axis_index("ka")
     half = lax.axis_index("ba")
     mine = lax.axis_index("ga")
@@ -143,17 +143,8 @@
             zip(ins, (qmap, owner, band_pairs, val_energy, cond_energy, start))
         )
     ]
-    height = screening.shape[2] // CHUNKS
-    chunks = [
-        pltpu.make_async_copy(
-            screening.at[0, part, pl.ds(c * height, height)],
-            screen_out.at[part, pl.ds(c * height, height)],
-            screen_sems.at[part, c],
-        )
-        for part in range(2)
-        for c in range(CHUNKS)
-    ]
-    for copy in copies + chunks:
+    load = pltpu.make_async_copy(screening.at[0, 0], screen_out, screen_sem)
+    for copy in copies + [load]:
         copy.start()
     pairs = vloc * val_count
     block = 2 * pairs
@@ -210,8 +201,7 @@
     second = jnp.where(second >= kcount, second - kcount, second).astype(jnp.float32) * first
     rest = jnp.zeros((EXTRA_ROWS - 3 - npol, lanes), jnp.float32)
     extras[...] = jnp.concatenate([vectors, energy, bands * first, second, rest], 0)
-    for copy in chunks:
-        copy.wait()
+    load.wait()
 
 
 def prepare(ka, dims, qmap, owner, band_pairs, val_energy, cond_energy, start, screening, after):
@@ -223,7 +213,7 @@
     return pl.pallas_call(
         functools.partial(prepare_kernel, ka, dims),
         out_shape=[
-            in_vmem(screening.shape[1:], screening.dtype),
+            in_vmem(screening.shape[2:], screening.dtype),
             in_vmem(table.shape, table.dtype),
             in_vmem(table.shape, table.dtype),
             in_vmem((EXTRA_ROWS, lanes), jnp.float32),
@@ -234,10 +224,10 @@
         + [
             pltpu.VMEM(start.shape, start.dtype),
             pltpu.SemaphoreType.DMA((6,)),
-            pltpu.SemaphoreType.DMA((2, CHUNKS)),
+            pltpu.SemaphoreType.DMA,
         ],
         cost_estimate=pl.CostEstimate(
-            flops=0, bytes_accessed=4 * screening.size, transcendentals=0
+            flops=0, bytes_accessed=2 * screening.size, transcendentals=0
         ),
         compiler_params=limits(table),
         name="prepare",
@@ -307,7 +297,7 @@
     return piece[:, :lanes] + piece[:, lanes:]
 
 
-def diagonal(crossed, ka, ba, share_rows, sign):
+def diagonal(crossed, ka, ba, share_rows):
     rows = crossed.shape[1] // 2
     lane = iota((share_rows, 2 * rows), 1)
     lane_j = lane % rows // (rows // ka)
@@ -319,51 +309,21 @@
             at = (h * ka + j) * 2 * share_rows
             real = crossed[at : at + share_rows]
             imag = crossed[at + share_rows : at + 2 * share_rows]
-            total = jnp.where(lane_j == j, jnp.where(straight, real, sign * imag), total)
+            total = jnp.where(lane_j == j, jnp.where(straight, real, imag), total)
         kernel.append(total)
     return jnp.concatenate(kernel, 0)
 
 
-def near_kernel(ka, ba, dims, *refs):
-    vloc, val_count, cond_count, npol = dims
-    screening, table, extras = refs[:3]
-    halves, cond_in, out = refs[3 : -1 - ba], refs[-1 - ba : -1], refs[-1]
-    codes = val_count * cond_count
-    columns = columns_of(lax.axis_index("ga"), halves[0].shape[1])
-    wide, turned = with_turned(halves, vloc * val_count)
-    real = jnp.concatenate([wide, turned], 0).astype(jnp.bfloat16)
-    imag = jnp.concatenate([turned, -wide], 0).astype(jnp.bfloat16)
-    form = (((1,), (1,)), ((), ()))
-    fields = lax.dot_general(
-        screening[0, :, columns], real, form, preferred_element_type=jnp.float32
-    ) + lax.dot_general(screening[1, :, columns], imag, form, preferred_element_type=jnp.float32)
-    both = jnp.concatenate(split(fields), 1)
-    cond = jnp.concatenate([ref[...] for ref in cond_in], 0)
-    crossed = jnp.dot(cond, both, preferred_element_type=jnp.float32)
-    half = crossed.shape[1] // 2
-    crossed = crossed[:, :half] + crossed[:, half:]
-    kernel = diagonal(crossed, ka, ba, cond_count // ba * cond_count, -1.0)
-    out[:codes, :] = placed_piece(kernel, table, dims, ba)
-    out[codes:, :] = extras[...]
-
-
-def near(ka, ba, dims, screening, table, extras, halves, cond_all):
-    vloc, val_count, cond_count, npol = dims
-    codes = val_count * cond_count
-    operands = [screening, table, extras, *halves, *cond_all]
-    return pl.pallas_call(
-        functools.partial(near_kernel, ka, ba, dims),
-        out_shape=in_vmem((codes + EXTRA_ROWS, 2 * ka * codes), jnp.float32),
-        in_specs=[vmem] * len(operands),
-        out_specs=vmem,
-        cost_estimate=LIGHT,
-        compiler_params=limits(*operands),
-        name="near",
-    )(*operands)
-
-
-def couple_kernel(ka, ga, ba, share_rows, screening, *refs):
-    cond_in, outs = refs[:ba], refs[ba:]
+def couple_kernel(ka, ga, ba, share_rows, screen_real, screening, *refs):
+    cond_in, outs, (screen_imag, sems) = refs[:ba], refs[ba:-2], refs[-2:]
+    height = screen_imag.shape[0] // CHUNKS
+    chunks = [pl.ds(c * height, height) for c in range(CHUNKS)]
+    loads = [
+        pltpu.make_async_copy(screening.at[0, 1, chunk], screen_imag.at[chunk], sems.at[c])
+        for c, chunk in enumerate(chunks)
+    ]
+    for load in loads:
+        load.start()
     mine = lax.axis_index("ga")
     wide = jnp.concatenate([ref[...].astype(jnp.float32) for ref in cond_in], 0)
     straight, turned = [], []
@@ -373,37 +333,47 @@
         turned += [imag, real]
     straight = jnp.concatenate(straight, 0).astype(jnp.bfloat16)
     turned = jnp.concatenate(turned, 0).astype(jnp.bfloat16)
-    width = screening.shape[2] // ga
-    for r in range(1, ga):
-        columns = columns_of(origin(mine, r, ga), width)
-        coupled = jnp.dot(
-            straight, screening[0, :, columns], preferred_element_type=jnp.float32
-        ) + jnp.dot(turned, screening[1, :, columns], preferred_element_type=jnp.float32)
-        high, low = split(coupled)
-        outs[r - 1][: coupled.shape[0], :] = high
-        outs[r - 1][coupled.shape[0] :, :] = low
-
-
-def couple(ka, ga, ba, dims, screening, cond_all):
+    width = screen_imag.shape[1] // ga
+    columns = [columns_of(origin(mine, r, ga), width) for r in range(ga)]
+    coupled = [
+        jnp.dot(straight, screen_real[:, block], preferred_element_type=jnp.float32) for block in columns
+    ]
+    for c, load in enumerate(loads):
+        load.wait()
+        part = turned[:, c * height : (c + 1) * height]
+        for r, block in enumerate(columns):
+            coupled[r] = coupled[r] + jnp.dot(
+                part, screen_imag[chunks[c], block], preferred_element_type=jnp.float32
+            )
+    for out, value in zip(outs, coupled):
+        high, low = split(value)
+        out[: value.shape[0], :] = high
+        out[value.shape[0] :, :] = low
+
+
+def couple(ka, ga, ba, dims, screen_real, screening, cond_all):
     share_rows = dims[2] // ba * dims[2]
     rows = 2 * sum(x.shape[0] for x in cond_all)
-    width = screening.shape[2] // ga
-    operands = [screening, *cond_all]
+    width = screen_real.shape[1] // ga
+    operands = [screen_real, *cond_all]
     return pl.pallas_call(
         functools.partial(couple_kernel, ka, ga, ba, share_rows),
-        out_shape=[in_vmem((rows, width), jnp.bfloat16)] * (ga - 1),
-        in_specs=[vmem] * len(operands),
-        out_specs=[vmem] * (ga - 1),
+        out_shape=[in_vmem((rows, width), jnp.bfloat16)] * ga,
+        in_specs=[vmem, anywhere] + [vmem] * len(cond_all),
+        out_specs=[vmem] * ga,
+        scratch_shapes=[
+            pltpu.VMEM(screen_real.shape, screen_real.dtype),
+            pltpu.SemaphoreType.DMA((CHUNKS,)),
+        ],
         cost_estimate=LIGHT,
         compiler_params=limits(*operands),
         name="couple",
-    )(*operands)
-
-
-def far_kernel(ka, ba, dims, *refs):
+    )(screen_real, placed(screening, pltpu.HBM), *cond_all)
+
+
+def contract_kernel(ka, ba, count, dims, *refs):
     vloc, val_count, cond_count, npol = dims
     table, held, out = refs[0], refs[1], refs[-1]
-    count = lax.axis_size("ga") - 1
     each = (len(refs) - 3 - count) // count
     codes = val_count * cond_count
     crossed = None
@@ -417,20 +387,25 @@
         crossed = term if crossed is None else crossed + term
     half = crossed.shape[0] // 2
     crossed = crossed[:half] + crossed[half:]
-    kernel = diagonal(crossed, ka, ba, cond_count // ba * cond_count, 1.0)
-    out[:codes, :] = held[:codes, :] + placed_piece(kernel, table, dims, ba)
-    out[codes:, :] = held[codes:, :]
-
-
-def far(ka, ba, dims, table, held, coupled, val_far):
-    operands = [table, held, *coupled, *val_far]
+    kernel = diagonal(crossed, ka, ba, cond_count // ba * cond_count)
+    piece = placed_piece(kernel, table, dims, ba)
+    before = held.shape[0] - EXTRA_ROWS
+    out[:codes, :] = piece + held[:codes, :] if before else piece
+    out[codes:, :] = held[before:, :]
+
+
+def contract(ka, ba, dims, table, held, coupled, valence, name):
+    val_count, cond_count = dims[1:3]
+    operands = [table, held, *coupled, *valence]
+    shape = (val_count * cond_count + EXTRA_ROWS, held.shape[1])
     return pl.pallas_call(
-        functools.partial(far_kernel, ka, ba, dims),
-        out_shape=in_vmem(held.shape, jnp.float32),
+        functools.partial(contract_kernel, ka, ba, len(coupled), dims),
+        out_shape=in_vmem(shape, jnp.float32),
         in_specs=[vmem] * len(operands),
         out_specs=vmem,
+        cost_estimate=LIGHT,
         compiler_params=limits(*operands),
-        name="far",
+        name=name,
     )(*operands)
 
 
@@ -570,7 +545,7 @@
     early = ka // 2
     val_early = regroup(blocks[:early], 0, 2 * pairs)
     far_early = [shifted(val_early, "ga", r) for r in range(1, ga)]
-    whole, near_table, far_table, extras = prepare(
+    real, near_table, far_table, extras = prepare(
         ka,
         dims,
         qpoint_map,
@@ -586,14 +561,15 @@
     far_late = [shifted(val_late, "ga", r) for r in range(1, ga)]
     cond_half = regroup(blocks, 2 * pairs, blocks[0].shape[0], (val_late, *far_early))
     cond_all = [cond_half] + [handed(cond_half, r) for r in range(1, ba)]
-    piece = near(ka, ba, dims, whole, near_table, extras, [val_early, val_late], cond_all)
+    coupled = couple(ka, ga, ba, dims, real, screening, cond_all)
+    near = [val_early, val_late]
+    piece = contract(ka, ba, dims, near_table, extras, coupled[:1], near, "near")
     if ga > 1:
-        coupled = couple(ka, ga, ba, dims, whole, cond_all)
-        val_far = [half for both in zip(far_early, far_late) for half in both]
-        piece = far(ka, ba, dims, far_table, piece, coupled, val_far)
+        far = [half for both in zip(far_early, far_late) for half in both]
+        piece = contract(ka, ba, dims, far_table, piece, coupled[1:], far, "far")
     piece = piece + sum(handed(piece, r) for r in range(1, ba))
     piece = summed(piece, "ga")
-    pieces = [piece] + [shifted(piece, "ka", j) for j in reversed(range(1, ka))]
+    pieces = [piece] + [shifted(piece, "ka", j) for j in range(1, ka)]
     scale_count = float(kcount * pair_count)
     return tuple(haydock(ka, pair_count, scale_count, npol, pieces))
 

time: 28.6 us -> 29 us (1.014)
  waiting for transfers between devices: 6 us -> 5.27 us
  starting transfers between devices: 14.6 us -> 15.2 us
  Pallas kernels: 7.21 us -> 7.59 us
    pallas_call x1, Pallas kernels: 0.5 us -> 2.29 us  [couple(): pl.pallas_call(functools.partial(couple_kernel, ka, ga, ba, share_rows),...]
    pallas_call x2, Pallas kernels: 1.79 us -> 1.08 us  [contract(): pl.pallas_call(functools.partial(contract_kernel, ka, ba, len(coupled), d...]
    pallas_call x1, Pallas kernels: 2.45 us -> 1.75 us  [prepare(): pl.pallas_call(functools.partial(prepare_kernel, ka, dims), out_shape=[in...]
    ppermute x9, waiting for transfers between devices: 4.95 us -> 4.24 us  [exchanged(): return lax.ppermute(value, (axis, 'ba'), pairs)]
    ppermute x9, starting transfers between devices: 14 us -> 14.5 us  [exchanged(): return lax.ppermute(value, (axis, 'ba'), pairs)]
  transfers between devices with their start and end apart: 11 -> 11, of which waited for: 6 -> 5; matrix products, arithmetic and copies ran while one was open for 0% -> 0% of each run, Pallas kernels for 15% -> 16%
where the time goes in v15:
time: 29 us; the launch traced here: 28.8 us
  starting transfers between devices  15.2 us (52%)
  Pallas kernels  7.59 us (26%)
  waiting for transfers between devices  5.27 us (18%)
  between operations  0.69 us (2%)
    ppermute x9, starting transfers between devices, exchanged(): return lax.ppermute(value, (axis, 'ba'), pairs)  14.5 us
    ppermute x9, waiting for transfers between devices, exchanged(): return lax.ppermute(value, (axis, 'ba'), pairs)  4.24 us
    pallas_call x1, Pallas kernels, couple(): pl.pallas_call(functools.partial(couple_kernel, ka, ga, ba, share_rows),...  2.29 us
    pallas_call x1, Pallas kernels, prepare(): pl.pallas_call(functools.partial(prepare_kernel, ka, dims), out_shape=[in...  1.75 us
    pallas_call x1, Pallas kernels, haydock(): pl.pallas_call(functools.partial(haydock_kernel, ka, codes, scale_count,...  1.41 us
    pallas_call x2, Pallas kernels, contract(): pl.pallas_call(functools.partial(contract_kernel, ka, ba, len(coupled), d...  1.08 us
    pallas_call x1, Pallas kernels, pack(): pl.pallas_call(functools.partial(pack_kernel, ka), out_shape=[shape] * ka...  1.05 us
    ppermute x2, waiting for transfers between devices, handed(): lax.ppermute(value, 'ba', [(h, (h + step) % size) for h in range(size)])  1.03 us
  transfers between devices with their start and end apart: 11, of which 5 were waited for; matrix products, arithmetic and copies ran while one was open for 0% of the time, Pallas kernels for 16%

profile of v15, /device:TPU:0, one launch (start us, length us, event | category | flops | bytes accessed | tf_op | source)
XLA Modules:
  0.0 28.8 jit_solution(10989510817226462223)
XLA Ops:
  0.6 1.0 %pack.1 = (bf16[32,768]{1,0:T(8,128)(2,1)S(1)}, bf16[32,768]{1,0:T(8,128)(2,1)S(1)}, bf16[32,768]{1,0:T(8,128)(2,1)S(1)}, bf16[32,768]{1,0:T(8,128)(2,1)S(1)}) custom-call(s32[4,4]{1,0:T(4,128)} %refs_0_.1, s32[4]{0:T(128)} %refs_1_.1, bf16[1,4,2,2,4,768]{5,4,3,2,1,0:T(4,128)(2,1)} %valence_in.1, bf16[1,4,2,4,4,768]{5,4,3,2,1,0:T(4,128)(2,1)} %conduction_in.1), custom_call_target="tpu_custom_call" | custom-call | tf_op jit(solution)/shard_map/pack/pallas_call | solution.py:115
  1.7 2.5 %collective-permute-start = (bf16[32,768]{1,0:T(8,128)(2,1)S(1)}, bf16[32,768]{1,0:T(8,128)(2,1)S(1)}, u32[]{:S(2)}, u32[]{:S(2)}) collective-permute-start(bf16[32,768]{1,0:T(8,128)(2,1)S(1)} %get-tuple-element.13), channel_id=1, source_target_pairs={{0,5},{1,4},{4,9},{5,8},{8,13},{9,12},{12,1},{13,0},{2,7},{3,6},{6... | collective-permute-start | bytes 147464 | tf_op jit(solution)/shard_map/ppermute | solution.py:61
  4.2 2.9 %collective-permute-start.1 = (bf16[32,768]{1,0:T(8,128)(2,1)S(1)}, bf16[32,768]{1,0:T(8,128)(2,1)S(1)}, u32[]{:S(2)}, u32[]{:S(2)}) collective-permute-start(bf16[32,768]{1,0:T(8,128)(2,1)S(1)} %get-tuple-element.18), channel_id=1, source_target_pairs={{0,9},{1,8},{4,13},{5,12},{8,1},{9,0},{12,5},{13,4},{2,11},{3,10},... | collective-permute-start | bytes 147464 | tf_op jit(solution)/shard_map/ppermute | solution.py:61
  7.1 0.8 %collective-permute-start.2 = (bf16[32,768]{1,0:T(8,128)(2,1)S(1)}, bf16[32,768]{1,0:T(8,128)(2,1)S(1)}, u32[]{:S(2)}, u32[]{:S(2)}) collective-permute-start(bf16[32,768]{1,0:T(8,128)(2,1)S(1)} %get-tuple-element.19), channel_id=1, source_target_pairs={{0,13},{1,12},{4,1},{5,0},{8,5},{9,4},{12,9},{13,8},{2,15},{3,14},... | collective-permute-start | bytes 147464 | tf_op jit(solution)/shard_map/ppermute | solution.py:61
  7.9 0.1 collective-permute-done.refs_1_
  8.0 2.0 %collective-permute-start.3 = (bf16[32,768]{1,0:T(8,128)(2,1)S(1)}, bf16[32,768]{1,0:T(8,128)(2,1)S(1)}, u32[]{:S(2)}, u32[]{:S(2)}) collective-permute-start(bf16[32,768]{1,0:T(8,128)(2,1)S(1)} %regroup.3.refs_7_.refs_3_), channel_id=1, source_target_pairs={{0,3},{1,2},{2,1},{3,0},{4,7},{5,6},{6,5},{7,4},{8,11},{9,10},{10,... | collective-permute-start | bytes 147464 | tf_op jit(solution)/shard_map/ppermute | solution.py:61
  10.0 1.7 %prepare.1 = (bf16[768,1536]{1,0:T(8,128)(2,1)S(1)}, bf16[128,512]{1,0:T(8,128)(2,1)S(1)}, bf16[128,512]{1,0:T(8,128)(2,1)S(1)}, f32[8,128]{1,0:T(8,128)S(1)}) custom-call(s32[4,4]{1,0:T(4,128)} %refs_0_.1, s32[4]{0:T(128)} %refs_1_.1, s32[16]{0:T(128)} %refs_2_.1, f32[1,4]{1,0:T(1,128)} %refs_3_.1, f32[1,4]{1,0:T(1,128)} %refs_4_.1, ...), custom_call_target="tpu_custom_call" | custom-call | bytes 4718592 | tf_op jit(solution)/shard_map/prepare/pallas_call | solution.py:213
  11.8 0.0 collective-permute-done.1.refs_0_.refs_2_
  11.8 0.0 collective-permute-done.2.refs_1_.refs_3_
  11.8 0.0 collective-permute-done.3.refs_5_.refs_3_
  11.9 0.5 %collective-permute-start.4 = (bf16[64,768]{1,0:T(8,128)(2,1)S(1)}, bf16[64,768]{1,0:T(8,128)(2,1)S(1)}, u32[]{:S(2)}, u32[]{:S(2)}) collective-permute-start(bf16[64,768]{1,0:T(8,128)(2,1)S(1)} %regroup.5.refs_0_), channel_id=1, source_target_pairs={{0,1},{1,0},{2,3},{3,2},{4,5},{5,4},{6,7},{7,6},{8,9},{9,8},{10,11... | collective-permute-start | bytes 294920 | tf_op jit(solution)/shard_map/ppermute | solution.py:70
  12.4 1.8 %collective-permute-start.5 = (bf16[32,768]{1,0:T(8,128)(2,1)S(1)}, bf16[32,768]{1,0:T(8,128)(2,1)S(1)}, u32[]{:S(2)}, u32[]{:S(2)}) collective-permute-start(bf16[32,768]{1,0:T(8,128)(2,1)S(1)} %regroup.4.refs_4_), channel_id=1, source_target_pairs={{0,3},{1,2},{2,1},{3,0},{4,7},{5,6},{6,5},{7,4},{8,11},{9,10},{10,... | collective-permute-start | bytes 147464 | tf_op jit(solution)/shard_map/ppermute | solution.py:61
  14.2 0.0 collective-permute-done.4.refs_1_
  14.2 2.3 %couple.1 = (bf16[256,768]{1,0:T(8,128)(2,1)S(1)}, bf16[256,768]{1,0:T(8,128)(2,1)S(1)}) custom-call(bf16[768,1536]{1,0:T(8,128)(2,1)S(1)} %get-tuple-element.17.screen_real, bf16[1,2,768,1536]{3,2,1,0:T(8,128)(2,1)} %screening.1, bf16[64,768]{1,0:T(8,128)(2,1)S(1)} %regroup.5.refs_0_, bf16[64,768]{1,0:T(8,128)(2,1)S(1)} %collective-permute-done.4.refs_1_), custom_call_target="tpu_custom_call" | custom-call | flops 1 | bytes 1 | tf_op jit(solution)/shard_map/couple/pallas_call | solution.py:359
  16.5 0.5 %near.1.refs_1_ = f32[24,128]{1,0:T(8,128)S(1)} custom-call(bf16[128,512]{1,0:T(8,128)(2,1)S(1)} %get-tuple-element.15.refs_0_, f32[8,128]{1,0:T(8,128)S(1)} %get-tuple-element.16.refs_2_.refs_1_, bf16[256,768]{1,0:T(8,128)(2,1)S(1)} %get-tuple-element.20.refs_2_, bf16[32,768]{1,0:T(8,128)(2,1)S(1)} %regroup.3.refs_7_.refs_3_, ...), custom_call_target="tpu_custom_call" | custom-call | flops 1 | bytes 1 | tf_op jit(solution)/shard_map/near/pallas_call | solution.py:401
  17.1 0.0 collective-permute-done.5.refs_4_
  17.1 0.5 %far.1 = f32[24,128]{1,0:T(8,128)S(1)} custom-call(bf16[128,512]{1,0:T(8,128)(2,1)S(1)} %get-tuple-element.14.refs_0_, f32[24,128]{1,0:T(8,128)S(1)} %near.1.refs_1_, bf16[256,768]{1,0:T(8,128)(2,1)S(1)} %get-tuple-element.21.refs_2_, bf16[32,768]{1,0:T(8,128)(2,1)S(1)} %collective-permute-done.3.refs_5_.refs_3_, ...), custom_call_target="tpu_custom_call" | custom-call | flops 1 | bytes 1 | tf_op jit(solution)/shard_map/far/pallas_call | solution.py:401
  17.6 0.2 collective-permute-start.6
  17.8 1.0 %collective-permute-done.6 = f32[24,128]{1,0:T(8,128)S(1)} collective-permute-done((f32[24,128]{1,0:T(8,128)S(1)}, f32[24,128]{1,0:T(8,128)S(1)}, u32[]{:S(2)}, u32[]{:S(2)}) %collective-permute-start.6) | collective-permute-done | bytes 12320 | tf_op jit(solution)/shard_map/ppermute | solution.py:70
  18.8 0.9 %collective-permute-start.7 = (f32[24,128]{1,0:T(8,128)S(1)}, f32[24,128]{1,0:T(8,128)S(1)}, u32[]{:S(2)}, u32[]{:S(2)}) collective-permute-start(f32[24,128]{1,0:T(8,128)S(1)} %add.6), channel_id=1, source_target_pairs={{0,3},{1,2},{2,1},{3,0},{4,7},{5,6},{6,5},{7,4},{8,11},{9,10},{10,... | collective-permute-start | bytes 36872 | tf_op jit(solution)/shard_map/ppermute | solution.py:61
  19.8 2.2 %collective-permute-done.7 = f32[24,128]{1,0:T(8,128)S(1)} collective-permute-done((f32[24,128]{1,0:T(8,128)S(1)}, f32[24,128]{1,0:T(8,128)S(1)}, u32[]{:S(2)}, u32[]{:S(2)}) %collective-permute-start.7) | collective-permute-done | bytes 12320 | tf_op jit(solution)/shard_map/ppermute | solution.py:61
  21.9 0.0 collective-permute-start.8
  21.9 2.3 %collective-permute-start.9 = (f32[24,128]{1,0:T(8,128)S(1)}, f32[24,128]{1,0:T(8,128)S(1)}, u32[]{:S(2)}, u32[]{:S(2)}) collective-permute-start(f32[24,128]{1,0:T(8,128)S(1)} %add.7.refs_0_), channel_id=1, source_target_pairs={{0,9},{1,8},{4,13},{5,12},{8,1},{9,0},{12,5},{13,4},{2,11},{3,10},... | collective-permute-start | bytes 36872 | tf_op jit(solution)/shard_map/ppermute | solution.py:61
  24.2 1.2 %collective-permute-start.10 = (f32[24,128]{1,0:T(8,128)S(1)}, f32[24,128]{1,0:T(8,128)S(1)}, u32[]{:S(2)}, u32[]{:S(2)}) collective-permute-start(f32[24,128]{1,0:T(8,128)S(1)} %add.7.refs_0_), channel_id=1, source_target_pairs={{0,13},{1,12},{4,1},{5,0},{8,5},{9,4},{12,9},{13,8},{2,15},{3,14},... | collective-permute-start | bytes 36872 | tf_op jit(solution)/shard_map/ppermute | solution.py:61
  25.5 1.4 %collective-permute-done.8.refs_1_ = f32[24,128]{1,0:T(8,128)S(1)} collective-permute-done((f32[24,128]{1,0:T(8,128)S(1)}, f32[24,128]{1,0:T(8,128)S(1)}, u32[]{:S(2)}, u32[]{:S(2)}) %collective-permute-start.8) | collective-permute-done | bytes 12320 | tf_op jit(solution)/shard_map/ppermute | solution.py:61
  26.8 0.0 collective-permute-done.9.refs_2_
  26.9 0.5 %collective-permute-done.10.refs_3_ = f32[24,128]{1,0:T(8,128)S(1)} collective-permute-done((f32[24,128]{1,0:T(8,128)S(1)}, f32[24,128]{1,0:T(8,128)S(1)}, u32[]{:S(2)}, u32[]{:S(2)}) %collective-permute-start.10) | collective-permute-done | bytes 12320 | tf_op jit(solution)/shard_map/ppermute | solution.py:61
  27.4 1.4 %haydock.1 = (f32[1,2,2,16]{3,2,1,0:T(2,128)}, f32[2,6]{1,0:T(2,128)}) custom-call(f32[24,128]{1,0:T(8,128)S(1)} %add.7.refs_0_, f32[24,128]{1,0:T(8,128)S(1)} %collective-permute-done.8.refs_1_, f32[24,128]{1,0:T(8,128)S(1)} %collective-permute-done.9.refs_2_, f32[24,128]{1,0:T(8,128)S(1)} %collective-permute-done.10.refs_3_), custom_call_target="tpu_custom_call" | custom-call | tf_op jit(solution)/shard_map/haydock/pallas_call | solution.py:498
  (5 shorter events, 0.0 us)
Async XLA Ops:
  1.7 6.3 %collective-permute-start = (bf16[32,768]{1,0:T(8,128)(2,1)S(1)}, bf16[32,768]{1,0:T(8,128)(2,1)S(1)}, u32[]{:S(2)}, u32[]{:S(2)}) collective-permute-start(bf16[32,768]{1,0:T(8,128)(2,1)S(1)} %get-tuple-element.13), channel_id=1, source_target_pairs={{0,5},{1,4},{4,9},{5,8},{8,13},{9,12},{12,1},{13,0},{2,7},{3,6},{6... | collective-permute-start | bytes 147464 | tf_op jit(solution)/shard_map/ppermute | solution.py:61
  4.2 7.6 %collective-permute-start.1 = (bf16[32,768]{1,0:T(8,128)(2,1)S(1)}, bf16[32,768]{1,0:T(8,128)(2,1)S(1)}, u32[]{:S(2)}, u32[]{:S(2)}) collective-permute-start(bf16[32,768]{1,0:T(8,128)(2,1)S(1)} %get-tuple-element.18), channel_id=1, source_target_pairs={{0,9},{1,8},{4,13},{5,12},{8,1},{9,0},{12,5},{13,4},{2,11},{3,10},... | collective-permute-start | bytes 147464 | tf_op jit(solution)/shard_map/ppermute | solution.py:61
  7.1 4.7 %collective-permute-start.2 = (bf16[32,768]{1,0:T(8,128)(2,1)S(1)}, bf16[32,768]{1,0:T(8,128)(2,1)S(1)}, u32[]{:S(2)}, u32[]{:S(2)}) collective-permute-start(bf16[32,768]{1,0:T(8,128)(2,1)S(1)} %get-tuple-element.19), channel_id=1, source_target_pairs={{0,13},{1,12},{4,1},{5,0},{8,5},{9,4},{12,9},{13,8},{2,15},{3,14},... | collective-permute-start | bytes 147464 | tf_op jit(solution)/shard_map/ppermute | solution.py:61
  8.0 3.9 %collective-permute-start.3 = (bf16[32,768]{1,0:T(8,128)(2,1)S(1)}, bf16[32,768]{1,0:T(8,128)(2,1)S(1)}, u32[]{:S(2)}, u32[]{:S(2)}) collective-permute-start(bf16[32,768]{1,0:T(8,128)(2,1)S(1)} %regroup.3.refs_7_.refs_3_), channel_id=1, source_target_pairs={{0,3},{1,2},{2,1},{3,0},{4,7},{5,6},{6,5},{7,4},{8,11},{9,10},{10,... | collective-permute-start | bytes 147464 | tf_op jit(solution)/shard_map/ppermute | solution.py:61
  11.9 2.4 %collective-permute-start.4 = (bf16[64,768]{1,0:T(8,128)(2,1)S(1)}, bf16[64,768]{1,0:T(8,128)(2,1)S(1)}, u32[]{:S(2)}, u32[]{:S(2)}) collective-permute-start(bf16[64,768]{1,0:T(8,128)(2,1)S(1)} %regroup.5.refs_0_), channel_id=1, source_target_pairs={{0,1},{1,0},{2,3},{3,2},{4,5},{5,4},{6,7},{7,6},{8,9},{9,8},{10,11... | collective-permute-start | bytes 294920 | tf_op jit(solution)/shard_map/ppermute | solution.py:70
  12.4 4.7 %collective-permute-start.5 = (bf16[32,768]{1,0:T(8,128)(2,1)S(1)}, bf16[32,768]{1,0:T(8,128)(2,1)S(1)}, u32[]{:S(2)}, u32[]{:S(2)}) collective-permute-start(bf16[32,768]{1,0:T(8,128)(2,1)S(1)} %regroup.4.refs_4_), channel_id=1, source_target_pairs={{0,3},{1,2},{2,1},{3,0},{4,7},{5,6},{6,5},{7,4},{8,11},{9,10},{10,... | collective-permute-start | bytes 147464 | tf_op jit(solution)/shard_map/ppermute | solution.py:61
  17.6 1.2 %collective-permute-start.6 = (f32[24,128]{1,0:T(8,128)S(1)}, f32[24,128]{1,0:T(8,128)S(1)}, u32[]{:S(2)}, u32[]{:S(2)}) collective-permute-start(f32[24,128]{1,0:T(8,128)S(1)} %far.1), channel_id=1, source_target_pairs={{0,1},{1,0},{2,3},{3,2},{4,5},{5,4},{6,7},{7,6},{8,9},{9,8},{10,11... | collective-permute-start | bytes 36872 | tf_op jit(solution)/shard_map/ppermute | solution.py:70
  18.8 3.1 %collective-permute-start.7 = (f32[24,128]{1,0:T(8,128)S(1)}, f32[24,128]{1,0:T(8,128)S(1)}, u32[]{:S(2)}, u32[]{:S(2)}) collective-permute-start(f32[24,128]{1,0:T(8,128)S(1)} %add.6), channel_id=1, source_target_pairs={{0,3},{1,2},{2,1},{3,0},{4,7},{5,6},{6,5},{7,4},{8,11},{9,10},{10,... | collective-permute-start | bytes 36872 | tf_op jit(solution)/shard_map/ppermute | solution.py:61
  21.9 4.9 %collective-permute-start.8 = (f32[24,128]{1,0:T(8,128)S(1)}, f32[24,128]{1,0:T(8,128)S(1)}, u32[]{:S(2)}, u32[]{:S(2)}) collective-permute-start(f32[24,128]{1,0:T(8,128)S(1)} %add.7.refs_0_), channel_id=1, source_target_pairs={{0,5},{1,4},{4,9},{5,8},{8,13},{9,12},{12,1},{13,0},{2,7},{3,6},{6... | collective-permute-start | bytes 36872 | tf_op jit(solution)/shard_map/ppermute | solution.py:61
  21.9 4.9 %collective-permute-start.9 = (f32[24,128]{1,0:T(8,128)S(1)}, f32[24,128]{1,0:T(8,128)S(1)}, u32[]{:S(2)}, u32[]{:S(2)}) collective-permute-start(f32[24,128]{1,0:T(8,128)S(1)} %add.7.refs_0_), channel_id=1, source_target_pairs={{0,9},{1,8},{4,13},{5,12},{8,1},{9,0},{12,5},{13,4},{2,11},{3,10},... | collective-permute-start | bytes 36872 | tf_op jit(solution)/shard_map/ppermute | solution.py:61
  24.2 3.1 %collective-permute-start.10 = (f32[24,128]{1,0:T(8,128)S(1)}, f32[24,128]{1,0:T(8,128)S(1)}, u32[]{:S(2)}, u32[]{:S(2)}) collective-permute-start(f32[24,128]{1,0:T(8,128)S(1)} %add.7.refs_0_), channel_id=1, source_target_pairs={{0,13},{1,12},{4,1},{5,0},{8,5},{9,4},{12,9},{13,8},{2,15},{3,14},... | collective-permute-start | bytes 36872 | tf_op jit(solution)/shard_map/ppermute | solution.py:61

commit v16 on v15

--- a/solution.py
+++ b/solution.py
@@ -17,7 +17,6 @@
 anywhere = pl.BlockSpec(memory_space=pl.ANY)
 EXTRA_ROWS = 8
 LIGHT = pl.CostEstimate(flops=1, bytes_accessed=1, transcendentals=0)
-CHUNKS = 3
 
 
 def in_vmem(shape, dtype):
@@ -125,6 +124,9 @@
             pltpu.VMEM(conduction.shape, conduction.dtype),
             pltpu.SemaphoreType.DMA((4,)),
         ],
+        cost_estimate=pl.CostEstimate(
+            flops=0, bytes_accessed=4 * (valence.size + conduction.size), transcendentals=0
+        ),
         compiler_params=limits(valence, conduction),
         name="pack",
     )(*operands)
@@ -132,8 +134,8 @@
 
 def prepare_kernel(ka, dims, *refs):
     vloc, val_count, cond_count, npol = dims
-    ins, screening, (screen_out, near_table, far_table, extras), scratch = refs[:6], refs[6], refs[8:12], refs[12:]
-    qmap, owner, band_pairs, val_energy, cond_energy, start, sems, screen_sem = scratch
+    ins, (near_table, far_table, extras), scratch = refs[:6], refs[7:10], refs[10:]
+    qmap, owner, band_pairs, val_energy, cond_energy, start, sems = scratch
     me = lax.axis_index("ka")
     half = lax.axis_index("ba")
     mine = lax.axis_index("ga")
@@ -143,8 +145,7 @@
             zip(ins, (qmap, owner, band_pairs, val_energy, cond_energy, start))
         )
     ]
-    load = pltpu.make_async_copy(screening.at[0, 0], screen_out, screen_sem)
-    for copy in copies + [load]:
+    for copy in copies:
         copy.start()
     pairs = vloc * val_count
     block = 2 * pairs
@@ -201,33 +202,30 @@
     second = jnp.where(second >= kcount, second - kcount, second).astype(jnp.float32) * first
     rest = jnp.zeros((EXTRA_ROWS - 3 - npol, lanes), jnp.float32)
     extras[...] = jnp.concatenate([vectors, energy, bands * first, second, rest], 0)
-    load.wait()
-
-
-def prepare(ka, dims, qmap, owner, band_pairs, val_energy, cond_energy, start, screening, after):
+
+
+def prepare(ka, dims, qmap, owner, band_pairs, val_energy, cond_energy, start, after):
     vloc, val_count, cond_count, npol = dims
     rows = 4 * ka * vloc * val_count
     lanes = 2 * ka * val_count * cond_count
-    operands = (qmap, owner, band_pairs, val_energy, cond_energy, start, screening)
+    operands = (qmap, owner, band_pairs, val_energy, cond_energy, start)
     table = jax.ShapeDtypeStruct((rows, val_count * lanes), jnp.bfloat16)
     return pl.pallas_call(
         functools.partial(prepare_kernel, ka, dims),
         out_shape=[
-            in_vmem(screening.shape[2:], screening.dtype),
             in_vmem(table.shape, table.dtype),
             in_vmem(table.shape, table.dtype),
             in_vmem((EXTRA_ROWS, lanes), jnp.float32),
         ],
-        in_specs=[anywhere] * 8,
-        out_specs=[vmem] * 4,
+        in_specs=[anywhere] * 7,
+        out_specs=[vmem] * 3,
         scratch_shapes=[pltpu.SMEM(x.shape, x.dtype) for x in operands[:5]]
         + [
             pltpu.VMEM(start.shape, start.dtype),
             pltpu.SemaphoreType.DMA((6,)),
-            pltpu.SemaphoreType.DMA,
         ],
         cost_estimate=pl.CostEstimate(
-            flops=0, bytes_accessed=2 * screening.size, transcendentals=0
+            flops=0, bytes_accessed=4 * math.prod(table.shape), transcendentals=0
         ),
         compiler_params=limits(table),
         name="prepare",
@@ -314,16 +312,8 @@
     return jnp.concatenate(kernel, 0)
 
 
-def couple_kernel(ka, ga, ba, share_rows, screen_real, screening, *refs):
-    cond_in, outs, (screen_imag, sems) = refs[:ba], refs[ba:-2], refs[-2:]
-    height = screen_imag.shape[0] // CHUNKS
-    chunks = [pl.ds(c * height, height) for c in range(CHUNKS)]
-    loads = [
-        pltpu.make_async_copy(screening.at[0, 1, chunk], screen_imag.at[chunk], sems.at[c])
-        for c, chunk in enumerate(chunks)
-    ]
-    for load in loads:
-        load.start()
+def couple_kernel(ka, ga, ba, share_rows, screening, *refs):
+    cond_in, outs = refs[:ba], refs[ba:]
     mine = lax.axis_index("ga")
     wide = jnp.concatenate([ref[...].astype(jnp.float32) for ref in cond_in], 0)
     straight, turned = [], []
@@ -333,42 +323,32 @@
         turned += [imag, real]
     straight = jnp.concatenate(straight, 0).astype(jnp.bfloat16)
     turned = jnp.concatenate(turned, 0).astype(jnp.bfloat16)
-    width = screen_imag.shape[1] // ga
+    width = screening.shape[3] // ga
     columns = [columns_of(origin(mine, r, ga), width) for r in range(ga)]
     coupled = [
-        jnp.dot(straight, screen_real[:, block], preferred_element_type=jnp.float32) for block in columns
+        jnp.dot(straight, screening[0, 0, :, block], preferred_element_type=jnp.float32)
+        + jnp.dot(turned, screening[0, 1, :, block], preferred_element_type=jnp.float32)
+        for block in columns
     ]
-    for c, load in enumerate(loads):
-        load.wait()
-        part = turned[:, c * height : (c + 1) * height]
-        for r, block in enumerate(columns):
-            coupled[r] = coupled[r] + jnp.dot(
-                part, screen_imag[chunks[c], block], preferred_element_type=jnp.float32
-            )
     for out, value in zip(outs, coupled):
         high, low = split(value)
         out[: value.shape[0], :] = high
         out[value.shape[0] :, :] = low
 
 
-def couple(ka, ga, ba, dims, screen_real, screening, cond_all):
+def couple(ka, ga, ba, dims, screening, cond_all):
     share_rows = dims[2] // ba * dims[2]
     rows = 2 * sum(x.shape[0] for x in cond_all)
-    width = screen_real.shape[1] // ga
-    operands = [screen_real, *cond_all]
+    width = screening.shape[3] // ga
     return pl.pallas_call(
         functools.partial(couple_kernel, ka, ga, ba, share_rows),
         out_shape=[in_vmem((rows, width), jnp.bfloat16)] * ga,
-        in_specs=[vmem, anywhere] + [vmem] * len(cond_all),
+        in_specs=[vmem] * (1 + len(cond_all)),
         out_specs=[vmem] * ga,
-        scratch_shapes=[
-            pltpu.VMEM(screen_real.shape, screen_real.dtype),
-            pltpu.SemaphoreType.DMA((CHUNKS,)),
-        ],
         cost_estimate=LIGHT,
-        compiler_params=limits(*operands),
+        compiler_params=limits(*cond_all),
         name="couple",
-    )(screen_real, placed(screening, pltpu.HBM), *cond_all)
+    )(placed(screening, pltpu.VMEM), *cond_all)
 
 
 def contract_kernel(ka, ba, count, dims, *refs):
@@ -540,12 +520,13 @@
     cond_count = conduction_density.shape[3]
     pairs = vloc * val_count
     dims = (vloc, val_count, cond_count, npol)
+    screening = lax.ppermute(screening, "ba", [(h, h) for h in range(ba)])
     packed = pack(ka, ba, qpoint_map, slot_owner, valence_density, conduction_density)
     blocks = [packed[0]] + [shifted(packed[j], "ka", j) for j in range(1, ka)]
     early = ka // 2
     val_early = regroup(blocks[:early], 0, 2 * pairs)
     far_early = [shifted(val_early, "ga", r) for r in range(1, ga)]
-    real, near_table, far_table, extras = prepare(
+    near_table, far_table, extras = prepare(
         ka,
         dims,
         qpoint_map,
@@ -554,14 +535,13 @@
         valence_energy,
         conduction_energy,
         start_vector,
-        screening,
         val_early,
     )
     val_late = regroup(blocks[early:], 0, 2 * pairs, (extras,))
     far_late = [shifted(val_late, "ga", r) for r in range(1, ga)]
     cond_half = regroup(blocks, 2 * pairs, blocks[0].shape[0], (val_late, *far_early))
     cond_all = [cond_half] + [handed(cond_half, r) for r in range(1, ba)]
-    coupled = couple(ka, ga, ba, dims, real, screening, cond_all)
+    coupled = couple(ka, ga, ba, dims, screening, cond_all)
     near = [val_early, val_late]
     piece = contract(ka, ba, dims, near_table, extras, coupled[:1], near, "near")
     if ga > 1:

time: 29 us -> 30.5 us (1.052)
  starting transfers between devices: 15.2 us -> 18.3 us
  Pallas kernels: 7.59 us -> 5.31 us
  waiting for transfers between devices: 5.27 us -> 6.07 us
    ppermute x0 -> x1, starting transfers between devices: none -> 2.34 us  [local(): screening = lax.ppermute(screening, 'ba', [(h, h) for h in range(ba)])]
    pallas_call x1, Pallas kernels: 2.29 us -> 0.83 us  [couple(): pl.pallas_call(functools.partial(couple_kernel, ka, ga, ba, share_rows),...]
    pallas_call x1, Pallas kernels: 1.75 us -> 0.95 us  [prepare(): pl.pallas_call(functools.partial(prepare_kernel, ka, dims), out_shape=[in...]
    ppermute x9, waiting for transfers between devices: 4.24 us -> 5.02 us  [exchanged(): return lax.ppermute(value, (axis, 'ba'), pairs)]
    ppermute x9, starting transfers between devices: 14.5 us -> 15.3 us  [exchanged(): return lax.ppermute(value, (axis, 'ba'), pairs)]
  transfers between devices with their start and end apart: 11 -> 12, of which waited for: 5 -> 8; matrix products, arithmetic and copies ran while one was open for 0% -> 0% of each run, Pallas kernels for 16% -> 11%
where the time goes in v16:
time: 30.5 us; the launch traced here: 30.3 us
  starting transfers between devices  18.3 us (60%)
  waiting for transfers between devices  6.07 us (20%)
  Pallas kernels  5.31 us (17%)
  between operations  0.68 us (2%)
    ppermute x9, starting transfers between devices, exchanged(): return lax.ppermute(value, (axis, 'ba'), pairs)  15.3 us
    ppermute x9, waiting for transfers between devices, exchanged(): return lax.ppermute(value, (axis, 'ba'), pairs)  5.02 us
    ppermute x1, starting transfers between devices, local(): screening = lax.ppermute(screening, 'ba', [(h, h) for h in range(ba)])  2.34 us
    pallas_call x1, Pallas kernels, haydock(): pl.pallas_call(functools.partial(haydock_kernel, ka, codes, scale_count,...  1.41 us
    pallas_call x2, Pallas kernels, contract(): pl.pallas_call(functools.partial(contract_kernel, ka, ba, len(coupled), d...  1.07 us
    ppermute x2, waiting for transfers between devices, handed(): lax.ppermute(value, 'ba', [(h, (h + step) % size) for h in range(size)])  1.05 us
    pallas_call x1, Pallas kernels, pack(): pl.pallas_call(functools.partial(pack_kernel, ka), out_shape=[shape] * ka...  1.04 us
    pallas_call x1, Pallas kernels, prepare(): pl.pallas_call(functools.partial(prepare_kernel, ka, dims), out_shape=[in...  0.95 us
  transfers between devices with their start and end apart: 12, of which 8 were waited for; matrix products, arithmetic and copies ran while one was open for 0% of the time, Pallas kernels for 11%

profile of v16, /device:TPU:0, one launch (start us, length us, event | category | flops | bytes accessed | tf_op | source)
XLA Modules:
  0.0 30.3 jit_solution(11181548927803496456)
XLA Ops:
  0.6 2.3 %collective-permute-start.1 = (bf16[1,2,768,1536]{3,2,1,0:T(8,128)(2,1)}, bf16[1,2,768,1536]{3,2,1,0:T(8,128)(2,1)S(1)}, u32[]{:S(2)}, u32[]{:S(2)}) collective-permute-start(bf16[1,2,768,1536]{3,2,1,0:T(8,128)(2,1)} %param.12), channel_id=1, source_target_pairs={{0,0},{1,1},{2,2},{3,3},{4,4},{5,5},{6,6},{7,7},{8,8},{9,9},{10,10... | collective-permute-start | bytes 14155784 | tf_op jit(solution)/shard_map/ppermute | solution.py:523
  3.0 1.0 %pack.1 = (bf16[32,768]{1,0:T(8,128)(2,1)S(1)}, bf16[32,768]{1,0:T(8,128)(2,1)S(1)}, bf16[32,768]{1,0:T(8,128)(2,1)S(1)}, bf16[32,768]{1,0:T(8,128)(2,1)S(1)}) custom-call(s32[4,4]{1,0:T(4,128)} %refs_0_.1, s32[4]{0:T(128)} %refs_1_.1, bf16[1,4,2,2,4,768]{5,4,3,2,1,0:T(4,128)(2,1)} %valence_in.1, bf16[1,4,2,4,4,768]{5,4,3,2,1,0:T(4,128)(2,1)} %conduction_in.1), custom_call_target="tpu_custom_call" | custom-call | bytes 589824 | tf_op jit(solution)/shard_map/pack/pallas_call | solution.py:114
  4.0 2.5 %collective-permute-start = (bf16[32,768]{1,0:T(8,128)(2,1)S(1)}, bf16[32,768]{1,0:T(8,128)(2,1)S(1)}, u32[]{:S(2)}, u32[]{:S(2)}) collective-permute-start(bf16[32,768]{1,0:T(8,128)(2,1)S(1)} %get-tuple-element.12), channel_id=1, source_target_pairs={{0,5},{1,4},{4,9},{5,8},{8,13},{9,12},{12,1},{13,0},{2,7},{3,6},{6... | collective-permute-start | bytes 147464 | tf_op jit(solution)/shard_map/ppermute | solution.py:60
  6.5 2.9 %collective-permute-start.2 = (bf16[32,768]{1,0:T(8,128)(2,1)S(1)}, bf16[32,768]{1,0:T(8,128)(2,1)S(1)}, u32[]{:S(2)}, u32[]{:S(2)}) collective-permute-start(bf16[32,768]{1,0:T(8,128)(2,1)S(1)} %get-tuple-element.16), channel_id=1, source_target_pairs={{0,9},{1,8},{4,13},{5,12},{8,1},{9,0},{12,5},{13,4},{2,11},{3,10},... | collective-permute-start | bytes 147464 | tf_op jit(solution)/shard_map/ppermute | solution.py:60
  9.4 0.8 %collective-permute-start.3 = (bf16[32,768]{1,0:T(8,128)(2,1)S(1)}, bf16[32,768]{1,0:T(8,128)(2,1)S(1)}, u32[]{:S(2)}, u32[]{:S(2)}) collective-permute-start(bf16[32,768]{1,0:T(8,128)(2,1)S(1)} %get-tuple-element.17), channel_id=1, source_target_pairs={{0,13},{1,12},{4,1},{5,0},{8,5},{9,4},{12,9},{13,8},{2,15},{3,14},... | collective-permute-start | bytes 147464 | tf_op jit(solution)/shard_map/ppermute | solution.py:60
  10.2 0.1 collective-permute-done.refs_1_
  10.3 2.0 %collective-permute-start.4 = (bf16[32,768]{1,0:T(8,128)(2,1)S(1)}, bf16[32,768]{1,0:T(8,128)(2,1)S(1)}, u32[]{:S(2)}, u32[]{:S(2)}) collective-permute-start(bf16[32,768]{1,0:T(8,128)(2,1)S(1)} %regroup.3.refs_6_.refs_3_), channel_id=1, source_target_pairs={{0,3},{1,2},{2,1},{3,0},{4,7},{5,6},{6,5},{7,4},{8,11},{9,10},{10,... | collective-permute-start | bytes 147464 | tf_op jit(solution)/shard_map/ppermute | solution.py:60
  12.4 1.0 %prepare.1 = (bf16[128,512]{1,0:T(8,128)(2,1)S(1)}, bf16[128,512]{1,0:T(8,128)(2,1)S(1)}, f32[8,128]{1,0:T(8,128)S(1)}) custom-call(s32[4,4]{1,0:T(4,128)} %refs_0_.1, s32[4]{0:T(128)} %refs_1_.1, s32[16]{0:T(128)} %refs_2_.1, f32[1,4]{1,0:T(1,128)} %refs_3_.1, f32[1,4]{1,0:T(1,128)} %refs_4_.1, f32[1,2,2,16]{3,2,1,0:T(2,128)} %refs_5_.1, ...), custom_call_target="tpu_custom_call" | custom-call | bytes 262144 | tf_op jit(solution)/shard_map/prepare/pallas_call | solution.py:213
  13.3 0.0 collective-permute-done.2.refs_0_.refs_2_
  13.3 0.5 %collective-permute-done.3.refs_1_.refs_3_ = bf16[32,768]{1,0:T(8,128)(2,1)S(1)} collective-permute-done((bf16[32,768]{1,0:T(8,128)(2,1)S(1)}, bf16[32,768]{1,0:T(8,128)(2,1)S(1)}, u32[]{:S(2)}, u32[]{:S(2)}) %collective-permute-start.3) | collective-permute-done | bytes 49184 | tf_op jit(solution)/shard_map/ppermute | solution.py:60
  13.9 0.3 %collective-permute-done.4.refs_5_.refs_3_ = bf16[32,768]{1,0:T(8,128)(2,1)S(1)} collective-permute-done((bf16[32,768]{1,0:T(8,128)(2,1)S(1)}, bf16[32,768]{1,0:T(8,128)(2,1)S(1)}, u32[]{:S(2)}, u32[]{:S(2)}) %collective-permute-start.4) | collective-permute-done | bytes 49184 | tf_op jit(solution)/shard_map/ppermute | solution.py:60
  14.2 0.5 %collective-permute-start.5 = (bf16[64,768]{1,0:T(8,128)(2,1)S(1)}, bf16[64,768]{1,0:T(8,128)(2,1)S(1)}, u32[]{:S(2)}, u32[]{:S(2)}) collective-permute-start(bf16[64,768]{1,0:T(8,128)(2,1)S(1)} %regroup.5.refs_0_), channel_id=1, source_target_pairs={{0,1},{1,0},{2,3},{3,2},{4,5},{5,4},{6,7},{7,6},{8,9},{9,8},{10,11... | collective-permute-start | bytes 294920 | tf_op jit(solution)/shard_map/ppermute | solution.py:69
  14.7 1.8 %collective-permute-start.6 = (bf16[32,768]{1,0:T(8,128)(2,1)S(1)}, bf16[32,768]{1,0:T(8,128)(2,1)S(1)}, u32[]{:S(2)}, u32[]{:S(2)}) collective-permute-start(bf16[32,768]{1,0:T(8,128)(2,1)S(1)} %regroup.4.refs_4_), channel_id=1, source_target_pairs={{0,3},{1,2},{2,1},{3,0},{4,7},{5,6},{6,5},{7,4},{8,11},{9,10},{10,... | collective-permute-start | bytes 147464 | tf_op jit(solution)/shard_map/ppermute | solution.py:60
  16.6 0.0 collective-permute-done.5.refs_1_
  16.6 0.0 collective-permute-done.1.screening
  16.6 0.8 %couple.1 = (bf16[256,768]{1,0:T(8,128)(2,1)S(1)}, bf16[256,768]{1,0:T(8,128)(2,1)S(1)}) custom-call(bf16[1,2,768,1536]{3,2,1,0:T(8,128)(2,1)S(1)} %collective-permute-done.1.screening, bf16[64,768]{1,0:T(8,128)(2,1)S(1)} %regroup.5.refs_0_, bf16[64,768]{1,0:T(8,128)(2,1)S(1)} %collective-permute-done.5.refs_1_), custom_call_target="tpu_custom_call" | custom-call | flops 1 | bytes 1 | tf_op jit(solution)/shard_map/couple/pallas_call | solution.py:343
  17.4 0.5 %near.1.refs_1_ = f32[24,128]{1,0:T(8,128)S(1)} custom-call(bf16[128,512]{1,0:T(8,128)(2,1)S(1)} %get-tuple-element.14.refs_0_, f32[8,128]{1,0:T(8,128)S(1)} %get-tuple-element.15.refs_2_.refs_1_, bf16[256,768]{1,0:T(8,128)(2,1)S(1)} %get-tuple-element.18.refs_2_, bf16[32,768]{1,0:T(8,128)(2,1)S(1)} %regroup.3.refs_6_.refs_3_, ...), custom_call_target="tpu_custom_call" | custom-call | flops 1 | bytes 1 | tf_op jit(solution)/shard_map/near/pallas_call | solution.py:381
  17.9 0.6 %collective-permute-done.6.refs_4_ = bf16[32,768]{1,0:T(8,128)(2,1)S(1)} collective-permute-done((bf16[32,768]{1,0:T(8,128)(2,1)S(1)}, bf16[32,768]{1,0:T(8,128)(2,1)S(1)}, u32[]{:S(2)}, u32[]{:S(2)}) %collective-permute-start.6) | collective-permute-done | bytes 49184 | tf_op jit(solution)/shard_map/ppermute | solution.py:60
  18.5 0.5 %far.1 = f32[24,128]{1,0:T(8,128)S(1)} custom-call(bf16[128,512]{1,0:T(8,128)(2,1)S(1)} %get-tuple-element.13.refs_0_, f32[24,128]{1,0:T(8,128)S(1)} %near.1.refs_1_, bf16[256,768]{1,0:T(8,128)(2,1)S(1)} %get-tuple-element.19.refs_2_, bf16[32,768]{1,0:T(8,128)(2,1)S(1)} %collective-permute-done.4.refs_5_.refs_3_, ...), custom_call_target="tpu_custom_call" | custom-call | flops 1 | bytes 1 | tf_op jit(solution)/shard_map/far/pallas_call | solution.py:381
  19.1 0.1 collective-permute-start.7
  19.2 1.0 %collective-permute-done.7 = f32[24,128]{1,0:T(8,128)S(1)} collective-permute-done((f32[24,128]{1,0:T(8,128)S(1)}, f32[24,128]{1,0:T(8,128)S(1)}, u32[]{:S(2)}, u32[]{:S(2)}) %collective-permute-start.7) | collective-permute-done | bytes 12320 | tf_op jit(solution)/shard_map/ppermute | solution.py:69
  20.3 1.5 %collective-permute-start.8 = (f32[24,128]{1,0:T(8,128)S(1)}, f32[24,128]{1,0:T(8,128)S(1)}, u32[]{:S(2)}, u32[]{:S(2)}) collective-permute-start(f32[24,128]{1,0:T(8,128)S(1)} %add.6), channel_id=1, source_target_pairs={{0,3},{1,2},{2,1},{3,0},{4,7},{5,6},{6,5},{7,4},{8,11},{9,10},{10,... | collective-permute-start | bytes 36872 | tf_op jit(solution)/shard_map/ppermute | solution.py:60
  21.8 1.6 %collective-permute-done.8 = f32[24,128]{1,0:T(8,128)S(1)} collective-permute-done((f32[24,128]{1,0:T(8,128)S(1)}, f32[24,128]{1,0:T(8,128)S(1)}, u32[]{:S(2)}, u32[]{:S(2)}) %collective-permute-start.8) | collective-permute-done | bytes 12320 | tf_op jit(solution)/shard_map/ppermute | solution.py:60
  23.4 0.2 collective-permute-start.9
  23.6 2.2 %collective-permute-start.10 = (f32[24,128]{1,0:T(8,128)S(1)}, f32[24,128]{1,0:T(8,128)S(1)}, u32[]{:S(2)}, u32[]{:S(2)}) collective-permute-start(f32[24,128]{1,0:T(8,128)S(1)} %add.7.refs_0_), channel_id=1, source_target_pairs={{0,9},{1,8},{4,13},{5,12},{8,1},{9,0},{12,5},{13,4},{2,11},{3,10},... | collective-permute-start | bytes 36872 | tf_op jit(solution)/shard_map/ppermute | solution.py:60
  25.8 1.3 %collective-permute-start.11 = (f32[24,128]{1,0:T(8,128)S(1)}, f32[24,128]{1,0:T(8,128)S(1)}, u32[]{:S(2)}, u32[]{:S(2)}) collective-permute-start(f32[24,128]{1,0:T(8,128)S(1)} %add.7.refs_0_), channel_id=1, source_target_pairs={{0,13},{1,12},{4,1},{5,0},{8,5},{9,4},{12,9},{13,8},{2,15},{3,14},... | collective-permute-start | bytes 36872 | tf_op jit(solution)/shard_map/ppermute | solution.py:60
  27.1 1.2 %collective-permute-done.9.refs_1_ = f32[24,128]{1,0:T(8,128)S(1)} collective-permute-done((f32[24,128]{1,0:T(8,128)S(1)}, f32[24,128]{1,0:T(8,128)S(1)}, u32[]{:S(2)}, u32[]{:S(2)}) %collective-permute-start.9) | collective-permute-done | bytes 12320 | tf_op jit(solution)/shard_map/ppermute | solution.py:60
  28.3 0.0 collective-permute-done.10.refs_2_
  28.3 0.6 %collective-permute-done.11.refs_3_ = f32[24,128]{1,0:T(8,128)S(1)} collective-permute-done((f32[24,128]{1,0:T(8,128)S(1)}, f32[24,128]{1,0:T(8,128)S(1)}, u32[]{:S(2)}, u32[]{:S(2)}) %collective-permute-start.11) | collective-permute-done | bytes 12320 | tf_op jit(solution)/shard_map/ppermute | solution.py:60
  28.9 1.4 %haydock.1 = (f32[1,2,2,16]{3,2,1,0:T(2,128)}, f32[2,6]{1,0:T(2,128)}) custom-call(f32[24,128]{1,0:T(8,128)S(1)} %add.7.refs_0_, f32[24,128]{1,0:T(8,128)S(1)} %collective-permute-done.9.refs_1_, f32[24,128]{1,0:T(8,128)S(1)} %collective-permute-done.10.refs_2_, f32[24,128]{1,0:T(8,128)S(1)} %collective-permute-done.11.refs_3_), custom_call_target="tpu_custom_call" | custom-call | tf_op jit(solution)/shard_map/haydock/pallas_call | solution.py:478
  (5 shorter events, 0.0 us)
Async XLA Ops:
  0.6 15.9 %collective-permute-start.1 = (bf16[1,2,768,1536]{3,2,1,0:T(8,128)(2,1)}, bf16[1,2,768,1536]{3,2,1,0:T(8,128)(2,1)S(1)}, u32[]{:S(2)}, u32[]{:S(2)}) collective-permute-start(bf16[1,2,768,1536]{3,2,1,0:T(8,128)(2,1)} %param.12), channel_id=1, source_target_pairs={{0,0},{1,1},{2,2},{3,3},{4,4},{5,5},{6,6},{7,7},{8,8},{9,9},{10,10... | collective-permute-start | bytes 14155784 | tf_op jit(solution)/shard_map/ppermute | solution.py:523
  4.0 6.3 %collective-permute-start = (bf16[32,768]{1,0:T(8,128)(2,1)S(1)}, bf16[32,768]{1,0:T(8,128)(2,1)S(1)}, u32[]{:S(2)}, u32[]{:S(2)}) collective-permute-start(bf16[32,768]{1,0:T(8,128)(2,1)S(1)} %get-tuple-element.12), channel_id=1, source_target_pairs={{0,5},{1,4},{4,9},{5,8},{8,13},{9,12},{12,1},{13,0},{2,7},{3,6},{6... | collective-permute-start | bytes 147464 | tf_op jit(solution)/shard_map/ppermute | solution.py:60
  6.5 6.8 %collective-permute-start.2 = (bf16[32,768]{1,0:T(8,128)(2,1)S(1)}, bf16[32,768]{1,0:T(8,128)(2,1)S(1)}, u32[]{:S(2)}, u32[]{:S(2)}) collective-permute-start(bf16[32,768]{1,0:T(8,128)(2,1)S(1)} %get-tuple-element.16), channel_id=1, source_target_pairs={{0,9},{1,8},{4,13},{5,12},{8,1},{9,0},{12,5},{13,4},{2,11},{3,10},... | collective-permute-start | bytes 147464 | tf_op jit(solution)/shard_map/ppermute | solution.py:60
  9.4 4.4 %collective-permute-start.3 = (bf16[32,768]{1,0:T(8,128)(2,1)S(1)}, bf16[32,768]{1,0:T(8,128)(2,1)S(1)}, u32[]{:S(2)}, u32[]{:S(2)}) collective-permute-start(bf16[32,768]{1,0:T(8,128)(2,1)S(1)} %get-tuple-element.17), channel_id=1, source_target_pairs={{0,13},{1,12},{4,1},{5,0},{8,5},{9,4},{12,9},{13,8},{2,15},{3,14},... | collective-permute-start | bytes 147464 | tf_op jit(solution)/shard_map/ppermute | solution.py:60
  10.3 3.9 %collective-permute-start.4 = (bf16[32,768]{1,0:T(8,128)(2,1)S(1)}, bf16[32,768]{1,0:T(8,128)(2,1)S(1)}, u32[]{:S(2)}, u32[]{:S(2)}) collective-permute-start(bf16[32,768]{1,0:T(8,128)(2,1)S(1)} %regroup.3.refs_6_.refs_3_), channel_id=1, source_target_pairs={{0,3},{1,2},{2,1},{3,0},{4,7},{5,6},{6,5},{7,4},{8,11},{9,10},{10,... | collective-permute-start | bytes 147464 | tf_op jit(solution)/shard_map/ppermute | solution.py:60
  14.2 2.4 %collective-permute-start.5 = (bf16[64,768]{1,0:T(8,128)(2,1)S(1)}, bf16[64,768]{1,0:T(8,128)(2,1)S(1)}, u32[]{:S(2)}, u32[]{:S(2)}) collective-permute-start(bf16[64,768]{1,0:T(8,128)(2,1)S(1)} %regroup.5.refs_0_), channel_id=1, source_target_pairs={{0,1},{1,0},{2,3},{3,2},{4,5},{5,4},{6,7},{7,6},{8,9},{9,8},{10,11... | collective-permute-start | bytes 294920 | tf_op jit(solution)/shard_map/ppermute | solution.py:69
  14.7 3.8 %collective-permute-start.6 = (bf16[32,768]{1,0:T(8,128)(2,1)S(1)}, bf16[32,768]{1,0:T(8,128)(2,1)S(1)}, u32[]{:S(2)}, u32[]{:S(2)}) collective-permute-start(bf16[32,768]{1,0:T(8,128)(2,1)S(1)} %regroup.4.refs_4_), channel_id=1, source_target_pairs={{0,3},{1,2},{2,1},{3,0},{4,7},{5,6},{6,5},{7,4},{8,11},{9,10},{10,... | collective-permute-start | bytes 147464 | tf_op jit(solution)/shard_map/ppermute | solution.py:60
  19.1 1.2 %collective-permute-start.7 = (f32[24,128]{1,0:T(8,128)S(1)}, f32[24,128]{1,0:T(8,128)S(1)}, u32[]{:S(2)}, u32[]{:S(2)}) collective-permute-start(f32[24,128]{1,0:T(8,128)S(1)} %far.1), channel_id=1, source_target_pairs={{0,1},{1,0},{2,3},{3,2},{4,5},{5,4},{6,7},{7,6},{8,9},{9,8},{10,11... | collective-permute-start | bytes 36872 | tf_op jit(solution)/shard_map/ppermute | solution.py:69
  20.3 3.1 %collective-permute-start.8 = (f32[24,128]{1,0:T(8,128)S(1)}, f32[24,128]{1,0:T(8,128)S(1)}, u32[]{:S(2)}, u32[]{:S(2)}) collective-permute-start(f32[24,128]{1,0:T(8,128)S(1)} %add.6), channel_id=1, source_target_pairs={{0,3},{1,2},{2,1},{3,0},{4,7},{5,6},{6,5},{7,4},{8,11},{9,10},{10,... | collective-permute-start | bytes 36872 | tf_op jit(solution)/shard_map/ppermute | solution.py:60
  23.4 4.9 %collective-permute-start.9 = (f32[24,128]{1,0:T(8,128)S(1)}, f32[24,128]{1,0:T(8,128)S(1)}, u32[]{:S(2)}, u32[]{:S(2)}) collective-permute-start(f32[24,128]{1,0:T(8,128)S(1)} %add.7.refs_0_), channel_id=1, source_target_pairs={{0,5},{1,4},{4,9},{5,8},{8,13},{9,12},{12,1},{13,0},{2,7},{3,6},{6... | collective-permute-start | bytes 36872 | tf_op jit(solution)/shard_map/ppermute | solution.py:60
  23.6 4.7 %collective-permute-start.10 = (f32[24,128]{1,0:T(8,128)S(1)}, f32[24,128]{1,0:T(8,128)S(1)}, u32[]{:S(2)}, u32[]{:S(2)}) collective-permute-start(f32[24,128]{1,0:T(8,128)S(1)} %add.7.refs_0_), channel_id=1, source_target_pairs={{0,9},{1,8},{4,13},{5,12},{8,1},{9,0},{12,5},{13,4},{2,11},{3,10},... | collective-permute-start | bytes 36872 | tf_op jit(solution)/shard_map/ppermute | solution.py:60
  25.8 3.1 %collective-permute-start.11 = (f32[24,128]{1,0:T(8,128)S(1)}, f32[24,128]{1,0:T(8,128)S(1)}, u32[]{:S(2)}, u32[]{:S(2)}) collective-permute-start(f32[24,128]{1,0:T(8,128)S(1)} %add.7.refs_0_), channel_id=1, source_target_pairs={{0,13},{1,12},{4,1},{5,0},{8,5},{9,4},{12,9},{13,8},{2,15},{3,14},... | collective-permute-start | bytes 36872 | tf_op jit(solution)/shard_map/ppermute | solution.py:60

commit v17 on v16

--- a/solution.py
+++ b/solution.py
@@ -17,6 +17,8 @@
 anywhere = pl.BlockSpec(memory_space=pl.ANY)
 EXTRA_ROWS = 8
 LIGHT = pl.CostEstimate(flops=1, bytes_accessed=1, transcendentals=0)
+CHUNKS = 4
+PARTS = 2
 
 
 def in_vmem(shape, dtype):
@@ -103,17 +105,24 @@
         outs[at][:val_rows, :] = block.astype(jnp.bfloat16)
         to = lax.rem(half + min(at, 1), lax.axis_size("ba"))
         block = conduction[0, k2, :, pl.ds(to * share, share)].astype(jnp.float32)
-        outs[at][val_rows:, :] = block.reshape(cond_rows, width).astype(jnp.bfloat16)
+        outs[at][val_rows : val_rows + cond_rows, :] = block.reshape(cond_rows, width).astype(jnp.bfloat16)
+    cores = lax.axis_size("ba")
+    for h in range(1, cores):
+        part = lax.rem(half + cores - h, cores)
+        block = conduction[0, partner[me], :, pl.ds(part * share, share)].astype(jnp.float32)
+        rows = slice(val_rows + h * cond_rows, val_rows + (h + 1) * cond_rows)
+        outs[0][rows, :] = block.reshape(cond_rows, width).astype(jnp.bfloat16)
 
 
 def pack(ka, ba, qmap, owner, valence, conduction):
     cond_count = conduction.shape[3]
-    rows = 2 * valence.shape[3] * valence.shape[4] + 2 * cond_count // ba * cond_count
-    shape = in_vmem((rows, valence.shape[5]), valence.dtype)
+    val_rows, cond_rows = 2 * valence.shape[3] * valence.shape[4], 2 * cond_count // ba * cond_count
+    own = in_vmem((val_rows + ba * cond_rows, valence.shape[5]), valence.dtype)
+    shape = in_vmem((val_rows + cond_rows, valence.shape[5]), valence.dtype)
     operands = [placed(x, pltpu.HBM) for x in (qmap, owner, valence, conduction)]
     return pl.pallas_call(
         functools.partial(pack_kernel, ka),
-        out_shape=[shape] * ka,
+        out_shape=[own] + [shape] * (ka - 1),
         in_specs=[anywhere] * 4,
         out_specs=[vmem] * ka,
         scratch_shapes=[
@@ -124,9 +133,6 @@
             pltpu.VMEM(conduction.shape, conduction.dtype),
             pltpu.SemaphoreType.DMA((4,)),
         ],
-        cost_estimate=pl.CostEstimate(
-            flops=0, bytes_accessed=4 * (valence.size + conduction.size), transcendentals=0
-        ),
         compiler_params=limits(valence, conduction),
         name="pack",
     )(*operands)
@@ -134,8 +140,8 @@
 
 def prepare_kernel(ka, dims, *refs):
     vloc, val_count, cond_count, npol = dims
-    ins, (near_table, far_table, extras), scratch = refs[:6], refs[7:10], refs[10:]
-    qmap, owner, band_pairs, val_energy, cond_energy, start, sems = scratch
+    ins, screening, (screen_out, near_table, far_table, extras), scratch = refs[:6], refs[6], refs[8:12], refs[12:]
+    qmap, owner, band_pairs, val_energy, cond_energy, start, sems, screen_sems = scratch
     me = lax.axis_index("ka")
     half = lax.axis_index("ba")
     mine = lax.axis_index("ga")
@@ -145,7 +151,17 @@
             zip(ins, (qmap, owner, band_pairs, val_energy, cond_energy, start))
         )
     ]
-    for copy in copies:
+    height = screening.shape[2] // CHUNKS
+    chunks = [
+        pltpu.make_async_copy(
+            screening.at[0, part, pl.ds(c * height, height)],
+            screen_out.at[part, pl.ds(c * height, height)],
+            screen_sems.at[part, c],
+        )
+        for part in range(2)
+        for c in range(CHUNKS)
+    ]
+    for copy in copies + chunks:
         copy.start()
     pairs = vloc * val_count
     block = 2 * pairs
@@ -202,53 +218,79 @@
     second = jnp.where(second >= kcount, second - kcount, second).astype(jnp.float32) * first
     rest = jnp.zeros((EXTRA_ROWS - 3 - npol, lanes), jnp.float32)
     extras[...] = jnp.concatenate([vectors, energy, bands * first, second, rest], 0)
-
-
-def prepare(ka, dims, qmap, owner, band_pairs, val_energy, cond_energy, start, after):
+    for copy in chunks:
+        copy.wait()
+
+
+def prepare(ka, dims, qmap, owner, band_pairs, val_energy, cond_energy, start, screening, after):
     vloc, val_count, cond_count, npol = dims
     rows = 4 * ka * vloc * val_count
     lanes = 2 * ka * val_count * cond_count
-    operands = (qmap, owner, band_pairs, val_energy, cond_energy, start)
+    operands = (qmap, owner, band_pairs, val_energy, cond_energy, start, screening)
     table = jax.ShapeDtypeStruct((rows, val_count * lanes), jnp.bfloat16)
     return pl.pallas_call(
         functools.partial(prepare_kernel, ka, dims),
         out_shape=[
+            in_vmem(screening.shape[1:], screening.dtype),
             in_vmem(table.shape, table.dtype),
             in_vmem(table.shape, table.dtype),
             in_vmem((EXTRA_ROWS, lanes), jnp.float32),
         ],
-        in_specs=[anywhere] * 7,
-        out_specs=[vmem] * 3,
+        in_specs=[anywhere] * 8,
+        out_specs=[vmem] * 4,
         scratch_shapes=[pltpu.SMEM(x.shape, x.dtype) for x in operands[:5]]
         + [
             pltpu.VMEM(start.shape, start.dtype),
             pltpu.SemaphoreType.DMA((6,)),
+            pltpu.SemaphoreType.DMA((2, CHUNKS)),
         ],
         cost_estimate=pl.CostEstimate(
-            flops=0, bytes_accessed=4 * math.prod(table.shape), transcendentals=0
+            flops=0, bytes_accessed=4 * screening.size, transcendentals=0
         ),
         compiler_params=limits(table),
         name="prepare",
     )(*[placed(x, pltpu.HBM) for x in operands], after)
 
 
-def regroup_kernel(count, first, last, *refs):
+def regroup_kernel(count, rows, columns, *refs):
     blocks, out = refs[:count], refs[-1]
-    rows = last - first
+    height = rows.stop - rows.start
     for at in range(count):
-        out[at * rows : (at + 1) * rows, :] = blocks[at][first:last, :]
-
-
-def regroup(blocks, first, last, after=()):
-    shape = (len(blocks) * (last - first), blocks[0].shape[1])
+        out[at * height : (at + 1) * height, :] = blocks[at][rows, columns]
+
+
+def regroup(blocks, rows, after=(), columns=None):
+    columns = columns or slice(0, blocks[0].shape[1])
+    shape = (len(blocks) * (rows.stop - rows.start), columns.stop - columns.start)
     return pl.pallas_call(
-        functools.partial(regroup_kernel, len(blocks), first, last),
+        functools.partial(regroup_kernel, len(blocks), rows, columns),
         out_shape=in_vmem(shape, blocks[0].dtype),
         in_specs=[vmem] * len(blocks) + [anywhere] * len(after),
         out_specs=vmem,
         compiler_params=limits(*blocks),
         name="regroup",
     )(*blocks, *after)
+
+
+def assemble_kernel(rows, own, *refs):
+    parts, out = refs[:-1], refs[-1]
+    height = rows.stop - rows.start
+    out[:height, :] = own[rows, :]
+    width = parts[0].shape[1]
+    for c, part in enumerate(parts):
+        out[height:, c * width : (c + 1) * width] = part[...]
+
+
+def assemble(rows, own, parts):
+    height = rows.stop - rows.start + parts[0].shape[0]
+    return pl.pallas_call(
+        functools.partial(assemble_kernel, rows),
+        out_shape=in_vmem((height, own.shape[1]), own.dtype),
+        in_specs=[vmem] * (1 + len(parts)),
+        out_specs=vmem,
+        compiler_params=limits(own, *parts),
+        name="assemble",
+    )(own, *parts)
 
 
 def with_turned(halves, pairs):
@@ -323,11 +365,11 @@
         turned += [imag, real]
     straight = jnp.concatenate(straight, 0).astype(jnp.bfloat16)
     turned = jnp.concatenate(turned, 0).astype(jnp.bfloat16)
-    width = screening.shape[3] // ga
+    width = screening.shape[2] // ga
     columns = [columns_of(origin(mine, r, ga), width) for r in range(ga)]
     coupled = [
-        jnp.dot(straight, screening[0, 0, :, block], preferred_element_type=jnp.float32)
-        + jnp.dot(turned, screening[0, 1, :, block], preferred_element_type=jnp.float32)
+        jnp.dot(straight, screening[0, :, block], preferred_element_type=jnp.float32)
+        + jnp.dot(turned, screening[1, :, block], preferred_element_type=jnp.float32)
         for block in columns
     ]
     for out, value in zip(outs, coupled):
@@ -339,16 +381,17 @@
 def couple(ka, ga, ba, dims, screening, cond_all):
     share_rows = dims[2] // ba * dims[2]
     rows = 2 * sum(x.shape[0] for x in cond_all)
-    width = screening.shape[3] // ga
+    width = screening.shape[2] // ga
+    operands = [screening, *cond_all]
     return pl.pallas_call(
         functools.partial(couple_kernel, ka, ga, ba, share_rows),
         out_shape=[in_vmem((rows, width), jnp.bfloat16)] * ga,
-        in_specs=[vmem] * (1 + len(cond_all)),
+        in_specs=[vmem] * len(operands),
         out_specs=[vmem] * ga,
         cost_estimate=LIGHT,
-        compiler_params=limits(*cond_all),
+        compiler_params=limits(*operands),
         name="couple",
-    )(placed(screening, pltpu.VMEM), *cond_all)
+    )(*operands)
 
 
 def contract_kernel(ka, ba, count, dims, *refs):
@@ -520,13 +563,13 @@
     cond_count = conduction_density.shape[3]
     pairs = vloc * val_count
     dims = (vloc, val_count, cond_count, npol)
-    screening = lax.ppermute(screening, "ba", [(h, h) for h in range(ba)])
     packed = pack(ka, ba, qpoint_map, slot_owner, valence_density, conduction_density)
     blocks = [packed[0]] + [shifted(packed[j], "ka", j) for j in range(1, ka)]
     early = ka // 2
-    val_early = regroup(blocks[:early], 0, 2 * pairs)
+    val_rows = slice(0, 2 * pairs)
+    val_early = regroup(blocks[:early], val_rows)
     far_early = [shifted(val_early, "ga", r) for r in range(1, ga)]
-    near_table, far_table, extras = prepare(
+    whole, near_table, far_table, extras = prepare(
         ka,
         dims,
         qpoint_map,
@@ -535,13 +578,24 @@
         valence_energy,
         conduction_energy,
         start_vector,
+        screening,
         val_early,
     )
-    val_late = regroup(blocks[early:], 0, 2 * pairs, (extras,))
+    val_late = regroup(blocks[early:], val_rows, (extras,))
     far_late = [shifted(val_late, "ga", r) for r in range(1, ga)]
-    cond_half = regroup(blocks, 2 * pairs, blocks[0].shape[0], (val_late, *far_early))
-    cond_all = [cond_half] + [handed(cond_half, r) for r in range(1, ba)]
-    coupled = couple(ka, ga, ba, dims, screening, cond_all)
+    height = 2 * cond_count // ba * cond_count
+    width = blocks[0].shape[1] // PARTS
+    cond_rows = slice(2 * pairs, 2 * pairs + height)
+    cond_parts = [
+        regroup(blocks[1:], cond_rows, (val_late, *far_early), slice(c * width, (c + 1) * width))
+        for c in range(PARTS)
+    ]
+    cond_all = [regroup(blocks, cond_rows)]
+    for r in range(1, ba):
+        own_rows = slice(2 * pairs + r * height, 2 * pairs + (r + 1) * height)
+        came = [handed(part, r) for part in cond_parts]
+        cond_all.append(assemble(own_rows, blocks[0], came))
+    coupled = couple(ka, ga, ba, dims, whole, cond_all)
     near = [val_early, val_late]
     piece = contract(ka, ba, dims, near_table, extras, coupled[:1], near, "near")
     if ga > 1:
@@ -549,7 +603,7 @@
         piece = contract(ka, ba, dims, far_table, piece, coupled[1:], far, "far")
     piece = piece + sum(handed(piece, r) for r in range(1, ba))
     piece = summed(piece, "ga")
-    pieces = [piece] + [shifted(piece, "ka", j) for j in range(1, ka)]
+    pieces = [piece] + [shifted(piece, "ka", j) for j in reversed(range(1, ka))]
     scale_count = float(kcount * pair_count)
     return tuple(haydock(ka, pair_count, scale_count, npol, pieces))
 

time: 30.5 us -> 28.4 us (0.931)
  starting transfers between devices: 18.3 us -> 14.4 us
  Pallas kernels: 5.31 us -> 6.86 us
    ppermute x1 -> x0, starting transfers between devices: 2.34 us -> none  [local(): screening = lax.ppermute(screening, 'ba', [(h, h) for h in range(ba)])]
    ppermute x9, starting transfers between devices: 15.3 us -> 13.5 us  [exchanged(): return lax.ppermute(value, (axis, 'ba'), pairs)]
    pallas_call x1, Pallas kernels: 0.95 us -> 2.45 us  [prepare(): pl.pallas_call(functools.partial(prepare_kernel, ka, dims), out_shape=[in...]
    ppermute x2 -> x3, waiting for transfers between devices: 1.05 us -> 1.92 us  [handed(): lax.ppermute(value, 'ba', [(h, (h + step) % size) for h in range(size)])]
    ppermute x9, waiting for transfers between devices: 5.02 us -> 4.31 us  [exchanged(): return lax.ppermute(value, (axis, 'ba'), pairs)]
    ppermute x2 -> x3, starting transfers between devices: 0.66 us -> 0.95 us  [handed(): lax.ppermute(value, 'ba', [(h, (h + step) % size) for h in range(size)])]
    pallas_call x4 -> x7, Pallas kernels: 1.06 us -> 1.09 us  [the longest x1 1.05 us: pack(): pl.pallas_call(functools.partial(pack_kernel, ka), out_shape=[own] + [sha...]
  transfers between devices with their start and end apart: 12 -> 12, of which waited for: 8 -> 8; matrix products, arithmetic and copies ran while one was open for 0% -> 0% of each run, Pallas kernels for 11% -> 14%
where the time goes in v17:
time: 28.4 us; the launch traced here: 28.2 us
  starting transfers between devices  14.4 us (51%)
  Pallas kernels  6.86 us (24%)
  waiting for transfers between devices  6.23 us (22%)
  between operations  0.7 us (2%)
    ppermute x9, starting transfers between devices, exchanged(): return lax.ppermute(value, (axis, 'ba'), pairs)  13.5 us
    ppermute x9, waiting for transfers between devices, exchanged(): return lax.ppermute(value, (axis, 'ba'), pairs)  4.31 us
    pallas_call x1, Pallas kernels, prepare(): pl.pallas_call(functools.partial(prepare_kernel, ka, dims), out_shape=[in...  2.45 us
    ppermute x3, waiting for transfers between devices, handed(): lax.ppermute(value, 'ba', [(h, (h + step) % size) for h in range(size)])  1.92 us
    pallas_call x1, Pallas kernels, haydock(): pl.pallas_call(functools.partial(haydock_kernel, ka, codes, scale_count,...  1.41 us
    pallas_call x2, Pallas kernels, contract(): pl.pallas_call(functools.partial(contract_kernel, ka, ba, len(coupled), d...  1.07 us
    pallas_call x1, Pallas kernels, pack(): pl.pallas_call(functools.partial(pack_kernel, ka), out_shape=[own] + [sha...  1.05 us
    ppermute x3, starting transfers between devices, handed(): lax.ppermute(value, 'ba', [(h, (h + step) % size) for h in range(size)])  0.95 us
  transfers between devices with their start and end apart: 12, of which 8 were waited for; matrix products, arithmetic and copies ran while one was open for 0% of the time, Pallas kernels for 14%

profile of v17, /device:TPU:0, one launch (start us, length us, event | category | flops | bytes accessed | tf_op | source)
XLA Modules:
  0.0 28.2 jit_solution(4308537224362763211)
XLA Ops:
  0.6 1.1 %pack.1 = (bf16[48,768]{1,0:T(8,128)(2,1)S(1)}, bf16[32,768]{1,0:T(8,128)(2,1)S(1)}, bf16[32,768]{1,0:T(8,128)(2,1)S(1)}, bf16[32,768]{1,0:T(8,128)(2,1)S(1)}) custom-call(s32[4,4]{1,0:T(4,128)} %refs_0_.1, s32[4]{0:T(128)} %refs_1_.1, bf16[1,4,2,2,4,768]{5,4,3,2,1,0:T(4,128)(2,1)} %valence_in.1, bf16[1,4,2,4,4,768]{5,4,3,2,1,0:T(4,128)(2,1)} %conduction_in.1), custom_call_target="tpu_custom_call" | custom-call | tf_op jit(solution)/shard_map/pack/pallas_call | solution.py:123
  1.7 2.5 %collective-permute-start = (bf16[32,768]{1,0:T(8,128)(2,1)S(1)}, bf16[32,768]{1,0:T(8,128)(2,1)S(1)}, u32[]{:S(2)}, u32[]{:S(2)}) collective-permute-start(bf16[32,768]{1,0:T(8,128)(2,1)S(1)} %get-tuple-element.13), channel_id=1, source_target_pairs={{0,5},{1,4},{4,9},{5,8},{8,13},{9,12},{12,1},{13,0},{2,7},{3,6},{6... | collective-permute-start | bytes 147464 | tf_op jit(solution)/shard_map/ppermute | solution.py:62
  4.2 2.9 %collective-permute-start.1 = (bf16[32,768]{1,0:T(8,128)(2,1)S(1)}, bf16[32,768]{1,0:T(8,128)(2,1)S(1)}, u32[]{:S(2)}, u32[]{:S(2)}) collective-permute-start(bf16[32,768]{1,0:T(8,128)(2,1)S(1)} %get-tuple-element.18), channel_id=1, source_target_pairs={{0,9},{1,8},{4,13},{5,12},{8,1},{9,0},{12,5},{13,4},{2,11},{3,10},... | collective-permute-start | bytes 147464 | tf_op jit(solution)/shard_map/ppermute | solution.py:62
  7.1 0.8 %collective-permute-start.2 = (bf16[32,768]{1,0:T(8,128)(2,1)S(1)}, bf16[32,768]{1,0:T(8,128)(2,1)S(1)}, u32[]{:S(2)}, u32[]{:S(2)}) collective-permute-start(bf16[32,768]{1,0:T(8,128)(2,1)S(1)} %get-tuple-element.19), channel_id=1, source_target_pairs={{0,13},{1,12},{4,1},{5,0},{8,5},{9,4},{12,9},{13,8},{2,15},{3,14},... | collective-permute-start | bytes 147464 | tf_op jit(solution)/shard_map/ppermute | solution.py:62
  7.9 0.1 collective-permute-done.refs_1_.refs_0_
  8.0 2.0 %collective-permute-start.3 = (bf16[32,768]{1,0:T(8,128)(2,1)S(1)}, bf16[32,768]{1,0:T(8,128)(2,1)S(1)}, u32[]{:S(2)}, u32[]{:S(2)}) collective-permute-start(bf16[32,768]{1,0:T(8,128)(2,1)S(1)} %regroup.5.refs_7_.refs_3_), channel_id=1, source_target_pairs={{0,3},{1,2},{2,1},{3,0},{4,7},{5,6},{6,5},{7,4},{8,11},{9,10},{10,... | collective-permute-start | bytes 147464 | tf_op jit(solution)/shard_map/ppermute | solution.py:62
  10.0 2.5 %prepare.1 = (bf16[2,768,1536]{2,1,0:T(8,128)(2,1)S(1)}, bf16[128,512]{1,0:T(8,128)(2,1)S(1)}, bf16[128,512]{1,0:T(8,128)(2,1)S(1)}, f32[8,128]{1,0:T(8,128)S(1)}) custom-call(s32[4,4]{1,0:T(4,128)} %refs_0_.1, s32[4]{0:T(128)} %refs_1_.1, s32[16]{0:T(128)} %refs_2_.1, f32[1,4]{1,0:T(1,128)} %refs_3_.1, f32[1,4]{1,0:T(1,128)} %refs_4_.1, ...), custom_call_target="tpu_custom_call" | custom-call | bytes 9437184 | tf_op jit(solution)/shard_map/prepare/pallas_call | solution.py:231
  12.5 0.0 collective-permute-done.1.refs_2_.refs_0_.refs_1_
  12.5 0.0 collective-permute-done.2.refs_3_.refs_1_.refs_2_
  12.5 0.4 %collective-permute-start.6 = (bf16[32,768]{1,0:T(8,128)(2,1)S(1)}, bf16[32,768]{1,0:T(8,128)(2,1)S(1)}, u32[]{:S(2)}, u32[]{:S(2)}) collective-permute-start(bf16[32,768]{1,0:T(8,128)(2,1)S(1)} %regroup.7.refs_3_.refs_4_), channel_id=1, source_target_pairs={{0,3},{1,2},{2,1},{3,0},{4,7},{5,6},{6,5},{7,4},{8,11},{9,10},{10,... | collective-permute-start | bytes 147464 | tf_op jit(solution)/shard_map/ppermute | solution.py:62
  12.9 0.0 collective-permute-done.3.refs_4_.refs_3_
  12.9 0.5 %collective-permute-start.4 = (bf16[48,384]{1,0:T(8,128)(2,1)S(1)}, bf16[48,384]{1,0:T(8,128)(2,1)S(1)}, u32[]{:S(2)}, u32[]{:S(2)}) collective-permute-start(bf16[48,384]{1,0:T(8,128)(2,1)S(1)} %regroup.8), channel_id=1, source_target_pairs={{0,1},{1,0},{2,3},{3,2},{4,5},{5,4},{6,7},{7,6},{8,9},{9,8},{10,11... | collective-permute-start | bytes 110600 | tf_op jit(solution)/shard_map/ppermute | solution.py:71
  13.4 0.1 collective-permute-start.5
  13.5 0.7 %collective-permute-done.4.refs_0_ = bf16[48,384]{1,0:T(8,128)(2,1)S(1)} collective-permute-done((bf16[48,384]{1,0:T(8,128)(2,1)S(1)}, bf16[48,384]{1,0:T(8,128)(2,1)S(1)}, u32[]{:S(2)}, u32[]{:S(2)}) %collective-permute-start.4) | collective-permute-done | bytes 36896 | tf_op jit(solution)/shard_map/ppermute | solution.py:71
  14.2 0.4 %collective-permute-done.5.refs_1_ = bf16[48,384]{1,0:T(8,128)(2,1)S(1)} collective-permute-done((bf16[48,384]{1,0:T(8,128)(2,1)S(1)}, bf16[48,384]{1,0:T(8,128)(2,1)S(1)}, u32[]{:S(2)}, u32[]{:S(2)}) %collective-permute-start.5) | collective-permute-done | bytes 36896 | tf_op jit(solution)/shard_map/ppermute | solution.py:71
  14.6 0.8 %couple.1 = (bf16[256,768]{1,0:T(8,128)(2,1)S(1)}, bf16[256,768]{1,0:T(8,128)(2,1)S(1)}) custom-call(bf16[2,768,1536]{2,1,0:T(8,128)(2,1)S(1)} %get-tuple-element.17.screening, bf16[64,768]{1,0:T(8,128)(2,1)S(1)} %regroup.6.refs_0_, bf16[64,768]{1,0:T(8,128)(2,1)S(1)} %assemble.1.refs_1_), custom_call_target="tpu_custom_call" | custom-call | flops 1 | bytes 1 | tf_op jit(solution)/shard_map/couple/pallas_call | solution.py:386
  15.5 0.5 %near.1.refs_1_ = f32[24,128]{1,0:T(8,128)S(1)} custom-call(bf16[128,512]{1,0:T(8,128)(2,1)S(1)} %get-tuple-element.15.refs_0_, f32[8,128]{1,0:T(8,128)S(1)} %get-tuple-element.16.refs_2_.refs_1_, bf16[256,768]{1,0:T(8,128)(2,1)S(1)} %get-tuple-element.20.refs_2_, bf16[32,768]{1,0:T(8,128)(2,1)S(1)} %regroup.5.refs_7_.refs_3_, ...), custom_call_target="tpu_custom_call" | custom-call | flops 1 | bytes 1 | tf_op jit(solution)/shard_map/near/pallas_call | solution.py:424
  16.0 0.1 collective-permute-done.6.refs_4_
  16.1 0.5 %far.1 = f32[24,128]{1,0:T(8,128)S(1)} custom-call(bf16[128,512]{1,0:T(8,128)(2,1)S(1)} %get-tuple-element.14.refs_0_, f32[24,128]{1,0:T(8,128)S(1)} %near.1.refs_1_, bf16[256,768]{1,0:T(8,128)(2,1)S(1)} %get-tuple-element.21.refs_2_, bf16[32,768]{1,0:T(8,128)(2,1)S(1)} %collective-permute-done.3.refs_4_.refs_3_, ...), custom_call_target="tpu_custom_call" | custom-call | flops 1 | bytes 1 | tf_op jit(solution)/shard_map/far/pallas_call | solution.py:424
  16.7 0.4 %collective-permute-start.7 = (f32[24,128]{1,0:T(8,128)S(1)}, f32[24,128]{1,0:T(8,128)S(1)}, u32[]{:S(2)}, u32[]{:S(2)}) collective-permute-start(f32[24,128]{1,0:T(8,128)S(1)} %far.1), channel_id=1, source_target_pairs={{0,1},{1,0},{2,3},{3,2},{4,5},{5,4},{6,7},{7,6},{8,9},{9,8},{10,11... | collective-permute-start | bytes 36872 | tf_op jit(solution)/shard_map/ppermute | solution.py:71
  17.0 0.8 %collective-permute-done.7 = f32[24,128]{1,0:T(8,128)S(1)} collective-permute-done((f32[24,128]{1,0:T(8,128)S(1)}, f32[24,128]{1,0:T(8,128)S(1)}, u32[]{:S(2)}, u32[]{:S(2)}) %collective-permute-start.7) | collective-permute-done | bytes 12320 | tf_op jit(solution)/shard_map/ppermute | solution.py:71
  17.9 1.3 %collective-permute-start.8 = (f32[24,128]{1,0:T(8,128)S(1)}, f32[24,128]{1,0:T(8,128)S(1)}, u32[]{:S(2)}, u32[]{:S(2)}) collective-permute-start(f32[24,128]{1,0:T(8,128)S(1)} %add.6), channel_id=1, source_target_pairs={{0,3},{1,2},{2,1},{3,0},{4,7},{5,6},{6,5},{7,4},{8,11},{9,10},{10,... | collective-permute-start | bytes 36872 | tf_op jit(solution)/shard_map/ppermute | solution.py:62
  19.1 1.9 %collective-permute-done.8 = f32[24,128]{1,0:T(8,128)S(1)} collective-permute-done((f32[24,128]{1,0:T(8,128)S(1)}, f32[24,128]{1,0:T(8,128)S(1)}, u32[]{:S(2)}, u32[]{:S(2)}) %collective-permute-start.8) | collective-permute-done | bytes 12320 | tf_op jit(solution)/shard_map/ppermute | solution.py:62
  21.0 0.6 %collective-permute-start.11 = (f32[24,128]{1,0:T(8,128)S(1)}, f32[24,128]{1,0:T(8,128)S(1)}, u32[]{:S(2)}, u32[]{:S(2)}) collective-permute-start(f32[24,128]{1,0:T(8,128)S(1)} %add.7.refs_0_), channel_id=1, source_target_pairs={{0,5},{1,4},{4,9},{5,8},{8,13},{9,12},{12,1},{13,0},{2,7},{3,6},{6... | collective-permute-start | bytes 36872 | tf_op jit(solution)/shard_map/ppermute | solution.py:62
  21.6 2.1 %collective-permute-start.10 = (f32[24,128]{1,0:T(8,128)S(1)}, f32[24,128]{1,0:T(8,128)S(1)}, u32[]{:S(2)}, u32[]{:S(2)}) collective-permute-start(f32[24,128]{1,0:T(8,128)S(1)} %add.7.refs_0_), channel_id=1, source_target_pairs={{0,9},{1,8},{4,13},{5,12},{8,1},{9,0},{12,5},{13,4},{2,11},{3,10},... | collective-permute-start | bytes 36872 | tf_op jit(solution)/shard_map/ppermute | solution.py:62
  23.7 0.9 %collective-permute-start.9 = (f32[24,128]{1,0:T(8,128)S(1)}, f32[24,128]{1,0:T(8,128)S(1)}, u32[]{:S(2)}, u32[]{:S(2)}) collective-permute-start(f32[24,128]{1,0:T(8,128)S(1)} %add.7.refs_0_), channel_id=1, source_target_pairs={{0,13},{1,12},{4,1},{5,0},{8,5},{9,4},{12,9},{13,8},{2,15},{3,14},... | collective-permute-start | bytes 36872 | tf_op jit(solution)/shard_map/ppermute | solution.py:62
  24.6 1.3 %collective-permute-done.11.refs_3_ = f32[24,128]{1,0:T(8,128)S(1)} collective-permute-done((f32[24,128]{1,0:T(8,128)S(1)}, f32[24,128]{1,0:T(8,128)S(1)}, u32[]{:S(2)}, u32[]{:S(2)}) %collective-permute-start.11) | collective-permute-done | bytes 12320 | tf_op jit(solution)/shard_map/ppermute | solution.py:62
  25.9 0.0 collective-permute-done.10.refs_2_
  25.9 0.9 %collective-permute-done.9.refs_1_ = f32[24,128]{1,0:T(8,128)S(1)} collective-permute-done((f32[24,128]{1,0:T(8,128)S(1)}, f32[24,128]{1,0:T(8,128)S(1)}, u32[]{:S(2)}, u32[]{:S(2)}) %collective-permute-start.9) | collective-permute-done | bytes 12320 | tf_op jit(solution)/shard_map/ppermute | solution.py:62
  26.8 1.4 %haydock.1 = (f32[1,2,2,16]{3,2,1,0:T(2,128)}, f32[2,6]{1,0:T(2,128)}) custom-call(f32[24,128]{1,0:T(8,128)S(1)} %add.7.refs_0_, f32[24,128]{1,0:T(8,128)S(1)} %collective-permute-done.9.refs_1_, f32[24,128]{1,0:T(8,128)S(1)} %collective-permute-done.10.refs_2_, f32[24,128]{1,0:T(8,128)S(1)} %collective-permute-done.11.refs_3_), custom_call_target="tpu_custom_call" | custom-call | tf_op jit(solution)/shard_map/haydock/pallas_call | solution.py:521
  (8 shorter events, 0.0 us)
Async XLA Ops:
  1.7 6.3 %collective-permute-start = (bf16[32,768]{1,0:T(8,128)(2,1)S(1)}, bf16[32,768]{1,0:T(8,128)(2,1)S(1)}, u32[]{:S(2)}, u32[]{:S(2)}) collective-permute-start(bf16[32,768]{1,0:T(8,128)(2,1)S(1)} %get-tuple-element.13), channel_id=1, source_target_pairs={{0,5},{1,4},{4,9},{5,8},{8,13},{9,12},{12,1},{13,0},{2,7},{3,6},{6... | collective-permute-start | bytes 147464 | tf_op jit(solution)/shard_map/ppermute | solution.py:62
  4.2 8.3 %collective-permute-start.1 = (bf16[32,768]{1,0:T(8,128)(2,1)S(1)}, bf16[32,768]{1,0:T(8,128)(2,1)S(1)}, u32[]{:S(2)}, u32[]{:S(2)}) collective-permute-start(bf16[32,768]{1,0:T(8,128)(2,1)S(1)} %get-tuple-element.18), channel_id=1, source_target_pairs={{0,9},{1,8},{4,13},{5,12},{8,1},{9,0},{12,5},{13,4},{2,11},{3,10},... | collective-permute-start | bytes 147464 | tf_op jit(solution)/shard_map/ppermute | solution.py:62
  7.1 5.4 %collective-permute-start.2 = (bf16[32,768]{1,0:T(8,128)(2,1)S(1)}, bf16[32,768]{1,0:T(8,128)(2,1)S(1)}, u32[]{:S(2)}, u32[]{:S(2)}) collective-permute-start(bf16[32,768]{1,0:T(8,128)(2,1)S(1)} %get-tuple-element.19), channel_id=1, source_target_pairs={{0,13},{1,12},{4,1},{5,0},{8,5},{9,4},{12,9},{13,8},{2,15},{3,14},... | collective-permute-start | bytes 147464 | tf_op jit(solution)/shard_map/ppermute | solution.py:62
  8.0 4.9 %collective-permute-start.3 = (bf16[32,768]{1,0:T(8,128)(2,1)S(1)}, bf16[32,768]{1,0:T(8,128)(2,1)S(1)}, u32[]{:S(2)}, u32[]{:S(2)}) collective-permute-start(bf16[32,768]{1,0:T(8,128)(2,1)S(1)} %regroup.5.refs_7_.refs_3_), channel_id=1, source_target_pairs={{0,3},{1,2},{2,1},{3,0},{4,7},{5,6},{6,5},{7,4},{8,11},{9,10},{10,... | collective-permute-start | bytes 147464 | tf_op jit(solution)/shard_map/ppermute | solution.py:62
  12.5 3.6 %collective-permute-start.6 = (bf16[32,768]{1,0:T(8,128)(2,1)S(1)}, bf16[32,768]{1,0:T(8,128)(2,1)S(1)}, u32[]{:S(2)}, u32[]{:S(2)}) collective-permute-start(bf16[32,768]{1,0:T(8,128)(2,1)S(1)} %regroup.7.refs_3_.refs_4_), channel_id=1, source_target_pairs={{0,3},{1,2},{2,1},{3,0},{4,7},{5,6},{6,5},{7,4},{8,11},{9,10},{10,... | collective-permute-start | bytes 147464 | tf_op jit(solution)/shard_map/ppermute | solution.py:62
  12.9 1.3 %collective-permute-start.4 = (bf16[48,384]{1,0:T(8,128)(2,1)S(1)}, bf16[48,384]{1,0:T(8,128)(2,1)S(1)}, u32[]{:S(2)}, u32[]{:S(2)}) collective-permute-start(bf16[48,384]{1,0:T(8,128)(2,1)S(1)} %regroup.8), channel_id=1, source_target_pairs={{0,1},{1,0},{2,3},{3,2},{4,5},{5,4},{6,7},{7,6},{8,9},{9,8},{10,11... | collective-permute-start | bytes 110600 | tf_op jit(solution)/shard_map/ppermute | solution.py:71
  13.4 1.2 %collective-permute-start.5 = (bf16[48,384]{1,0:T(8,128)(2,1)S(1)}, bf16[48,384]{1,0:T(8,128)(2,1)S(1)}, u32[]{:S(2)}, u32[]{:S(2)}) collective-permute-start(bf16[48,384]{1,0:T(8,128)(2,1)S(1)} %regroup.9), channel_id=1, source_target_pairs={{0,1},{1,0},{2,3},{3,2},{4,5},{5,4},{6,7},{7,6},{8,9},{9,8},{10,11... | collective-permute-start | bytes 110600 | tf_op jit(solution)/shard_map/ppermute | solution.py:71
  16.7 1.2 %collective-permute-start.7 = (f32[24,128]{1,0:T(8,128)S(1)}, f32[24,128]{1,0:T(8,128)S(1)}, u32[]{:S(2)}, u32[]{:S(2)}) collective-permute-start(f32[24,128]{1,0:T(8,128)S(1)} %far.1), channel_id=1, source_target_pairs={{0,1},{1,0},{2,3},{3,2},{4,5},{5,4},{6,7},{7,6},{8,9},{9,8},{10,11... | collective-permute-start | bytes 36872 | tf_op jit(solution)/shard_map/ppermute | solution.py:71
  17.9 3.1 %collective-permute-start.8 = (f32[24,128]{1,0:T(8,128)S(1)}, f32[24,128]{1,0:T(8,128)S(1)}, u32[]{:S(2)}, u32[]{:S(2)}) collective-permute-start(f32[24,128]{1,0:T(8,128)S(1)} %add.6), channel_id=1, source_target_pairs={{0,3},{1,2},{2,1},{3,0},{4,7},{5,6},{6,5},{7,4},{8,11},{9,10},{10,... | collective-permute-start | bytes 36872 | tf_op jit(solution)/shard_map/ppermute | solution.py:62
  21.0 4.9 %collective-permute-start.11 = (f32[24,128]{1,0:T(8,128)S(1)}, f32[24,128]{1,0:T(8,128)S(1)}, u32[]{:S(2)}, u32[]{:S(2)}) collective-permute-start(f32[24,128]{1,0:T(8,128)S(1)} %add.7.refs_0_), channel_id=1, source_target_pairs={{0,5},{1,4},{4,9},{5,8},{8,13},{9,12},{12,1},{13,0},{2,7},{3,6},{6... | collective-permute-start | bytes 36872 | tf_op jit(solution)/shard_map/ppermute | solution.py:62
  21.6 4.3 %collective-permute-start.10 = (f32[24,128]{1,0:T(8,128)S(1)}, f32[24,128]{1,0:T(8,128)S(1)}, u32[]{:S(2)}, u32[]{:S(2)}) collective-permute-start(f32[24,128]{1,0:T(8,128)S(1)} %add.7.refs_0_), channel_id=1, source_target_pairs={{0,9},{1,8},{4,13},{5,12},{8,1},{9,0},{12,5},{13,4},{2,11},{3,10},... | collective-permute-start | bytes 36872 | tf_op jit(solution)/shard_map/ppermute | solution.py:62
  23.7 3.1 %collective-permute-start.9 = (f32[24,128]{1,0:T(8,128)S(1)}, f32[24,128]{1,0:T(8,128)S(1)}, u32[]{:S(2)}, u32[]{:S(2)}) collective-permute-start(f32[24,128]{1,0:T(8,128)S(1)} %add.7.refs_0_), channel_id=1, source_target_pairs={{0,13},{1,12},{4,1},{5,0},{8,5},{9,4},{12,9},{13,8},{2,15},{3,14},... | collective-permute-start | bytes 36872 | tf_op jit(solution)/shard_map/ppermute | solution.py:62

commit v18 on v17

--- a/solution.py
+++ b/solution.py
@@ -273,7 +273,7 @@
 
 
 def assemble_kernel(rows, own, *refs):
-    parts, out = refs[:-1], refs[-1]
+    parts, out = refs[:PARTS], refs[-1]
     height = rows.stop - rows.start
     out[:height, :] = own[rows, :]
     width = parts[0].shape[1]
@@ -281,16 +281,16 @@
         out[height:, c * width : (c + 1) * width] = part[...]
 
 
-def assemble(rows, own, parts):
+def assemble(rows, own, parts, after):
     height = rows.stop - rows.start + parts[0].shape[0]
     return pl.pallas_call(
         functools.partial(assemble_kernel, rows),
         out_shape=in_vmem((height, own.shape[1]), own.dtype),
-        in_specs=[vmem] * (1 + len(parts)),
+        in_specs=[vmem] * (1 + len(parts)) + [anywhere],
         out_specs=vmem,
         compiler_params=limits(own, *parts),
         name="assemble",
-    )(own, *parts)
+    )(own, *parts, after)
 
 
 def with_turned(halves, pairs):
@@ -337,7 +337,7 @@
     return piece[:, :lanes] + piece[:, lanes:]
 
 
-def diagonal(crossed, ka, ba, share_rows):
+def diagonal(crossed, ka, ba, share_rows, sign):
     rows = crossed.shape[1] // 2
     lane = iota((share_rows, 2 * rows), 1)
     lane_j = lane % rows // (rows // ka)
@@ -349,9 +349,68 @@
             at = (h * ka + j) * 2 * share_rows
             real = crossed[at : at + share_rows]
             imag = crossed[at + share_rows : at + 2 * share_rows]
-            total = jnp.where(lane_j == j, jnp.where(straight, real, imag), total)
+            total = jnp.where(lane_j == j, jnp.where(straight, real, sign * imag), total)
         kernel.append(total)
     return jnp.concatenate(kernel, 0)
+
+
+def field_kernel(pairs, screening, *refs):
+    halves, out = refs[:-1], refs[-1]
+    columns = columns_of(lax.axis_index("ga"), halves[0].shape[1])
+    wide, turned = with_turned(halves, pairs)
+    real = jnp.concatenate([wide, turned], 0).astype(jnp.bfloat16)
+    imag = jnp.concatenate([turned, -wide], 0).astype(jnp.bfloat16)
+    form = (((1,), (1,)), ((), ()))
+    fields = lax.dot_general(
+        screening[0, :, columns], real, form, preferred_element_type=jnp.float32
+    ) + lax.dot_general(screening[1, :, columns], imag, form, preferred_element_type=jnp.float32)
+    lanes = fields.shape[1]
+    high, low = split(fields)
+    out[:, :lanes] = high
+    out[:, lanes:] = low
+
+
+def field(pairs, screening, halves):
+    operands = [screening, *halves]
+    rows = sum(half.shape[0] for half in halves)
+    return pl.pallas_call(
+        functools.partial(field_kernel, pairs),
+        out_shape=in_vmem((screening.shape[1], 4 * rows), jnp.bfloat16),
+        in_specs=[vmem] * len(operands),
+        out_specs=vmem,
+        cost_estimate=LIGHT,
+        compiler_params=limits(*operands),
+        name="field",
+    )(*operands)
+
+
+def near_kernel(ka, ba, dims, *refs):
+    vloc, val_count, cond_count, npol = dims
+    fields, table, extras = refs[:3]
+    cond_in, out = refs[3:-1], refs[-1]
+    codes = val_count * cond_count
+    cond = jnp.concatenate([ref[...] for ref in cond_in], 0)
+    crossed = jnp.dot(cond, fields[...], preferred_element_type=jnp.float32)
+    half = crossed.shape[1] // 2
+    crossed = crossed[:, :half] + crossed[:, half:]
+    kernel = diagonal(crossed, ka, ba, cond_count // ba * cond_count, -1.0)
+    out[:codes, :] = placed_piece(kernel, table, dims, ba)
+    out[codes:, :] = extras[...]
+
+
+def near(ka, ba, dims, fields, table, extras, cond_all):
+    vloc, val_count, cond_count, npol = dims
+    operands = [fields, table, extras, *cond_all]
+    shape = (val_count * cond_count + EXTRA_ROWS, extras.shape[1])
+    return pl.pallas_call(
+        functools.partial(near_kernel, ka, ba, dims),
+        out_shape=in_vmem(shape, jnp.float32),
+        in_specs=[vmem] * len(operands),
+        out_specs=vmem,
+        cost_estimate=LIGHT,
+        compiler_params=limits(*operands),
+        name="near",
+    )(*operands)
 
 
 def couple_kernel(ka, ga, ba, share_rows, screening, *refs):
@@ -366,7 +425,7 @@
     straight = jnp.concatenate(straight, 0).astype(jnp.bfloat16)
     turned = jnp.concatenate(turned, 0).astype(jnp.bfloat16)
     width = screening.shape[2] // ga
-    columns = [columns_of(origin(mine, r, ga), width) for r in range(ga)]
+    columns = [columns_of(origin(mine, r, ga), width) for r in range(1, ga)]
     coupled = [
         jnp.dot(straight, screening[0, :, block], preferred_element_type=jnp.float32)
         + jnp.dot(turned, screening[1, :, block], preferred_element_type=jnp.float32)
@@ -385,9 +444,9 @@
     operands = [screening, *cond_all]
     return pl.pallas_call(
         functools.partial(couple_kernel, ka, ga, ba, share_rows),
-        out_shape=[in_vmem((rows, width), jnp.bfloat16)] * ga,
+        out_shape=[in_vmem((rows, width), jnp.bfloat16)] * (ga - 1),
         in_specs=[vmem] * len(operands),
-        out_specs=[vmem] * ga,
+        out_specs=[vmem] * (ga - 1),
         cost_estimate=LIGHT,
         compiler_params=limits(*operands),
         name="couple",
@@ -410,7 +469,7 @@
         crossed = term if crossed is None else crossed + term
     half = crossed.shape[0] // 2
     crossed = crossed[:half] + crossed[half:]
-    kernel = diagonal(crossed, ka, ba, cond_count // ba * cond_count)
+    kernel = diagonal(crossed, ka, ba, cond_count // ba * cond_count, 1.0)
     piece = placed_piece(kernel, table, dims, ba)
     before = held.shape[0] - EXTRA_ROWS
     out[:codes, :] = piece + held[:codes, :] if before else piece
@@ -590,20 +649,20 @@
         regroup(blocks[1:], cond_rows, (val_late, *far_early), slice(c * width, (c + 1) * width))
         for c in range(PARTS)
     ]
+    fields = field(pairs, whole, [val_early, val_late])
     cond_all = [regroup(blocks, cond_rows)]
     for r in range(1, ba):
         own_rows = slice(2 * pairs + r * height, 2 * pairs + (r + 1) * height)
         came = [handed(part, r) for part in cond_parts]
-        cond_all.append(assemble(own_rows, blocks[0], came))
-    coupled = couple(ka, ga, ba, dims, whole, cond_all)
-    near = [val_early, val_late]
-    piece = contract(ka, ba, dims, near_table, extras, coupled[:1], near, "near")
+        cond_all.append(assemble(own_rows, blocks[0], came, fields))
+    piece = near(ka, ba, dims, fields, near_table, extras, cond_all)
     if ga > 1:
+        coupled = couple(ka, ga, ba, dims, whole, cond_all)
         far = [half for both in zip(far_early, far_late) for half in both]
-        piece = contract(ka, ba, dims, far_table, piece, coupled[1:], far, "far")
+        piece = contract(ka, ba, dims, far_table, piece, coupled, far, "far")
     piece = piece + sum(handed(piece, r) for r in range(1, ba))
     piece = summed(piece, "ga")
-    pieces = [piece] + [shifted(piece, "ka", j) for j in reversed(range(1, ka))]
+    pieces = [piece] + [shifted(piece, "ka", j) for j in range(1, ka)]
     scale_count = float(kcount * pair_count)
     return tuple(haydock(ka, pair_count, scale_count, npol, pieces))
 

time: 28.4 us -> 28.1 us (0.989)
  starting transfers between devices: 14.4 us -> 14 us
  Pallas kernels: 6.86 us -> 7.25 us
    pallas_call x0 -> x2, Pallas kernels: none -> 1.26 us  [the longest x1 0.78 us: field(): pl.pallas_call(functools.partial(field_kernel, pairs), out_shape=in_vmem(...]
    ppermute x3, waiting for transfers between devices: 1.92 us -> 1.12 us  [handed(): lax.ppermute(value, 'ba', [(h, (h + step) % size) for h in range(size)])]
    ppermute x9, waiting for transfers between devices: 4.31 us -> 4.84 us  [exchanged(): return lax.ppermute(value, (axis, 'ba'), pairs)]
    pallas_call x2 -> x1, Pallas kernels: 1.07 us -> 0.53 us  [contract(): pl.pallas_call(functools.partial(contract_kernel, ka, ba, len(coupled), d...]
    ppermute x9, starting transfers between devices: 13.5 us -> 13.1 us  [exchanged(): return lax.ppermute(value, (axis, 'ba'), pairs)]
    pallas_call x1, Pallas kernels: 0.84 us -> 0.51 us  [couple(): pl.pallas_call(functools.partial(couple_kernel, ka, ga, ba, share_rows),...]
  transfers between devices with their start and end apart: 12 -> 12, of which waited for: 8 -> 7; matrix products, arithmetic and copies ran while one was open for 0% -> 0% of each run, Pallas kernels for 14% -> 15%
where the time goes in v18:
time: 28.1 us; the launch traced here: 28 us
  starting transfers between devices  14 us (50%)
  Pallas kernels  7.25 us (26%)
  waiting for transfers between devices  5.97 us (21%)
  between operations  0.72 us (3%)
    ppermute x9, starting transfers between devices, exchanged(): return lax.ppermute(value, (axis, 'ba'), pairs)  13.1 us
    ppermute x9, waiting for transfers between devices, exchanged(): return lax.ppermute(value, (axis, 'ba'), pairs)  4.84 us
    pallas_call x1, Pallas kernels, prepare(): pl.pallas_call(functools.partial(prepare_kernel, ka, dims), out_shape=[in...  2.45 us
    pallas_call x1, Pallas kernels, haydock(): pl.pallas_call(functools.partial(haydock_kernel, ka, codes, scale_count,...  1.41 us
    ppermute x3, waiting for transfers between devices, handed(): lax.ppermute(value, 'ba', [(h, (h + step) % size) for h in range(size)])  1.12 us
    pallas_call x1, Pallas kernels, pack(): pl.pallas_call(functools.partial(pack_kernel, ka), out_shape=[own] + [sha...  1.05 us
    ppermute x3, starting transfers between devices, handed(): lax.ppermute(value, 'ba', [(h, (h + step) % size) for h in range(size)])  0.95 us
    pallas_call x1, Pallas kernels, field(): pl.pallas_call(functools.partial(field_kernel, pairs), out_shape=in_vmem(...  0.78 us
  transfers between devices with their start and end apart: 12, of which 7 were waited for; matrix products, arithmetic and copies ran while one was open for 0% of the time, Pallas kernels for 15%

profile of v18, /device:TPU:0, one launch (start us, length us, event | category | flops | bytes accessed | tf_op | source)
XLA Modules:
  0.0 28.0 jit_solution(10142752093303979393)
XLA Ops:
  0.6 1.1 %pack.1 = (bf16[48,768]{1,0:T(8,128)(2,1)S(1)}, bf16[32,768]{1,0:T(8,128)(2,1)S(1)}, bf16[32,768]{1,0:T(8,128)(2,1)S(1)}, bf16[32,768]{1,0:T(8,128)(2,1)S(1)}) custom-call(s32[4,4]{1,0:T(4,128)} %refs_0_.1, s32[4]{0:T(128)} %refs_1_.1, bf16[1,4,2,2,4,768]{5,4,3,2,1,0:T(4,128)(2,1)} %valence_in.1, bf16[1,4,2,4,4,768]{5,4,3,2,1,0:T(4,128)(2,1)} %conduction_in.1), custom_call_target="tpu_custom_call" | custom-call | tf_op jit(solution)/shard_map/pack/pallas_call | solution.py:123
  1.7 2.5 %collective-permute-start = (bf16[32,768]{1,0:T(8,128)(2,1)S(1)}, bf16[32,768]{1,0:T(8,128)(2,1)S(1)}, u32[]{:S(2)}, u32[]{:S(2)}) collective-permute-start(bf16[32,768]{1,0:T(8,128)(2,1)S(1)} %get-tuple-element.11), channel_id=1, source_target_pairs={{0,5},{1,4},{4,9},{5,8},{8,13},{9,12},{12,1},{13,0},{2,7},{3,6},{6... | collective-permute-start | bytes 147464 | tf_op jit(solution)/shard_map/ppermute | solution.py:62
  4.2 2.9 %collective-permute-start.1 = (bf16[32,768]{1,0:T(8,128)(2,1)S(1)}, bf16[32,768]{1,0:T(8,128)(2,1)S(1)}, u32[]{:S(2)}, u32[]{:S(2)}) collective-permute-start(bf16[32,768]{1,0:T(8,128)(2,1)S(1)} %get-tuple-element.14), channel_id=1, source_target_pairs={{0,9},{1,8},{4,13},{5,12},{8,1},{9,0},{12,5},{13,4},{2,11},{3,10},... | collective-permute-start | bytes 147464 | tf_op jit(solution)/shard_map/ppermute | solution.py:62
  7.1 0.8 %collective-permute-start.2 = (bf16[32,768]{1,0:T(8,128)(2,1)S(1)}, bf16[32,768]{1,0:T(8,128)(2,1)S(1)}, u32[]{:S(2)}, u32[]{:S(2)}) collective-permute-start(bf16[32,768]{1,0:T(8,128)(2,1)S(1)} %get-tuple-element.15), channel_id=1, source_target_pairs={{0,13},{1,12},{4,1},{5,0},{8,5},{9,4},{12,9},{13,8},{2,15},{3,14},... | collective-permute-start | bytes 147464 | tf_op jit(solution)/shard_map/ppermute | solution.py:62
  7.9 0.1 collective-permute-done.refs_1_.refs_0_
  8.0 2.0 %collective-permute-start.3 = (bf16[32,768]{1,0:T(8,128)(2,1)S(1)}, bf16[32,768]{1,0:T(8,128)(2,1)S(1)}, u32[]{:S(2)}, u32[]{:S(2)}) collective-permute-start(bf16[32,768]{1,0:T(8,128)(2,1)S(1)} %regroup.5.refs_7_.refs_0_), channel_id=1, source_target_pairs={{0,3},{1,2},{2,1},{3,0},{4,7},{5,6},{6,5},{7,4},{8,11},{9,10},{10,... | collective-permute-start | bytes 147464 | tf_op jit(solution)/shard_map/ppermute | solution.py:62
  10.0 2.5 %prepare.1 = (bf16[2,768,1536]{2,1,0:T(8,128)(2,1)S(1)}, bf16[128,512]{1,0:T(8,128)(2,1)S(1)}, bf16[128,512]{1,0:T(8,128)(2,1)S(1)}, f32[8,128]{1,0:T(8,128)S(1)}) custom-call(s32[4,4]{1,0:T(4,128)} %refs_0_.1, s32[4]{0:T(128)} %refs_1_.1, s32[16]{0:T(128)} %refs_2_.1, f32[1,4]{1,0:T(1,128)} %refs_3_.1, f32[1,4]{1,0:T(1,128)} %refs_4_.1, ...), custom_call_target="tpu_custom_call" | custom-call | bytes 9437184 | tf_op jit(solution)/shard_map/prepare/pallas_call | solution.py:231
  12.5 0.0 collective-permute-done.1.refs_0_.refs_2_.refs_1_
  12.5 0.0 collective-permute-done.2.refs_1_.refs_3_.refs_2_
  12.5 0.4 %collective-permute-start.6 = (bf16[32,768]{1,0:T(8,128)(2,1)S(1)}, bf16[32,768]{1,0:T(8,128)(2,1)S(1)}, u32[]{:S(2)}, u32[]{:S(2)}) collective-permute-start(bf16[32,768]{1,0:T(8,128)(2,1)S(1)} %regroup.6.refs_1_.refs_3_), channel_id=1, source_target_pairs={{0,3},{1,2},{2,1},{3,0},{4,7},{5,6},{6,5},{7,4},{8,11},{9,10},{10,... | collective-permute-start | bytes 147464 | tf_op jit(solution)/shard_map/ppermute | solution.py:62
  12.9 0.0 collective-permute-done.3.refs_4_.refs_3_
  12.9 0.5 %collective-permute-start.4 = (bf16[48,384]{1,0:T(8,128)(2,1)S(1)}, bf16[48,384]{1,0:T(8,128)(2,1)S(1)}, u32[]{:S(2)}, u32[]{:S(2)}) collective-permute-start(bf16[48,384]{1,0:T(8,128)(2,1)S(1)} %regroup.8), channel_id=1, source_target_pairs={{0,1},{1,0},{2,3},{3,2},{4,5},{5,4},{6,7},{7,6},{8,9},{9,8},{10,11... | collective-permute-start | bytes 110600 | tf_op jit(solution)/shard_map/ppermute | solution.py:71
  13.4 0.1 collective-permute-start.5
  13.5 0.8 %field.1.refs_2_.refs_0_ = bf16[768,256]{1,0:T(8,128)(2,1)S(1)} custom-call(bf16[2,768,1536]{2,1,0:T(8,128)(2,1)S(1)} %get-tuple-element.13.screening, bf16[32,768]{1,0:T(8,128)(2,1)S(1)} %regroup.5.refs_7_.refs_0_, bf16[32,768]{1,0:T(8,128)(2,1)S(1)} %regroup.6.refs_1_.refs_3_), custom_call_target="tpu_custom_call" | custom-call | flops 1 | bytes 1 | tf_op jit(solution)/shard_map/field/pallas_call | solution.py:376
  14.3 0.0 collective-permute-done.4.refs_0_
  14.3 0.3 %collective-permute-done.5.refs_1_ = bf16[48,384]{1,0:T(8,128)(2,1)S(1)} collective-permute-done((bf16[48,384]{1,0:T(8,128)(2,1)S(1)}, bf16[48,384]{1,0:T(8,128)(2,1)S(1)}, u32[]{:S(2)}, u32[]{:S(2)}) %collective-permute-start.5) | collective-permute-done | bytes 36896 | tf_op jit(solution)/shard_map/ppermute | solution.py:71
  14.6 0.5 %couple.1.refs_2_ = bf16[256,768]{1,0:T(8,128)(2,1)S(1)} custom-call(bf16[2,768,1536]{2,1,0:T(8,128)(2,1)S(1)} %get-tuple-element.13.screening, bf16[64,768]{1,0:T(8,128)(2,1)S(1)} %regroup.7.refs_3_.refs_0_, bf16[64,768]{1,0:T(8,128)(2,1)S(1)} %assemble.1.refs_4_.refs_1_), custom_call_target="tpu_custom_call" | custom-call | flops 1 | bytes 1 | tf_op jit(solution)/shard_map/couple/pallas_call | solution.py:445
  15.1 0.5 %near.1.refs_1_ = f32[24,128]{1,0:T(8,128)S(1)} custom-call(bf16[768,256]{1,0:T(8,128)(2,1)S(1)} %field.1.refs_2_.refs_0_, bf16[128,512]{1,0:T(8,128)(2,1)S(1)} %get-tuple-element.17.refs_1_, f32[8,128]{1,0:T(8,128)S(1)} %get-tuple-element.16.refs_2_, bf16[64,768]{1,0:T(8,128)(2,1)S(1)} %regroup.7.refs_3_.refs_0_, bf16[64,768]{1,0:T(8,128)(2,1)S(1)} %assemble.1.refs_4_.refs_1_), custom_call_target="tpu_custom_call" | custom-call | flops 1 | bytes 1 | tf_op jit(solution)/shard_map/near/pallas_call | solution.py:405
  15.6 0.5 %collective-permute-done.6.refs_4_ = bf16[32,768]{1,0:T(8,128)(2,1)S(1)} collective-permute-done((bf16[32,768]{1,0:T(8,128)(2,1)S(1)}, bf16[32,768]{1,0:T(8,128)(2,1)S(1)}, u32[]{:S(2)}, u32[]{:S(2)}) %collective-permute-start.6) | collective-permute-done | bytes 49184 | tf_op jit(solution)/shard_map/ppermute | solution.py:62
  16.1 0.5 %far.1 = f32[24,128]{1,0:T(8,128)S(1)} custom-call(bf16[128,512]{1,0:T(8,128)(2,1)S(1)} %get-tuple-element.12.refs_0_, f32[24,128]{1,0:T(8,128)S(1)} %near.1.refs_1_, bf16[256,768]{1,0:T(8,128)(2,1)S(1)} %couple.1.refs_2_, bf16[32,768]{1,0:T(8,128)(2,1)S(1)} %collective-permute-done.3.refs_4_.refs_3_, bf16[32,768]{1,0:T(8,128)(2,1)S(1)} %collective-permute-done.6.refs_4_), custom_call_target="tpu_custom_call" | custom-call | flops 1 | bytes 1 | tf_op jit(solution)/shard_map/far/pallas_call | solution.py:483
  16.7 0.4 %collective-permute-start.7 = (f32[24,128]{1,0:T(8,128)S(1)}, f32[24,128]{1,0:T(8,128)S(1)}, u32[]{:S(2)}, u32[]{:S(2)}) collective-permute-start(f32[24,128]{1,0:T(8,128)S(1)} %far.1), channel_id=1, source_target_pairs={{0,1},{1,0},{2,3},{3,2},{4,5},{5,4},{6,7},{7,6},{8,9},{9,8},{10,11... | collective-permute-start | bytes 36872 | tf_op jit(solution)/shard_map/ppermute | solution.py:71
  17.0 0.8 %collective-permute-done.7 = f32[24,128]{1,0:T(8,128)S(1)} collective-permute-done((f32[24,128]{1,0:T(8,128)S(1)}, f32[24,128]{1,0:T(8,128)S(1)}, u32[]{:S(2)}, u32[]{:S(2)}) %collective-permute-start.7) | collective-permute-done | bytes 12320 | tf_op jit(solution)/shard_map/ppermute | solution.py:71
  17.9 0.9 %collective-permute-start.8 = (f32[24,128]{1,0:T(8,128)S(1)}, f32[24,128]{1,0:T(8,128)S(1)}, u32[]{:S(2)}, u32[]{:S(2)}) collective-permute-start(f32[24,128]{1,0:T(8,128)S(1)} %add.6), channel_id=1, source_target_pairs={{0,3},{1,2},{2,1},{3,0},{4,7},{5,6},{6,5},{7,4},{8,11},{9,10},{10,... | collective-permute-start | bytes 36872 | tf_op jit(solution)/shard_map/ppermute | solution.py:62
  18.8 2.2 %collective-permute-done.8 = f32[24,128]{1,0:T(8,128)S(1)} collective-permute-done((f32[24,128]{1,0:T(8,128)S(1)}, f32[24,128]{1,0:T(8,128)S(1)}, u32[]{:S(2)}, u32[]{:S(2)}) %collective-permute-start.8) | collective-permute-done | bytes 12320 | tf_op jit(solution)/shard_map/ppermute | solution.py:62
  21.0 0.4 %collective-permute-start.9 = (f32[24,128]{1,0:T(8,128)S(1)}, f32[24,128]{1,0:T(8,128)S(1)}, u32[]{:S(2)}, u32[]{:S(2)}) collective-permute-start(f32[24,128]{1,0:T(8,128)S(1)} %add.7.refs_0_), channel_id=1, source_target_pairs={{0,5},{1,4},{4,9},{5,8},{8,13},{9,12},{12,1},{13,0},{2,7},{3,6},{6... | collective-permute-start | bytes 36872 | tf_op jit(solution)/shard_map/ppermute | solution.py:62
  21.4 1.9 %collective-permute-start.10 = (f32[24,128]{1,0:T(8,128)S(1)}, f32[24,128]{1,0:T(8,128)S(1)}, u32[]{:S(2)}, u32[]{:S(2)}) collective-permute-start(f32[24,128]{1,0:T(8,128)S(1)} %add.7.refs_0_), channel_id=1, source_target_pairs={{0,9},{1,8},{4,13},{5,12},{8,1},{9,0},{12,5},{13,4},{2,11},{3,10},... | collective-permute-start | bytes 36872 | tf_op jit(solution)/shard_map/ppermute | solution.py:62
  23.3 1.3 %collective-permute-start.11 = (f32[24,128]{1,0:T(8,128)S(1)}, f32[24,128]{1,0:T(8,128)S(1)}, u32[]{:S(2)}, u32[]{:S(2)}) collective-permute-start(f32[24,128]{1,0:T(8,128)S(1)} %add.7.refs_0_), channel_id=1, source_target_pairs={{0,13},{1,12},{4,1},{5,0},{8,5},{9,4},{12,9},{13,8},{2,15},{3,14},... | collective-permute-start | bytes 36872 | tf_op jit(solution)/shard_map/ppermute | solution.py:62
  24.6 1.3 %collective-permute-done.9.refs_1_ = f32[24,128]{1,0:T(8,128)S(1)} collective-permute-done((f32[24,128]{1,0:T(8,128)S(1)}, f32[24,128]{1,0:T(8,128)S(1)}, u32[]{:S(2)}, u32[]{:S(2)}) %collective-permute-start.9) | collective-permute-done | bytes 12320 | tf_op jit(solution)/shard_map/ppermute | solution.py:62
  25.9 0.0 collective-permute-done.10.refs_2_
  25.9 0.6 %collective-permute-done.11.refs_3_ = f32[24,128]{1,0:T(8,128)S(1)} collective-permute-done((f32[24,128]{1,0:T(8,128)S(1)}, f32[24,128]{1,0:T(8,128)S(1)}, u32[]{:S(2)}, u32[]{:S(2)}) %collective-permute-start.11) | collective-permute-done | bytes 12320 | tf_op jit(solution)/shard_map/ppermute | solution.py:62
  26.6 1.4 %haydock.1 = (f32[1,2,2,16]{3,2,1,0:T(2,128)}, f32[2,6]{1,0:T(2,128)}) custom-call(f32[24,128]{1,0:T(8,128)S(1)} %add.7.refs_0_, f32[24,128]{1,0:T(8,128)S(1)} %collective-permute-done.9.refs_1_, f32[24,128]{1,0:T(8,128)S(1)} %collective-permute-done.10.refs_2_, f32[24,128]{1,0:T(8,128)S(1)} %collective-permute-done.11.refs_3_), custom_call_target="tpu_custom_call" | custom-call | tf_op jit(solution)/shard_map/haydock/pallas_call | solution.py:580
  (8 shorter events, 0.0 us)
Async XLA Ops:
  1.7 6.3 %collective-permute-start = (bf16[32,768]{1,0:T(8,128)(2,1)S(1)}, bf16[32,768]{1,0:T(8,128)(2,1)S(1)}, u32[]{:S(2)}, u32[]{:S(2)}) collective-permute-start(bf16[32,768]{1,0:T(8,128)(2,1)S(1)} %get-tuple-element.11), channel_id=1, source_target_pairs={{0,5},{1,4},{4,9},{5,8},{8,13},{9,12},{12,1},{13,0},{2,7},{3,6},{6... | collective-permute-start | bytes 147464 | tf_op jit(solution)/shard_map/ppermute | solution.py:62
  4.2 8.3 %collective-permute-start.1 = (bf16[32,768]{1,0:T(8,128)(2,1)S(1)}, bf16[32,768]{1,0:T(8,128)(2,1)S(1)}, u32[]{:S(2)}, u32[]{:S(2)}) collective-permute-start(bf16[32,768]{1,0:T(8,128)(2,1)S(1)} %get-tuple-element.14), channel_id=1, source_target_pairs={{0,9},{1,8},{4,13},{5,12},{8,1},{9,0},{12,5},{13,4},{2,11},{3,10},... | collective-permute-start | bytes 147464 | tf_op jit(solution)/shard_map/ppermute | solution.py:62
  7.1 5.4 %collective-permute-start.2 = (bf16[32,768]{1,0:T(8,128)(2,1)S(1)}, bf16[32,768]{1,0:T(8,128)(2,1)S(1)}, u32[]{:S(2)}, u32[]{:S(2)}) collective-permute-start(bf16[32,768]{1,0:T(8,128)(2,1)S(1)} %get-tuple-element.15), channel_id=1, source_target_pairs={{0,13},{1,12},{4,1},{5,0},{8,5},{9,4},{12,9},{13,8},{2,15},{3,14},... | collective-permute-start | bytes 147464 | tf_op jit(solution)/shard_map/ppermute | solution.py:62
  8.0 4.9 %collective-permute-start.3 = (bf16[32,768]{1,0:T(8,128)(2,1)S(1)}, bf16[32,768]{1,0:T(8,128)(2,1)S(1)}, u32[]{:S(2)}, u32[]{:S(2)}) collective-permute-start(bf16[32,768]{1,0:T(8,128)(2,1)S(1)} %regroup.5.refs_7_.refs_0_), channel_id=1, source_target_pairs={{0,3},{1,2},{2,1},{3,0},{4,7},{5,6},{6,5},{7,4},{8,11},{9,10},{10,... | collective-permute-start | bytes 147464 | tf_op jit(solution)/shard_map/ppermute | solution.py:62
  12.5 3.6 %collective-permute-start.6 = (bf16[32,768]{1,0:T(8,128)(2,1)S(1)}, bf16[32,768]{1,0:T(8,128)(2,1)S(1)}, u32[]{:S(2)}, u32[]{:S(2)}) collective-permute-start(bf16[32,768]{1,0:T(8,128)(2,1)S(1)} %regroup.6.refs_1_.refs_3_), channel_id=1, source_target_pairs={{0,3},{1,2},{2,1},{3,0},{4,7},{5,6},{6,5},{7,4},{8,11},{9,10},{10,... | collective-permute-start | bytes 147464 | tf_op jit(solution)/shard_map/ppermute | solution.py:62
  12.9 1.4 %collective-permute-start.4 = (bf16[48,384]{1,0:T(8,128)(2,1)S(1)}, bf16[48,384]{1,0:T(8,128)(2,1)S(1)}, u32[]{:S(2)}, u32[]{:S(2)}) collective-permute-start(bf16[48,384]{1,0:T(8,128)(2,1)S(1)} %regroup.8), channel_id=1, source_target_pairs={{0,1},{1,0},{2,3},{3,2},{4,5},{5,4},{6,7},{7,6},{8,9},{9,8},{10,11... | collective-permute-start | bytes 110600 | tf_op jit(solution)/shard_map/ppermute | solution.py:71
  13.4 1.2 %collective-permute-start.5 = (bf16[48,384]{1,0:T(8,128)(2,1)S(1)}, bf16[48,384]{1,0:T(8,128)(2,1)S(1)}, u32[]{:S(2)}, u32[]{:S(2)}) collective-permute-start(bf16[48,384]{1,0:T(8,128)(2,1)S(1)} %regroup.9), channel_id=1, source_target_pairs={{0,1},{1,0},{2,3},{3,2},{4,5},{5,4},{6,7},{7,6},{8,9},{9,8},{10,11... | collective-permute-start | bytes 110600 | tf_op jit(solution)/shard_map/ppermute | solution.py:71
  16.7 1.2 %collective-permute-start.7 = (f32[24,128]{1,0:T(8,128)S(1)}, f32[24,128]{1,0:T(8,128)S(1)}, u32[]{:S(2)}, u32[]{:S(2)}) collective-permute-start(f32[24,128]{1,0:T(8,128)S(1)} %far.1), channel_id=1, source_target_pairs={{0,1},{1,0},{2,3},{3,2},{4,5},{5,4},{6,7},{7,6},{8,9},{9,8},{10,11... | collective-permute-start | bytes 36872 | tf_op jit(solution)/shard_map/ppermute | solution.py:71
  17.9 3.1 %collective-permute-start.8 = (f32[24,128]{1,0:T(8,128)S(1)}, f32[24,128]{1,0:T(8,128)S(1)}, u32[]{:S(2)}, u32[]{:S(2)}) collective-permute-start(f32[24,128]{1,0:T(8,128)S(1)} %add.6), channel_id=1, source_target_pairs={{0,3},{1,2},{2,1},{3,0},{4,7},{5,6},{6,5},{7,4},{8,11},{9,10},{10,... | collective-permute-start | bytes 36872 | tf_op jit(solution)/shard_map/ppermute | solution.py:62
  21.0 4.9 %collective-permute-start.9 = (f32[24,128]{1,0:T(8,128)S(1)}, f32[24,128]{1,0:T(8,128)S(1)}, u32[]{:S(2)}, u32[]{:S(2)}) collective-permute-start(f32[24,128]{1,0:T(8,128)S(1)} %add.7.refs_0_), channel_id=1, source_target_pairs={{0,5},{1,4},{4,9},{5,8},{8,13},{9,12},{12,1},{13,0},{2,7},{3,6},{6... | collective-permute-start | bytes 36872 | tf_op jit(solution)/shard_map/ppermute | solution.py:62
  21.4 4.5 %collective-permute-start.10 = (f32[24,128]{1,0:T(8,128)S(1)}, f32[24,128]{1,0:T(8,128)S(1)}, u32[]{:S(2)}, u32[]{:S(2)}) collective-permute-start(f32[24,128]{1,0:T(8,128)S(1)} %add.7.refs_0_), channel_id=1, source_target_pairs={{0,9},{1,8},{4,13},{5,12},{8,1},{9,0},{12,5},{13,4},{2,11},{3,10},... | collective-permute-start | bytes 36872 | tf_op jit(solution)/shard_map/ppermute | solution.py:62
  23.3 3.3 %collective-permute-start.11 = (f32[24,128]{1,0:T(8,128)S(1)}, f32[24,128]{1,0:T(8,128)S(1)}, u32[]{:S(2)}, u32[]{:S(2)}) collective-permute-start(f32[24,128]{1,0:T(8,128)S(1)} %add.7.refs_0_), channel_id=1, source_target_pairs={{0,13},{1,12},{4,1},{5,0},{8,5},{9,4},{12,9},{13,8},{2,15},{3,14},... | collective-permute-start | bytes 36872 | tf_op jit(solution)/shard_map/ppermute | solution.py:62

commit v19 on v18

--- a/solution.py
+++ b/solution.py
@@ -320,21 +320,14 @@
     share_rows = share * cond_count
     c_of_row = origin(half, crow // share_rows, ba) * share + crow % share_rows // cond_count
     same_c = c_of_row == iota((cond_rows, lanes), 1) % cond_count
-    spread = jnp.concatenate(
-        [
-            jnp.where(same_c, spread[:, v2 * lanes : (v2 + 1) * lanes], 0.0)
-            for v2 in range(val_count)
-        ],
-        0,
-    )
-    out_row = iota((codes, val_count * cond_rows), 0)
-    out_col = iota((codes, val_count * cond_rows), 1)
-    fold = (out_row // cond_count == out_col // cond_rows) & (
-        out_row % cond_count == out_col % cond_count
-    )
-    fold = jnp.where(fold, 1.0, 0.0).astype(jnp.bfloat16)
-    piece = jnp.dot(fold, jnp.concatenate(split(spread), 1), preferred_element_type=jnp.float32)
-    return piece[:, :lanes] + piece[:, lanes:]
+    rows = []
+    for v2 in range(val_count):
+        kept = jnp.where(same_c, spread[:, v2 * lanes : (v2 + 1) * lanes], 0.0)
+        parts = [kept[c * cond_count : (c + 1) * cond_count] for c in range(cond_count)]
+        while len(parts) > 1:
+            parts = [x + y for x, y in zip(parts[::2], parts[1::2])] + parts[len(parts) // 2 * 2 :]
+        rows.append(parts[0])
+    return jnp.concatenate(rows, 0)
 
 
 def diagonal(crossed, ka, ba, share_rows, sign):
@@ -492,8 +485,8 @@
 
 
 def haydock_kernel(ka, codes, scale_count, npol, *refs):
-    pieces = refs[:-3]
-    next_out, coef_out, matrix = refs[-3:]
+    pieces = refs[:-2]
+    next_out, coef_out = refs[-2:]
     lanes = pieces[0].shape[1]
     mid = lanes // 2
     height = codes + EXTRA_ROWS
@@ -506,14 +499,15 @@
         slots.append((ref[at : at + codes, :], rows[npol + 2 : npol + 3]))
     own = pieces[0][codes:height, :]
     sign = jnp.where(iota((1, lanes), 1) < mid, -1.0, 1.0)
+    top = []
     for k2 in range(ka):
         block = jnp.zeros((codes, lanes), jnp.float32)
         for piece, second in slots:
             block = jnp.where(second == float(k2), piece, block)
-        matrix[k2 * codes : (k2 + 1) * codes, :] = block
-        matrix[mid + k2 * codes : mid + (k2 + 1) * codes, :] = sign * pltpu.roll(block, mid, 1)
-    high, low = split(matrix[...])
-    full = jnp.concatenate([high, low], 1)
+        top.append(block)
+    top = jnp.concatenate(top, 0)
+    matrix = jnp.concatenate([top, sign * pltpu.roll(top, mid, 1)], 0)
+    full = jnp.concatenate(split(matrix), 1)
     start = extras[:npol]
     energy = extras[npol : npol + 1]
 
@@ -585,7 +579,6 @@
         ],
         in_specs=[vmem] * len(pieces),
         out_specs=[vmem, vmem],
-        scratch_shapes=[pltpu.VMEM(square.shape, square.dtype)],
         compiler_params=limits(*pieces, square),
         name="haydock",
     )(*pieces)

time: 28.1 us -> 28.1 us (level)
  no operation moved by 1% of the time
where the time goes in v19:
time: 28.1 us; the launch traced here: 27.9 us
  starting transfers between devices  14 us (50%)
  Pallas kernels  7.03 us (25%)
  waiting for transfers between devices  6.19 us (22%)
  between operations  0.72 us (3%)
    ppermute x9, starting transfers between devices, exchanged(): return lax.ppermute(value, (axis, 'ba'), pairs)  13 us
    ppermute x9, waiting for transfers between devices, exchanged(): return lax.ppermute(value, (axis, 'ba'), pairs)  5.07 us
    pallas_call x1, Pallas kernels, prepare(): pl.pallas_call(functools.partial(prepare_kernel, ka, dims), out_shape=[in...  2.45 us
    pallas_call x1, Pallas kernels, haydock(): pl.pallas_call(functools.partial(haydock_kernel, ka, codes, scale_count,...  1.41 us
    ppermute x3, waiting for transfers between devices, handed(): lax.ppermute(value, 'ba', [(h, (h + step) % size) for h in range(size)])  1.12 us
    pallas_call x1, Pallas kernels, pack(): pl.pallas_call(functools.partial(pack_kernel, ka), out_shape=[own] + [sha...  1.05 us
    ppermute x3, starting transfers between devices, handed(): lax.ppermute(value, 'ba', [(h, (h + step) % size) for h in range(size)])  1 us
    pallas_call x1, Pallas kernels, field(): pl.pallas_call(functools.partial(field_kernel, pairs), out_shape=in_vmem(...  0.78 us
  transfers between devices with their start and end apart: 12, of which 7 were waited for; matrix products, arithmetic and copies ran while one was open for 0% of the time, Pallas kernels for 15%

profile of v19, /device:TPU:0, one launch (start us, length us, event | category | flops | bytes accessed | tf_op | source)
XLA Modules:
  0.0 27.9 jit_solution(11756261032536252286)
XLA Ops:
  0.6 1.1 %pack.1 = (bf16[48,768]{1,0:T(8,128)(2,1)S(1)}, bf16[32,768]{1,0:T(8,128)(2,1)S(1)}, bf16[32,768]{1,0:T(8,128)(2,1)S(1)}, bf16[32,768]{1,0:T(8,128)(2,1)S(1)}) custom-call(s32[4,4]{1,0:T(4,128)} %refs_0_.1, s32[4]{0:T(128)} %refs_1_.1, bf16[1,4,2,2,4,768]{5,4,3,2,1,0:T(4,128)(2,1)} %valence_in.1, bf16[1,4,2,4,4,768]{5,4,3,2,1,0:T(4,128)(2,1)} %conduction_in.1), custom_call_target="tpu_custom_call" | custom-call | tf_op jit(solution)/shard_map/pack/pallas_call | solution.py:123
  1.7 2.5 %collective-permute-start = (bf16[32,768]{1,0:T(8,128)(2,1)S(1)}, bf16[32,768]{1,0:T(8,128)(2,1)S(1)}, u32[]{:S(2)}, u32[]{:S(2)}) collective-permute-start(bf16[32,768]{1,0:T(8,128)(2,1)S(1)} %get-tuple-element.11), channel_id=1, source_target_pairs={{0,5},{1,4},{4,9},{5,8},{8,13},{9,12},{12,1},{13,0},{2,7},{3,6},{6... | collective-permute-start | bytes 147464 | tf_op jit(solution)/shard_map/ppermute | solution.py:62
  4.2 2.9 %collective-permute-start.1 = (bf16[32,768]{1,0:T(8,128)(2,1)S(1)}, bf16[32,768]{1,0:T(8,128)(2,1)S(1)}, u32[]{:S(2)}, u32[]{:S(2)}) collective-permute-start(bf16[32,768]{1,0:T(8,128)(2,1)S(1)} %get-tuple-element.14), channel_id=1, source_target_pairs={{0,9},{1,8},{4,13},{5,12},{8,1},{9,0},{12,5},{13,4},{2,11},{3,10},... | collective-permute-start | bytes 147464 | tf_op jit(solution)/shard_map/ppermute | solution.py:62
  7.1 0.8 %collective-permute-start.2 = (bf16[32,768]{1,0:T(8,128)(2,1)S(1)}, bf16[32,768]{1,0:T(8,128)(2,1)S(1)}, u32[]{:S(2)}, u32[]{:S(2)}) collective-permute-start(bf16[32,768]{1,0:T(8,128)(2,1)S(1)} %get-tuple-element.15), channel_id=1, source_target_pairs={{0,13},{1,12},{4,1},{5,0},{8,5},{9,4},{12,9},{13,8},{2,15},{3,14},... | collective-permute-start | bytes 147464 | tf_op jit(solution)/shard_map/ppermute | solution.py:62
  7.9 0.1 collective-permute-done.refs_1_.refs_0_
  8.0 2.0 %collective-permute-start.3 = (bf16[32,768]{1,0:T(8,128)(2,1)S(1)}, bf16[32,768]{1,0:T(8,128)(2,1)S(1)}, u32[]{:S(2)}, u32[]{:S(2)}) collective-permute-start(bf16[32,768]{1,0:T(8,128)(2,1)S(1)} %regroup.5.refs_7_.refs_0_), channel_id=1, source_target_pairs={{0,3},{1,2},{2,1},{3,0},{4,7},{5,6},{6,5},{7,4},{8,11},{9,10},{10,... | collective-permute-start | bytes 147464 | tf_op jit(solution)/shard_map/ppermute | solution.py:62
  10.0 2.5 %prepare.1 = (bf16[2,768,1536]{2,1,0:T(8,128)(2,1)S(1)}, bf16[128,512]{1,0:T(8,128)(2,1)S(1)}, bf16[128,512]{1,0:T(8,128)(2,1)S(1)}, f32[8,128]{1,0:T(8,128)S(1)}) custom-call(s32[4,4]{1,0:T(4,128)} %refs_0_.1, s32[4]{0:T(128)} %refs_1_.1, s32[16]{0:T(128)} %refs_2_.1, f32[1,4]{1,0:T(1,128)} %refs_3_.1, f32[1,4]{1,0:T(1,128)} %refs_4_.1, ...), custom_call_target="tpu_custom_call" | custom-call | bytes 9437184 | tf_op jit(solution)/shard_map/prepare/pallas_call | solution.py:231
  12.5 0.0 collective-permute-done.1.refs_0_.refs_2_.refs_1_
  12.5 0.0 collective-permute-done.2.refs_1_.refs_3_.refs_2_
  12.5 0.4 %collective-permute-start.6 = (bf16[32,768]{1,0:T(8,128)(2,1)S(1)}, bf16[32,768]{1,0:T(8,128)(2,1)S(1)}, u32[]{:S(2)}, u32[]{:S(2)}) collective-permute-start(bf16[32,768]{1,0:T(8,128)(2,1)S(1)} %regroup.6.refs_1_.refs_3_), channel_id=1, source_target_pairs={{0,3},{1,2},{2,1},{3,0},{4,7},{5,6},{6,5},{7,4},{8,11},{9,10},{10,... | collective-permute-start | bytes 147464 | tf_op jit(solution)/shard_map/ppermute | solution.py:62
  12.9 0.0 collective-permute-done.3.refs_4_.refs_3_
  12.9 0.5 %collective-permute-start.4 = (bf16[48,384]{1,0:T(8,128)(2,1)S(1)}, bf16[48,384]{1,0:T(8,128)(2,1)S(1)}, u32[]{:S(2)}, u32[]{:S(2)}) collective-permute-start(bf16[48,384]{1,0:T(8,128)(2,1)S(1)} %regroup.8), channel_id=1, source_target_pairs={{0,1},{1,0},{2,3},{3,2},{4,5},{5,4},{6,7},{7,6},{8,9},{9,8},{10,11... | collective-permute-start | bytes 110600 | tf_op jit(solution)/shard_map/ppermute | solution.py:71
  13.4 0.1 collective-permute-start.5
  13.5 0.8 %field.1.refs_2_.refs_0_ = bf16[768,256]{1,0:T(8,128)(2,1)S(1)} custom-call(bf16[2,768,1536]{2,1,0:T(8,128)(2,1)S(1)} %get-tuple-element.13.screening, bf16[32,768]{1,0:T(8,128)(2,1)S(1)} %regroup.5.refs_7_.refs_0_, bf16[32,768]{1,0:T(8,128)(2,1)S(1)} %regroup.6.refs_1_.refs_3_), custom_call_target="tpu_custom_call" | custom-call | flops 1 | bytes 1 | tf_op jit(solution)/shard_map/field/pallas_call | solution.py:369
  14.3 0.0 collective-permute-done.4.refs_0_
  14.3 0.3 %collective-permute-done.5.refs_1_ = bf16[48,384]{1,0:T(8,128)(2,1)S(1)} collective-permute-done((bf16[48,384]{1,0:T(8,128)(2,1)S(1)}, bf16[48,384]{1,0:T(8,128)(2,1)S(1)}, u32[]{:S(2)}, u32[]{:S(2)}) %collective-permute-start.5) | collective-permute-done | bytes 36896 | tf_op jit(solution)/shard_map/ppermute | solution.py:71
  14.6 0.5 %couple.1.refs_2_ = bf16[256,768]{1,0:T(8,128)(2,1)S(1)} custom-call(bf16[2,768,1536]{2,1,0:T(8,128)(2,1)S(1)} %get-tuple-element.13.screening, bf16[64,768]{1,0:T(8,128)(2,1)S(1)} %regroup.7.refs_3_.refs_0_, bf16[64,768]{1,0:T(8,128)(2,1)S(1)} %assemble.1.refs_4_.refs_1_), custom_call_target="tpu_custom_call" | custom-call | flops 1 | bytes 1 | tf_op jit(solution)/shard_map/couple/pallas_call | solution.py:438
  15.1 0.4 %near.1.refs_1_ = f32[24,128]{1,0:T(8,128)S(1)} custom-call(bf16[768,256]{1,0:T(8,128)(2,1)S(1)} %field.1.refs_2_.refs_0_, bf16[128,512]{1,0:T(8,128)(2,1)S(1)} %get-tuple-element.17.refs_1_, f32[8,128]{1,0:T(8,128)S(1)} %get-tuple-element.16.refs_2_, bf16[64,768]{1,0:T(8,128)(2,1)S(1)} %regroup.7.refs_3_.refs_0_, bf16[64,768]{1,0:T(8,128)(2,1)S(1)} %assemble.1.refs_4_.refs_1_), custom_call_target="tpu_custom_call" | custom-call | flops 1 | bytes 1 | tf_op jit(solution)/shard_map/near/pallas_call | solution.py:398
  15.5 0.6 %collective-permute-done.6.refs_4_ = bf16[32,768]{1,0:T(8,128)(2,1)S(1)} collective-permute-done((bf16[32,768]{1,0:T(8,128)(2,1)S(1)}, bf16[32,768]{1,0:T(8,128)(2,1)S(1)}, u32[]{:S(2)}, u32[]{:S(2)}) %collective-permute-start.6) | collective-permute-done | bytes 49184 | tf_op jit(solution)/shard_map/ppermute | solution.py:62
  16.1 0.4 %far.1 = f32[24,128]{1,0:T(8,128)S(1)} custom-call(bf16[128,512]{1,0:T(8,128)(2,1)S(1)} %get-tuple-element.12.refs_0_, f32[24,128]{1,0:T(8,128)S(1)} %near.1.refs_1_, bf16[256,768]{1,0:T(8,128)(2,1)S(1)} %couple.1.refs_2_, bf16[32,768]{1,0:T(8,128)(2,1)S(1)} %collective-permute-done.3.refs_4_.refs_3_, bf16[32,768]{1,0:T(8,128)(2,1)S(1)} %collective-permute-done.6.refs_4_), custom_call_target="tpu_custom_call" | custom-call | flops 1 | bytes 1 | tf_op jit(solution)/shard_map/far/pallas_call | solution.py:476
  16.6 0.4 %collective-permute-start.7 = (f32[24,128]{1,0:T(8,128)S(1)}, f32[24,128]{1,0:T(8,128)S(1)}, u32[]{:S(2)}, u32[]{:S(2)}) collective-permute-start(f32[24,128]{1,0:T(8,128)S(1)} %far.1), channel_id=1, source_target_pairs={{0,1},{1,0},{2,3},{3,2},{4,5},{5,4},{6,7},{7,6},{8,9},{9,8},{10,11... | collective-permute-start | bytes 36872 | tf_op jit(solution)/shard_map/ppermute | solution.py:71
  17.0 0.8 %collective-permute-done.7 = f32[24,128]{1,0:T(8,128)S(1)} collective-permute-done((f32[24,128]{1,0:T(8,128)S(1)}, f32[24,128]{1,0:T(8,128)S(1)}, u32[]{:S(2)}, u32[]{:S(2)}) %collective-permute-start.7) | collective-permute-done | bytes 12320 | tf_op jit(solution)/shard_map/ppermute | solution.py:71
  17.8 0.8 %collective-permute-start.8 = (f32[24,128]{1,0:T(8,128)S(1)}, f32[24,128]{1,0:T(8,128)S(1)}, u32[]{:S(2)}, u32[]{:S(2)}) collective-permute-start(f32[24,128]{1,0:T(8,128)S(1)} %add.6), channel_id=1, source_target_pairs={{0,3},{1,2},{2,1},{3,0},{4,7},{5,6},{6,5},{7,4},{8,11},{9,10},{10,... | collective-permute-start | bytes 36872 | tf_op jit(solution)/shard_map/ppermute | solution.py:62
  18.6 2.4 %collective-permute-done.8 = f32[24,128]{1,0:T(8,128)S(1)} collective-permute-done((f32[24,128]{1,0:T(8,128)S(1)}, f32[24,128]{1,0:T(8,128)S(1)}, u32[]{:S(2)}, u32[]{:S(2)}) %collective-permute-start.8) | collective-permute-done | bytes 12320 | tf_op jit(solution)/shard_map/ppermute | solution.py:62
  20.9 0.4 %collective-permute-start.9 = (f32[24,128]{1,0:T(8,128)S(1)}, f32[24,128]{1,0:T(8,128)S(1)}, u32[]{:S(2)}, u32[]{:S(2)}) collective-permute-start(f32[24,128]{1,0:T(8,128)S(1)} %add.7.refs_0_), channel_id=1, source_target_pairs={{0,5},{1,4},{4,9},{5,8},{8,13},{9,12},{12,1},{13,0},{2,7},{3,6},{6... | collective-permute-start | bytes 36872 | tf_op jit(solution)/shard_map/ppermute | solution.py:62
  21.3 1.9 %collective-permute-start.10 = (f32[24,128]{1,0:T(8,128)S(1)}, f32[24,128]{1,0:T(8,128)S(1)}, u32[]{:S(2)}, u32[]{:S(2)}) collective-permute-start(f32[24,128]{1,0:T(8,128)S(1)} %add.7.refs_0_), channel_id=1, source_target_pairs={{0,9},{1,8},{4,13},{5,12},{8,1},{9,0},{12,5},{13,4},{2,11},{3,10},... | collective-permute-start | bytes 36872 | tf_op jit(solution)/shard_map/ppermute | solution.py:62
  23.2 1.3 %collective-permute-start.11 = (f32[24,128]{1,0:T(8,128)S(1)}, f32[24,128]{1,0:T(8,128)S(1)}, u32[]{:S(2)}, u32[]{:S(2)}) collective-permute-start(f32[24,128]{1,0:T(8,128)S(1)} %add.7.refs_0_), channel_id=1, source_target_pairs={{0,13},{1,12},{4,1},{5,0},{8,5},{9,4},{12,9},{13,8},{2,15},{3,14},... | collective-permute-start | bytes 36872 | tf_op jit(solution)/shard_map/ppermute | solution.py:62
  24.6 1.3 %collective-permute-done.9.refs_1_ = f32[24,128]{1,0:T(8,128)S(1)} collective-permute-done((f32[24,128]{1,0:T(8,128)S(1)}, f32[24,128]{1,0:T(8,128)S(1)}, u32[]{:S(2)}, u32[]{:S(2)}) %collective-permute-start.9) | collective-permute-done | bytes 12320 | tf_op jit(solution)/shard_map/ppermute | solution.py:62
  25.9 0.0 collective-permute-done.10.refs_2_
  25.9 0.6 %collective-permute-done.11.refs_3_ = f32[24,128]{1,0:T(8,128)S(1)} collective-permute-done((f32[24,128]{1,0:T(8,128)S(1)}, f32[24,128]{1,0:T(8,128)S(1)}, u32[]{:S(2)}, u32[]{:S(2)}) %collective-permute-start.11) | collective-permute-done | bytes 12320 | tf_op jit(solution)/shard_map/ppermute | solution.py:62
  26.5 1.4 %haydock.1 = (f32[1,2,2,16]{3,2,1,0:T(2,128)}, f32[2,6]{1,0:T(2,128)}) custom-call(f32[24,128]{1,0:T(8,128)S(1)} %add.7.refs_0_, f32[24,128]{1,0:T(8,128)S(1)} %collective-permute-done.9.refs_1_, f32[24,128]{1,0:T(8,128)S(1)} %collective-permute-done.10.refs_2_, f32[24,128]{1,0:T(8,128)S(1)} %collective-permute-done.11.refs_3_), custom_call_target="tpu_custom_call" | custom-call | tf_op jit(solution)/shard_map/haydock/pallas_call | solution.py:574
  (8 shorter events, 0.0 us)
Async XLA Ops:
  1.7 6.3 %collective-permute-start = (bf16[32,768]{1,0:T(8,128)(2,1)S(1)}, bf16[32,768]{1,0:T(8,128)(2,1)S(1)}, u32[]{:S(2)}, u32[]{:S(2)}) collective-permute-start(bf16[32,768]{1,0:T(8,128)(2,1)S(1)} %get-tuple-element.11), channel_id=1, source_target_pairs={{0,5},{1,4},{4,9},{5,8},{8,13},{9,12},{12,1},{13,0},{2,7},{3,6},{6... | collective-permute-start | bytes 147464 | tf_op jit(solution)/shard_map/ppermute | solution.py:62
  4.2 8.3 %collective-permute-start.1 = (bf16[32,768]{1,0:T(8,128)(2,1)S(1)}, bf16[32,768]{1,0:T(8,128)(2,1)S(1)}, u32[]{:S(2)}, u32[]{:S(2)}) collective-permute-start(bf16[32,768]{1,0:T(8,128)(2,1)S(1)} %get-tuple-element.14), channel_id=1, source_target_pairs={{0,9},{1,8},{4,13},{5,12},{8,1},{9,0},{12,5},{13,4},{2,11},{3,10},... | collective-permute-start | bytes 147464 | tf_op jit(solution)/shard_map/ppermute | solution.py:62
  7.1 5.4 %collective-permute-start.2 = (bf16[32,768]{1,0:T(8,128)(2,1)S(1)}, bf16[32,768]{1,0:T(8,128)(2,1)S(1)}, u32[]{:S(2)}, u32[]{:S(2)}) collective-permute-start(bf16[32,768]{1,0:T(8,128)(2,1)S(1)} %get-tuple-element.15), channel_id=1, source_target_pairs={{0,13},{1,12},{4,1},{5,0},{8,5},{9,4},{12,9},{13,8},{2,15},{3,14},... | collective-permute-start | bytes 147464 | tf_op jit(solution)/shard_map/ppermute | solution.py:62
  8.0 4.9 %collective-permute-start.3 = (bf16[32,768]{1,0:T(8,128)(2,1)S(1)}, bf16[32,768]{1,0:T(8,128)(2,1)S(1)}, u32[]{:S(2)}, u32[]{:S(2)}) collective-permute-start(bf16[32,768]{1,0:T(8,128)(2,1)S(1)} %regroup.5.refs_7_.refs_0_), channel_id=1, source_target_pairs={{0,3},{1,2},{2,1},{3,0},{4,7},{5,6},{6,5},{7,4},{8,11},{9,10},{10,... | collective-permute-start | bytes 147464 | tf_op jit(solution)/shard_map/ppermute | solution.py:62
  12.5 3.6 %collective-permute-start.6 = (bf16[32,768]{1,0:T(8,128)(2,1)S(1)}, bf16[32,768]{1,0:T(8,128)(2,1)S(1)}, u32[]{:S(2)}, u32[]{:S(2)}) collective-permute-start(bf16[32,768]{1,0:T(8,128)(2,1)S(1)} %regroup.6.refs_1_.refs_3_), channel_id=1, source_target_pairs={{0,3},{1,2},{2,1},{3,0},{4,7},{5,6},{6,5},{7,4},{8,11},{9,10},{10,... | collective-permute-start | bytes 147464 | tf_op jit(solution)/shard_map/ppermute | solution.py:62
  12.9 1.4 %collective-permute-start.4 = (bf16[48,384]{1,0:T(8,128)(2,1)S(1)}, bf16[48,384]{1,0:T(8,128)(2,1)S(1)}, u32[]{:S(2)}, u32[]{:S(2)}) collective-permute-start(bf16[48,384]{1,0:T(8,128)(2,1)S(1)} %regroup.8), channel_id=1, source_target_pairs={{0,1},{1,0},{2,3},{3,2},{4,5},{5,4},{6,7},{7,6},{8,9},{9,8},{10,11... | collective-permute-start | bytes 110600 | tf_op jit(solution)/shard_map/ppermute | solution.py:71
  13.4 1.2 %collective-permute-start.5 = (bf16[48,384]{1,0:T(8,128)(2,1)S(1)}, bf16[48,384]{1,0:T(8,128)(2,1)S(1)}, u32[]{:S(2)}, u32[]{:S(2)}) collective-permute-start(bf16[48,384]{1,0:T(8,128)(2,1)S(1)} %regroup.9), channel_id=1, source_target_pairs={{0,1},{1,0},{2,3},{3,2},{4,5},{5,4},{6,7},{7,6},{8,9},{9,8},{10,11... | collective-permute-start | bytes 110600 | tf_op jit(solution)/shard_map/ppermute | solution.py:71
  16.6 1.3 %collective-permute-start.7 = (f32[24,128]{1,0:T(8,128)S(1)}, f32[24,128]{1,0:T(8,128)S(1)}, u32[]{:S(2)}, u32[]{:S(2)}) collective-permute-start(f32[24,128]{1,0:T(8,128)S(1)} %far.1), channel_id=1, source_target_pairs={{0,1},{1,0},{2,3},{3,2},{4,5},{5,4},{6,7},{7,6},{8,9},{9,8},{10,11... | collective-permute-start | bytes 36872 | tf_op jit(solution)/shard_map/ppermute | solution.py:71
  17.8 3.1 %collective-permute-start.8 = (f32[24,128]{1,0:T(8,128)S(1)}, f32[24,128]{1,0:T(8,128)S(1)}, u32[]{:S(2)}, u32[]{:S(2)}) collective-permute-start(f32[24,128]{1,0:T(8,128)S(1)} %add.6), channel_id=1, source_target_pairs={{0,3},{1,2},{2,1},{3,0},{4,7},{5,6},{6,5},{7,4},{8,11},{9,10},{10,... | collective-permute-start | bytes 36872 | tf_op jit(solution)/shard_map/ppermute | solution.py:62
  20.9 4.9 %collective-permute-start.9 = (f32[24,128]{1,0:T(8,128)S(1)}, f32[24,128]{1,0:T(8,128)S(1)}, u32[]{:S(2)}, u32[]{:S(2)}) collective-permute-start(f32[24,128]{1,0:T(8,128)S(1)} %add.7.refs_0_), channel_id=1, source_target_pairs={{0,5},{1,4},{4,9},{5,8},{8,13},{9,12},{12,1},{13,0},{2,7},{3,6},{6... | collective-permute-start | bytes 36872 | tf_op jit(solution)/shard_map/ppermute | solution.py:62
  21.3 4.5 %collective-permute-start.10 = (f32[24,128]{1,0:T(8,128)S(1)}, f32[24,128]{1,0:T(8,128)S(1)}, u32[]{:S(2)}, u32[]{:S(2)}) collective-permute-start(f32[24,128]{1,0:T(8,128)S(1)} %add.7.refs_0_), channel_id=1, source_target_pairs={{0,9},{1,8},{4,13},{5,12},{8,1},{9,0},{12,5},{13,4},{2,11},{3,10},... | collective-permute-start | bytes 36872 | tf_op jit(solution)/shard_map/ppermute | solution.py:62
  23.2 3.3 %collective-permute-start.11 = (f32[24,128]{1,0:T(8,128)S(1)}, f32[24,128]{1,0:T(8,128)S(1)}, u32[]{:S(2)}, u32[]{:S(2)}) collective-permute-start(f32[24,128]{1,0:T(8,128)S(1)} %add.7.refs_0_), channel_id=1, source_target_pairs={{0,13},{1,12},{4,1},{5,0},{8,5},{9,4},{12,9},{13,8},{2,15},{3,14},... | collective-permute-start | bytes 36872 | tf_op jit(solution)/shard_map/ppermute | solution.py:62

commit v20 on v19

--- a/solution.py
+++ b/solution.py
@@ -286,11 +286,11 @@
     return pl.pallas_call(
         functools.partial(assemble_kernel, rows),
         out_shape=in_vmem((height, own.shape[1]), own.dtype),
-        in_specs=[vmem] * (1 + len(parts)) + [anywhere],
+        in_specs=[vmem] * (1 + len(parts)) + [anywhere] * len(after),
         out_specs=vmem,
         compiler_params=limits(own, *parts),
         name="assemble",
-    )(own, *parts, after)
+    )(own, *parts, *after)
 
 
 def with_turned(halves, pairs):
@@ -380,7 +380,7 @@
 def near_kernel(ka, ba, dims, *refs):
     vloc, val_count, cond_count, npol = dims
     fields, table, extras = refs[:3]
-    cond_in, out = refs[3:-1], refs[-1]
+    cond_in, out = refs[3 : 3 + ba], refs[-1]
     codes = val_count * cond_count
     cond = jnp.concatenate([ref[...] for ref in cond_in], 0)
     crossed = jnp.dot(cond, fields[...], preferred_element_type=jnp.float32)
@@ -391,19 +391,19 @@
     out[codes:, :] = extras[...]
 
 
-def near(ka, ba, dims, fields, table, extras, cond_all):
+def near(ka, ba, dims, fields, table, extras, cond_all, after):
     vloc, val_count, cond_count, npol = dims
     operands = [fields, table, extras, *cond_all]
     shape = (val_count * cond_count + EXTRA_ROWS, extras.shape[1])
     return pl.pallas_call(
         functools.partial(near_kernel, ka, ba, dims),
         out_shape=in_vmem(shape, jnp.float32),
-        in_specs=[vmem] * len(operands),
+        in_specs=[vmem] * len(operands) + [anywhere] * len(after),
         out_specs=vmem,
         cost_estimate=LIGHT,
         compiler_params=limits(*operands),
         name="near",
-    )(*operands)
+    )(*operands, *after)
 
 
 def couple_kernel(ka, ga, ba, share_rows, screening, *refs):
@@ -617,10 +617,6 @@
     dims = (vloc, val_count, cond_count, npol)
     packed = pack(ka, ba, qpoint_map, slot_owner, valence_density, conduction_density)
     blocks = [packed[0]] + [shifted(packed[j], "ka", j) for j in range(1, ka)]
-    early = ka // 2
-    val_rows = slice(0, 2 * pairs)
-    val_early = regroup(blocks[:early], val_rows)
-    far_early = [shifted(val_early, "ga", r) for r in range(1, ga)]
     whole, near_table, far_table, extras = prepare(
         ka,
         dims,
@@ -631,15 +627,19 @@
         conduction_energy,
         start_vector,
         screening,
-        val_early,
+        packed[0],
     )
-    val_late = regroup(blocks[early:], val_rows, (extras,))
+    early = ka // 2
+    val_rows = slice(0, 2 * pairs)
+    val_early = regroup(blocks[:early], val_rows, (extras,))
+    far_early = [shifted(val_early, "ga", r) for r in range(1, ga)]
+    val_late = regroup(blocks[early:], val_rows)
     far_late = [shifted(val_late, "ga", r) for r in range(1, ga)]
     height = 2 * cond_count // ba * cond_count
     width = blocks[0].shape[1] // PARTS
     cond_rows = slice(2 * pairs, 2 * pairs + height)
     cond_parts = [
-        regroup(blocks[1:], cond_rows, (val_late, *far_early), slice(c * width, (c + 1) * width))
+        regroup(blocks[1:], cond_rows, (val_late,), slice(c * width, (c + 1) * width))
         for c in range(PARTS)
     ]
     fields = field(pairs, whole, [val_early, val_late])
@@ -647,8 +647,8 @@
     for r in range(1, ba):
         own_rows = slice(2 * pairs + r * height, 2 * pairs + (r + 1) * height)
         came = [handed(part, r) for part in cond_parts]
-        cond_all.append(assemble(own_rows, blocks[0], came, fields))
-    piece = near(ka, ba, dims, fields, near_table, extras, cond_all)
+        cond_all.append(assemble(own_rows, blocks[0], came, (fields,)))
+    piece = near(ka, ba, dims, fields, near_table, extras, cond_all, far_early)
     if ga > 1:
         coupled = couple(ka, ga, ba, dims, whole, cond_all)
         far = [half for both in zip(far_early, far_late) for half in both]

time: 28.1 us -> 28.1 us (level)
  starting transfers between devices: 14 us -> 13.6 us
  waiting for transfers between devices: 6.19 us -> 6.59 us
    ppermute x3, starting transfers between devices: 1 us -> 0.69 us  [handed(): lax.ppermute(value, 'ba', [(h, (h + step) % size) for h in range(size)])]
  transfers between devices with their start and end apart: 12 -> 12, of which waited for: 7 -> 6; matrix products, arithmetic and copies ran while one was open for 0% -> 0% of each run, Pallas kernels for 15% -> 15%
where the time goes in v20:
time: 28.1 us; the launch traced here: 27.9 us
  starting transfers between devices  13.6 us (48%)
  Pallas kernels  7.02 us (25%)
  waiting for transfers between devices  6.59 us (23%)
  between operations  0.72 us (3%)
    ppermute x9, starting transfers between devices, exchanged(): return lax.ppermute(value, (axis, 'ba'), pairs)  12.9 us
    ppermute x9, waiting for transfers between devices, exchanged(): return lax.ppermute(value, (axis, 'ba'), pairs)  5.23 us
    pallas_call x1, Pallas kernels, prepare(): pl.pallas_call(functools.partial(prepare_kernel, ka, dims), out_shape=[in...  2.45 us
    pallas_call x1, Pallas kernels, haydock(): pl.pallas_call(functools.partial(haydock_kernel, ka, codes, scale_count,...  1.41 us
    ppermute x3, waiting for transfers between devices, handed(): lax.ppermute(value, 'ba', [(h, (h + step) % size) for h in range(size)])  1.35 us
    pallas_call x1, Pallas kernels, pack(): pl.pallas_call(functools.partial(pack_kernel, ka), out_shape=[own] + [sha...  1.05 us
    pallas_call x1, Pallas kernels, field(): pl.pallas_call(functools.partial(field_kernel, pairs), out_shape=in_vmem(...  0.77 us
    ppermute x3, starting transfers between devices, handed(): lax.ppermute(value, 'ba', [(h, (h + step) % size) for h in range(size)])  0.69 us
  transfers between devices with their start and end apart: 12, of which 6 were waited for; matrix products, arithmetic and copies ran while one was open for 0% of the time, Pallas kernels for 15%

profile of v20, /device:TPU:0, one launch (start us, length us, event | category | flops | bytes accessed | tf_op | source)
XLA Modules:
  0.0 27.9 jit_solution(9525449661283125431)
XLA Ops:
  0.6 1.1 %pack.1 = (bf16[48,768]{1,0:T(8,128)(2,1)S(1)}, bf16[32,768]{1,0:T(8,128)(2,1)S(1)}, bf16[32,768]{1,0:T(8,128)(2,1)S(1)}, bf16[32,768]{1,0:T(8,128)(2,1)S(1)}) custom-call(s32[4,4]{1,0:T(4,128)} %refs_0_.1, s32[4]{0:T(128)} %refs_1_.1, bf16[1,4,2,2,4,768]{5,4,3,2,1,0:T(4,128)(2,1)} %valence_in.1, bf16[1,4,2,4,4,768]{5,4,3,2,1,0:T(4,128)(2,1)} %conduction_in.1), custom_call_target="tpu_custom_call" | custom-call | tf_op jit(solution)/shard_map/pack/pallas_call | solution.py:123
  1.7 2.5 %collective-permute-start = (bf16[32,768]{1,0:T(8,128)(2,1)S(1)}, bf16[32,768]{1,0:T(8,128)(2,1)S(1)}, u32[]{:S(2)}, u32[]{:S(2)}) collective-permute-start(bf16[32,768]{1,0:T(8,128)(2,1)S(1)} %get-tuple-element.13), channel_id=1, source_target_pairs={{0,5},{1,4},{4,9},{5,8},{8,13},{9,12},{12,1},{13,0},{2,7},{3,6},{6... | collective-permute-start | bytes 147464 | tf_op jit(solution)/shard_map/ppermute | solution.py:62
  4.2 2.9 %collective-permute-start.1 = (bf16[32,768]{1,0:T(8,128)(2,1)S(1)}, bf16[32,768]{1,0:T(8,128)(2,1)S(1)}, u32[]{:S(2)}, u32[]{:S(2)}) collective-permute-start(bf16[32,768]{1,0:T(8,128)(2,1)S(1)} %get-tuple-element.15), channel_id=1, source_target_pairs={{0,9},{1,8},{4,13},{5,12},{8,1},{9,0},{12,5},{13,4},{2,11},{3,10},... | collective-permute-start | bytes 147464 | tf_op jit(solution)/shard_map/ppermute | solution.py:62
  7.1 0.8 %collective-permute-start.2 = (bf16[32,768]{1,0:T(8,128)(2,1)S(1)}, bf16[32,768]{1,0:T(8,128)(2,1)S(1)}, u32[]{:S(2)}, u32[]{:S(2)}) collective-permute-start(bf16[32,768]{1,0:T(8,128)(2,1)S(1)} %get-tuple-element.16), channel_id=1, source_target_pairs={{0,13},{1,12},{4,1},{5,0},{8,5},{9,4},{12,9},{13,8},{2,15},{3,14},... | collective-permute-start | bytes 147464 | tf_op jit(solution)/shard_map/ppermute | solution.py:62
  7.9 2.5 %prepare.1 = (bf16[2,768,1536]{2,1,0:T(8,128)(2,1)S(1)}, bf16[128,512]{1,0:T(8,128)(2,1)S(1)}, bf16[128,512]{1,0:T(8,128)(2,1)S(1)}, f32[8,128]{1,0:T(8,128)S(1)}) custom-call(s32[4,4]{1,0:T(4,128)} %refs_0_.1, s32[4]{0:T(128)} %refs_1_.1, s32[16]{0:T(128)} %refs_2_.1, f32[1,4]{1,0:T(1,128)} %refs_3_.1, f32[1,4]{1,0:T(1,128)} %refs_4_.1, ...), custom_call_target="tpu_custom_call" | custom-call | bytes 9437184 | tf_op jit(solution)/shard_map/prepare/pallas_call | solution.py:231
  10.3 0.0 collective-permute-done.refs_1_.refs_0_
  10.3 1.8 %collective-permute-start.5 = (bf16[32,768]{1,0:T(8,128)(2,1)S(1)}, bf16[32,768]{1,0:T(8,128)(2,1)S(1)}, u32[]{:S(2)}, u32[]{:S(2)}) collective-permute-start(bf16[32,768]{1,0:T(8,128)(2,1)S(1)} %regroup.5.refs_0_), channel_id=1, source_target_pairs={{0,3},{1,2},{2,1},{3,0},{4,7},{5,6},{6,5},{7,4},{8,11},{9,10},{10,... | collective-permute-start | bytes 147464 | tf_op jit(solution)/shard_map/ppermute | solution.py:62
  12.2 0.0 collective-permute-done.1.refs_0_.refs_2_.refs_1_
  12.2 0.0 collective-permute-done.2.refs_1_.refs_3_.refs_2_
  12.2 0.7 %collective-permute-start.6 = (bf16[32,768]{1,0:T(8,128)(2,1)S(1)}, bf16[32,768]{1,0:T(8,128)(2,1)S(1)}, u32[]{:S(2)}, u32[]{:S(2)}) collective-permute-start(bf16[32,768]{1,0:T(8,128)(2,1)S(1)} %regroup.6.refs_1_.refs_3_), channel_id=1, source_target_pairs={{0,3},{1,2},{2,1},{3,0},{4,7},{5,6},{6,5},{7,4},{8,11},{9,10},{10,... | collective-permute-start | bytes 147464 | tf_op jit(solution)/shard_map/ppermute | solution.py:62
  12.9 0.4 %collective-permute-start.3 = (bf16[48,384]{1,0:T(8,128)(2,1)S(1)}, bf16[48,384]{1,0:T(8,128)(2,1)S(1)}, u32[]{:S(2)}, u32[]{:S(2)}) collective-permute-start(bf16[48,384]{1,0:T(8,128)(2,1)S(1)} %regroup.8), channel_id=1, source_target_pairs={{0,1},{1,0},{2,3},{3,2},{4,5},{5,4},{6,7},{7,6},{8,9},{9,8},{10,11... | collective-permute-start | bytes 110600 | tf_op jit(solution)/shard_map/ppermute | solution.py:71
  13.3 0.1 collective-permute-start.4
  13.4 0.8 %field.1.refs_2_.refs_0_ = bf16[768,256]{1,0:T(8,128)(2,1)S(1)} custom-call(bf16[2,768,1536]{2,1,0:T(8,128)(2,1)S(1)} %get-tuple-element.12.screening, bf16[32,768]{1,0:T(8,128)(2,1)S(1)} %regroup.5.refs_0_, bf16[32,768]{1,0:T(8,128)(2,1)S(1)} %regroup.6.refs_1_.refs_3_), custom_call_target="tpu_custom_call" | custom-call | flops 1 | bytes 1 | tf_op jit(solution)/shard_map/field/pallas_call | solution.py:369
  14.2 0.0 collective-permute-done.3.refs_0_
  14.2 0.3 %collective-permute-done.4.refs_1_ = bf16[48,384]{1,0:T(8,128)(2,1)S(1)} collective-permute-done((bf16[48,384]{1,0:T(8,128)(2,1)S(1)}, bf16[48,384]{1,0:T(8,128)(2,1)S(1)}, u32[]{:S(2)}, u32[]{:S(2)}) %collective-permute-start.4) | collective-permute-done | bytes 36896 | tf_op jit(solution)/shard_map/ppermute | solution.py:71
  14.6 0.5 %couple.1.refs_2_ = bf16[256,768]{1,0:T(8,128)(2,1)S(1)} custom-call(bf16[2,768,1536]{2,1,0:T(8,128)(2,1)S(1)} %get-tuple-element.12.screening, bf16[64,768]{1,0:T(8,128)(2,1)S(1)} %regroup.7.refs_3_.refs_0_, bf16[64,768]{1,0:T(8,128)(2,1)S(1)} %assemble.1.refs_4_.refs_1_), custom_call_target="tpu_custom_call" | custom-call | flops 1 | bytes 1 | tf_op jit(solution)/shard_map/couple/pallas_call | solution.py:438
  15.1 0.0 collective-permute-done.5.refs_5_.refs_3_
  15.1 0.4 %near.1.refs_1_ = f32[24,128]{1,0:T(8,128)S(1)} custom-call(bf16[768,256]{1,0:T(8,128)(2,1)S(1)} %field.1.refs_2_.refs_0_, bf16[128,512]{1,0:T(8,128)(2,1)S(1)} %get-tuple-element.17.refs_1_, f32[8,128]{1,0:T(8,128)S(1)} %get-tuple-element.14.refs_2_, bf16[64,768]{1,0:T(8,128)(2,1)S(1)} %regroup.7.refs_3_.refs_0_, ...), custom_call_target="tpu_custom_call" | custom-call | flops 1 | bytes 1 | tf_op jit(solution)/shard_map/near/pallas_call | solution.py:398
  15.5 0.8 %collective-permute-done.6.refs_4_ = bf16[32,768]{1,0:T(8,128)(2,1)S(1)} collective-permute-done((bf16[32,768]{1,0:T(8,128)(2,1)S(1)}, bf16[32,768]{1,0:T(8,128)(2,1)S(1)}, u32[]{:S(2)}, u32[]{:S(2)}) %collective-permute-start.6) | collective-permute-done | bytes 49184 | tf_op jit(solution)/shard_map/ppermute | solution.py:62
  16.3 0.4 %far.1 = f32[24,128]{1,0:T(8,128)S(1)} custom-call(bf16[128,512]{1,0:T(8,128)(2,1)S(1)} %get-tuple-element.11.refs_0_, f32[24,128]{1,0:T(8,128)S(1)} %near.1.refs_1_, bf16[256,768]{1,0:T(8,128)(2,1)S(1)} %couple.1.refs_2_, bf16[32,768]{1,0:T(8,128)(2,1)S(1)} %collective-permute-done.5.refs_5_.refs_3_, bf16[32,768]{1,0:T(8,128)(2,1)S(1)} %collective-permute-done.6.refs_4_), custom_call_target="tpu_custom_call" | custom-call | flops 1 | bytes 1 | tf_op jit(solution)/shard_map/far/pallas_call | solution.py:476
  16.7 0.2 collective-permute-start.7
  16.9 1.1 %collective-permute-done.7 = f32[24,128]{1,0:T(8,128)S(1)} collective-permute-done((f32[24,128]{1,0:T(8,128)S(1)}, f32[24,128]{1,0:T(8,128)S(1)}, u32[]{:S(2)}, u32[]{:S(2)}) %collective-permute-start.7) | collective-permute-done | bytes 12320 | tf_op jit(solution)/shard_map/ppermute | solution.py:71
  18.0 0.6 %collective-permute-start.8 = (f32[24,128]{1,0:T(8,128)S(1)}, f32[24,128]{1,0:T(8,128)S(1)}, u32[]{:S(2)}, u32[]{:S(2)}) collective-permute-start(f32[24,128]{1,0:T(8,128)S(1)} %add.6), channel_id=1, source_target_pairs={{0,3},{1,2},{2,1},{3,0},{4,7},{5,6},{6,5},{7,4},{8,11},{9,10},{10,... | collective-permute-start | bytes 36872 | tf_op jit(solution)/shard_map/ppermute | solution.py:62
  18.6 2.5 %collective-permute-done.8 = f32[24,128]{1,0:T(8,128)S(1)} collective-permute-done((f32[24,128]{1,0:T(8,128)S(1)}, f32[24,128]{1,0:T(8,128)S(1)}, u32[]{:S(2)}, u32[]{:S(2)}) %collective-permute-start.8) | collective-permute-done | bytes 12320 | tf_op jit(solution)/shard_map/ppermute | solution.py:62
  21.1 0.4 %collective-permute-start.9 = (f32[24,128]{1,0:T(8,128)S(1)}, f32[24,128]{1,0:T(8,128)S(1)}, u32[]{:S(2)}, u32[]{:S(2)}) collective-permute-start(f32[24,128]{1,0:T(8,128)S(1)} %add.7.refs_0_), channel_id=1, source_target_pairs={{0,5},{1,4},{4,9},{5,8},{8,13},{9,12},{12,1},{13,0},{2,7},{3,6},{6... | collective-permute-start | bytes 36872 | tf_op jit(solution)/shard_map/ppermute | solution.py:62
  21.5 1.6 %collective-permute-start.10 = (f32[24,128]{1,0:T(8,128)S(1)}, f32[24,128]{1,0:T(8,128)S(1)}, u32[]{:S(2)}, u32[]{:S(2)}) collective-permute-start(f32[24,128]{1,0:T(8,128)S(1)} %add.7.refs_0_), channel_id=1, source_target_pairs={{0,9},{1,8},{4,13},{5,12},{8,1},{9,0},{12,5},{13,4},{2,11},{3,10},... | collective-permute-start | bytes 36872 | tf_op jit(solution)/shard_map/ppermute | solution.py:62
  23.1 1.5 %collective-permute-start.11 = (f32[24,128]{1,0:T(8,128)S(1)}, f32[24,128]{1,0:T(8,128)S(1)}, u32[]{:S(2)}, u32[]{:S(2)}) collective-permute-start(f32[24,128]{1,0:T(8,128)S(1)} %add.7.refs_0_), channel_id=1, source_target_pairs={{0,13},{1,12},{4,1},{5,0},{8,5},{9,4},{12,9},{13,8},{2,15},{3,14},... | collective-permute-start | bytes 36872 | tf_op jit(solution)/shard_map/ppermute | solution.py:62
  24.6 1.4 %collective-permute-done.9.refs_1_ = f32[24,128]{1,0:T(8,128)S(1)} collective-permute-done((f32[24,128]{1,0:T(8,128)S(1)}, f32[24,128]{1,0:T(8,128)S(1)}, u32[]{:S(2)}, u32[]{:S(2)}) %collective-permute-start.9) | collective-permute-done | bytes 12320 | tf_op jit(solution)/shard_map/ppermute | solution.py:62
  26.0 0.0 collective-permute-done.10.refs_2_
  26.0 0.5 %collective-permute-done.11.refs_3_ = f32[24,128]{1,0:T(8,128)S(1)} collective-permute-done((f32[24,128]{1,0:T(8,128)S(1)}, f32[24,128]{1,0:T(8,128)S(1)}, u32[]{:S(2)}, u32[]{:S(2)}) %collective-permute-start.11) | collective-permute-done | bytes 12320 | tf_op jit(solution)/shard_map/ppermute | solution.py:62
  26.5 1.4 %haydock.1 = (f32[1,2,2,16]{3,2,1,0:T(2,128)}, f32[2,6]{1,0:T(2,128)}) custom-call(f32[24,128]{1,0:T(8,128)S(1)} %add.7.refs_0_, f32[24,128]{1,0:T(8,128)S(1)} %collective-permute-done.9.refs_1_, f32[24,128]{1,0:T(8,128)S(1)} %collective-permute-done.10.refs_2_, f32[24,128]{1,0:T(8,128)S(1)} %collective-permute-done.11.refs_3_), custom_call_target="tpu_custom_call" | custom-call | tf_op jit(solution)/shard_map/haydock/pallas_call | solution.py:574
  (8 shorter events, 0.0 us)
Async XLA Ops:
  1.7 8.6 %collective-permute-start = (bf16[32,768]{1,0:T(8,128)(2,1)S(1)}, bf16[32,768]{1,0:T(8,128)(2,1)S(1)}, u32[]{:S(2)}, u32[]{:S(2)}) collective-permute-start(bf16[32,768]{1,0:T(8,128)(2,1)S(1)} %get-tuple-element.13), channel_id=1, source_target_pairs={{0,5},{1,4},{4,9},{5,8},{8,13},{9,12},{12,1},{13,0},{2,7},{3,6},{6... | collective-permute-start | bytes 147464 | tf_op jit(solution)/shard_map/ppermute | solution.py:62
  4.2 8.0 %collective-permute-start.1 = (bf16[32,768]{1,0:T(8,128)(2,1)S(1)}, bf16[32,768]{1,0:T(8,128)(2,1)S(1)}, u32[]{:S(2)}, u32[]{:S(2)}) collective-permute-start(bf16[32,768]{1,0:T(8,128)(2,1)S(1)} %get-tuple-element.15), channel_id=1, source_target_pairs={{0,9},{1,8},{4,13},{5,12},{8,1},{9,0},{12,5},{13,4},{2,11},{3,10},... | collective-permute-start | bytes 147464 | tf_op jit(solution)/shard_map/ppermute | solution.py:62
  7.1 5.1 %collective-permute-start.2 = (bf16[32,768]{1,0:T(8,128)(2,1)S(1)}, bf16[32,768]{1,0:T(8,128)(2,1)S(1)}, u32[]{:S(2)}, u32[]{:S(2)}) collective-permute-start(bf16[32,768]{1,0:T(8,128)(2,1)S(1)} %get-tuple-element.16), channel_id=1, source_target_pairs={{0,13},{1,12},{4,1},{5,0},{8,5},{9,4},{12,9},{13,8},{2,15},{3,14},... | collective-permute-start | bytes 147464 | tf_op jit(solution)/shard_map/ppermute | solution.py:62
  10.3 4.7 %collective-permute-start.5 = (bf16[32,768]{1,0:T(8,128)(2,1)S(1)}, bf16[32,768]{1,0:T(8,128)(2,1)S(1)}, u32[]{:S(2)}, u32[]{:S(2)}) collective-permute-start(bf16[32,768]{1,0:T(8,128)(2,1)S(1)} %regroup.5.refs_0_), channel_id=1, source_target_pairs={{0,3},{1,2},{2,1},{3,0},{4,7},{5,6},{6,5},{7,4},{8,11},{9,10},{10,... | collective-permute-start | bytes 147464 | tf_op jit(solution)/shard_map/ppermute | solution.py:62
  12.2 4.1 %collective-permute-start.6 = (bf16[32,768]{1,0:T(8,128)(2,1)S(1)}, bf16[32,768]{1,0:T(8,128)(2,1)S(1)}, u32[]{:S(2)}, u32[]{:S(2)}) collective-permute-start(bf16[32,768]{1,0:T(8,128)(2,1)S(1)} %regroup.6.refs_1_.refs_3_), channel_id=1, source_target_pairs={{0,3},{1,2},{2,1},{3,0},{4,7},{5,6},{6,5},{7,4},{8,11},{9,10},{10,... | collective-permute-start | bytes 147464 | tf_op jit(solution)/shard_map/ppermute | solution.py:62
  12.9 1.3 %collective-permute-start.3 = (bf16[48,384]{1,0:T(8,128)(2,1)S(1)}, bf16[48,384]{1,0:T(8,128)(2,1)S(1)}, u32[]{:S(2)}, u32[]{:S(2)}) collective-permute-start(bf16[48,384]{1,0:T(8,128)(2,1)S(1)} %regroup.8), channel_id=1, source_target_pairs={{0,1},{1,0},{2,3},{3,2},{4,5},{5,4},{6,7},{7,6},{8,9},{9,8},{10,11... | collective-permute-start | bytes 110600 | tf_op jit(solution)/shard_map/ppermute | solution.py:71
  13.3 1.2 %collective-permute-start.4 = (bf16[48,384]{1,0:T(8,128)(2,1)S(1)}, bf16[48,384]{1,0:T(8,128)(2,1)S(1)}, u32[]{:S(2)}, u32[]{:S(2)}) collective-permute-start(bf16[48,384]{1,0:T(8,128)(2,1)S(1)} %regroup.9), channel_id=1, source_target_pairs={{0,1},{1,0},{2,3},{3,2},{4,5},{5,4},{6,7},{7,6},{8,9},{9,8},{10,11... | collective-permute-start | bytes 110600 | tf_op jit(solution)/shard_map/ppermute | solution.py:71
  16.7 1.2 %collective-permute-start.7 = (f32[24,128]{1,0:T(8,128)S(1)}, f32[24,128]{1,0:T(8,128)S(1)}, u32[]{:S(2)}, u32[]{:S(2)}) collective-permute-start(f32[24,128]{1,0:T(8,128)S(1)} %far.1), channel_id=1, source_target_pairs={{0,1},{1,0},{2,3},{3,2},{4,5},{5,4},{6,7},{7,6},{8,9},{9,8},{10,11... | collective-permute-start | bytes 36872 | tf_op jit(solution)/shard_map/ppermute | solution.py:71
  18.0 3.1 %collective-permute-start.8 = (f32[24,128]{1,0:T(8,128)S(1)}, f32[24,128]{1,0:T(8,128)S(1)}, u32[]{:S(2)}, u32[]{:S(2)}) collective-permute-start(f32[24,128]{1,0:T(8,128)S(1)} %add.6), channel_id=1, source_target_pairs={{0,3},{1,2},{2,1},{3,0},{4,7},{5,6},{6,5},{7,4},{8,11},{9,10},{10,... | collective-permute-start | bytes 36872 | tf_op jit(solution)/shard_map/ppermute | solution.py:62
  21.1 4.9 %collective-permute-start.9 = (f32[24,128]{1,0:T(8,128)S(1)}, f32[24,128]{1,0:T(8,128)S(1)}, u32[]{:S(2)}, u32[]{:S(2)}) collective-permute-start(f32[24,128]{1,0:T(8,128)S(1)} %add.7.refs_0_), channel_id=1, source_target_pairs={{0,5},{1,4},{4,9},{5,8},{8,13},{9,12},{12,1},{13,0},{2,7},{3,6},{6... | collective-permute-start | bytes 36872 | tf_op jit(solution)/shard_map/ppermute | solution.py:62
  21.5 4.5 %collective-permute-start.10 = (f32[24,128]{1,0:T(8,128)S(1)}, f32[24,128]{1,0:T(8,128)S(1)}, u32[]{:S(2)}, u32[]{:S(2)}) collective-permute-start(f32[24,128]{1,0:T(8,128)S(1)} %add.7.refs_0_), channel_id=1, source_target_pairs={{0,9},{1,8},{4,13},{5,12},{8,1},{9,0},{12,5},{13,4},{2,11},{3,10},... | collective-permute-start | bytes 36872 | tf_op jit(solution)/shard_map/ppermute | solution.py:62
  23.1 3.4 %collective-permute-start.11 = (f32[24,128]{1,0:T(8,128)S(1)}, f32[24,128]{1,0:T(8,128)S(1)}, u32[]{:S(2)}, u32[]{:S(2)}) collective-permute-start(f32[24,128]{1,0:T(8,128)S(1)} %add.7.refs_0_), channel_id=1, source_target_pairs={{0,13},{1,12},{4,1},{5,0},{8,5},{9,4},{12,9},{13,8},{2,15},{3,14},... | collective-permute-start | bytes 36872 | tf_op jit(solution)/shard_map/ppermute | solution.py:62

commit v21 on v19

--- a/solution.py
+++ b/solution.py
@@ -516,10 +516,10 @@
         return jnp.concatenate([top, vector - top], 0).astype(jnp.bfloat16)
 
     def mean(values):
-        return jnp.sum(values, axis=1, keepdims=True) / scale_count
-
-    def norm(vector):
-        return jnp.sqrt(mean(vector * vector) + EPSILON)
+        return jnp.sum(values, axis=1, keepdims=True) * (1.0 / scale_count)
+
+    def square_norm(vector):
+        return mean(vector * vector) + EPSILON
 
     def swap(vector):
         return pltpu.roll(vector, mid, 1)
@@ -536,19 +536,18 @@
         return real * vector + imag * (sign * swap(vector))
 
     start_image = hamiltonian(start)
-    scale = 1.0 / norm(start)
+    scale = lax.rsqrt(square_norm(start))
     first = start * scale
-    first_image = start_image * scale
-    alpha_real, alpha_imag = inner(first, first_image)
-    first_resid = first_image - times(alpha_real, alpha_imag, first)
+    alpha_real, alpha_imag = (value * (scale * scale) for value in inner(start, start_image))
+    first_resid = start_image * scale - times(alpha_real, alpha_imag, first)
     resid_image = hamiltonian(first_resid)
-    beta_one = norm(first_resid)
-    scale = 1.0 / beta_one
+    square_one = square_norm(first_resid)
+    scale, beta_one = lax.rsqrt(square_one), jnp.sqrt(square_one)
     second = first_resid * scale
-    second_image = resid_image * scale
-    gamma_real, gamma_imag = inner(second, second_image)
-    second_resid = second_image - times(gamma_real, gamma_imag, second) - beta_one * first
-    beta_two = norm(second_resid)
+    gamma_real, gamma_imag = (value * (scale * scale) for value in inner(first_resid, resid_image))
+    second_resid = resid_image * scale - beta_one * first - times(gamma_real, gamma_imag, second)
+    square_two = square_norm(second_resid)
+    beta_two = jnp.sqrt(square_two)
 
     coef_lane = iota(coef_out.shape, 1)
     coefs = jnp.zeros(coef_out.shape, jnp.float32)
@@ -563,7 +562,7 @@
     picked = lax.dot_general(
         halves(second_resid), pick, (((1,), (1,)), ((), ())), preferred_element_type=jnp.float32
     )
-    picked = (picked[:npol] + picked[npol:]) / beta_two
+    picked = (picked[:npol] + picked[npol:]) * lax.rsqrt(square_two)
     next_out[0, :, 0, :] = picked[:, :codes]
     next_out[0, :, 1, :] = picked[:, codes:]
 

time: 28.1 us -> 28.1 us (level)
  no operation moved by 1% of the time
where the time goes in v21:
time: 28.1 us; the launch traced here: 27.9 us
  starting transfers between devices  14 us (50%)
  Pallas kernels  7.02 us (25%)
  waiting for transfers between devices  6.19 us (22%)
  between operations  0.72 us (3%)
    ppermute x9, starting transfers between devices, exchanged(): return lax.ppermute(value, (axis, 'ba'), pairs)  13 us
    ppermute x9, waiting for transfers between devices, exchanged(): return lax.ppermute(value, (axis, 'ba'), pairs)  5.07 us
    pallas_call x1, Pallas kernels, prepare(): pl.pallas_call(functools.partial(prepare_kernel, ka, dims), out_shape=[in...  2.45 us
    pallas_call x1, Pallas kernels, haydock(): pl.pallas_call(functools.partial(haydock_kernel, ka, codes, scale_count,...  1.41 us
    ppermute x3, waiting for transfers between devices, handed(): lax.ppermute(value, 'ba', [(h, (h + step) % size) for h in range(size)])  1.12 us
    pallas_call x1, Pallas kernels, pack(): pl.pallas_call(functools.partial(pack_kernel, ka), out_shape=[own] + [sha...  1.05 us
    ppermute x3, starting transfers between devices, handed(): lax.ppermute(value, 'ba', [(h, (h + step) % size) for h in range(size)])  1 us
    pallas_call x1, Pallas kernels, field(): pl.pallas_call(functools.partial(field_kernel, pairs), out_shape=in_vmem(...  0.78 us
  transfers between devices with their start and end apart: 12, of which 7 were waited for; matrix products, arithmetic and copies ran while one was open for 0% of the time, Pallas kernels for 15%

profile of v21, /device:TPU:0, one launch (start us, length us, event | category | flops | bytes accessed | tf_op | source)
XLA Modules:
  0.0 27.9 jit_solution(8018722549465783791)
XLA Ops:
  0.6 1.1 %pack.1 = (bf16[48,768]{1,0:T(8,128)(2,1)S(1)}, bf16[32,768]{1,0:T(8,128)(2,1)S(1)}, bf16[32,768]{1,0:T(8,128)(2,1)S(1)}, bf16[32,768]{1,0:T(8,128)(2,1)S(1)}) custom-call(s32[4,4]{1,0:T(4,128)} %refs_0_.1, s32[4]{0:T(128)} %refs_1_.1, bf16[1,4,2,2,4,768]{5,4,3,2,1,0:T(4,128)(2,1)} %valence_in.1, bf16[1,4,2,4,4,768]{5,4,3,2,1,0:T(4,128)(2,1)} %conduction_in.1), custom_call_target="tpu_custom_call" | custom-call | tf_op jit(solution)/shard_map/pack/pallas_call | solution.py:123
  1.7 2.5 %collective-permute-start = (bf16[32,768]{1,0:T(8,128)(2,1)S(1)}, bf16[32,768]{1,0:T(8,128)(2,1)S(1)}, u32[]{:S(2)}, u32[]{:S(2)}) collective-permute-start(bf16[32,768]{1,0:T(8,128)(2,1)S(1)} %get-tuple-element.11), channel_id=1, source_target_pairs={{0,5},{1,4},{4,9},{5,8},{8,13},{9,12},{12,1},{13,0},{2,7},{3,6},{6... | collective-permute-start | bytes 147464 | tf_op jit(solution)/shard_map/ppermute | solution.py:62
  4.2 2.9 %collective-permute-start.1 = (bf16[32,768]{1,0:T(8,128)(2,1)S(1)}, bf16[32,768]{1,0:T(8,128)(2,1)S(1)}, u32[]{:S(2)}, u32[]{:S(2)}) collective-permute-start(bf16[32,768]{1,0:T(8,128)(2,1)S(1)} %get-tuple-element.14), channel_id=1, source_target_pairs={{0,9},{1,8},{4,13},{5,12},{8,1},{9,0},{12,5},{13,4},{2,11},{3,10},... | collective-permute-start | bytes 147464 | tf_op jit(solution)/shard_map/ppermute | solution.py:62
  7.1 0.8 %collective-permute-start.2 = (bf16[32,768]{1,0:T(8,128)(2,1)S(1)}, bf16[32,768]{1,0:T(8,128)(2,1)S(1)}, u32[]{:S(2)}, u32[]{:S(2)}) collective-permute-start(bf16[32,768]{1,0:T(8,128)(2,1)S(1)} %get-tuple-element.15), channel_id=1, source_target_pairs={{0,13},{1,12},{4,1},{5,0},{8,5},{9,4},{12,9},{13,8},{2,15},{3,14},... | collective-permute-start | bytes 147464 | tf_op jit(solution)/shard_map/ppermute | solution.py:62
  7.9 0.1 collective-permute-done.refs_1_.refs_0_
  8.0 2.0 %collective-permute-start.3 = (bf16[32,768]{1,0:T(8,128)(2,1)S(1)}, bf16[32,768]{1,0:T(8,128)(2,1)S(1)}, u32[]{:S(2)}, u32[]{:S(2)}) collective-permute-start(bf16[32,768]{1,0:T(8,128)(2,1)S(1)} %regroup.5.refs_7_.refs_0_), channel_id=1, source_target_pairs={{0,3},{1,2},{2,1},{3,0},{4,7},{5,6},{6,5},{7,4},{8,11},{9,10},{10,... | collective-permute-start | bytes 147464 | tf_op jit(solution)/shard_map/ppermute | solution.py:62
  10.0 2.5 %prepare.1 = (bf16[2,768,1536]{2,1,0:T(8,128)(2,1)S(1)}, bf16[128,512]{1,0:T(8,128)(2,1)S(1)}, bf16[128,512]{1,0:T(8,128)(2,1)S(1)}, f32[8,128]{1,0:T(8,128)S(1)}) custom-call(s32[4,4]{1,0:T(4,128)} %refs_0_.1, s32[4]{0:T(128)} %refs_1_.1, s32[16]{0:T(128)} %refs_2_.1, f32[1,4]{1,0:T(1,128)} %refs_3_.1, f32[1,4]{1,0:T(1,128)} %refs_4_.1, ...), custom_call_target="tpu_custom_call" | custom-call | bytes 9437184 | tf_op jit(solution)/shard_map/prepare/pallas_call | solution.py:231
  12.5 0.0 collective-permute-done.1.refs_0_.refs_2_.refs_1_
  12.5 0.0 collective-permute-done.2.refs_1_.refs_3_.refs_2_
  12.5 0.4 %collective-permute-start.6 = (bf16[32,768]{1,0:T(8,128)(2,1)S(1)}, bf16[32,768]{1,0:T(8,128)(2,1)S(1)}, u32[]{:S(2)}, u32[]{:S(2)}) collective-permute-start(bf16[32,768]{1,0:T(8,128)(2,1)S(1)} %regroup.6.refs_1_.refs_3_), channel_id=1, source_target_pairs={{0,3},{1,2},{2,1},{3,0},{4,7},{5,6},{6,5},{7,4},{8,11},{9,10},{10,... | collective-permute-start | bytes 147464 | tf_op jit(solution)/shard_map/ppermute | solution.py:62
  12.9 0.0 collective-permute-done.3.refs_4_.refs_3_
  12.9 0.5 %collective-permute-start.4 = (bf16[48,384]{1,0:T(8,128)(2,1)S(1)}, bf16[48,384]{1,0:T(8,128)(2,1)S(1)}, u32[]{:S(2)}, u32[]{:S(2)}) collective-permute-start(bf16[48,384]{1,0:T(8,128)(2,1)S(1)} %regroup.8), channel_id=1, source_target_pairs={{0,1},{1,0},{2,3},{3,2},{4,5},{5,4},{6,7},{7,6},{8,9},{9,8},{10,11... | collective-permute-start | bytes 110600 | tf_op jit(solution)/shard_map/ppermute | solution.py:71
  13.4 0.1 collective-permute-start.5
  13.5 0.8 %field.1.refs_2_.refs_0_ = bf16[768,256]{1,0:T(8,128)(2,1)S(1)} custom-call(bf16[2,768,1536]{2,1,0:T(8,128)(2,1)S(1)} %get-tuple-element.13.screening, bf16[32,768]{1,0:T(8,128)(2,1)S(1)} %regroup.5.refs_7_.refs_0_, bf16[32,768]{1,0:T(8,128)(2,1)S(1)} %regroup.6.refs_1_.refs_3_), custom_call_target="tpu_custom_call" | custom-call | flops 1 | bytes 1 | tf_op jit(solution)/shard_map/field/pallas_call | solution.py:369
  14.3 0.0 collective-permute-done.4.refs_0_
  14.3 0.3 %collective-permute-done.5.refs_1_ = bf16[48,384]{1,0:T(8,128)(2,1)S(1)} collective-permute-done((bf16[48,384]{1,0:T(8,128)(2,1)S(1)}, bf16[48,384]{1,0:T(8,128)(2,1)S(1)}, u32[]{:S(2)}, u32[]{:S(2)}) %collective-permute-start.5) | collective-permute-done | bytes 36896 | tf_op jit(solution)/shard_map/ppermute | solution.py:71
  14.6 0.5 %couple.1.refs_2_ = bf16[256,768]{1,0:T(8,128)(2,1)S(1)} custom-call(bf16[2,768,1536]{2,1,0:T(8,128)(2,1)S(1)} %get-tuple-element.13.screening, bf16[64,768]{1,0:T(8,128)(2,1)S(1)} %regroup.7.refs_3_.refs_0_, bf16[64,768]{1,0:T(8,128)(2,1)S(1)} %assemble.1.refs_4_.refs_1_), custom_call_target="tpu_custom_call" | custom-call | flops 1 | bytes 1 | tf_op jit(solution)/shard_map/couple/pallas_call | solution.py:438
  15.1 0.4 %near.1.refs_1_ = f32[24,128]{1,0:T(8,128)S(1)} custom-call(bf16[768,256]{1,0:T(8,128)(2,1)S(1)} %field.1.refs_2_.refs_0_, bf16[128,512]{1,0:T(8,128)(2,1)S(1)} %get-tuple-element.17.refs_1_, f32[8,128]{1,0:T(8,128)S(1)} %get-tuple-element.16.refs_2_, bf16[64,768]{1,0:T(8,128)(2,1)S(1)} %regroup.7.refs_3_.refs_0_, bf16[64,768]{1,0:T(8,128)(2,1)S(1)} %assemble.1.refs_4_.refs_1_), custom_call_target="tpu_custom_call" | custom-call | flops 1 | bytes 1 | tf_op jit(solution)/shard_map/near/pallas_call | solution.py:398
  15.5 0.6 %collective-permute-done.6.refs_4_ = bf16[32,768]{1,0:T(8,128)(2,1)S(1)} collective-permute-done((bf16[32,768]{1,0:T(8,128)(2,1)S(1)}, bf16[32,768]{1,0:T(8,128)(2,1)S(1)}, u32[]{:S(2)}, u32[]{:S(2)}) %collective-permute-start.6) | collective-permute-done | bytes 49184 | tf_op jit(solution)/shard_map/ppermute | solution.py:62
  16.1 0.4 %far.1 = f32[24,128]{1,0:T(8,128)S(1)} custom-call(bf16[128,512]{1,0:T(8,128)(2,1)S(1)} %get-tuple-element.12.refs_0_, f32[24,128]{1,0:T(8,128)S(1)} %near.1.refs_1_, bf16[256,768]{1,0:T(8,128)(2,1)S(1)} %couple.1.refs_2_, bf16[32,768]{1,0:T(8,128)(2,1)S(1)} %collective-permute-done.3.refs_4_.refs_3_, bf16[32,768]{1,0:T(8,128)(2,1)S(1)} %collective-permute-done.6.refs_4_), custom_call_target="tpu_custom_call" | custom-call | flops 1 | bytes 1 | tf_op jit(solution)/shard_map/far/pallas_call | solution.py:476
  16.6 0.4 %collective-permute-start.7 = (f32[24,128]{1,0:T(8,128)S(1)}, f32[24,128]{1,0:T(8,128)S(1)}, u32[]{:S(2)}, u32[]{:S(2)}) collective-permute-start(f32[24,128]{1,0:T(8,128)S(1)} %far.1), channel_id=1, source_target_pairs={{0,1},{1,0},{2,3},{3,2},{4,5},{5,4},{6,7},{7,6},{8,9},{9,8},{10,11... | collective-permute-start | bytes 36872 | tf_op jit(solution)/shard_map/ppermute | solution.py:71
  17.0 0.8 %collective-permute-done.7 = f32[24,128]{1,0:T(8,128)S(1)} collective-permute-done((f32[24,128]{1,0:T(8,128)S(1)}, f32[24,128]{1,0:T(8,128)S(1)}, u32[]{:S(2)}, u32[]{:S(2)}) %collective-permute-start.7) | collective-permute-done | bytes 12320 | tf_op jit(solution)/shard_map/ppermute | solution.py:71
  17.8 0.8 %collective-permute-start.8 = (f32[24,128]{1,0:T(8,128)S(1)}, f32[24,128]{1,0:T(8,128)S(1)}, u32[]{:S(2)}, u32[]{:S(2)}) collective-permute-start(f32[24,128]{1,0:T(8,128)S(1)} %add.6), channel_id=1, source_target_pairs={{0,3},{1,2},{2,1},{3,0},{4,7},{5,6},{6,5},{7,4},{8,11},{9,10},{10,... | collective-permute-start | bytes 36872 | tf_op jit(solution)/shard_map/ppermute | solution.py:62
  18.6 2.4 %collective-permute-done.8 = f32[24,128]{1,0:T(8,128)S(1)} collective-permute-done((f32[24,128]{1,0:T(8,128)S(1)}, f32[24,128]{1,0:T(8,128)S(1)}, u32[]{:S(2)}, u32[]{:S(2)}) %collective-permute-start.8) | collective-permute-done | bytes 12320 | tf_op jit(solution)/shard_map/ppermute | solution.py:62
  20.9 0.4 %collective-permute-start.9 = (f32[24,128]{1,0:T(8,128)S(1)}, f32[24,128]{1,0:T(8,128)S(1)}, u32[]{:S(2)}, u32[]{:S(2)}) collective-permute-start(f32[24,128]{1,0:T(8,128)S(1)} %add.7.refs_0_), channel_id=1, source_target_pairs={{0,5},{1,4},{4,9},{5,8},{8,13},{9,12},{12,1},{13,0},{2,7},{3,6},{6... | collective-permute-start | bytes 36872 | tf_op jit(solution)/shard_map/ppermute | solution.py:62
  21.3 1.9 %collective-permute-start.10 = (f32[24,128]{1,0:T(8,128)S(1)}, f32[24,128]{1,0:T(8,128)S(1)}, u32[]{:S(2)}, u32[]{:S(2)}) collective-permute-start(f32[24,128]{1,0:T(8,128)S(1)} %add.7.refs_0_), channel_id=1, source_target_pairs={{0,9},{1,8},{4,13},{5,12},{8,1},{9,0},{12,5},{13,4},{2,11},{3,10},... | collective-permute-start | bytes 36872 | tf_op jit(solution)/shard_map/ppermute | solution.py:62
  23.2 1.3 %collective-permute-start.11 = (f32[24,128]{1,0:T(8,128)S(1)}, f32[24,128]{1,0:T(8,128)S(1)}, u32[]{:S(2)}, u32[]{:S(2)}) collective-permute-start(f32[24,128]{1,0:T(8,128)S(1)} %add.7.refs_0_), channel_id=1, source_target_pairs={{0,13},{1,12},{4,1},{5,0},{8,5},{9,4},{12,9},{13,8},{2,15},{3,14},... | collective-permute-start | bytes 36872 | tf_op jit(solution)/shard_map/ppermute | solution.py:62
  24.6 1.3 %collective-permute-done.9.refs_1_ = f32[24,128]{1,0:T(8,128)S(1)} collective-permute-done((f32[24,128]{1,0:T(8,128)S(1)}, f32[24,128]{1,0:T(8,128)S(1)}, u32[]{:S(2)}, u32[]{:S(2)}) %collective-permute-start.9) | collective-permute-done | bytes 12320 | tf_op jit(solution)/shard_map/ppermute | solution.py:62
  25.9 0.0 collective-permute-done.10.refs_2_
  25.9 0.6 %collective-permute-done.11.refs_3_ = f32[24,128]{1,0:T(8,128)S(1)} collective-permute-done((f32[24,128]{1,0:T(8,128)S(1)}, f32[24,128]{1,0:T(8,128)S(1)}, u32[]{:S(2)}, u32[]{:S(2)}) %collective-permute-start.11) | collective-permute-done | bytes 12320 | tf_op jit(solution)/shard_map/ppermute | solution.py:62
  26.5 1.4 %haydock.1 = (f32[1,2,2,16]{3,2,1,0:T(2,128)}, f32[2,6]{1,0:T(2,128)}) custom-call(f32[24,128]{1,0:T(8,128)S(1)} %add.7.refs_0_, f32[24,128]{1,0:T(8,128)S(1)} %collective-permute-done.9.refs_1_, f32[24,128]{1,0:T(8,128)S(1)} %collective-permute-done.10.refs_2_, f32[24,128]{1,0:T(8,128)S(1)} %collective-permute-done.11.refs_3_), custom_call_target="tpu_custom_call" | custom-call | tf_op jit(solution)/shard_map/haydock/pallas_call | solution.py:573
  (8 shorter events, 0.0 us)
Async XLA Ops:
  1.7 6.3 %collective-permute-start = (bf16[32,768]{1,0:T(8,128)(2,1)S(1)}, bf16[32,768]{1,0:T(8,128)(2,1)S(1)}, u32[]{:S(2)}, u32[]{:S(2)}) collective-permute-start(bf16[32,768]{1,0:T(8,128)(2,1)S(1)} %get-tuple-element.11), channel_id=1, source_target_pairs={{0,5},{1,4},{4,9},{5,8},{8,13},{9,12},{12,1},{13,0},{2,7},{3,6},{6... | collective-permute-start | bytes 147464 | tf_op jit(solution)/shard_map/ppermute | solution.py:62
  4.2 8.3 %collective-permute-start.1 = (bf16[32,768]{1,0:T(8,128)(2,1)S(1)}, bf16[32,768]{1,0:T(8,128)(2,1)S(1)}, u32[]{:S(2)}, u32[]{:S(2)}) collective-permute-start(bf16[32,768]{1,0:T(8,128)(2,1)S(1)} %get-tuple-element.14), channel_id=1, source_target_pairs={{0,9},{1,8},{4,13},{5,12},{8,1},{9,0},{12,5},{13,4},{2,11},{3,10},... | collective-permute-start | bytes 147464 | tf_op jit(solution)/shard_map/ppermute | solution.py:62
  7.1 5.4 %collective-permute-start.2 = (bf16[32,768]{1,0:T(8,128)(2,1)S(1)}, bf16[32,768]{1,0:T(8,128)(2,1)S(1)}, u32[]{:S(2)}, u32[]{:S(2)}) collective-permute-start(bf16[32,768]{1,0:T(8,128)(2,1)S(1)} %get-tuple-element.15), channel_id=1, source_target_pairs={{0,13},{1,12},{4,1},{5,0},{8,5},{9,4},{12,9},{13,8},{2,15},{3,14},... | collective-permute-start | bytes 147464 | tf_op jit(solution)/shard_map/ppermute | solution.py:62
  8.0 4.9 %collective-permute-start.3 = (bf16[32,768]{1,0:T(8,128)(2,1)S(1)}, bf16[32,768]{1,0:T(8,128)(2,1)S(1)}, u32[]{:S(2)}, u32[]{:S(2)}) collective-permute-start(bf16[32,768]{1,0:T(8,128)(2,1)S(1)} %regroup.5.refs_7_.refs_0_), channel_id=1, source_target_pairs={{0,3},{1,2},{2,1},{3,0},{4,7},{5,6},{6,5},{7,4},{8,11},{9,10},{10,... | collective-permute-start | bytes 147464 | tf_op jit(solution)/shard_map/ppermute | solution.py:62
  12.5 3.6 %collective-permute-start.6 = (bf16[32,768]{1,0:T(8,128)(2,1)S(1)}, bf16[32,768]{1,0:T(8,128)(2,1)S(1)}, u32[]{:S(2)}, u32[]{:S(2)}) collective-permute-start(bf16[32,768]{1,0:T(8,128)(2,1)S(1)} %regroup.6.refs_1_.refs_3_), channel_id=1, source_target_pairs={{0,3},{1,2},{2,1},{3,0},{4,7},{5,6},{6,5},{7,4},{8,11},{9,10},{10,... | collective-permute-start | bytes 147464 | tf_op jit(solution)/shard_map/ppermute | solution.py:62
  12.9 1.4 %collective-permute-start.4 = (bf16[48,384]{1,0:T(8,128)(2,1)S(1)}, bf16[48,384]{1,0:T(8,128)(2,1)S(1)}, u32[]{:S(2)}, u32[]{:S(2)}) collective-permute-start(bf16[48,384]{1,0:T(8,128)(2,1)S(1)} %regroup.8), channel_id=1, source_target_pairs={{0,1},{1,0},{2,3},{3,2},{4,5},{5,4},{6,7},{7,6},{8,9},{9,8},{10,11... | collective-permute-start | bytes 110600 | tf_op jit(solution)/shard_map/ppermute | solution.py:71
  13.4 1.2 %collective-permute-start.5 = (bf16[48,384]{1,0:T(8,128)(2,1)S(1)}, bf16[48,384]{1,0:T(8,128)(2,1)S(1)}, u32[]{:S(2)}, u32[]{:S(2)}) collective-permute-start(bf16[48,384]{1,0:T(8,128)(2,1)S(1)} %regroup.9), channel_id=1, source_target_pairs={{0,1},{1,0},{2,3},{3,2},{4,5},{5,4},{6,7},{7,6},{8,9},{9,8},{10,11... | collective-permute-start | bytes 110600 | tf_op jit(solution)/shard_map/ppermute | solution.py:71
  16.6 1.3 %collective-permute-start.7 = (f32[24,128]{1,0:T(8,128)S(1)}, f32[24,128]{1,0:T(8,128)S(1)}, u32[]{:S(2)}, u32[]{:S(2)}) collective-permute-start(f32[24,128]{1,0:T(8,128)S(1)} %far.1), channel_id=1, source_target_pairs={{0,1},{1,0},{2,3},{3,2},{4,5},{5,4},{6,7},{7,6},{8,9},{9,8},{10,11... | collective-permute-start | bytes 36872 | tf_op jit(solution)/shard_map/ppermute | solution.py:71
  17.8 3.1 %collective-permute-start.8 = (f32[24,128]{1,0:T(8,128)S(1)}, f32[24,128]{1,0:T(8,128)S(1)}, u32[]{:S(2)}, u32[]{:S(2)}) collective-permute-start(f32[24,128]{1,0:T(8,128)S(1)} %add.6), channel_id=1, source_target_pairs={{0,3},{1,2},{2,1},{3,0},{4,7},{5,6},{6,5},{7,4},{8,11},{9,10},{10,... | collective-permute-start | bytes 36872 | tf_op jit(solution)/shard_map/ppermute | solution.py:62
  20.9 4.9 %collective-permute-start.9 = (f32[24,128]{1,0:T(8,128)S(1)}, f32[24,128]{1,0:T(8,128)S(1)}, u32[]{:S(2)}, u32[]{:S(2)}) collective-permute-start(f32[24,128]{1,0:T(8,128)S(1)} %add.7.refs_0_), channel_id=1, source_target_pairs={{0,5},{1,4},{4,9},{5,8},{8,13},{9,12},{12,1},{13,0},{2,7},{3,6},{6... | collective-permute-start | bytes 36872 | tf_op jit(solution)/shard_map/ppermute | solution.py:62
  21.3 4.5 %collective-permute-start.10 = (f32[24,128]{1,0:T(8,128)S(1)}, f32[24,128]{1,0:T(8,128)S(1)}, u32[]{:S(2)}, u32[]{:S(2)}) collective-permute-start(f32[24,128]{1,0:T(8,128)S(1)} %add.7.refs_0_), channel_id=1, source_target_pairs={{0,9},{1,8},{4,13},{5,12},{8,1},{9,0},{12,5},{13,4},{2,11},{3,10},... | collective-permute-start | bytes 36872 | tf_op jit(solution)/shard_map/ppermute | solution.py:62
  23.2 3.3 %collective-permute-start.11 = (f32[24,128]{1,0:T(8,128)S(1)}, f32[24,128]{1,0:T(8,128)S(1)}, u32[]{:S(2)}, u32[]{:S(2)}) collective-permute-start(f32[24,128]{1,0:T(8,128)S(1)} %add.7.refs_0_), channel_id=1, source_target_pairs={{0,13},{1,12},{4,1},{5,0},{8,5},{9,4},{12,9},{13,8},{2,15},{3,14},... | collective-permute-start | bytes 36872 | tf_op jit(solution)/shard_map/ppermute | solution.py:62

commit v22 on v21

--- a/solution.py
+++ b/solution.py
@@ -654,7 +654,8 @@
         piece = contract(ka, ba, dims, far_table, piece, coupled, far, "far")
     piece = piece + sum(handed(piece, r) for r in range(1, ba))
     piece = summed(piece, "ga")
-    pieces = [piece] + [shifted(piece, "ka", j) for j in range(1, ka)]
+    order = sorted(range(1, ka), key=lambda j: (-min(j, ka - j), j))
+    pieces = [piece] + [shifted(piece, "ka", j) for j in order]
     scale_count = float(kcount * pair_count)
     return tuple(haydock(ka, pair_count, scale_count, npol, pieces))
 

time: 28.1 us -> 28.4 us (1.011)
  starting transfers between devices: 14 us -> 14.9 us
  waiting for transfers between devices: 6.19 us -> 5.66 us
    ppermute x9, starting transfers between devices: 13 us -> 13.9 us  [exchanged(): return lax.ppermute(value, (axis, 'ba'), pairs)]
    ppermute x9, waiting for transfers between devices: 5.07 us -> 4.53 us  [exchanged(): return lax.ppermute(value, (axis, 'ba'), pairs)]
  transfers between devices with their start and end apart: 12 -> 12, of which waited for: 7 -> 6; matrix products, arithmetic and copies ran while one was open for 0% -> 0% of each run, Pallas kernels for 15% -> 15%
where the time goes in v22:
time: 28.4 us; the launch traced here: 28.3 us
  starting transfers between devices  14.9 us (52%)
  Pallas kernels  7.02 us (25%)
  waiting for transfers between devices  5.66 us (20%)
  between operations  0.72 us (3%)
    ppermute x9, starting transfers between devices, exchanged(): return lax.ppermute(value, (axis, 'ba'), pairs)  13.9 us
    ppermute x9, waiting for transfers between devices, exchanged(): return lax.ppermute(value, (axis, 'ba'), pairs)  4.53 us
    pallas_call x1, Pallas kernels, prepare(): pl.pallas_call(functools.partial(prepare_kernel, ka, dims), out_shape=[in...  2.45 us
    pallas_call x1, Pallas kernels, haydock(): pl.pallas_call(functools.partial(haydock_kernel, ka, codes, scale_count,...  1.41 us
    ppermute x3, waiting for transfers between devices, handed(): lax.ppermute(value, 'ba', [(h, (h + step) % size) for h in range(size)])  1.12 us
    pallas_call x1, Pallas kernels, pack(): pl.pallas_call(functools.partial(pack_kernel, ka), out_shape=[own] + [sha...  1.05 us
    ppermute x3, starting transfers between devices, handed(): lax.ppermute(value, 'ba', [(h, (h + step) % size) for h in range(size)])  1 us
    pallas_call x1, Pallas kernels, field(): pl.pallas_call(functools.partial(field_kernel, pairs), out_shape=in_vmem(...  0.78 us
  transfers between devices with their start and end apart: 12, of which 6 were waited for; matrix products, arithmetic and copies ran while one was open for 0% of the time, Pallas kernels for 15%

profile of v22, /device:TPU:0, one launch (start us, length us, event | category | flops | bytes accessed | tf_op | source)
XLA Modules:
  0.0 28.3 jit_solution(2189989057819139214)
XLA Ops:
  0.6 1.1 %pack.1 = (bf16[48,768]{1,0:T(8,128)(2,1)S(1)}, bf16[32,768]{1,0:T(8,128)(2,1)S(1)}, bf16[32,768]{1,0:T(8,128)(2,1)S(1)}, bf16[32,768]{1,0:T(8,128)(2,1)S(1)}) custom-call(s32[4,4]{1,0:T(4,128)} %refs_0_.1, s32[4]{0:T(128)} %refs_1_.1, bf16[1,4,2,2,4,768]{5,4,3,2,1,0:T(4,128)(2,1)} %valence_in.1, bf16[1,4,2,4,4,768]{5,4,3,2,1,0:T(4,128)(2,1)} %conduction_in.1), custom_call_target="tpu_custom_call" | custom-call | tf_op jit(solution)/shard_map/pack/pallas_call | solution.py:123
  1.7 2.5 %collective-permute-start = (bf16[32,768]{1,0:T(8,128)(2,1)S(1)}, bf16[32,768]{1,0:T(8,128)(2,1)S(1)}, u32[]{:S(2)}, u32[]{:S(2)}) collective-permute-start(bf16[32,768]{1,0:T(8,128)(2,1)S(1)} %get-tuple-element.11), channel_id=1, source_target_pairs={{0,5},{1,4},{4,9},{5,8},{8,13},{9,12},{12,1},{13,0},{2,7},{3,6},{6... | collective-permute-start | bytes 147464 | tf_op jit(solution)/shard_map/ppermute | solution.py:62
  4.2 2.9 %collective-permute-start.1 = (bf16[32,768]{1,0:T(8,128)(2,1)S(1)}, bf16[32,768]{1,0:T(8,128)(2,1)S(1)}, u32[]{:S(2)}, u32[]{:S(2)}) collective-permute-start(bf16[32,768]{1,0:T(8,128)(2,1)S(1)} %get-tuple-element.14), channel_id=1, source_target_pairs={{0,9},{1,8},{4,13},{5,12},{8,1},{9,0},{12,5},{13,4},{2,11},{3,10},... | collective-permute-start | bytes 147464 | tf_op jit(solution)/shard_map/ppermute | solution.py:62
  7.1 0.8 %collective-permute-start.2 = (bf16[32,768]{1,0:T(8,128)(2,1)S(1)}, bf16[32,768]{1,0:T(8,128)(2,1)S(1)}, u32[]{:S(2)}, u32[]{:S(2)}) collective-permute-start(bf16[32,768]{1,0:T(8,128)(2,1)S(1)} %get-tuple-element.15), channel_id=1, source_target_pairs={{0,13},{1,12},{4,1},{5,0},{8,5},{9,4},{12,9},{13,8},{2,15},{3,14},... | collective-permute-start | bytes 147464 | tf_op jit(solution)/shard_map/ppermute | solution.py:62
  7.9 0.1 collective-permute-done.refs_1_.refs_0_
  8.0 2.0 %collective-permute-start.3 = (bf16[32,768]{1,0:T(8,128)(2,1)S(1)}, bf16[32,768]{1,0:T(8,128)(2,1)S(1)}, u32[]{:S(2)}, u32[]{:S(2)}) collective-permute-start(bf16[32,768]{1,0:T(8,128)(2,1)S(1)} %regroup.5.refs_7_.refs_0_), channel_id=1, source_target_pairs={{0,3},{1,2},{2,1},{3,0},{4,7},{5,6},{6,5},{7,4},{8,11},{9,10},{10,... | collective-permute-start | bytes 147464 | tf_op jit(solution)/shard_map/ppermute | solution.py:62
  10.0 2.5 %prepare.1 = (bf16[2,768,1536]{2,1,0:T(8,128)(2,1)S(1)}, bf16[128,512]{1,0:T(8,128)(2,1)S(1)}, bf16[128,512]{1,0:T(8,128)(2,1)S(1)}, f32[8,128]{1,0:T(8,128)S(1)}) custom-call(s32[4,4]{1,0:T(4,128)} %refs_0_.1, s32[4]{0:T(128)} %refs_1_.1, s32[16]{0:T(128)} %refs_2_.1, f32[1,4]{1,0:T(1,128)} %refs_3_.1, f32[1,4]{1,0:T(1,128)} %refs_4_.1, ...), custom_call_target="tpu_custom_call" | custom-call | bytes 9437184 | tf_op jit(solution)/shard_map/prepare/pallas_call | solution.py:231
  12.5 0.0 collective-permute-done.1.refs_0_.refs_2_.refs_1_
  12.5 0.0 collective-permute-done.2.refs_1_.refs_3_.refs_2_
  12.5 0.4 %collective-permute-start.6 = (bf16[32,768]{1,0:T(8,128)(2,1)S(1)}, bf16[32,768]{1,0:T(8,128)(2,1)S(1)}, u32[]{:S(2)}, u32[]{:S(2)}) collective-permute-start(bf16[32,768]{1,0:T(8,128)(2,1)S(1)} %regroup.6.refs_1_.refs_3_), channel_id=1, source_target_pairs={{0,3},{1,2},{2,1},{3,0},{4,7},{5,6},{6,5},{7,4},{8,11},{9,10},{10,... | collective-permute-start | bytes 147464 | tf_op jit(solution)/shard_map/ppermute | solution.py:62
  12.9 0.0 collective-permute-done.3.refs_4_.refs_3_
  12.9 0.5 %collective-permute-start.4 = (bf16[48,384]{1,0:T(8,128)(2,1)S(1)}, bf16[48,384]{1,0:T(8,128)(2,1)S(1)}, u32[]{:S(2)}, u32[]{:S(2)}) collective-permute-start(bf16[48,384]{1,0:T(8,128)(2,1)S(1)} %regroup.8), channel_id=1, source_target_pairs={{0,1},{1,0},{2,3},{3,2},{4,5},{5,4},{6,7},{7,6},{8,9},{9,8},{10,11... | collective-permute-start | bytes 110600 | tf_op jit(solution)/shard_map/ppermute | solution.py:71
  13.4 0.1 collective-permute-start.5
  13.5 0.8 %field.1.refs_2_.refs_0_ = bf16[768,256]{1,0:T(8,128)(2,1)S(1)} custom-call(bf16[2,768,1536]{2,1,0:T(8,128)(2,1)S(1)} %get-tuple-element.13.screening, bf16[32,768]{1,0:T(8,128)(2,1)S(1)} %regroup.5.refs_7_.refs_0_, bf16[32,768]{1,0:T(8,128)(2,1)S(1)} %regroup.6.refs_1_.refs_3_), custom_call_target="tpu_custom_call" | custom-call | flops 1 | bytes 1 | tf_op jit(solution)/shard_map/field/pallas_call | solution.py:369
  14.3 0.0 collective-permute-done.4.refs_0_
  14.3 0.3 %collective-permute-done.5.refs_1_ = bf16[48,384]{1,0:T(8,128)(2,1)S(1)} collective-permute-done((bf16[48,384]{1,0:T(8,128)(2,1)S(1)}, bf16[48,384]{1,0:T(8,128)(2,1)S(1)}, u32[]{:S(2)}, u32[]{:S(2)}) %collective-permute-start.5) | collective-permute-done | bytes 36896 | tf_op jit(solution)/shard_map/ppermute | solution.py:71
  14.6 0.5 %couple.1.refs_2_ = bf16[256,768]{1,0:T(8,128)(2,1)S(1)} custom-call(bf16[2,768,1536]{2,1,0:T(8,128)(2,1)S(1)} %get-tuple-element.13.screening, bf16[64,768]{1,0:T(8,128)(2,1)S(1)} %regroup.7.refs_3_.refs_0_, bf16[64,768]{1,0:T(8,128)(2,1)S(1)} %assemble.1.refs_4_.refs_1_), custom_call_target="tpu_custom_call" | custom-call | flops 1 | bytes 1 | tf_op jit(solution)/shard_map/couple/pallas_call | solution.py:438
  15.1 0.4 %near.1.refs_1_ = f32[24,128]{1,0:T(8,128)S(1)} custom-call(bf16[768,256]{1,0:T(8,128)(2,1)S(1)} %field.1.refs_2_.refs_0_, bf16[128,512]{1,0:T(8,128)(2,1)S(1)} %get-tuple-element.17.refs_1_, f32[8,128]{1,0:T(8,128)S(1)} %get-tuple-element.16.refs_2_, bf16[64,768]{1,0:T(8,128)(2,1)S(1)} %regroup.7.refs_3_.refs_0_, bf16[64,768]{1,0:T(8,128)(2,1)S(1)} %assemble.1.refs_4_.refs_1_), custom_call_target="tpu_custom_call" | custom-call | flops 1 | bytes 1 | tf_op jit(solution)/shard_map/near/pallas_call | solution.py:398
  15.5 0.6 %collective-permute-done.6.refs_4_ = bf16[32,768]{1,0:T(8,128)(2,1)S(1)} collective-permute-done((bf16[32,768]{1,0:T(8,128)(2,1)S(1)}, bf16[32,768]{1,0:T(8,128)(2,1)S(1)}, u32[]{:S(2)}, u32[]{:S(2)}) %collective-permute-start.6) | collective-permute-done | bytes 49184 | tf_op jit(solution)/shard_map/ppermute | solution.py:62
  16.1 0.4 %far.1 = f32[24,128]{1,0:T(8,128)S(1)} custom-call(bf16[128,512]{1,0:T(8,128)(2,1)S(1)} %get-tuple-element.12.refs_0_, f32[24,128]{1,0:T(8,128)S(1)} %near.1.refs_1_, bf16[256,768]{1,0:T(8,128)(2,1)S(1)} %couple.1.refs_2_, bf16[32,768]{1,0:T(8,128)(2,1)S(1)} %collective-permute-done.3.refs_4_.refs_3_, bf16[32,768]{1,0:T(8,128)(2,1)S(1)} %collective-permute-done.6.refs_4_), custom_call_target="tpu_custom_call" | custom-call | flops 1 | bytes 1 | tf_op jit(solution)/shard_map/far/pallas_call | solution.py:476
  16.6 0.4 %collective-permute-start.7 = (f32[24,128]{1,0:T(8,128)S(1)}, f32[24,128]{1,0:T(8,128)S(1)}, u32[]{:S(2)}, u32[]{:S(2)}) collective-permute-start(f32[24,128]{1,0:T(8,128)S(1)} %far.1), channel_id=1, source_target_pairs={{0,1},{1,0},{2,3},{3,2},{4,5},{5,4},{6,7},{7,6},{8,9},{9,8},{10,11... | collective-permute-start | bytes 36872 | tf_op jit(solution)/shard_map/ppermute | solution.py:71
  17.0 0.8 %collective-permute-done.7 = f32[24,128]{1,0:T(8,128)S(1)} collective-permute-done((f32[24,128]{1,0:T(8,128)S(1)}, f32[24,128]{1,0:T(8,128)S(1)}, u32[]{:S(2)}, u32[]{:S(2)}) %collective-permute-start.7) | collective-permute-done | bytes 12320 | tf_op jit(solution)/shard_map/ppermute | solution.py:71
  17.8 0.8 %collective-permute-start.8 = (f32[24,128]{1,0:T(8,128)S(1)}, f32[24,128]{1,0:T(8,128)S(1)}, u32[]{:S(2)}, u32[]{:S(2)}) collective-permute-start(f32[24,128]{1,0:T(8,128)S(1)} %add.6), channel_id=1, source_target_pairs={{0,3},{1,2},{2,1},{3,0},{4,7},{5,6},{6,5},{7,4},{8,11},{9,10},{10,... | collective-permute-start | bytes 36872 | tf_op jit(solution)/shard_map/ppermute | solution.py:62
  18.6 2.4 %collective-permute-done.8 = f32[24,128]{1,0:T(8,128)S(1)} collective-permute-done((f32[24,128]{1,0:T(8,128)S(1)}, f32[24,128]{1,0:T(8,128)S(1)}, u32[]{:S(2)}, u32[]{:S(2)}) %collective-permute-start.8) | collective-permute-done | bytes 12320 | tf_op jit(solution)/shard_map/ppermute | solution.py:62
  20.9 1.0 %collective-permute-start.9 = (f32[24,128]{1,0:T(8,128)S(1)}, f32[24,128]{1,0:T(8,128)S(1)}, u32[]{:S(2)}, u32[]{:S(2)}) collective-permute-start(f32[24,128]{1,0:T(8,128)S(1)} %add.7.refs_0_), channel_id=1, source_target_pairs={{0,9},{1,8},{4,13},{5,12},{8,1},{9,0},{12,5},{13,4},{2,11},{3,10},... | collective-permute-start | bytes 36872 | tf_op jit(solution)/shard_map/ppermute | solution.py:62
  21.9 1.3 %collective-permute-start.10 = (f32[24,128]{1,0:T(8,128)S(1)}, f32[24,128]{1,0:T(8,128)S(1)}, u32[]{:S(2)}, u32[]{:S(2)}) collective-permute-start(f32[24,128]{1,0:T(8,128)S(1)} %add.7.refs_0_), channel_id=1, source_target_pairs={{0,5},{1,4},{4,9},{5,8},{8,13},{9,12},{12,1},{13,0},{2,7},{3,6},{6... | collective-permute-start | bytes 36872 | tf_op jit(solution)/shard_map/ppermute | solution.py:62
  23.2 2.2 %collective-permute-start.11 = (f32[24,128]{1,0:T(8,128)S(1)}, f32[24,128]{1,0:T(8,128)S(1)}, u32[]{:S(2)}, u32[]{:S(2)}) collective-permute-start(f32[24,128]{1,0:T(8,128)S(1)} %add.7.refs_0_), channel_id=1, source_target_pairs={{0,13},{1,12},{4,1},{5,0},{8,5},{9,4},{12,9},{13,8},{2,15},{3,14},... | collective-permute-start | bytes 36872 | tf_op jit(solution)/shard_map/ppermute | solution.py:62
  25.5 0.0 collective-permute-done.9.refs_1_
  25.5 1.4 %collective-permute-done.10.refs_2_ = f32[24,128]{1,0:T(8,128)S(1)} collective-permute-done((f32[24,128]{1,0:T(8,128)S(1)}, f32[24,128]{1,0:T(8,128)S(1)}, u32[]{:S(2)}, u32[]{:S(2)}) %collective-permute-start.10) | collective-permute-done | bytes 12320 | tf_op jit(solution)/shard_map/ppermute | solution.py:62
  26.8 0.0 collective-permute-done.11.refs_3_
  26.9 1.4 %haydock.1 = (f32[1,2,2,16]{3,2,1,0:T(2,128)}, f32[2,6]{1,0:T(2,128)}) custom-call(f32[24,128]{1,0:T(8,128)S(1)} %add.7.refs_0_, f32[24,128]{1,0:T(8,128)S(1)} %collective-permute-done.9.refs_1_, f32[24,128]{1,0:T(8,128)S(1)} %collective-permute-done.10.refs_2_, f32[24,128]{1,0:T(8,128)S(1)} %collective-permute-done.11.refs_3_), custom_call_target="tpu_custom_call" | custom-call | tf_op jit(solution)/shard_map/haydock/pallas_call | solution.py:573
  (8 shorter events, 0.0 us)
Async XLA Ops:
  1.7 6.3 %collective-permute-start = (bf16[32,768]{1,0:T(8,128)(2,1)S(1)}, bf16[32,768]{1,0:T(8,128)(2,1)S(1)}, u32[]{:S(2)}, u32[]{:S(2)}) collective-permute-start(bf16[32,768]{1,0:T(8,128)(2,1)S(1)} %get-tuple-element.11), channel_id=1, source_target_pairs={{0,5},{1,4},{4,9},{5,8},{8,13},{9,12},{12,1},{13,0},{2,7},{3,6},{6... | collective-permute-start | bytes 147464 | tf_op jit(solution)/shard_map/ppermute | solution.py:62
  4.2 8.3 %collective-permute-start.1 = (bf16[32,768]{1,0:T(8,128)(2,1)S(1)}, bf16[32,768]{1,0:T(8,128)(2,1)S(1)}, u32[]{:S(2)}, u32[]{:S(2)}) collective-permute-start(bf16[32,768]{1,0:T(8,128)(2,1)S(1)} %get-tuple-element.14), channel_id=1, source_target_pairs={{0,9},{1,8},{4,13},{5,12},{8,1},{9,0},{12,5},{13,4},{2,11},{3,10},... | collective-permute-start | bytes 147464 | tf_op jit(solution)/shard_map/ppermute | solution.py:62
  7.1 5.4 %collective-permute-start.2 = (bf16[32,768]{1,0:T(8,128)(2,1)S(1)}, bf16[32,768]{1,0:T(8,128)(2,1)S(1)}, u32[]{:S(2)}, u32[]{:S(2)}) collective-permute-start(bf16[32,768]{1,0:T(8,128)(2,1)S(1)} %get-tuple-element.15), channel_id=1, source_target_pairs={{0,13},{1,12},{4,1},{5,0},{8,5},{9,4},{12,9},{13,8},{2,15},{3,14},... | collective-permute-start | bytes 147464 | tf_op jit(solution)/shard_map/ppermute | solution.py:62
  8.0 4.9 %collective-permute-start.3 = (bf16[32,768]{1,0:T(8,128)(2,1)S(1)}, bf16[32,768]{1,0:T(8,128)(2,1)S(1)}, u32[]{:S(2)}, u32[]{:S(2)}) collective-permute-start(bf16[32,768]{1,0:T(8,128)(2,1)S(1)} %regroup.5.refs_7_.refs_0_), channel_id=1, source_target_pairs={{0,3},{1,2},{2,1},{3,0},{4,7},{5,6},{6,5},{7,4},{8,11},{9,10},{10,... | collective-permute-start | bytes 147464 | tf_op jit(solution)/shard_map/ppermute | solution.py:62
  12.5 3.6 %collective-permute-start.6 = (bf16[32,768]{1,0:T(8,128)(2,1)S(1)}, bf16[32,768]{1,0:T(8,128)(2,1)S(1)}, u32[]{:S(2)}, u32[]{:S(2)}) collective-permute-start(bf16[32,768]{1,0:T(8,128)(2,1)S(1)} %regroup.6.refs_1_.refs_3_), channel_id=1, source_target_pairs={{0,3},{1,2},{2,1},{3,0},{4,7},{5,6},{6,5},{7,4},{8,11},{9,10},{10,... | collective-permute-start | bytes 147464 | tf_op jit(solution)/shard_map/ppermute | solution.py:62
  12.9 1.4 %collective-permute-start.4 = (bf16[48,384]{1,0:T(8,128)(2,1)S(1)}, bf16[48,384]{1,0:T(8,128)(2,1)S(1)}, u32[]{:S(2)}, u32[]{:S(2)}) collective-permute-start(bf16[48,384]{1,0:T(8,128)(2,1)S(1)} %regroup.8), channel_id=1, source_target_pairs={{0,1},{1,0},{2,3},{3,2},{4,5},{5,4},{6,7},{7,6},{8,9},{9,8},{10,11... | collective-permute-start | bytes 110600 | tf_op jit(solution)/shard_map/ppermute | solution.py:71
  13.4 1.2 %collective-permute-start.5 = (bf16[48,384]{1,0:T(8,128)(2,1)S(1)}, bf16[48,384]{1,0:T(8,128)(2,1)S(1)}, u32[]{:S(2)}, u32[]{:S(2)}) collective-permute-start(bf16[48,384]{1,0:T(8,128)(2,1)S(1)} %regroup.9), channel_id=1, source_target_pairs={{0,1},{1,0},{2,3},{3,2},{4,5},{5,4},{6,7},{7,6},{8,9},{9,8},{10,11... | collective-permute-start | bytes 110600 | tf_op jit(solution)/shard_map/ppermute | solution.py:71
  16.6 1.3 %collective-permute-start.7 = (f32[24,128]{1,0:T(8,128)S(1)}, f32[24,128]{1,0:T(8,128)S(1)}, u32[]{:S(2)}, u32[]{:S(2)}) collective-permute-start(f32[24,128]{1,0:T(8,128)S(1)} %far.1), channel_id=1, source_target_pairs={{0,1},{1,0},{2,3},{3,2},{4,5},{5,4},{6,7},{7,6},{8,9},{9,8},{10,11... | collective-permute-start | bytes 36872 | tf_op jit(solution)/shard_map/ppermute | solution.py:71
  17.8 3.1 %collective-permute-start.8 = (f32[24,128]{1,0:T(8,128)S(1)}, f32[24,128]{1,0:T(8,128)S(1)}, u32[]{:S(2)}, u32[]{:S(2)}) collective-permute-start(f32[24,128]{1,0:T(8,128)S(1)} %add.6), channel_id=1, source_target_pairs={{0,3},{1,2},{2,1},{3,0},{4,7},{5,6},{6,5},{7,4},{8,11},{9,10},{10,... | collective-permute-start | bytes 36872 | tf_op jit(solution)/shard_map/ppermute | solution.py:62
  20.9 4.5 %collective-permute-start.9 = (f32[24,128]{1,0:T(8,128)S(1)}, f32[24,128]{1,0:T(8,128)S(1)}, u32[]{:S(2)}, u32[]{:S(2)}) collective-permute-start(f32[24,128]{1,0:T(8,128)S(1)} %add.7.refs_0_), channel_id=1, source_target_pairs={{0,9},{1,8},{4,13},{5,12},{8,1},{9,0},{12,5},{13,4},{2,11},{3,10},... | collective-permute-start | bytes 36872 | tf_op jit(solution)/shard_map/ppermute | solution.py:62
  21.9 4.9 %collective-permute-start.10 = (f32[24,128]{1,0:T(8,128)S(1)}, f32[24,128]{1,0:T(8,128)S(1)}, u32[]{:S(2)}, u32[]{:S(2)}) collective-permute-start(f32[24,128]{1,0:T(8,128)S(1)} %add.7.refs_0_), channel_id=1, source_target_pairs={{0,5},{1,4},{4,9},{5,8},{8,13},{9,12},{12,1},{13,0},{2,7},{3,6},{6... | collective-permute-start | bytes 36872 | tf_op jit(solution)/shard_map/ppermute | solution.py:62
  23.2 3.6 %collective-permute-start.11 = (f32[24,128]{1,0:T(8,128)S(1)}, f32[24,128]{1,0:T(8,128)S(1)}, u32[]{:S(2)}, u32[]{:S(2)}) collective-permute-start(f32[24,128]{1,0:T(8,128)S(1)} %add.7.refs_0_), channel_id=1, source_target_pairs={{0,13},{1,12},{4,1},{5,0},{8,5},{9,4},{12,9},{13,8},{2,15},{3,14},... | collective-permute-start | bytes 36872 | tf_op jit(solution)/shard_map/ppermute | solution.py:62

commit v23 on v21

--- a/solution.py
+++ b/solution.py
@@ -42,6 +42,10 @@
 def limits(*arrays):
     held = sum(math.prod(a.shape) * a.dtype.itemsize for a in arrays)
     return pltpu.CompilerParams(vmem_limit_bytes=min(VMEM_MOST, VMEM_LEAST + 4 * held))
+
+
+def order(size):
+    return [0] + sorted(range(1, size), key=lambda j: (-min(j, size - j), j))
 
 
 def target(me, step, size):
@@ -100,7 +104,7 @@
     copies[2].wait()
     copies[3].wait()
     for at in range(ka):
-        k2 = partner[target(me, at, ka)]
+        k2 = partner[target(me, order(ka)[at], ka)]
         block = valence[0, k2].astype(jnp.float32).reshape(val_rows, width)
         outs[at][:val_rows, :] = block.astype(jnp.bfloat16)
         to = lax.rem(half + min(at, 1), lax.axis_size("ba"))
@@ -172,12 +176,16 @@
     row = iota((2 * rows, lanes), 0)
     col = iota((2 * rows, lanes), 1)
     j_of_row = row % rows // block
+    position = iota((2 * rows, 1), 0) % rows // block
+    step = jnp.zeros((2 * rows, 1), jnp.int32)
+    for at, j in enumerate(order(ka)):
+        step = jnp.where(position == at, j, step)
     cores = lax.axis_size("ba")
     for moves, table in enumerate((near_table, far_table)):
         share = lax.rem(half + 2 * cores - moves - jnp.where(j_of_row == 0, 0, 1), cores)
         want = (
             (row % block // pairs) * mid
-            + origin(me, j_of_row, ka) * codes
+            + origin(me, step, ka) * codes
             + (share * vloc + row % pairs // val_count) * cond_count
         )
         joined = (col - want >= 0) & (col - want < cond_count)
@@ -615,7 +623,7 @@
     pairs = vloc * val_count
     dims = (vloc, val_count, cond_count, npol)
     packed = pack(ka, ba, qpoint_map, slot_owner, valence_density, conduction_density)
-    blocks = [packed[0]] + [shifted(packed[j], "ka", j) for j in range(1, ka)]
+    blocks = [packed[0]] + [shifted(packed[at], "ka", j) for at, j in enumerate(order(ka)) if at]
     early = ka // 2
     val_rows = slice(0, 2 * pairs)
     val_early = regroup(blocks[:early], val_rows)

time: 28.1 us -> 29.8 us (1.060)
  waiting for transfers between devices: 6.19 us -> 8.29 us
  starting transfers between devices: 14 us -> 13.6 us
    ppermute x9, waiting for transfers between devices: 5.07 us -> 6.91 us  [exchanged(): return lax.ppermute(value, (axis, 'ba'), pairs)]
  transfers between devices with their start and end apart: 12 -> 12, of which waited for: 7 -> 6; matrix products, arithmetic and copies ran while one was open for 0% -> 0% of each run, Pallas kernels for 15% -> 14%
where the time goes in v23:
time: 29.8 us; the launch traced here: 29.7 us
  starting transfers between devices  13.6 us (46%)
  waiting for transfers between devices  8.29 us (28%)
  Pallas kernels  7.02 us (24%)
  between operations  0.72 us (2%)
    ppermute x9, starting transfers between devices, exchanged(): return lax.ppermute(value, (axis, 'ba'), pairs)  12.8 us
    ppermute x9, waiting for transfers between devices, exchanged(): return lax.ppermute(value, (axis, 'ba'), pairs)  6.91 us
    pallas_call x1, Pallas kernels, prepare(): pl.pallas_call(functools.partial(prepare_kernel, ka, dims), out_shape=[in...  2.45 us
    pallas_call x1, Pallas kernels, haydock(): pl.pallas_call(functools.partial(haydock_kernel, ka, codes, scale_count,...  1.41 us
    ppermute x3, waiting for transfers between devices, handed(): lax.ppermute(value, 'ba', [(h, (h + step) % size) for h in range(size)])  1.38 us
    pallas_call x1, Pallas kernels, pack(): pl.pallas_call(functools.partial(pack_kernel, ka), out_shape=[own] + [sha...  1.05 us
    ppermute x3, starting transfers between devices, handed(): lax.ppermute(value, 'ba', [(h, (h + step) % size) for h in range(size)])  0.82 us
    pallas_call x1, Pallas kernels, field(): pl.pallas_call(functools.partial(field_kernel, pairs), out_shape=in_vmem(...  0.77 us
  transfers between devices with their start and end apart: 12, of which 6 were waited for; matrix products, arithmetic and copies ran while one was open for 0% of the time, Pallas kernels for 14%

profile of v23, /device:TPU:0, one launch (start us, length us, event | category | flops | bytes accessed | tf_op | source)
XLA Modules:
  0.0 29.7 jit_solution(3583292563642465882)
XLA Ops:
  0.6 1.1 %pack.1 = (bf16[48,768]{1,0:T(8,128)(2,1)S(1)}, bf16[32,768]{1,0:T(8,128)(2,1)S(1)}, bf16[32,768]{1,0:T(8,128)(2,1)S(1)}, bf16[32,768]{1,0:T(8,128)(2,1)S(1)}) custom-call(s32[4,4]{1,0:T(4,128)} %refs_0_.1, s32[4]{0:T(128)} %refs_1_.1, bf16[1,4,2,2,4,768]{5,4,3,2,1,0:T(4,128)(2,1)} %valence_in.1, bf16[1,4,2,4,4,768]{5,4,3,2,1,0:T(4,128)(2,1)} %conduction_in.1), custom_call_target="tpu_custom_call" | custom-call | tf_op jit(solution)/shard_map/pack/pallas_call | solution.py:127
  1.7 3.5 %collective-permute-start = (bf16[32,768]{1,0:T(8,128)(2,1)S(1)}, bf16[32,768]{1,0:T(8,128)(2,1)S(1)}, u32[]{:S(2)}, u32[]{:S(2)}) collective-permute-start(bf16[32,768]{1,0:T(8,128)(2,1)S(1)} %get-tuple-element.11), channel_id=1, source_target_pairs={{0,9},{1,8},{4,13},{5,12},{8,1},{9,0},{12,5},{13,4},{2,11},{3,10},... | collective-permute-start | bytes 147464 | tf_op jit(solution)/shard_map/ppermute | solution.py:66
  5.2 1.9 %collective-permute-start.1 = (bf16[32,768]{1,0:T(8,128)(2,1)S(1)}, bf16[32,768]{1,0:T(8,128)(2,1)S(1)}, u32[]{:S(2)}, u32[]{:S(2)}) collective-permute-start(bf16[32,768]{1,0:T(8,128)(2,1)S(1)} %get-tuple-element.14), channel_id=1, source_target_pairs={{0,5},{1,4},{4,9},{5,8},{8,13},{9,12},{12,1},{13,0},{2,7},{3,6},{6... | collective-permute-start | bytes 147464 | tf_op jit(solution)/shard_map/ppermute | solution.py:66
  7.1 1.7 %collective-permute-start.2 = (bf16[32,768]{1,0:T(8,128)(2,1)S(1)}, bf16[32,768]{1,0:T(8,128)(2,1)S(1)}, u32[]{:S(2)}, u32[]{:S(2)}) collective-permute-start(bf16[32,768]{1,0:T(8,128)(2,1)S(1)} %get-tuple-element.15), channel_id=1, source_target_pairs={{0,13},{1,12},{4,1},{5,0},{8,5},{9,4},{12,9},{13,8},{2,15},{3,14},... | collective-permute-start | bytes 147464 | tf_op jit(solution)/shard_map/ppermute | solution.py:66
  8.8 0.0 collective-permute-done.refs_1_.refs_0_
  8.8 1.8 %collective-permute-start.3 = (bf16[32,768]{1,0:T(8,128)(2,1)S(1)}, bf16[32,768]{1,0:T(8,128)(2,1)S(1)}, u32[]{:S(2)}, u32[]{:S(2)}) collective-permute-start(bf16[32,768]{1,0:T(8,128)(2,1)S(1)} %regroup.5.refs_7_.refs_0_), channel_id=1, source_target_pairs={{0,3},{1,2},{2,1},{3,0},{4,7},{5,6},{6,5},{7,4},{8,11},{9,10},{10,... | collective-permute-start | bytes 147464 | tf_op jit(solution)/shard_map/ppermute | solution.py:66
  10.6 2.5 %prepare.1 = (bf16[2,768,1536]{2,1,0:T(8,128)(2,1)S(1)}, bf16[128,512]{1,0:T(8,128)(2,1)S(1)}, bf16[128,512]{1,0:T(8,128)(2,1)S(1)}, f32[8,128]{1,0:T(8,128)S(1)}) custom-call(s32[4,4]{1,0:T(4,128)} %refs_0_.1, s32[4]{0:T(128)} %refs_1_.1, s32[16]{0:T(128)} %refs_2_.1, f32[1,4]{1,0:T(1,128)} %refs_3_.1, f32[1,4]{1,0:T(1,128)} %refs_4_.1, ...), custom_call_target="tpu_custom_call" | custom-call | bytes 9437184 | tf_op jit(solution)/shard_map/prepare/pallas_call | solution.py:239
  13.1 0.0 collective-permute-done.1.refs_0_.refs_2_.refs_1_
  13.1 0.0 collective-permute-done.2.refs_1_.refs_3_.refs_2_
  13.1 0.2 collective-permute-start.6
  13.3 0.0 collective-permute-done.3.refs_4_.refs_3_
  13.3 0.6 %collective-permute-start.4 = (bf16[48,384]{1,0:T(8,128)(2,1)S(1)}, bf16[48,384]{1,0:T(8,128)(2,1)S(1)}, u32[]{:S(2)}, u32[]{:S(2)}) collective-permute-start(bf16[48,384]{1,0:T(8,128)(2,1)S(1)} %regroup.8), channel_id=1, source_target_pairs={{0,1},{1,0},{2,3},{3,2},{4,5},{5,4},{6,7},{7,6},{8,9},{9,8},{10,11... | collective-permute-start | bytes 110600 | tf_op jit(solution)/shard_map/ppermute | solution.py:75
  13.9 0.1 collective-permute-start.5
  14.0 0.8 %field.1.refs_2_.refs_0_ = bf16[768,256]{1,0:T(8,128)(2,1)S(1)} custom-call(bf16[2,768,1536]{2,1,0:T(8,128)(2,1)S(1)} %get-tuple-element.13.screening, bf16[32,768]{1,0:T(8,128)(2,1)S(1)} %regroup.5.refs_7_.refs_0_, bf16[32,768]{1,0:T(8,128)(2,1)S(1)} %regroup.6.refs_1_.refs_3_), custom_call_target="tpu_custom_call" | custom-call | flops 1 | bytes 1 | tf_op jit(solution)/shard_map/field/pallas_call | solution.py:377
  14.8 0.0 collective-permute-done.4.refs_0_
  14.8 0.3 %collective-permute-done.5.refs_1_ = bf16[48,384]{1,0:T(8,128)(2,1)S(1)} collective-permute-done((bf16[48,384]{1,0:T(8,128)(2,1)S(1)}, bf16[48,384]{1,0:T(8,128)(2,1)S(1)}, u32[]{:S(2)}, u32[]{:S(2)}) %collective-permute-start.5) | collective-permute-done | bytes 36896 | tf_op jit(solution)/shard_map/ppermute | solution.py:75
  15.1 0.5 %couple.1.refs_2_ = bf16[256,768]{1,0:T(8,128)(2,1)S(1)} custom-call(bf16[2,768,1536]{2,1,0:T(8,128)(2,1)S(1)} %get-tuple-element.13.screening, bf16[64,768]{1,0:T(8,128)(2,1)S(1)} %regroup.7.refs_3_.refs_0_, bf16[64,768]{1,0:T(8,128)(2,1)S(1)} %assemble.1.refs_4_.refs_1_), custom_call_target="tpu_custom_call" | custom-call | flops 1 | bytes 1 | tf_op jit(solution)/shard_map/couple/pallas_call | solution.py:446
  15.6 0.4 %near.1.refs_1_ = f32[24,128]{1,0:T(8,128)S(1)} custom-call(bf16[768,256]{1,0:T(8,128)(2,1)S(1)} %field.1.refs_2_.refs_0_, bf16[128,512]{1,0:T(8,128)(2,1)S(1)} %get-tuple-element.17.refs_1_, f32[8,128]{1,0:T(8,128)S(1)} %get-tuple-element.16.refs_2_, bf16[64,768]{1,0:T(8,128)(2,1)S(1)} %regroup.7.refs_3_.refs_0_, bf16[64,768]{1,0:T(8,128)(2,1)S(1)} %assemble.1.refs_4_.refs_1_), custom_call_target="tpu_custom_call" | custom-call | flops 1 | bytes 1 | tf_op jit(solution)/shard_map/near/pallas_call | solution.py:406
  16.0 1.2 %collective-permute-done.6.refs_4_ = bf16[32,768]{1,0:T(8,128)(2,1)S(1)} collective-permute-done((bf16[32,768]{1,0:T(8,128)(2,1)S(1)}, bf16[32,768]{1,0:T(8,128)(2,1)S(1)}, u32[]{:S(2)}, u32[]{:S(2)}) %collective-permute-start.6) | collective-permute-done | bytes 49184 | tf_op jit(solution)/shard_map/ppermute | solution.py:66
  17.2 0.4 %far.1 = f32[24,128]{1,0:T(8,128)S(1)} custom-call(bf16[128,512]{1,0:T(8,128)(2,1)S(1)} %get-tuple-element.12.refs_0_, f32[24,128]{1,0:T(8,128)S(1)} %near.1.refs_1_, bf16[256,768]{1,0:T(8,128)(2,1)S(1)} %couple.1.refs_2_, bf16[32,768]{1,0:T(8,128)(2,1)S(1)} %collective-permute-done.3.refs_4_.refs_3_, bf16[32,768]{1,0:T(8,128)(2,1)S(1)} %collective-permute-done.6.refs_4_), custom_call_target="tpu_custom_call" | custom-call | flops 1 | bytes 1 | tf_op jit(solution)/shard_map/far/pallas_call | solution.py:484
  17.6 0.2 collective-permute-start.7
  17.8 1.1 %collective-permute-done.7 = f32[24,128]{1,0:T(8,128)S(1)} collective-permute-done((f32[24,128]{1,0:T(8,128)S(1)}, f32[24,128]{1,0:T(8,128)S(1)}, u32[]{:S(2)}, u32[]{:S(2)}) %collective-permute-start.7) | collective-permute-done | bytes 12320 | tf_op jit(solution)/shard_map/ppermute | solution.py:75
  18.9 0.1 collective-permute-start.8
  19.0 3.0 %collective-permute-done.8 = f32[24,128]{1,0:T(8,128)S(1)} collective-permute-done((f32[24,128]{1,0:T(8,128)S(1)}, f32[24,128]{1,0:T(8,128)S(1)}, u32[]{:S(2)}, u32[]{:S(2)}) %collective-permute-start.8) | collective-permute-done | bytes 12320 | tf_op jit(solution)/shard_map/ppermute | solution.py:66
  22.0 0.0 collective-permute-start.9
  22.0 3.1 %collective-permute-start.10 = (f32[24,128]{1,0:T(8,128)S(1)}, f32[24,128]{1,0:T(8,128)S(1)}, u32[]{:S(2)}, u32[]{:S(2)}) collective-permute-start(f32[24,128]{1,0:T(8,128)S(1)} %add.7.refs_0_), channel_id=1, source_target_pairs={{0,9},{1,8},{4,13},{5,12},{8,1},{9,0},{12,5},{13,4},{2,11},{3,10},... | collective-permute-start | bytes 36872 | tf_op jit(solution)/shard_map/ppermute | solution.py:66
  25.1 0.4 %collective-permute-start.11 = (f32[24,128]{1,0:T(8,128)S(1)}, f32[24,128]{1,0:T(8,128)S(1)}, u32[]{:S(2)}, u32[]{:S(2)}) collective-permute-start(f32[24,128]{1,0:T(8,128)S(1)} %add.7.refs_0_), channel_id=1, source_target_pairs={{0,13},{1,12},{4,1},{5,0},{8,5},{9,4},{12,9},{13,8},{2,15},{3,14},... | collective-permute-start | bytes 36872 | tf_op jit(solution)/shard_map/ppermute | solution.py:66
  25.5 1.4 %collective-permute-done.9.refs_1_ = f32[24,128]{1,0:T(8,128)S(1)} collective-permute-done((f32[24,128]{1,0:T(8,128)S(1)}, f32[24,128]{1,0:T(8,128)S(1)}, u32[]{:S(2)}, u32[]{:S(2)}) %collective-permute-start.9) | collective-permute-done | bytes 12320 | tf_op jit(solution)/shard_map/ppermute | solution.py:66
  26.9 0.0 collective-permute-done.10.refs_2_
  26.9 1.3 %collective-permute-done.11.refs_3_ = f32[24,128]{1,0:T(8,128)S(1)} collective-permute-done((f32[24,128]{1,0:T(8,128)S(1)}, f32[24,128]{1,0:T(8,128)S(1)}, u32[]{:S(2)}, u32[]{:S(2)}) %collective-permute-start.11) | collective-permute-done | bytes 12320 | tf_op jit(solution)/shard_map/ppermute | solution.py:66
  28.3 1.4 %haydock.1 = (f32[1,2,2,16]{3,2,1,0:T(2,128)}, f32[2,6]{1,0:T(2,128)}) custom-call(f32[24,128]{1,0:T(8,128)S(1)} %add.7.refs_0_, f32[24,128]{1,0:T(8,128)S(1)} %collective-permute-done.9.refs_1_, f32[24,128]{1,0:T(8,128)S(1)} %collective-permute-done.10.refs_2_, f32[24,128]{1,0:T(8,128)S(1)} %collective-permute-done.11.refs_3_), custom_call_target="tpu_custom_call" | custom-call | tf_op jit(solution)/shard_map/haydock/pallas_call | solution.py:581
  (8 shorter events, 0.0 us)
Async XLA Ops:
  1.7 7.1 %collective-permute-start = (bf16[32,768]{1,0:T(8,128)(2,1)S(1)}, bf16[32,768]{1,0:T(8,128)(2,1)S(1)}, u32[]{:S(2)}, u32[]{:S(2)}) collective-permute-start(bf16[32,768]{1,0:T(8,128)(2,1)S(1)} %get-tuple-element.11), channel_id=1, source_target_pairs={{0,9},{1,8},{4,13},{5,12},{8,1},{9,0},{12,5},{13,4},{2,11},{3,10},... | collective-permute-start | bytes 147464 | tf_op jit(solution)/shard_map/ppermute | solution.py:66
  5.2 7.8 %collective-permute-start.1 = (bf16[32,768]{1,0:T(8,128)(2,1)S(1)}, bf16[32,768]{1,0:T(8,128)(2,1)S(1)}, u32[]{:S(2)}, u32[]{:S(2)}) collective-permute-start(bf16[32,768]{1,0:T(8,128)(2,1)S(1)} %get-tuple-element.14), channel_id=1, source_target_pairs={{0,5},{1,4},{4,9},{5,8},{8,13},{9,12},{12,1},{13,0},{2,7},{3,6},{6... | collective-permute-start | bytes 147464 | tf_op jit(solution)/shard_map/ppermute | solution.py:66
  7.1 6.0 %collective-permute-start.2 = (bf16[32,768]{1,0:T(8,128)(2,1)S(1)}, bf16[32,768]{1,0:T(8,128)(2,1)S(1)}, u32[]{:S(2)}, u32[]{:S(2)}) collective-permute-start(bf16[32,768]{1,0:T(8,128)(2,1)S(1)} %get-tuple-element.15), channel_id=1, source_target_pairs={{0,13},{1,12},{4,1},{5,0},{8,5},{9,4},{12,9},{13,8},{2,15},{3,14},... | collective-permute-start | bytes 147464 | tf_op jit(solution)/shard_map/ppermute | solution.py:66
  8.8 4.6 %collective-permute-start.3 = (bf16[32,768]{1,0:T(8,128)(2,1)S(1)}, bf16[32,768]{1,0:T(8,128)(2,1)S(1)}, u32[]{:S(2)}, u32[]{:S(2)}) collective-permute-start(bf16[32,768]{1,0:T(8,128)(2,1)S(1)} %regroup.5.refs_7_.refs_0_), channel_id=1, source_target_pairs={{0,3},{1,2},{2,1},{3,0},{4,7},{5,6},{6,5},{7,4},{8,11},{9,10},{10,... | collective-permute-start | bytes 147464 | tf_op jit(solution)/shard_map/ppermute | solution.py:66
  13.1 4.1 %collective-permute-start.6 = (bf16[32,768]{1,0:T(8,128)(2,1)S(1)}, bf16[32,768]{1,0:T(8,128)(2,1)S(1)}, u32[]{:S(2)}, u32[]{:S(2)}) collective-permute-start(bf16[32,768]{1,0:T(8,128)(2,1)S(1)} %regroup.6.refs_1_.refs_3_), channel_id=1, source_target_pairs={{0,3},{1,2},{2,1},{3,0},{4,7},{5,6},{6,5},{7,4},{8,11},{9,10},{10,... | collective-permute-start | bytes 147464 | tf_op jit(solution)/shard_map/ppermute | solution.py:66
  13.3 1.4 %collective-permute-start.4 = (bf16[48,384]{1,0:T(8,128)(2,1)S(1)}, bf16[48,384]{1,0:T(8,128)(2,1)S(1)}, u32[]{:S(2)}, u32[]{:S(2)}) collective-permute-start(bf16[48,384]{1,0:T(8,128)(2,1)S(1)} %regroup.8), channel_id=1, source_target_pairs={{0,1},{1,0},{2,3},{3,2},{4,5},{5,4},{6,7},{7,6},{8,9},{9,8},{10,11... | collective-permute-start | bytes 110600 | tf_op jit(solution)/shard_map/ppermute | solution.py:75
  13.9 1.2 %collective-permute-start.5 = (bf16[48,384]{1,0:T(8,128)(2,1)S(1)}, bf16[48,384]{1,0:T(8,128)(2,1)S(1)}, u32[]{:S(2)}, u32[]{:S(2)}) collective-permute-start(bf16[48,384]{1,0:T(8,128)(2,1)S(1)} %regroup.9), channel_id=1, source_target_pairs={{0,1},{1,0},{2,3},{3,2},{4,5},{5,4},{6,7},{7,6},{8,9},{9,8},{10,11... | collective-permute-start | bytes 110600 | tf_op jit(solution)/shard_map/ppermute | solution.py:75
  17.6 1.2 %collective-permute-start.7 = (f32[24,128]{1,0:T(8,128)S(1)}, f32[24,128]{1,0:T(8,128)S(1)}, u32[]{:S(2)}, u32[]{:S(2)}) collective-permute-start(f32[24,128]{1,0:T(8,128)S(1)} %far.1), channel_id=1, source_target_pairs={{0,1},{1,0},{2,3},{3,2},{4,5},{5,4},{6,7},{7,6},{8,9},{9,8},{10,11... | collective-permute-start | bytes 36872 | tf_op jit(solution)/shard_map/ppermute | solution.py:75
  18.9 3.1 %collective-permute-start.8 = (f32[24,128]{1,0:T(8,128)S(1)}, f32[24,128]{1,0:T(8,128)S(1)}, u32[]{:S(2)}, u32[]{:S(2)}) collective-permute-start(f32[24,128]{1,0:T(8,128)S(1)} %add.6), channel_id=1, source_target_pairs={{0,3},{1,2},{2,1},{3,0},{4,7},{5,6},{6,5},{7,4},{8,11},{9,10},{10,... | collective-permute-start | bytes 36872 | tf_op jit(solution)/shard_map/ppermute | solution.py:66
  22.0 4.9 %collective-permute-start.9 = (f32[24,128]{1,0:T(8,128)S(1)}, f32[24,128]{1,0:T(8,128)S(1)}, u32[]{:S(2)}, u32[]{:S(2)}) collective-permute-start(f32[24,128]{1,0:T(8,128)S(1)} %add.7.refs_0_), channel_id=1, source_target_pairs={{0,5},{1,4},{4,9},{5,8},{8,13},{9,12},{12,1},{13,0},{2,7},{3,6},{6... | collective-permute-start | bytes 36872 | tf_op jit(solution)/shard_map/ppermute | solution.py:66
  22.0 4.9 %collective-permute-start.10 = (f32[24,128]{1,0:T(8,128)S(1)}, f32[24,128]{1,0:T(8,128)S(1)}, u32[]{:S(2)}, u32[]{:S(2)}) collective-permute-start(f32[24,128]{1,0:T(8,128)S(1)} %add.7.refs_0_), channel_id=1, source_target_pairs={{0,9},{1,8},{4,13},{5,12},{8,1},{9,0},{12,5},{13,4},{2,11},{3,10},... | collective-permute-start | bytes 36872 | tf_op jit(solution)/shard_map/ppermute | solution.py:66
  25.1 3.1 %collective-permute-start.11 = (f32[24,128]{1,0:T(8,128)S(1)}, f32[24,128]{1,0:T(8,128)S(1)}, u32[]{:S(2)}, u32[]{:S(2)}) collective-permute-start(f32[24,128]{1,0:T(8,128)S(1)} %add.7.refs_0_), channel_id=1, source_target_pairs={{0,13},{1,12},{4,1},{5,0},{8,5},{9,4},{12,9},{13,8},{2,15},{3,14},... | collective-permute-start | bytes 36872 | tf_op jit(solution)/shard_map/ppermute | solution.py:66
